TPU v7x, 32 devices: a whole 2x2x4 slice. The times are simulated.
32 devices in a mesh: dp: 8 (over z, y), chan: 4 (over x, core).
Axes of the slice: x: 2, y: 2, z: 4, core: 2. Of those that a mesh axis runs over, the one named last changes fastest.
Arguments:
- images: bfloat16 [64, 256, 256], P(None, 'dp'), may hold values from -14 to 14
- mask: int32 [64, 64], P('dp'), may hold values from 0 to 1, as said below
- cotangent: bfloat16 [64, 64, 512], P('dp', None, 'chan'), may hold values from -14 to 14
- w_first: float32 [2304, 512], P('dp', 'chan'), may hold values from -0.125 to 0.125
- w_second: float32 [4608, 512], P('dp', 'chan'), may hold values from -0.09375 to 0.09375
- w_proj: float32 [256, 512], P('dp', 'chan'), may hold values from -0.375 to 0.375
- norm_params: float32 [6, 512], P(None, 'chan'), may hold values from -2.8 to 2.8, as said below
- mom_first: float32 [2304, 512], P('dp', 'chan'), may hold values from -0.0625 to 0.0625
- mom_second: float32 [4608, 512], P('dp', 'chan'), may hold values from -0.046875 to 0.046875
- mom_proj: float32 [256, 512], P('dp', 'chan'), may hold values from -0.1875 to 0.1875
- mom_norm: float32 [6, 512], P(None, 'chan'), may hold values from -1.8 to 1.8
- avg_first: float32 [2304, 512], P('dp', 'chan'), may hold values from -0.125 to 0.125
- avg_second: float32 [4608, 512], P('dp', 'chan'), may hold values from -0.09375 to 0.09375
- avg_proj: float32 [256, 512], P('dp', 'chan'), may hold values from -0.375 to 0.375
- avg_norm: float32 [6, 512], P(None, 'chan'), may hold values from 0.5 to 1.5
Outputs:
- output: bfloat16 [64, 64, 512], P('dp', None, 'chan')
- grad_images: bfloat16 [64, 256, 256], P(None, 'dp', 'chan')
- new_first: float32 [2304, 512], P('dp', 'chan')
- new_mom_first: float32 [2304, 512], P('dp', 'chan')
- new_avg_first: float32 [2304, 512], P('dp', 'chan')
- new_second: float32 [4608, 512], P('dp', 'chan')
- new_mom_second: float32 [4608, 512], P('dp', 'chan')
- new_avg_second: float32 [4608, 512], P('dp', 'chan')
- new_proj: float32 [256, 512], P('dp', 'chan')
- new_mom_proj: float32 [256, 512], P('dp', 'chan')
- new_avg_proj: float32 [256, 512], P('dp', 'chan')
- new_norm: float32 [6, 512], P(None, 'chan')
- new_mom_norm: float32 [6, 512], P(None, 'chan')
- new_avg_norm: float32 [6, 512], P(None, 'chan')
Inputs may be any that keep to these rules, and one draw needn't show every extreme that they name: `mask`: each image's valid output pixels form a rectangle of h by w pixels at its top-left corner, with h and w at least 3. So every gradient of an output-side array is zero outside that rectangle, grad_hidden is zero outside the first h + 1 rows and w + 1 columns of its image, and the input's gradient is zero outside the first 2 h rows and 2 w columns of its image; a program may send only the pixels outside these zero regions. `norm_params`: rows 0, 2 and 4 are positive.
All inputs are finite; a program needn't handle non-finite values.
Results may differ from a plain program's by a relative error of at most 0.0075.
Values may be sent and summed in bfloat16 or wider, within the bound.
No kernel may reach another device: no remote copies, remote signals or barrier semaphores. Data moves between devices by JAX's collectives and lax.ppermute only.
A program may use at most 64 MiB of HBM per device.

v0:
```python
import jax
import jax.numpy as jnp
from jax import lax
from jax.experimental import pallas as pl
from jax.experimental.pallas import tpu as pltpu
from jax.sharding import PartitionSpec as P

BF = jnp.bfloat16
F32 = jnp.float32

epsilon = 1e-05
learn_rate = 0.4
trust_coef = 0.5
momentum = 0.5
avg_decay = 0.6
weight_decay = 5e-05
tiny_term = 1e-06

SIDE = 8
TAIL = 16


class whole:
    def __init__(self, array):
        self.arrays, self.dims, self.dtype = [array], array.shape, array.dtype

    def copies(self):
        return len(self.arrays)

    def plan(self, refs, local):
        return [(refs[0], local)]


class stack(whole):
    def __init__(self, arrays, slot):
        self.arrays, self.dtype = list(arrays), arrays[0].dtype
        self.dims, self.slot = (len(arrays),) + arrays[0].shape, slot

    def plan(self, refs, local):
        return [(ref, local.at[self.slot(k)]) for k, ref in enumerate(refs)]


class pick(whole):
    def __init__(self, array, index):
        self.arrays, self.dtype, self.index = [array], array.dtype, index
        self.dims = array.shape[1:]

    def plan(self, refs, local):
        return [(refs[0].at[self.index()], local)]


class result:
    def __init__(self, dims, dtype=F32):
        self.dims, self.dtype = tuple(dims), dtype
        self.outs = [jax.ShapeDtypeStruct(self.dims, dtype)]

    def copies(self):
        return len(self.outs)

    def plan(self, local, refs):
        return [(local, refs[0])]


class split(result):
    def __init__(self, slots, dims, dtype=F32, part=None):
        self.dims, self.dtype, self.slots = tuple(dims), dtype, slots
        self.outs = [jax.ShapeDtypeStruct(self.dims[1:], dtype) for _ in slots]

    def plan(self, local, refs):
        return [(local.at[slot()], ref) for slot, ref in zip(self.slots, refs)]


class parts_of(result):
    def __init__(self, source, slots, count, dims, dtype):
        self.source, self.slots, self.count, self.dims = source, slots, count, None
        dims = (count,) + tuple(dims[1:])
        self.outs = [jax.ShapeDtypeStruct(dims, dtype) for _ in slots]

    def plan(self, local, refs):
        return [
            (local.at[pl.ds(slot(), self.count)], ref) for slot, ref in zip(self.slots, refs)
        ]


class Taken:
    def __init__(self, local, copies):
        self.local, self.copies, self.waited = local, copies, False

    def ref(self):
        if not self.waited:
            for copy in self.copies:
                copy.wait()
            self.waited = True
        return self.local

    def __getitem__(self, index):
        return self.ref()[index]

    @property
    def shape(self):
        return self.local.shape


class Given:
    def __init__(self, local, copies, source=None):
        self.local, self.copies, self.sent, self.source = local, copies, False, source

    def send(self):
        if not self.sent:
            if self.source is not None:
                self.source.ref()
            for copy in self.copies:
                copy.start()
            self.sent = True

    def __setitem__(self, index, value):
        self.local[index] = value

    @property
    def shape(self):
        return self.local.shape


def call(body, takes, gives, scratch=(), flops=0, limit=40, later=()):
    takes = [t if isinstance(t, whole) else whole(t) for t in takes]
    arrays = [a for t in takes for a in t.arrays]
    outs = [o for g in gives for o in g.outs]
    n_later, n_in, n_out = len(later), len(arrays), len(outs)
    n_copies = sum(t.copies() for t in takes) + sum(g.copies() for g in gives)

    def kernel(*refs):
        refs = refs[n_later:]
        ins, res = list(refs[:n_in]), list(refs[n_in : n_in + n_out])
        local = list(refs[n_in + n_out : -1])
        sems = refs[-1]
        used = 0
        taken, given = [], []
        for t in takes:
            mine, ins = ins[: len(t.arrays)], ins[len(t.arrays) :]
            copies = []
            for a, b in t.plan(mine, local[0]):
                copies.append(pltpu.make_async_copy(a, b, sems.at[used]))
                used += 1
            for copy in copies:
                copy.start()
            taken.append(Taken(local.pop(0), copies))
        for g in gives:
            mine, res = res[: len(g.outs)], res[len(g.outs) :]
            copies = []
            source = taken[g.source] if g.dims is None else None
            place = source.local if source else local.pop(0)
            for a, b in g.plan(place, mine):
                copies.append(pltpu.make_async_copy(a, b, sems.at[used]))
                used += 1
            given.append(Given(place, copies, source))
        body(*taken, *given, *local)
        for t in taken:
            t.ref()
        for g in given:
            g.send()
        for g in given:
            for copy in g.copies:
                copy.wait()

    moved = sum(a.size * a.dtype.itemsize for a in arrays + outs)
    spec = pl.BlockSpec(memory_space=pltpu.HBM)
    values = pl.pallas_call(
        kernel,
        out_shape=[pltpu.HBM(o.shape, o.dtype) for o in outs],
        in_specs=[spec] * (n_later + n_in),
        out_specs=[spec] * n_out,
        scratch_shapes=[pltpu.VMEM(t.dims, t.dtype) for t in takes]
        + [pltpu.VMEM(g.dims, g.dtype) for g in gives if g.dims is not None]
        + [pltpu.VMEM(dims, dtype) for dims, dtype in scratch]
        + [pltpu.SemaphoreType.DMA((n_copies,))],
        compiler_params=pltpu.CompilerParams(vmem_limit_bytes=limit * 2**20),
        cost_estimate=pl.CostEstimate(flops=flops, bytes_accessed=moved, transcendentals=0),
        name=body.__name__,
    )(*(pltpu.with_memory_space_constraint(a, pltpu.HBM) for a in [*later, *arrays]))
    return list(values)


def dot(a, b):
    return jnp.dot(a, b, preferred_element_type=F32)


def dot_nt(a, b):
    return lax.dot_general(a, b, (((1,), (1,)), ((), ())), preferred_element_type=F32)


def dot_tn(a, b):
    return lax.dot_general(a, b, (((0,), (0,)), ((), ())), preferred_element_type=F32)


def shift_col(x, step):
    rows, lanes = x.shape
    grouped = x.reshape(rows // SIDE, SIDE, lanes)
    rolled = pltpu.roll(grouped, step % SIDE, 1)
    col = lax.broadcasted_iota(jnp.int32, grouped.shape, 1)
    edge = 0 if step > 0 else SIDE - 1
    return jnp.where(col == edge, 0.0, rolled).reshape(rows, lanes)


def shift_row(x, step):
    part = x.shape[0] // SIDE
    blank = jnp.zeros((part, x.shape[1]), x.dtype)
    if step > 0:
        return jnp.concatenate([blank, x[:-part]], axis=0)
    return jnp.concatenate([x[part:], blank], axis=0)


def swap_orders(x, batch):
    pieces = [
        x[(b * SIDE + r) * SIDE : (b * SIDE + r + 1) * SIDE] for r in range(SIDE) for b in range(batch)
    ]
    return jnp.concatenate(pieces, axis=0)


def swap_back(x, batch):
    pieces = [
        x[(r * batch + b) * SIDE : (r * batch + b + 1) * SIDE] for b in range(batch) for r in range(SIDE)
    ]
    return jnp.concatenate(pieces, axis=0)


def col_sum(x):
    return jnp.sum(x, axis=0, keepdims=True)


def lane_sum(x):
    return jnp.sum(col_sum(x), axis=1, keepdims=True)


def rows_of(*rows):
    pad = SIDE - len(rows)
    tail = [jnp.zeros((pad, rows[0].shape[1]), F32)] if pad else []
    return jnp.concatenate(list(rows) + tail, axis=0)


def spread_rows(out, rows):
    out[...] = jnp.broadcast_to(rows[None], out.shape)


def mean_inverse(total, squares, count):
    center = total / count
    spread = squares / count - center * center
    return center, lax.rsqrt(spread + epsilon)


def slope(v):
    sigma = jax.nn.sigmoid(v)
    return sigma * (1.0 + v * (1.0 - sigma))


def add_up(pieces):
    total = pieces[0].astype(F32)
    for piece in pieces[1:]:
        total = total + piece.astype(F32)
    return total


def three_rows(values):
    high = values.astype(BF).astype(F32)
    rest = values - high
    middle = rest.astype(BF).astype(F32)
    low = rest - middle
    blank = jnp.zeros((TAIL - 3 * values.shape[0], values.shape[1]), F32)
    return jnp.concatenate([high, middle, low, blank], axis=0).astype(BF)


def one_row(parts, count):
    return parts[:count] + parts[count : 2 * count] + parts[2 * count : 3 * count]


def tail_sums(blocks, count):
    return one_row(jnp.sum(blocks[:, -TAIL:].astype(F32), axis=0), count)


def pixels_of(blocks):
    data = blocks[:, :-TAIL]
    return data.reshape(-1, data.shape[2]).astype(F32)


def expand_mask(inside):
    images, wide = inside.shape
    dims = (images, SIDE, wide)
    lane = lax.broadcasted_iota(jnp.int32, dims, 2)
    col = lax.broadcasted_iota(jnp.int32, dims, 1)
    picked = jnp.where(lane == col, jnp.broadcast_to(inside[:, None, :], dims), 0.0)
    return jnp.broadcast_to(jnp.sum(picked, axis=2, keepdims=True), dims).reshape(-1, wide)


def widen(mask, wide):
    return jnp.concatenate(
        [mask, jnp.zeros((mask.shape[0], wide - mask.shape[1]), mask.dtype)], axis=1
    )


def lane_row(x):
    return col_sum(x * x)


def pack_weights(w, p, mask, w_next, out, out_next, rows):
    depth, wide = p.shape
    w_ref = w.ref()
    inside = widen(mask[...].astype(F32), wide)
    blank = jnp.zeros((TAIL - inside.shape[0], wide), F32)
    pieces = [w_ref[pl.ds(tap, depth, stride=9), :] for tap in range(9)]
    rows_all = jnp.concatenate(pieces + [p[...], inside, blank], axis=0).astype(BF)
    out[...] = rows_all
    out.send()
    depth = out_next.shape[1]
    w_ref = w_next.ref()
    for tap in range(9):
        out_next[tap] = w_ref[pl.ds(tap, depth, stride=9), :].astype(BF)
    out_next.send()
    rows[...] = rows_of(lane_row(w[...]), lane_row(p[...]), lane_row(w_next[...]))


def pack_images(images, mask, even_out, odd_out, part_out, valid_out, scratch):
    count, pix, lanes = images.shape
    wide = valid_out.shape[1]
    half = count * pix // 2
    for k in range(lanes // wide):
        cut = slice(k * wide, (k + 1) * wide)
        scratch[k] = images[:, :, cut].astype(F32).reshape(count * pix, wide)
        for col in range(2):
            taken = scratch[k, pl.ds(col, half, stride=2), :].reshape(count, 2, SIDE, wide)
            odd = taken[:, 1].reshape(half // 2, wide).astype(BF)
            odd_out[col, :, cut] = odd
            part_out[col, :, cut] = odd
            even_out[col, :, cut] = taken[:, 0].reshape(half // 2, wide).astype(BF)
    part_out.send()
    inside = widen(mask[...].astype(F32), wide)
    part = inside.shape[0] * SIDE
    for row in range(SIDE):
        turned = pltpu.roll(inside, (wide - SIDE * row) % wide, 1)
        valid_out[row * part : (row + 1) * part] = expand_mask(turned)


def tap_major(w):
    return w.reshape(-1, 9, w.shape[1]).transpose(1, 0, 2)


def taps_of(w):
    def taps(*which):
        return jnp.concatenate([w[:, t].reshape(-1, w.shape[3]) for t in which], axis=1)

    return taps


def first_taps_of(w):
    depth = (w.shape[1] - TAIL) // 10

    def taps(*which):
        return jnp.concatenate(
            [w[:, t * depth : (t + 1) * depth].reshape(-1, w.shape[2]) for t in which], axis=1
        )

    return taps


def make_conv_first(mask_rides):
    def conv_first(*refs):
        w, x0, x1, xh, n = refs[:5]
        zb_out, zp_out, pay, sums_out, valid_out, w_out = refs[-6:]
        taps = first_taps_of(w)
        wide = w.shape[2]
        y00 = dot(x0[0], taps(4, 9))
        y01 = dot(x0[1], taps(5, 3))
        y10 = dot(x1[0], taps(7))
        y11 = dot(x1[1], taps(8, 6))
        yh0 = dot(xh[0], taps(1))
        yh1 = dot(xh[1], taps(2, 0))
        here = (y00[:, :wide] + y01[:, :wide]) + (y10 + y11[:, :wide]) + (yh0 + yh1[:, :wide])
        z = here + shift_col(y01[:, wide:] + y11[:, wide:] + yh1[:, wide:], 1)
        zp = y00[:, wide:]
        if mask_rides:
            inside = w[:, w.shape[1] - TAIL :].astype(F32)[:, :SIDE].reshape(-1, wide)
            turn = (wide - SIDE * lax.axis_index("dp")) % wide
            valid = expand_mask(pltpu.roll(inside, turn, 1))
        else:
            valid = refs[5][...]
        zb = z.astype(BF)
        vz, vzp = valid * z, valid * zp
        values = [col_sum(vz), col_sum(vz * z), col_sum(valid), n[0:1], n[1:2]]
        rows = three_rows(jnp.concatenate(values, axis=0))
        part = pay.shape[1] - TAIL
        pay[:, :part] = zb.reshape(SIDE, part, wide)
        pay[:, part:] = jnp.broadcast_to(rows[None], (SIDE, TAIL, wide))
        pay.send()
        w_out.send()
        zb_out[...] = zb
        zp_out[...] = zp
        sums_out[...] = rows_of(col_sum(vzp), col_sum(vzp * zp))
        valid_out[...] = valid

    return conv_first


def first_norm(z, rows):
    count = rows[2:3]
    center, inverse = mean_inverse(rows[0:1], rows[1:2], count)
    hat = (z - center) * inverse
    return hat, hat * rows[3:4] + rows[4:5], inverse


def conv_second(got, m, w, zp, sums, h_out, z2_out, pay, tot_out, w_out):
    blocks, wide = got.shape[0], got.shape[3]
    part = pay.shape[1] - TAIL
    pay[:, :part] = zp[...].astype(BF).reshape(SIDE, part, wide)
    valid = m[...]
    hidden = []
    for k in range(blocks):
        block = got[k]
        total = tail_sums(block, 5)
        own = one_row(got[k, 0, part:].astype(F32), 5)
        rows = rows_of(total[0:1], total[1:2], total[2:3], own[3:4], own[4:5])
        tot_out[k] = rows
        _, lin, _ = first_norm(pixels_of(block), rows)
        hidden.append((lin * jax.nn.sigmoid(lin) * valid).astype(BF))
        h_out[:, k * wide : (k + 1) * wide] = hidden[-1]
    hidden = jnp.concatenate(hidden, axis=1)
    taps = taps_of(w)
    moved = []
    for col in range(3):
        y = dot(hidden, taps(col, 3 + col, 6 + col))
        moved.append(
            shift_row(y[:, :wide], 1) + y[:, wide : 2 * wide] + shift_row(y[:, 2 * wide :], -1)
        )
    z2 = moved[1] + shift_col(moved[0], 1) + shift_col(moved[2], -1)
    vz = valid * z2
    rows = jnp.concatenate([col_sum(vz), col_sum(vz * z2), sums[0:1], sums[1:2]], axis=0)
    pay[:, part:] = jnp.broadcast_to(three_rows(rows)[None], (SIDE, TAIL, wide))
    pay.send()
    w_out.send()
    z2_out[...] = z2


def block_output(z2, got, tot1, m, n, cot, out, e_out, pay, tot_out):
    count = tot1[2:3]
    total = tail_sums(got[...], 4)
    tot_out[...] = rows_of(total[0:1], total[1:2], total[2:3], total[3:4])
    center2, inverse2 = mean_inverse(total[0:1], total[1:2], count)
    center_p, inverse_p = mean_inverse(total[2:3], total[3:4], count)
    hat2 = (z2[...] - center2) * inverse2
    hat_p = (pixels_of(got[...]) - center_p) * inverse_p
    summed = hat2 * n[2:3] + n[3:4] + (hat_p * n[4:5] + n[5:6])
    sigma = jax.nn.sigmoid(summed)
    valid = m[...]
    batch, pix, wide = out.shape
    back = swap_orders(cot[...].astype(F32).reshape(batch * pix, wide), batch)
    e = back * valid * (sigma * (1.0 + summed * (1.0 - sigma)))
    part = pay.shape[1] - TAIL
    pay[:, :part] = e.astype(BF).reshape(SIDE, part, wide)
    rows = jnp.concatenate([col_sum(e), col_sum(e * hat2), col_sum(e * hat_p)], axis=0)
    pay[:, part:] = jnp.broadcast_to(three_rows(rows)[None], (SIDE, TAIL, wide))
    pay.send()
    e_out[...] = e
    out[...] = swap_back(summed * sigma * valid, batch).astype(BF).reshape(out.shape)


def grad_outputs(z2, e, got, tot2, tot1, n, m, m_rows, zp, g2_out, gp_out, tot_out):
    count = tot1[2:3]
    center2, inverse2 = mean_inverse(tot2[0:1], tot2[1:2], count)
    center_p, inverse_p = mean_inverse(tot2[2:3], tot2[3:4], count)
    back = tail_sums(got[...], 3)
    tot_out[...] = rows_of(back[0:1], back[1:2], back[2:3])
    hat2 = (z2[...] - center2) * inverse2
    g2 = n[2:3] * inverse2 * (e[...] - m[...] * ((back[0:1] + hat2 * back[1:2]) / count))
    g2_out[...] = g2.astype(BF)
    g2_out.send()
    hat_p = (zp[...] - center_p) * inverse_p
    loss = m_rows[...] * ((back[0:1] + hat_p * back[2:3]) / count)
    gp_out[...] = (n[4:5] * inverse_p * (pixels_of(got[...]) - loss)).astype(BF)


def grad_hidden(w, g2, got, tot1, m, pay):
    blocks, _, wide = g2.shape
    depth = w.shape[1] * w.shape[3]
    moved = []
    for col in range(3):
        y = 0.0
        for k in range(blocks):
            block = w[k]
            taps = [block[:, 3 * row + col].reshape(depth, wide) for row in range(3)]
            y = y + dot_nt(g2[k], jnp.concatenate(taps, axis=0))
        moved.append(
            shift_row(y[:, :depth], -1) + y[:, depth : 2 * depth] + shift_row(y[:, 2 * depth :], 1)
        )
    gh = moved[1] + shift_col(moved[0], -1) + shift_col(moved[2], 1)
    part = pay.shape[1] - TAIL
    pay[:, :part] = gh.astype(BF).reshape(SIDE, part, depth)
    hat, lin, _ = first_norm(pixels_of(got[...]), tot1[...])
    b = gh * (slope(lin) * m[...])
    rows = three_rows(jnp.concatenate([col_sum(b), col_sum(b * hat)], axis=0))
    pay[:, part:] = jnp.broadcast_to(rows[None], (SIDE, TAIL, depth))


def grad_second(h, g2, x, gp, g_out):
    groups, rows, wide = g_out.shape
    share = h.shape[1] // groups
    h, g2 = h[...], g2[...].astype(F32)
    moved = [shift_col(g2, step).astype(BF) if step else g2.astype(BF) for step in (-1, 0, 1)]

    def put(rows, g):
        g_out[:, rows] = g.astype(BF).reshape(groups, -1, wide)

    for tap in range(9):
        step = tap // 3 - 1
        g = shift_row(moved[tap % 3], step) if step else moved[tap % 3]
        put(slice(tap * share, (tap + 1) * share), dot_tn(h, g))
    put(slice(9 * share, rows), dot_tn(x[...], gp[...]))


def grad_first(got, zb, tot1, n, m, x0, x1, xh, gp, g_out, blocks_out, tot_out):
    wide = got.shape[2]
    back, gh = tail_sums(got[...], 2), pixels_of(got[...])
    tot_out[...] = rows_of(back[0:1], back[1:2])
    count, valid = tot1[2:3], m[...]
    hat, lin, inverse = first_norm(zb[...].astype(F32), tot1[...])
    b = gh * (slope(lin) * valid)
    g = n[0:1] * inverse * (b - valid * ((back[0:1] + hat * back[1:2]) / count))
    here = g.astype(BF)
    g_out[0] = here
    g_out[1] = gp[...]
    g_out.send()
    both = jnp.concatenate([here, shift_col(g, -1).astype(BF)], axis=1)
    groups = blocks_out.shape[0]
    share = x0.shape[2] // groups

    def put(tap, grad):
        rows = grad.astype(BF).reshape(groups, share, wide)
        blocks_out[:, tap * share : (tap + 1) * share] = rows

    for x, plain, (right, left) in ((x0, 4, (5, 3)), (x1, 7, (8, 6)), (xh, 1, (2, 0))):
        put(plain, dot_tn(x[0], here))
        pair = dot_tn(x[1], both)
        put(right, pair[:, :wide])
        put(left, pair[:, wide:])


def grad_images(g, w, out, next_out):
    blocks, count = w.shape[0], w.shape[1]
    depth = (w.shape[2] - TAIL) // 10
    half, wide = count * depth, w.shape[3]

    def taps(k, *which):
        return jnp.concatenate(
            [w[k, :, t * depth : (t + 1) * depth].reshape(half, wide) for t in which], axis=0
        )

    plain, moved, proj = 0.0, 0.0, 0.0
    for k in range(blocks):
        plain = plain + dot_nt(g[k, 0], taps(k, 4, 5, 7, 8, 1, 2))
        moved = moved + dot_nt(g[k, 0], taps(k, 3, 3, 6, 6, 0, 0))
        proj = proj + dot_nt(g[k, 1], taps(k, 9, 9))
    lane = lax.broadcasted_iota(jnp.int32, moved.shape, 1) % (2 * half)
    total = plain + jnp.where(lane >= half, shift_col(moved, -1), 0.0)
    next_out[...] = total[:, 4 * half :].astype(BF)
    next_out.send()
    lane = lax.broadcasted_iota(jnp.int32, proj.shape, 1)
    out[0] = total[:, : 2 * half] + jnp.where(lane < half, proj, 0.0)
    out[1] = total[:, 2 * half : 4 * half]


def finish_images(own, come, out, scratch):
    images, pix, half = out.shape
    wide = own.shape[2]
    odd = own[1] + come[...].astype(F32)
    total = [part.reshape(images, 1, SIDE, wide) for part in (own[0], odd)]
    rows = images * pix // 2
    total = jnp.concatenate(total, axis=1).reshape(rows, wide)
    scratch[pl.ds(0, rows, stride=2), :] = total
    scratch[pl.ds(1, rows, stride=2), :] = pltpu.roll(total, half, 1)
    out[...] = scratch[...][:, :half].astype(BF).reshape(out.shape)


def reduce_second(*refs):
    *parts, g_out, gp_out, rows = refs
    total = add_up([part[...] for part in parts])
    depth = g_out.shape[0] // 9
    for tap in range(9):
        g_out.local[pl.ds(tap, depth, stride=9), :] = total[tap * depth : (tap + 1) * depth]
    conv, proj = total[: 9 * depth], total[9 * depth :]
    gp_out[...] = proj
    rows[...] = rows_of(lane_row(conv), lane_row(proj))


def reduce_first(x, sw, sg, t3, t4, n, g_out, pay):
    total = add_up([x[k] for k in range(x.shape[0])])
    depth = g_out.shape[0] // 9
    conv = [sw[0:1], lane_row(total), sw[2:3], sg[0:1], sw[1:2], sg[1:2]]
    nw, gn = n[...], norm_grad(t3, t4)
    blank = jnp.zeros((2, nw.shape[1]), F32)
    cols = [
        jnp.sum(jnp.concatenate(conv + [blank], axis=0), axis=1, keepdims=True),
        jnp.sum(jnp.concatenate([nw * nw, blank], axis=0), axis=1, keepdims=True),
        jnp.sum(jnp.concatenate([gn * gn, blank], axis=0), axis=1, keepdims=True),
    ]
    lane = lax.broadcasted_iota(jnp.int32, pay.shape[1:], 1)
    block = jnp.zeros(pay.shape[1:], F32)
    for place, col in enumerate(cols):
        block = jnp.where(lane == place, col, block)
    spread_rows(pay, block)
    pay.send()
    for tap in range(9):
        g_out.local[pl.ds(tap, depth, stride=9), :] = total[tap * depth : (tap + 1) * depth]


def norm_grad(t3, t4):
    return jnp.concatenate([t4[1:2], t4[0:1], t3[1:2], t3[0:1], t3[2:3], t3[0:1]], axis=0)


def step_of(w, g, m, a, weight_sq, grad_sq):
    weight_len = jnp.sqrt(weight_sq)
    trust = trust_coef * weight_len / (jnp.sqrt(grad_sq) + weight_decay * weight_len + tiny_term)
    step = trust * (g + weight_decay * w)
    m_new = momentum * m + step
    w_new = w - learn_rate * (step + momentum * m_new)
    return w_new, m_new, avg_decay * a + (1.0 - avg_decay) * w_new


def make_update(dp_count):
    def update(*refs):
        r6, t3, t4 = refs[:3]
        ins, outs = refs[3:18], refs[18:]
        total = jnp.sum(r6[...], axis=0)
        for place in range(3):
            w, g, m, a = (ref[...] for ref in ins[4 * place : 4 * place + 4])
            weight_sq = total[2 * place : 2 * place + 1, 0:1]
            grad_sq = total[2 * place + 1 : 2 * place + 2, 0:1]
            for ref, value in zip(outs[3 * place :], step_of(w, g, m, a, weight_sq, grad_sq)):
                ref[...] = value
                ref.send()
        w, m, a = (ref[...] for ref in ins[12:15])
        weight_sq, grad_sq = total[0:6, 1:2] / dp_count, total[0:6, 2:3] / dp_count
        g = norm_grad(t3, t4)
        for ref, value in zip(outs[9:], step_of(w, g, m, a, weight_sq, grad_sq)):
            ref[...] = value

    return update


def exchange(blocks, axes):
    return lax.all_to_all(blocks, axes, 0, 0)


def swap(array, axis, bits):
    return lax.ppermute(array, axis, [(i, i ^ bits) for i in range(lax.axis_size(axis))])


def away(axis, k):
    return lambda: lax.axis_index(axis) ^ k


def plain_parts(values):
    high = lax.reduce_precision(values, 8, 7)
    middle = lax.reduce_precision(values - high, 8, 7)
    low = values - high - middle
    blank = jnp.zeros((TAIL - 3 * values.shape[0], values.shape[1]), F32)
    return jnp.concatenate([high, middle, low, blank], axis=0).astype(BF)


def in_groups(taps, groups):
    return taps.reshape(taps.shape[0], groups, -1, taps.shape[2]).transpose(1, 0, 2, 3)


def regroup(blocks, taps, groups):
    blocks = blocks.reshape(blocks.shape[0], taps, -1, blocks.shape[2]).transpose(1, 0, 2, 3)
    blocks = in_groups(blocks.reshape(taps, -1, blocks.shape[3]), groups)
    return blocks.reshape(groups, -1, blocks.shape[3])


def as_messages(data, values):
    tail = jnp.zeros((data.shape[0], TAIL, data.shape[2]), BF).at[0].set(plain_parts(values))
    return jnp.concatenate([data.astype(BF), tail], axis=1)


def plain_forward(pay):
    part = pay.shape[1] - TAIL
    rows = one_row(pay[0, part:].astype(F32), 5)
    sums = lax.psum(rows[:3], "dp")
    own = as_messages(pay[:, :part], jnp.concatenate([sums, rows[3:]], axis=0))
    return lax.all_gather(own, "chan")


def plain_sums(pay, count):
    part = pay.shape[1] - TAIL
    return as_messages(
        pay[:, :part], lax.psum(one_row(pay[0, part:].astype(F32), count), "dp")
    )


def per_device(
    images, mask, cotangent, w_first, w_second, w_proj, norm_params, mom_first, mom_second,
    mom_proj, mom_norm, avg_first, avg_second, avg_proj, avg_norm,
):
    everyone = ("dp", "chan")
    dp_count, ch_count = lax.axis_size("dp"), lax.axis_size("chan")
    n_all = dp_count * ch_count
    batch = mask.shape[0]
    pix_here, d_in = images.shape[1], images.shape[2]
    wide = w_first.shape[1]
    d_out = wide * ch_count
    part = batch * SIDE
    pix = SIDE * part
    first_here, second_here = d_in // dp_count, d_out // dp_count
    eight = dp_count == SIDE and pix_here == 4 * SIDE
    groups = SIDE
    square_rows = result((SIDE, wide))
    pixel_pair = (2, pix, d_in)

    message = result((SIDE, part + TAIL, wide), BF)
    all_ch = [away("chan", k) for k in range(ch_count)]

    def slot_dp(k):
        return lax.axis_index("dp") ^ k

    def slot_ch(k):
        return lax.axis_index("chan") ^ k

    if eight:
        own, own_second, squares = call(
            pack_weights,
            [w_first, w_proj, mask, w_second],
            [
                result((10 * first_here + TAIL, wide), BF),
                result((9, second_here, wide), BF),
                square_rows,
            ],
        )
        taps_second = whole(lax.all_gather(own_second, "dp"))
        near = [swap(own, "dp", k) for k in (4, 1, 2, 3)]
        even, odd, send, valid = call(
            pack_images,
            [images, mask],
            [
                result(pixel_pair, BF),
                result(pixel_pair, BF),
                split([lambda: lax.axis_index("chan") % 2], pixel_pair, BF),
                result((pix, wide)),
            ],
            scratch=[((d_in // wide, images.shape[0] * pix_here, wide), F32)],
            later=[own],
        )
        come = lax.ppermute(send, "dp", [(i, i + 1) for i in range(dp_count - 1)])
        come, *near = lax.optimization_barrier((come, *near))
        pieces = [own, *near[1:], near[0]] + [swap(near[0], "dp", k) for k in (1, 2, 3)]
        taps_first, masks = stack(pieces, slot_dp), []
        halo = stack([come, swap(come, "chan", 1)], lambda k: (lax.axis_index("chan") % 2) ^ k)
    else:
        inside = mask.reshape(batch, SIDE, SIDE).transpose(1, 0, 2).reshape(pix, 1).astype(F32)
        valid = jnp.broadcast_to(inside, (pix, wide))
        masks = [valid]
        own = jnp.concatenate([tap_major(w_first), w_proj[None]], axis=0).astype(BF)
        own = in_groups(lax.all_gather(own, "dp", axis=1, tiled=True), groups)
        own = own.reshape(groups, 10 * d_in // groups, wide)
        taps_first = whole(jnp.pad(own, ((0, 0), (0, TAIL), (0, 0))))
        squares = jnp.zeros((SIDE, wide), F32).at[0].set(jnp.sum(w_first * w_first, axis=0))
        squares = squares.at[1].set(jnp.sum(w_proj * w_proj, axis=0))
        own = images.reshape(dp_count, batch, pix_here, d_in)
        own = exchange(own, "dp").transpose(1, 0, 2, 3)
        own = own.reshape(batch, SIDE, 2, SIDE, 2, d_in).transpose(2, 4, 1, 0, 3, 5)
        even, odd = own.reshape(2, 2, pix, d_in)
        halo = jnp.pad(odd, ((0, 0), (part, 0), (0, 0)))[:, :pix]

    macs = pix * 9 * wide * d_in
    per_block = groups // ch_count
    block_slots = [lambda k=k: (lax.axis_index("chan") ^ k) * per_block for k in range(ch_count)]
    z_rows, z_proj, pay, sums_proj, valid_rows, *turned_first = call(
        make_conv_first(eight),
        [taps_first, even, odd, halo, norm_params] + masks,
        [
            result((pix, wide), BF),
            result((pix, wide)),
            message,
            square_rows,
            result((pix, wide)),
            parts_of(0, block_slots, per_block, taps_first.dims, BF),
        ],
        flops=2 * macs,
    )
    if eight:
        got1_mine = exchange(pay, "dp")
        far = swap(got1_mine, "chan", 2)
        got1 = stack([got1_mine, swap(got1_mine, "chan", 1), far, swap(far, "chan", 1)], slot_ch)
    else:
        got1 = plain_forward(pay)
        own_second = lax.all_gather(tap_major(w_second).astype(BF), "dp", axis=1, tiled=True)
        taps_second = whole(in_groups(own_second, groups))
        squares = squares.at[2].set(jnp.sum(w_second * w_second, axis=0))

    hidden, z_second, pay, total1, *turned = call(
        conv_second,
        [got1, valid, taps_second, z_proj, sums_proj],
        [
            result((pix, d_out), BF),
            result((pix, wide)),
            message,
            result((ch_count, SIDE, wide)),
            parts_of(2, block_slots, per_block, taps_second.dims, BF),
        ],
        flops=4 * macs,
    )
    turned = turned[:1] + [swap(block, "chan", k) for k, block in enumerate(turned) if k]
    turned_first = turned_first[:1] + [
        swap(block, "chan", k) for k, block in enumerate(turned_first) if k
    ]
    total1_own = pick(total1, away("chan", 0))
    got2 = exchange(pay, "dp") if eight else plain_sums(pay, 4)
    output, e, pay, total2 = call(
        block_output,
        [z_second, got2, total1_own, valid, norm_params, cotangent],
        [result((batch, SIDE * SIDE, wide), BF), result((pix, wide)), message, square_rows],
    )
    got3 = exchange(pay, "dp") if eight else plain_sums(pay, 3)

    g_second_out, g_proj_out, total3 = call(
        grad_outputs,
        [z_second, e, got3, total2, total1_own, norm_params, valid, valid_rows, z_proj],
        [result((pix, wide), BF), result((pix, wide), BF), square_rows],
        later=turned[1:] + turned_first[1:],
    )
    far = swap(g_second_out, "chan", 2)
    g_all = [g_second_out, swap(g_second_out, "chan", 1), far, swap(far, "chan", 1)]

    rows_second = 9 * (d_out // groups) + d_in // groups
    takes = [hidden, g_second_out, pick(even, lambda: 0), g_proj_out]
    (grads,) = call(
        grad_second,
        takes,
        [result((groups, rows_second, wide), BF)],
        flops=4 * macs,
    )
    if eight:
        *g_all, grads = lax.optimization_barrier((*g_all, grads))
        grads = grads.reshape(groups * rows_second, wide)
        for axis_groups in ([[0, 2, 4, 6], [1, 3, 5, 7]], [[0, 1], [2, 3], [4, 5], [6, 7]]):
            grads = lax.psum_scatter(
                grads, "dp", scatter_dimension=0, axis_index_groups=axis_groups, tiled=True
            )
        takes = [grads]
    else:
        cut = 9 * (d_out // groups)
        grads = [regroup(grads[:, :cut], 9, dp_count), regroup(grads[:, cut:], 1, dp_count)]
        grads = jnp.concatenate(grads, axis=1)
        takes = [jnp.sum(exchange(grads, "dp").astype(F32), axis=0)]
    reduced_second, reduced_proj, squares_second = call(
        reduce_second, takes, [result(w_second.shape), result(w_proj.shape), square_rows]
    )

    got1_own = got1_mine if eight else pick(got1, away("chan", 0))
    (pay,) = call(
        grad_hidden,
        [stack(turned, slot_ch), stack(g_all, slot_ch), got1_own, total1_own, valid],
        [message],
        flops=4 * macs,
    )
    got4 = exchange(pay, "dp") if eight else plain_sums(pay, 2)

    g_first_out, grads, total4 = call(
        grad_first,
        [got4, z_rows, total1_own, norm_params, valid_rows, even, odd, halo, g_proj_out],
        [
            result((2, pix, wide), BF),
            result((groups, 9 * (d_in // groups), wide), BF),
            square_rows,
        ],
        flops=2 * macs,
    )
    if not eight:
        grads = regroup(grads, 9, dp_count)
    got_first = exchange(grads, "dp")

    far = swap(g_first_out, "chan", 2)
    g_all = [g_first_out, swap(g_first_out, "chan", 1), far, swap(far, "chan", 1)]
    own, above = call(
        grad_images,
        [stack(g_all, slot_ch), stack(turned_first, slot_ch)],
        [result((2, pix, wide)), result((pix, wide), BF)],
        flops=2 * macs,
    )
    half = wide // 2
    if eight:
        come = lax.ppermute(above, "dp", [(i + 1, i) for i in range(dp_count - 1)])
        (grad_pixels,) = call(
            finish_images,
            [own, come],
            [result((images.shape[0], pix_here, half), BF)],
            scratch=[((images.shape[0] * pix_here, wide), F32)],
        )
    else:
        cols = pix_here // 2
        above = jnp.pad(above, ((0, part), (0, 0)))[part:].astype(F32)
        total = jnp.stack([own[0], own[1] + above]).astype(BF)
        total = total.reshape(2, SIDE, batch, SIDE // cols, cols, wide)
        total = total.transpose(1, 0, 3, 2, 4, 5).reshape(dp_count, batch, cols, wide)
        grad_pixels = exchange(total, "dp").reshape(dp_count * batch, pix_here, half)

    reduced_first, pay = call(
        reduce_first,
        [got_first, squares, squares_second, total3, total4, norm_params],
        [result(w_first.shape), result((n_all, SIDE, wide))],
    )
    got6 = exchange(pay, everyone)

    conv = (
        (w_first, reduced_first, mom_first, avg_first),
        (w_second, reduced_second, mom_second, avg_second),
        (w_proj, reduced_proj, mom_proj, avg_proj),
    )
    results = call(
        make_update(dp_count),
        [got6, total3, total4, *(array for group in conv for array in group)]
        + [norm_params, mom_norm, avg_norm],
        [result(group[0].shape) for group in conv for _ in range(3)]
        + [result(norm_params.shape)] * 3,
    )
    return (output, grad_pixels, *results)


def solution(mesh):
    rows, cols, batch = P("dp", "chan"), P(None, "chan"), P("dp", None, "chan")
    weights = (rows, rows, rows, cols)
    in_specs = (P(None, "dp", None), P("dp", None), batch) + weights * 3
    out_specs = (batch, P(None, "dp", "chan")) + (rows,) * 9 + (cols,) * 3
    return jax.shard_map(
        per_device, mesh=mesh, in_specs=in_specs, out_specs=out_specs, check_vma=False
    )
```

profile of v0, /device:TPU:0, one launch (start us, length us, event | category | flops | bytes accessed | tf_op | source)
XLA Modules:
  0.0 198.1 jit_solution(11742129785641713699)
XLA Ops:
  7.2 1.8 pack_weights.1
  9.1 2.8 %pack_images.1 = (bf16[2,512,256]{2,1,0:T(8,128)(2,1)}, bf16[2,512,256]{2,1,0:T(8,128)(2,1)}, bf16[512,256]{1,0:T(8,128)(2,1)}, f32[512,128]{1,0:T(8,128)}) custom-call(bf16[336,128]{1,0:T(8,128)(2,1)} %get-tuple-element.77.refs_0_, bf16[64,32,256]{2,1,0:T(8,128)(2,1)} %refs_1_.3, s32[8,64]{1,0:T(8,128)} %refs_2_.3), custom_call_target="tpu_custom_call" | custom-call | bytes 2623488 | tf_op jit(solution)/shard_map/pack_images/pallas_call | solution.py:167
  11.9 4.9 %collective-permute-start = (bf16[512,256]{1,0:T(8,128)(2,1)}, bf16[512,256]{1,0:T(8,128)(2,1)S(1)}, u32[]{:S(2)}, u32[]{:S(2)}) collective-permute-start(bf16[512,256]{1,0:T(8,128)(2,1)} %get-tuple-element.78), channel_id=1, source_target_pairs={{0,4},{4,8},{8,12},{12,16},{16,20},{20,24},{24,28},{1,5},{5,9},{9,... | collective-permute-start | bytes 786440 | tf_op jit(solution)/shard_map/ppermute | solution.py:747
  16.8 2.6 %collective-permute-start.4 = (bf16[336,128]{1,0:T(8,128)(2,1)S(1)}, bf16[336,128]{1,0:T(8,128)(2,1)S(1)}, u32[]{:S(2)}, u32[]{:S(2)}) collective-permute-start(bf16[336,128]{1,0:T(8,128)(2,1)S(1)} %copy-done.13), channel_id=1, source_target_pairs={{0,12},{4,8},{8,4},{12,0},{16,28},{20,24},{24,20},{28,16},{1,13},{... | collective-permute-start | bytes 258056 | tf_op jit(solution)/shard_map/ppermute | solution.py:650
  20.4 2.6 %collective-permute-start.1 = (bf16[336,128]{1,0:T(8,128)(2,1)S(1)}, bf16[336,128]{1,0:T(8,128)(2,1)S(1)}, u32[]{:S(2)}, u32[]{:S(2)}) collective-permute-start(bf16[336,128]{1,0:T(8,128)(2,1)S(1)} %copy-done.13), channel_id=1, source_target_pairs={{0,16},{4,20},{8,24},{12,28},{16,0},{20,4},{24,8},{28,12},{1,17},{... | collective-permute-start | bytes 258056 | tf_op jit(solution)/shard_map/ppermute | solution.py:650
  23.2 3.7 %collective-permute-done.3.refs_2_ = bf16[336,128]{1,0:T(8,128)(2,1)S(1)} collective-permute-done((bf16[336,128]{1,0:T(8,128)(2,1)S(1)}, bf16[336,128]{1,0:T(8,128)(2,1)S(1)}, u32[]{:S(2)}, u32[]{:S(2)}) %collective-permute-start.3) | collective-permute-done | bytes 86048 | tf_op jit(solution)/shard_map/ppermute | solution.py:650
  26.9 1.0 collective-permute-done.2.refs_1_
  27.9 6.6 %collective-permute-start.7 = (bf16[336,128]{1,0:T(8,128)(2,1)S(1)}, bf16[336,128]{1,0:T(8,128)(2,1)S(1)}, u32[]{:S(2)}, u32[]{:S(2)}) collective-permute-start(bf16[336,128]{1,0:T(8,128)(2,1)S(1)} %collective-permute-done.1.refs_4_), channel_id=1, source_target_pairs={{0,12},{4,8},{8,4},{12,0},{16,28},{20,24},{24,20},{28,16},{1,13},{... | collective-permute-start | bytes 258056 | tf_op jit(solution)/shard_map/ppermute | solution.py:650
  34.5 1.4 collective-permute-start.6
  35.9 2.1 %collective-permute-done.7.refs_7_ = bf16[336,128]{1,0:T(8,128)(2,1)S(1)} collective-permute-done((bf16[336,128]{1,0:T(8,128)(2,1)S(1)}, bf16[336,128]{1,0:T(8,128)(2,1)S(1)}, u32[]{:S(2)}, u32[]{:S(2)}) %collective-permute-start.7) | collective-permute-done | bytes 86048 | tf_op jit(solution)/shard_map/ppermute | solution.py:650
  38.0 2.6 %collective-permute-done.6.refs_6_ = bf16[336,128]{1,0:T(8,128)(2,1)S(1)} collective-permute-done((bf16[336,128]{1,0:T(8,128)(2,1)S(1)}, bf16[336,128]{1,0:T(8,128)(2,1)S(1)}, u32[]{:S(2)}, u32[]{:S(2)}) %collective-permute-start.6) | collective-permute-done | bytes 86048 | tf_op jit(solution)/shard_map/ppermute | solution.py:650
  41.4 3.8 %conv_first.1 = (bf16[512,128]{1,0:T(8,128)(2,1)}, f32[512,128]{1,0:T(8,128)}, bf16[8,80,128]{2,1,0:T(8,128)(2,1)}, f32[8,128]{1,0:T(8,128)}, f32[512,128]{1,0:T...) custom-call(bf16[336,128]{1,0:T(8,128)(2,1)} %get-tuple-element.77.r, ...), custom_call_target="tpu_custom_call" | custom-call | flops 301989888 | bytes 3775488 | tf_op jit(solution)/shard_map/conv_first/pallas_call | solution.py:167
  45.2 15.2 %all_to_all.30.refs_0_.refs_8_ = bf16[8,80,128]{2,1,0:T(8,128)(2,1)S(1)} all-to-all(bf16[8,80,128]{2,1,0:T(8,128)(2,1)} %get-tuple-element.86), channel_id=1, replica_groups=mesh['dp'=8,'chan'=4] {'dp'}, dimensions={0} | all-to-all | bytes 327680 | tf_op jit(solution)/shard_map/all_to_all | solution.py:646
  60.4 1.5 collective-permute-start.10
  61.8 3.8 %collective-permute-done.10.refs_2_ = bf16[8,80,128]{2,1,0:T(8,128)(2,1)S(1)} collective-permute-done((bf16[8,80,128]{2,1,0:T(8,128)(2,1)S(1)}, bf16[8,80,128]{2,1,0:T(8,128)(2,1)S(1)}, u32[]{:S(2)}, u32[]{:S(2)}) %collective-permute-start.10) | collective-permute-done | bytes 163872 | tf_op jit(solution)/shard_map/ppermute | solution.py:650
  65.7 1.4 collective-permute-done.11.refs_3_
  67.7 4.7 %conv_second.1 = (bf16[512,512]{1,0:T(8,128)(2,1)}, f32[512,128]{1,0:T(8,128)}, bf16[8,80,128]{2,1,0:T(8,128)(2,1)}, f32[4,8,128]{2,1,0:T(8,128)}, bf16[2,9,64,1...) custom-call(bf16[8,80,128]{2,1,0:T(8,128)(2,1)} %copy-done.1, ...), custom_call_target="tpu_custom_call" | custom-call | flops 603979776 | bytes 4509696 | tf_op jit(solution)/shard_map/conv_second/pallas_call | solution.py:167
  72.5 3.5 %all-to-all-start.1 = ((bf16[8,80,128]{2,1,0:T(8,128)(2,1)}), bf16[8,80,128]{2,1,0:T(8,128)(2,1)S(1)}, u32[]{:S(2)}, u32[]{:S(2)}) async-start(bf16[8,80,128]{2,1,0:T(8,128)(2,1)} %get-tuple-element.92), calls=%async_computation.1 | async-start | bytes 327680 | tf_op jit(solution)/shard_map/all_to_all | solution.py:646
  76.6 1.5 collective-permute-start.13
  78.1 5.9 %all-to-all-done.1.refs_1_ = bf16[8,80,128]{2,1,0:T(8,128)(2,1)S(1)} async-done(((bf16[8,80,128]{2,1,0:T(8,128)(2,1)}), bf16[8,80,128]{2,1,0:T(8,128)(2,1)S(1)}, u32[]{:S(2)}, u32[]{:S(2)}) %all-to-all-start.1) | async-done | bytes 163872 | tf_op jit(solution)/shard_map/all_to_all | solution.py:646
  84.7 2.2 %block_output.1 = (bf16[8,64,128]{2,1,0:T(8,128)(2,1)}, f32[512,128]{1,0:T(8,128)}, bf16[8,80,128]{2,1,0:T(8,128)(2,1)}, f32[8,128]{1,0:T(8,128)}) custom-call(f32[512,128]{1,0:T(8,128)} %get-tuple-element.91.refs_0_.refs_6_, bf16[8,80,128]{2,1,0:T(8,128)(2,1)} %copy-done.11, f32[4,8,128]{2,1,0:T(8,128)} %get-tuple-element.93.refs_2_.refs_10_.refs_9_, ...), custom_call_target="tpu_custom_call" | custom-call | bytes 1399808 | tf_op jit(solution)/shard_map/block_output/pallas_call | solution.py:167
  86.9 3.4 %all-to-all-start.2 = ((bf16[8,80,128]{2,1,0:T(8,128)(2,1)}), bf16[8,80,128]{2,1,0:T(8,128)(2,1)S(1)}, u32[]{:S(2)}, u32[]{:S(2)}) async-start(bf16[8,80,128]{2,1,0:T(8,128)(2,1)} %get-tuple-element.103), calls=%async_computation.2 | async-start | bytes 327680 | tf_op jit(solution)/shard_map/all_to_all | solution.py:646
  90.3 1.5 collective-permute-start.16
  92.0 4.9 %collective-permute-done.16.refs_4_.refs_6_ = bf16[2,336,128]{2,1,0:T(8,128)(2,1)S(1)} collective-permute-done((bf16[2,336,128]{2,1,0:T(8,128)(2,1)S(1)}, bf16[2,336,128]{2,1,0:T(8,128)(2,1)S(1)}, u32[]{:S(2)}, u32[]{:S(2)}) %collective-permute-start.16) | collective-permute-done | bytes 172064 | tf_op jit(solution)/shard_map/ppermute | solution.py:650
  96.8 1.8 collective-permute-done.17.refs_5_.refs_7_
  99.6 2.2 %grad_outputs.1 = (bf16[512,128]{1,0:T(8,128)(2,1)}, bf16[512,128]{1,0:T(8,128)(2,1)}, f32[8,128]{1,0:T(8,128)}) custom-call(bf16[2,9,64,128]{3,2,1,0:T(8,128)(2,1)} %copy-done.2, bf16[2,9,64,128]{3,2,1,0:T(8,128)(2,1)} %copy-done.3, bf16[2,9,64,128]{3,2,1,0:T(8,128)(2,1)} %copy-done.4, bf16[2,336,128]{2,1,0:T(8,128)(2,1)} %copy-done.7, ...), custom_call_target="tpu_custom_call" | custom-call | bytes 1764352 | tf_op jit(solution)/shard_map/grad_outputs/pallas_call | solution.py:167
  101.8 0.7 collective-permute-start.19
  102.5 1.3 collective-permute-start.18
  103.9 4.4 %collective-permute-done.19.refs_6_ = bf16[512,128]{1,0:T(8,128)(2,1)S(1)} collective-permute-done((bf16[512,128]{1,0:T(8,128)(2,1)}, bf16[512,128]{1,0:T(8,128)(2,1)S(1)}, u32[]{:S(2)}, u32[]{:S(2)}) %collective-permute-start.19) | collective-permute-done | bytes 131104 | tf_op jit(solution)/shard_map/ppermute | solution.py:650
  108.3 4.0 %grad_second.1 = bf16[8,608,128]{2,1,0:T(8,128)(2,1)} custom-call(bf16[512,512]{1,0:T(8,128)(2,1)} %get-tuple-element.107.refs_0_, bf16[512,128]{1,0:T(8,128)(2,1)} %get-tuple-element.109.refs_1_.refs_4_, bf16[2,512,256]{2,1,0:T(8,128)(2,1)} %get-tuple-element.83.refs_8_.refs_2_.refs_5_, bf16[512,128]{1,0:T(8,128)(2,1)} %get-tuple-element.108.refs_3_.refs_9_), custom_call_target="tpu_custom_call" | custom-call | flops 603979776 | bytes 2555904 | tf_op jit(solution)/shard_map/grad_second/pallas_call | solution.py:167
  113.1 3.8 %grad_hidden.1 = bf16[8,80,128]{2,1,0:T(8,128)(2,1)} custom-call(bf16[2,9,64,128]{3,2,1,0:T(8,128)(2,1)} %get-tuple-element.95.refs_0_, bf16[2,9,64,128]{3,2,1,0:T(8,128)(2,1)} %copy-done.2, bf16[2,9,64,128]{3,2,1,0:T(8,128)(2,1)} %copy-done.3, bf16[2,9,64,128]{3,2,1,0:T(8,128)(2,1)} %copy-done.4, bf16[512,128]{1,0:T(8,128)(2,1)} %get-tuple-element.109.refs_1_.refs_4_, ...), custom_call_target="tpu_custom_call" | custom-call | flops 603979776 | bytes 2310144 | tf_op jit(solution)/shard_map/grad_hidden/pallas_call | solution.py:167
  116.9 18.2 %all_to_all.31.refs_0_ = bf16[8,80,128]{2,1,0:T(8,128)(2,1)} all-to-all(bf16[8,80,128]{2,1,0:T(8,128)(2,1)} %grad_hidden.1), channel_id=1, replica_groups=mesh['dp'=8,'chan'=4] {'dp'}, dimensions={0} | all-to-all | bytes 327680 | tf_op jit(solution)/shard_map/all_to_all | solution.py:646
  135.1 3.7 %grad_first.1 = (bf16[2,512,128]{2,1,0:T(8,128)(2,1)}, bf16[8,288,128]{2,1,0:T(8,128)(2,1)}, f32[8,128]{1,0:T(8,128)}) custom-call(bf16[8,80,128]{2,1,0:T(8,128)(2,1)} %all_to_all.31.refs_0_, bf16[512,128]{1,0:T(8,128)(2,1)} %get-tuple-element.113.refs_1_, f32[4,8,128]{2,1,0:T(8,128)} %get-tuple-element.93.refs_2_.refs_10_.refs_9_, f32[6,128]{1,0:T(8,128)} %refs_15_.1, ...), custom_call_target="tpu_custom_call" | custom-call | flops 301989888 | bytes 3136512 | tf_op jit(solution)/shard_map/grad_first/pallas_call | solution.py:167
  138.8 3.7 %all-to-all-start.4 = ((bf16[8,288,128]{2,1,0:T(8,128)(2,1)}), bf16[8,288,128]{2,1,0:T(8,128)(2,1)S(1)}, u32[]{:S(2)}, u32[]{:S(2)}) async-start(bf16[8,288,128]{2,1,0:T(8,128)(2,1)} %get-tuple-element.118), calls=%async_computation.4 | async-start | bytes 1179648 | tf_op jit(solution)/shard_map/all_to_all | solution.py:646
  142.5 3.3 %reduce-scatter.3.cloned.1.call-done = bf16[1216,128]{1,0:T(8,128)(2,1)} async-done(((bf16[4864,128]{1,0:T(8,128)(2,1)}), bf16[1216,128]{1,0:T(8,128)(2,1)}) %reduce-scatter.3.cloned.1.call-update) | async-done | bytes 311312 | tf_op jit(solution)/shard_map/reduce_scatter | solution.py:840
  145.8 1.5 collective-permute-start.22
  147.3 6.4 %collective-permute-done.22.refs_2_ = bf16[2,512,128]{2,1,0:T(8,128)(2,1)S(1)} collective-permute-done((bf16[2,512,128]{2,1,0:T(8,128)(2,1)S(1)}, bf16[2,512,128]{2,1,0:T(8,128)(2,1)S(1)}, u32[]{:S(2)}, u32[]{:S(2)}) %collective-permute-start.22) | collective-permute-done | bytes 262176 | tf_op jit(solution)/shard_map/ppermute | solution.py:650
  153.8 10.2 %reduce-scatter.5.cloned.1.call-done.refs_0_ = bf16[608,128]{1,0:T(8,128)(2,1)} async-done(((bf16[1216,128]{1,0:T(8,128)(2,1)}), bf16[608,128]{1,0:T(8,128)(2,1)}) %reduce-scatter.5.cloned.1.call-update) | async-done | bytes 155664 | tf_op jit(solution)/shard_map/reduce_scatter | solution.py:840
  164.0 1.7 reduce_second.1
  165.7 0.8 copy-done
  166.5 2.1 %reduce_first.1 = (f32[288,128]{1,0:T(8,128)}, f32[32,8,128]{2,1,0:T(8,128)}) custom-call(bf16[8,288,128]{2,1,0:T(8,128)(2,1)} %copy-done, f32[8,128]{1,0:T(8,128)} %get-tuple-element.119.refs_1_, f32[8,128]{1,0:T(8,128)} %get-tuple-element.121.refs_2_, f32[8,128]{1,0:T(8,128)} %get-tuple-element.122.refs_3_.refs_1_, ...), custom_call_target="tpu_custom_call" | custom-call | bytes 887808 | tf_op jit(solution)/shard_map/reduce_first/pallas_call | solution.py:167
  168.6 4.6 %all-to-all-start.5 = ((f32[32,8,128]{2,1,0:T(8,128)}), f32[32,8,128]{2,1,0:T(8,128)S(1)}, u32[]{:S(2)}, u32[]{:S(2)}) async-start(f32[32,8,128]{2,1,0:T(8,128)} %get-tuple-element.124), calls=%async_computation.7 | async-start | bytes 262144 | tf_op jit(solution)/shard_map/all_to_all | solution.py:646
  173.3 0.7 copy-done.16
  174.0 3.4 %grad_images.1 = (f32[2,512,128]{2,1,0:T(8,128)}, bf16[512,128]{1,0:T(8,128)(2,1)}) custom-call(bf16[2,512,128]{2,1,0:T(8,128)(2,1)} %get-tuple-element.114.refs_0_, bf16[2,512,128]{2,1,0:T(8,128)(2,1)} %copy-done.16, bf16[2,512,128]{2,1,0:T(8,128)(2,1)} %copy-done.15, bf16[2,512,128]{2,1,0:T(8,128)(2,1)} %copy-done.17, ...), custom_call_target="tpu_custom_call" | custom-call | flops 301989888 | bytes 2392064 | tf_op jit(solution)/shard_map/grad_images/pallas_call | solution.py:167
  177.4 1.3 collective-permute-start.24
  178.7 6.5 %collective-permute-done.24.refs_1_ = bf16[512,128]{1,0:T(8,128)(2,1)S(1)} collective-permute-done((bf16[512,128]{1,0:T(8,128)(2,1)}, bf16[512,128]{1,0:T(8,128)(2,1)S(1)}, u32[]{:S(2)}, u32[]{:S(2)}) %collective-permute-start.24) | collective-permute-done | bytes 131104 | tf_op jit(solution)/shard_map/ppermute | solution.py:886
  185.8 2.2 %finish_images.1 = bf16[64,32,64]{2,1,0:T(8,128)(2,1)} custom-call(f32[2,512,128]{2,1,0:T(8,128)} %get-tuple-element.116.refs_0_, bf16[512,128]{1,0:T(8,128)(2,1)} %copy-done.24), custom_call_target="tpu_custom_call" | custom-call | bytes 917504 | tf_op jit(solution)/shard_map/finish_images/pallas_call | solution.py:167
  188.7 2.9 %update.1 = (f32[288,128]{1,0:T(8,128)}, f32[288,128]{1,0:T(8,128)}, f32[288,128]{1,0:T(8,128)}, f32[576,128]{1,0:T(8,128)}, f32[576,128]{1,0:T(8,128)}, /*index...) custom-call(f32[32,8,128]{2,1,0:T(8,128)} %copy-done.12, ...), custom_call_target="tpu_custom_call" | custom-call | bytes 3368960 | tf_op jit(solution)/shard_map/update/pallas_call | solution.py:167
  (105 shorter events, 7.2 us)
Async XLA Ops:
  7.2 59.9 %all-gather.3.cloned.1.call-start = ((), (), s32[]{:S(2)}) async-start(), calls=%async_computation.10 | async-start | bytes 1327104 | tf_op jit(solution)/shard_map/all_gather | solution.py:733
  9.1 7.7 %copy-start.13 = (bf16[336,128]{1,0:T(8,128)(2,1)S(1)}, bf16[336,128]{1,0:T(8,128)(2,1)}, u32[]{:S(2)}) copy-start(bf16[336,128]{1,0:T(8,128)(2,1)} %get-tuple-element.77.refs_0_) | copy-start | bytes 258052
  11.9 15.9 %collective-permute-start = (bf16[512,256]{1,0:T(8,128)(2,1)}, bf16[512,256]{1,0:T(8,128)(2,1)S(1)}, u32[]{:S(2)}, u32[]{:S(2)}) collective-permute-start(bf16[512,256]{1,0:T(8,128)(2,1)} %get-tuple-element.78), channel_id=1, source_target_pairs={{0,4},{4,8},{8,12},{12,16},{16,20},{20,24},{24,28},{1,5},{5,9},{9,... | collective-permute-start | bytes 786440 | tf_op jit(solution)/shard_map/ppermute | solution.py:747
  16.8 6.3 %collective-permute-start.4 = (bf16[336,128]{1,0:T(8,128)(2,1)S(1)}, bf16[336,128]{1,0:T(8,128)(2,1)S(1)}, u32[]{:S(2)}, u32[]{:S(2)}) collective-permute-start(bf16[336,128]{1,0:T(8,128)(2,1)S(1)} %copy-done.13), channel_id=1, source_target_pairs={{0,12},{4,8},{8,4},{12,0},{16,28},{20,24},{24,20},{28,16},{1,13},{... | collective-permute-start | bytes 258056 | tf_op jit(solution)/shard_map/ppermute | solution.py:650
  19.4 7.5 %collective-permute-start.3 = (bf16[336,128]{1,0:T(8,128)(2,1)S(1)}, bf16[336,128]{1,0:T(8,128)(2,1)S(1)}, u32[]{:S(2)}, u32[]{:S(2)}) collective-permute-start(bf16[336,128]{1,0:T(8,128)(2,1)S(1)} %copy-done.13), channel_id=1, source_target_pairs={{0,8},{4,12},{8,0},{12,4},{16,24},{20,28},{24,16},{28,20},{1,9},{5... | collective-permute-start | bytes 258056 | tf_op jit(solution)/shard_map/ppermute | solution.py:650
  19.8 8.0 %collective-permute-start.2 = (bf16[336,128]{1,0:T(8,128)(2,1)S(1)}, bf16[336,128]{1,0:T(8,128)(2,1)S(1)}, u32[]{:S(2)}, u32[]{:S(2)}) collective-permute-start(bf16[336,128]{1,0:T(8,128)(2,1)S(1)} %copy-done.13), channel_id=1, source_target_pairs={{0,4},{4,0},{8,12},{12,8},{16,20},{20,16},{24,28},{28,24},{1,5},{5... | collective-permute-start | bytes 258056 | tf_op jit(solution)/shard_map/ppermute | solution.py:650
  20.4 7.5 %collective-permute-start.1 = (bf16[336,128]{1,0:T(8,128)(2,1)S(1)}, bf16[336,128]{1,0:T(8,128)(2,1)S(1)}, u32[]{:S(2)}, u32[]{:S(2)}) collective-permute-start(bf16[336,128]{1,0:T(8,128)(2,1)S(1)} %copy-done.13), channel_id=1, source_target_pairs={{0,16},{4,20},{8,24},{12,28},{16,0},{20,4},{24,8},{28,12},{1,17},{... | collective-permute-start | bytes 258056 | tf_op jit(solution)/shard_map/ppermute | solution.py:650
  23.2 17.5 %copy-start.25 = (bf16[336,128]{1,0:T(8,128)(2,1)}, bf16[336,128]{1,0:T(8,128)(2,1)S(1)}, u32[]{:S(2)}) copy-start(bf16[336,128]{1,0:T(8,128)(2,1)S(1)} %collective-permute-done.4.refs_3_) | copy-start | bytes 258052
  26.9 13.8 %copy-start.26 = (bf16[336,128]{1,0:T(8,128)(2,1)}, bf16[336,128]{1,0:T(8,128)(2,1)S(1)}, u32[]{:S(2)}) copy-start(bf16[336,128]{1,0:T(8,128)(2,1)S(1)} %collective-permute-done.3.refs_2_) | copy-start | bytes 258052
  27.8 12.8 %copy-start.27 = (bf16[336,128]{1,0:T(8,128)(2,1)}, bf16[336,128]{1,0:T(8,128)(2,1)S(1)}, u32[]{:S(2)}) copy-start(bf16[336,128]{1,0:T(8,128)(2,1)S(1)} %collective-permute-done.2.refs_1_) | copy-start | bytes 258052
  27.8 12.8 %copy-start.28 = (bf16[336,128]{1,0:T(8,128)(2,1)}, bf16[336,128]{1,0:T(8,128)(2,1)S(1)}, u32[]{:S(2)}) copy-start(bf16[336,128]{1,0:T(8,128)(2,1)S(1)} %collective-permute-done.1.refs_4_) | copy-start | bytes 258052
  27.8 12.8 %copy-start.5 = (bf16[512,256]{1,0:T(8,128)(2,1)}, bf16[512,256]{1,0:T(8,128)(2,1)S(1)}, u32[]{:S(2)}) copy-start(bf16[512,256]{1,0:T(8,128)(2,1)S(1)} %collective-permute-done.refs_10_.refs_7_) | copy-start | bytes 786436
  27.8 12.8 %collective-permute-start.8 = (bf16[512,256]{1,0:T(8,128)(2,1)S(1)}, bf16[512,256]{1,0:T(8,128)(2,1)S(1)}, u32[]{:S(2)}, u32[]{:S(2)}) collective-permute-start(bf16[512,256]{1,0:T(8,128)(2,1)S(1)} %collective-permute-done.refs_10_.refs_7_), channel_id=1, source_target_pairs={{0,1},{1,0},{2,3},{3,2},{4,5},{5,4},{6,7},{7,6},{8,9},{9,8},{10,11... | collective-permute-start | bytes 786440 | tf_op jit(solution)/shard_map/ppermute | solution.py:650
  27.9 10.1 %collective-permute-start.7 = (bf16[336,128]{1,0:T(8,128)(2,1)S(1)}, bf16[336,128]{1,0:T(8,128)(2,1)S(1)}, u32[]{:S(2)}, u32[]{:S(2)}) collective-permute-start(bf16[336,128]{1,0:T(8,128)(2,1)S(1)} %collective-permute-done.1.refs_4_), channel_id=1, source_target_pairs={{0,12},{4,8},{8,4},{12,0},{16,28},{20,24},{24,20},{28,16},{1,13},{... | collective-permute-start | bytes 258056 | tf_op jit(solution)/shard_map/ppermute | solution.py:650
  34.5 6.1 %collective-permute-start.6 = (bf16[336,128]{1,0:T(8,128)(2,1)S(1)}, bf16[336,128]{1,0:T(8,128)(2,1)S(1)}, u32[]{:S(2)}, u32[]{:S(2)}) collective-permute-start(bf16[336,128]{1,0:T(8,128)(2,1)S(1)} %collective-permute-done.1.refs_4_), channel_id=1, source_target_pairs={{0,8},{4,12},{8,0},{12,4},{16,24},{20,28},{24,16},{28,20},{1,9},{5... | collective-permute-start | bytes 258056 | tf_op jit(solution)/shard_map/ppermute | solution.py:650
  35.9 4.7 %collective-permute-start.5 = (bf16[336,128]{1,0:T(8,128)(2,1)S(1)}, bf16[336,128]{1,0:T(8,128)(2,1)S(1)}, u32[]{:S(2)}, u32[]{:S(2)}) collective-permute-start(bf16[336,128]{1,0:T(8,128)(2,1)S(1)} %collective-permute-done.1.refs_4_), channel_id=1, source_target_pairs={{0,4},{4,0},{8,12},{12,8},{16,20},{20,16},{24,28},{28,24},{1,5},{5... | collective-permute-start | bytes 258056 | tf_op jit(solution)/shard_map/ppermute | solution.py:650
  38.0 2.7 %copy-start.29 = (bf16[336,128]{1,0:T(8,128)(2,1)}, bf16[336,128]{1,0:T(8,128)(2,1)S(1)}, u32[]{:S(2)}) copy-start(bf16[336,128]{1,0:T(8,128)(2,1)S(1)} %collective-permute-done.7.refs_7_) | copy-start | bytes 258052
  60.4 6.7 %copy-start.1 = (bf16[8,80,128]{2,1,0:T(8,128)(2,1)}, bf16[8,80,128]{2,1,0:T(8,128)(2,1)S(1)}, u32[]{:S(2)}) copy-start(bf16[8,80,128]{2,1,0:T(8,128)(2,1)S(1)} %all_to_all.30.refs_0_.refs_8_) | copy-start | bytes 491524
  60.4 5.3 %collective-permute-start.10 = (bf16[8,80,128]{2,1,0:T(8,128)(2,1)S(1)}, bf16[8,80,128]{2,1,0:T(8,128)(2,1)S(1)}, u32[]{:S(2)}, u32[]{:S(2)}) collective-permute-start(bf16[8,80,128]{2,1,0:T(8,128)(2,1)S(1)} %all_to_all.30.refs_0_.refs_8_), channel_id=1, source_target_pairs={{0,2},{1,3},{2,0},{3,1},{4,6},{5,7},{6,4},{7,5},{8,10},{9,11},{10,... | collective-permute-start | bytes 491528 | tf_op jit(solution)/shard_map/ppermute | solution.py:650
  61.8 3.9 %collective-permute-start.9 = (bf16[8,80,128]{2,1,0:T(8,128)(2,1)S(1)}, bf16[8,80,128]{2,1,0:T(8,128)(2,1)S(1)}, u32[]{:S(2)}, u32[]{:S(2)}) collective-permute-start(bf16[8,80,128]{2,1,0:T(8,128)(2,1)S(1)} %all_to_all.30.refs_0_.refs_8_), channel_id=1, source_target_pairs={{0,1},{1,0},{2,3},{3,2},{4,5},{5,4},{6,7},{7,6},{8,9},{9,8},{10,11... | collective-permute-start | bytes 491528 | tf_op jit(solution)/shard_map/ppermute | solution.py:650
  65.7 1.4 collective-permute-start.11
  67.7 8.3 %copy-start.34 = (bf16[2,336,128]{2,1,0:T(8,128)(2,1)S(1)}, bf16[2,336,128]{2,1,0:T(8,128)(2,1)}, u32[]{:S(2)}) copy-start(bf16[2,336,128]{2,1,0:T(8,128)(2,1)} %get-tuple-element.99) | copy-start | bytes 516100
  72.5 17.9 %copy-start.33 = (bf16[2,336,128]{2,1,0:T(8,128)(2,1)S(1)}, bf16[2,336,128]{2,1,0:T(8,128)(2,1)}, u32[]{:S(2)}) copy-start(bf16[2,336,128]{2,1,0:T(8,128)(2,1)} %get-tuple-element.100) | copy-start | bytes 516100
  72.5 19.4 %copy-start.32 = (bf16[2,336,128]{2,1,0:T(8,128)(2,1)S(1)}, bf16[2,336,128]{2,1,0:T(8,128)(2,1)}, u32[]{:S(2)}) copy-start(bf16[2,336,128]{2,1,0:T(8,128)(2,1)} %get-tuple-element.101) | copy-start | bytes 516100
  72.5 11.5 %all-to-all-start.1 = ((bf16[8,80,128]{2,1,0:T(8,128)(2,1)}), bf16[8,80,128]{2,1,0:T(8,128)(2,1)S(1)}, u32[]{:S(2)}, u32[]{:S(2)}) async-start(bf16[8,80,128]{2,1,0:T(8,128)(2,1)} %get-tuple-element.92), calls=%async_computation.1 | async-start | bytes 327680 | tf_op jit(solution)/shard_map/all_to_all | solution.py:646
  76.0 15.8 %collective-permute-start.15 = (bf16[2,336,128]{2,1,0:T(8,128)(2,1)S(1)}, bf16[2,336,128]{2,1,0:T(8,128)(2,1)S(1)}, u32[]{:S(2)}, u32[]{:S(2)}) collective-permute-start(bf16[2,336,128]{2,1,0:T(8,128)(2,1)S(1)} %copy-done.34), channel_id=1, source_target_pairs={{0,1},{1,0},{2,3},{3,2},{4,5},{5,4},{6,7},{7,6},{8,9},{9,8},{10,11... | collective-permute-start | bytes 516104 | tf_op jit(solution)/shard_map/ppermute | solution.py:650
  76.2 22.4 %collective-permute-start.12 = (bf16[2,9,64,128]{3,2,1,0:T(8,128)(2,1)}, bf16[2,9,64,128]{3,2,1,0:T(8,128)(2,1)S(1)}, u32[]{:S(2)}, u32[]{:S(2)}) collective-permute-start(bf16[2,9,64,128]{3,2,1,0:T(8,128)(2,1)} %get-tuple-element.96), channel_id=1, source_target_pairs={{0,1},{1,0},{2,3},{3,2},{4,5},{5,4},{6,7},{7,6},{8,9},{9,8},{10,11... | collective-permute-start | bytes 884744 | tf_op jit(solution)/shard_map/ppermute | solution.py:650
  76.6 22.0 %collective-permute-start.13 = (bf16[2,9,64,128]{3,2,1,0:T(8,128)(2,1)}, bf16[2,9,64,128]{3,2,1,0:T(8,128)(2,1)S(1)}, u32[]{:S(2)}, u32[]{:S(2)}) collective-permute-start(bf16[2,9,64,128]{3,2,1,0:T(8,128)(2,1)} %get-tuple-element.97), channel_id=1, source_target_pairs={{0,2},{1,3},{2,0},{3,1},{4,6},{5,7},{6,4},{7,5},{8,10},{9,11},{10,... | collective-permute-start | bytes 884744 | tf_op jit(solution)/shard_map/ppermute | solution.py:650
  78.1 20.6 %collective-permute-start.14 = (bf16[2,9,64,128]{3,2,1,0:T(8,128)(2,1)}, bf16[2,9,64,128]{3,2,1,0:T(8,128)(2,1)S(1)}, u32[]{:S(2)}, u32[]{:S(2)}) collective-permute-start(bf16[2,9,64,128]{3,2,1,0:T(8,128)(2,1)} %get-tuple-element.98), channel_id=1, source_target_pairs={{0,3},{1,2},{2,1},{3,0},{4,7},{5,6},{6,5},{7,4},{8,11},{9,10},{10,... | collective-permute-start | bytes 884744 | tf_op jit(solution)/shard_map/ppermute | solution.py:650
  86.9 11.8 %all-to-all-start.2 = ((bf16[8,80,128]{2,1,0:T(8,128)(2,1)}), bf16[8,80,128]{2,1,0:T(8,128)(2,1)S(1)}, u32[]{:S(2)}, u32[]{:S(2)}) async-start(bf16[8,80,128]{2,1,0:T(8,128)(2,1)} %get-tuple-element.103), calls=%async_computation.2 | async-start | bytes 327680 | tf_op jit(solution)/shard_map/all_to_all | solution.py:646
  90.3 55.5 %reduce-scatter.3.cloned.1.call-start = ((), (), s32[]{:S(2)}) async-start(), calls=%async_computation.8 | async-start | bytes 1556480 | tf_op jit(solution)/shard_map/reduce_scatter | solution.py:840
  90.3 6.5 %collective-permute-start.16 = (bf16[2,336,128]{2,1,0:T(8,128)(2,1)S(1)}, bf16[2,336,128]{2,1,0:T(8,128)(2,1)S(1)}, u32[]{:S(2)}, u32[]{:S(2)}) collective-permute-start(bf16[2,336,128]{2,1,0:T(8,128)(2,1)S(1)} %copy-done.33), channel_id=1, source_target_pairs={{0,2},{1,3},{2,0},{3,1},{4,6},{5,7},{6,4},{7,5},{8,10},{9,11},{10,... | collective-permute-start | bytes 516104 | tf_op jit(solution)/shard_map/ppermute | solution.py:650
  91.9 6.8 %copy-start.7 = (bf16[2,336,128]{2,1,0:T(8,128)(2,1)}, bf16[2,336,128]{2,1,0:T(8,128)(2,1)S(1)}, u32[]{:S(2)}) copy-start(bf16[2,336,128]{2,1,0:T(8,128)(2,1)S(1)} %collective-permute-done.15.refs_3_.refs_5_) | copy-start | bytes 516100
  91.9 6.7 %collective-permute-start.17 = (bf16[2,336,128]{2,1,0:T(8,128)(2,1)S(1)}, bf16[2,336,128]{2,1,0:T(8,128)(2,1)S(1)}, u32[]{:S(2)}, u32[]{:S(2)}) collective-permute-start(bf16[2,336,128]{2,1,0:T(8,128)(2,1)S(1)} %copy-done.32), channel_id=1, source_target_pairs={{0,3},{1,2},{2,1},{3,0},{4,7},{5,6},{6,5},{7,4},{8,11},{9,10},{10,... | collective-permute-start | bytes 516104 | tf_op jit(solution)/shard_map/ppermute | solution.py:650
  96.8 1.9 copy-start.8
  101.8 6.5 %collective-permute-start.19 = (bf16[512,128]{1,0:T(8,128)(2,1)}, bf16[512,128]{1,0:T(8,128)(2,1)S(1)}, u32[]{:S(2)}, u32[]{:S(2)}) collective-permute-start(bf16[512,128]{1,0:T(8,128)(2,1)} %get-tuple-element.109.refs_1_.refs_4_), channel_id=1, source_target_pairs={{0,2},{1,3},{2,0},{3,1},{4,6},{5,7},{6,4},{7,5},{8,10},{9,11},{10,... | collective-permute-start | bytes 393224 | tf_op jit(solution)/shard_map/ppermute | solution.py:650
  102.5 9.8 %collective-permute-start.18 = (bf16[512,128]{1,0:T(8,128)(2,1)}, bf16[512,128]{1,0:T(8,128)(2,1)S(1)}, u32[]{:S(2)}, u32[]{:S(2)}) collective-permute-start(bf16[512,128]{1,0:T(8,128)(2,1)} %get-tuple-element.109.refs_1_.refs_4_), channel_id=1, source_target_pairs={{0,1},{1,0},{2,3},{3,2},{4,5},{5,4},{6,7},{7,6},{8,9},{9,8},{10,11... | collective-permute-start | bytes 393224 | tf_op jit(solution)/shard_map/ppermute | solution.py:650
  108.3 4.0 %copy-start.21 = (bf16[512,128]{1,0:T(8,128)(2,1)}, bf16[512,128]{1,0:T(8,128)(2,1)S(1)}, u32[]{:S(2)}) copy-start(bf16[512,128]{1,0:T(8,128)(2,1)S(1)} %collective-permute-done.19.refs_6_) | copy-start | bytes 393220
  108.3 4.0 %collective-permute-start.20 = (bf16[512,128]{1,0:T(8,128)(2,1)S(1)}, bf16[512,128]{1,0:T(8,128)(2,1)S(1)}, u32[]{:S(2)}, u32[]{:S(2)}) collective-permute-start(bf16[512,128]{1,0:T(8,128)(2,1)S(1)} %collective-permute-done.19.refs_6_), channel_id=1, source_target_pairs={{0,1},{1,0},{2,3},{3,2},{4,5},{5,4},{6,7},{7,6},{8,9},{9,8},{10,11... | collective-permute-start | bytes 393224 | tf_op jit(solution)/shard_map/ppermute | solution.py:650
  138.7 7.1 %copy-start.14 = (bf16[2,512,128]{2,1,0:T(8,128)(2,1)S(1)}, bf16[2,512,128]{2,1,0:T(8,128)(2,1)}, u32[]{:S(2)}) copy-start(bf16[2,512,128]{2,1,0:T(8,128)(2,1)} %get-tuple-element.114.refs_0_) | copy-start | bytes 786436
  138.8 26.9 %all-to-all-start.4 = ((bf16[8,288,128]{2,1,0:T(8,128)(2,1)}), bf16[8,288,128]{2,1,0:T(8,128)(2,1)S(1)}, u32[]{:S(2)}, u32[]{:S(2)}) async-start(bf16[8,288,128]{2,1,0:T(8,128)(2,1)} %get-tuple-element.118), calls=%async_computation.4 | async-start | bytes 1179648 | tf_op jit(solution)/shard_map/all_to_all | solution.py:646
  142.4 21.5 %reduce-scatter.5.cloned.1.call-start = ((), (), s32[]{:S(2)}) async-start(), calls=%async_computation.9 | async-start | bytes 466944 | tf_op jit(solution)/shard_map/reduce_scatter | solution.py:840
  145.8 8.0 %collective-permute-start.22 = (bf16[2,512,128]{2,1,0:T(8,128)(2,1)S(1)}, bf16[2,512,128]{2,1,0:T(8,128)(2,1)S(1)}, u32[]{:S(2)}, u32[]{:S(2)}) collective-permute-start(bf16[2,512,128]{2,1,0:T(8,128)(2,1)S(1)} %copy-done.14), channel_id=1, source_target_pairs={{0,2},{1,3},{2,0},{3,1},{4,6},{5,7},{6,4},{7,5},{8,10},{9,11},{10,... | collective-permute-start | bytes 786440 | tf_op jit(solution)/shard_map/ppermute | solution.py:650
  147.3 25.9 %collective-permute-start.21 = (bf16[2,512,128]{2,1,0:T(8,128)(2,1)S(1)}, bf16[2,512,128]{2,1,0:T(8,128)(2,1)S(1)}, u32[]{:S(2)}, u32[]{:S(2)}) collective-permute-start(bf16[2,512,128]{2,1,0:T(8,128)(2,1)S(1)} %copy-done.14), channel_id=1, source_target_pairs={{0,1},{1,0},{2,3},{3,2},{4,5},{5,4},{6,7},{7,6},{8,9},{9,8},{10,11... | collective-permute-start | bytes 786440 | tf_op jit(solution)/shard_map/ppermute | solution.py:650
  153.8 19.5 %copy-start.15 = (bf16[2,512,128]{2,1,0:T(8,128)(2,1)}, bf16[2,512,128]{2,1,0:T(8,128)(2,1)S(1)}, u32[]{:S(2)}) copy-start(bf16[2,512,128]{2,1,0:T(8,128)(2,1)S(1)} %collective-permute-done.22.refs_2_) | copy-start | bytes 786436
  153.8 19.5 %collective-permute-start.23 = (bf16[2,512,128]{2,1,0:T(8,128)(2,1)S(1)}, bf16[2,512,128]{2,1,0:T(8,128)(2,1)S(1)}, u32[]{:S(2)}, u32[]{:S(2)}) collective-permute-start(bf16[2,512,128]{2,1,0:T(8,128)(2,1)S(1)} %collective-permute-done.22.refs_2_), channel_id=1, source_target_pairs={{0,1},{1,0},{2,3},{3,2},{4,5},{5,4},{6,7},{7,6},{8,9},{9,8},{10,11... | collective-permute-start | bytes 786440 | tf_op jit(solution)/shard_map/ppermute | solution.py:650
  168.6 19.4 %all-to-all-start.5 = ((f32[32,8,128]{2,1,0:T(8,128)}), f32[32,8,128]{2,1,0:T(8,128)S(1)}, u32[]{:S(2)}, u32[]{:S(2)}) async-start(f32[32,8,128]{2,1,0:T(8,128)} %get-tuple-element.124), calls=%async_computation.7 | async-start | bytes 262144 | tf_op jit(solution)/shard_map/all_to_all | solution.py:646
  177.4 7.8 %collective-permute-start.24 = (bf16[512,128]{1,0:T(8,128)(2,1)}, bf16[512,128]{1,0:T(8,128)(2,1)S(1)}, u32[]{:S(2)}, u32[]{:S(2)}) collective-permute-start(bf16[512,128]{1,0:T(8,128)(2,1)} %get-tuple-element.117), channel_id=1, source_target_pairs={{4,0},{8,4},{12,8},{16,12},{20,16},{24,20},{28,24},{5,1},{9,5},{13... | collective-permute-start | bytes 393224 | tf_op jit(solution)/shard_map/ppermute | solution.py:886
  (19 other events, 15.3 us)
Sparse Core Ops, SparseCore 0:
  10.8 47.3 all-gather.2
  112.5 33.2 reduce-scatter.2
  148.1 15.8 reduce-scatter.4
where the time goes:
time: 199 us; the launch traced here: 198 us
  waiting for transfers between devices  58.2 us (29%)
  starting transfers between devices  44.4 us (22%)
  Pallas kernels  41.3 us (21%)
  blocking collectives  33.4 us (17%)
  between operations  14.3 us (7%)
  local copies, waits for them, and re-layouts  6.56 us (3%)
    pallas_call x14, Pallas kernels, call(): pl.pallas_call(kernel, out_shape=[pltpu.HBM(o.shape, o.dtype) for o in ou...  41.3 us
    all_to_all x2, blocking collectives, exchange(): return lax.all_to_all(blocks, axes, 0, 0)  33.4 us
    ppermute x23, waiting for transfers between devices, swap(): lax.ppermute(array, axis, [(i, i ^ bits) for i in range(lax.axis_size(axi...  32.3 us
    ppermute x23, starting transfers between devices, swap(): lax.ppermute(array, axis, [(i, i ^ bits) for i in range(lax.axis_size(axi...  22.9 us
    all_to_all x4, starting transfers between devices, exchange(): return lax.all_to_all(blocks, axes, 0, 0)  15.2 us
    reduce_scatter x2, waiting for transfers between devices, per_device(): lax.psum_scatter(grads, 'dp', scatter_dimension=0, axis_index_groups=axis...  13.5 us
    unnamed x70, local copies, waits for them, and re-layouts  6.56 us
    ppermute x1, waiting for transfers between devices, per_device(): come = lax.ppermute(above, 'dp', [(i + 1, i) for i in range(dp_count - 1)])  6.46 us
  transfers between devices with their start and end apart: 32, of which 15 were waited for; matrix products, arithmetic and copies ran while one was open for 0% of the time, Pallas kernels for 15%

commit v1 on v0

--- a/solution.py
+++ b/solution.py
@@ -18,9 +18,12 @@
 
 SIDE = 8
 TAIL = 16
+RING = [0, 2, 4, 6, 7, 5, 3, 1]
 
 
 class whole:
+    loose = 0
+
     def __init__(self, array):
         self.arrays, self.dims, self.dtype = [array], array.shape, array.dtype
 
@@ -31,9 +34,13 @@
         return [(refs[0], local)]
 
 
+class fresh(whole):
+    loose = 1
+
+
 class stack(whole):
-    def __init__(self, arrays, slot):
-        self.arrays, self.dtype = list(arrays), arrays[0].dtype
+    def __init__(self, arrays, slot, loose=0):
+        self.arrays, self.dtype, self.loose = list(arrays), arrays[0].dtype, loose
         self.dims, self.slot = (len(arrays),) + arrays[0].shape, slot
 
     def plan(self, refs, local):
@@ -49,6 +56,20 @@
         return [(refs[0].at[self.index()], local)]
 
 
+class spread(whole):
+    def __init__(self, array, order, first, rows):
+        self.arrays, self.dtype, self.order = [array], array.dtype, order
+        self.first, self.rows = first, rows
+        self.dims = (array.shape[0], rows) + array.shape[2:]
+
+    def copies(self):
+        return self.dims[0]
+
+    def plan(self, refs, local):
+        cut = pl.ds(self.first, self.rows)
+        return [(refs[0].at[k, cut], local.at[place()]) for k, place in enumerate(self.order)]
+
+
 class result:
     def __init__(self, dims, dtype=F32):
         self.dims, self.dtype = tuple(dims), dtype
@@ -71,14 +92,17 @@
 
 
 class parts_of(result):
-    def __init__(self, source, slots, count, dims, dtype):
-        self.source, self.slots, self.count, self.dims = source, slots, count, None
-        dims = (count,) + tuple(dims[1:])
-        self.outs = [jax.ShapeDtypeStruct(dims, dtype) for _ in slots]
+    dims = None
+
+    def __init__(self, source, slots, count, first, rows, array):
+        self.source, self.slots, self.count, self.cut = source, slots, count, pl.ds(first, rows)
+        dims = (count, rows) + array.shape[2:]
+        self.outs = [jax.ShapeDtypeStruct(dims, array.dtype) for _ in slots]
 
     def plan(self, local, refs):
         return [
-            (local.at[pl.ds(slot(), self.count)], ref) for slot, ref in zip(self.slots, refs)
+            (local.at[pl.ds(slot(), self.count), self.cut], ref)
+            for slot, ref in zip(self.slots, refs)
         ]
 
 
@@ -102,13 +126,11 @@
 
 
 class Given:
-    def __init__(self, local, copies, source=None):
-        self.local, self.copies, self.sent, self.source = local, copies, False, source
+    def __init__(self, local, copies):
+        self.local, self.copies, self.sent = local, copies, False
 
     def send(self):
         if not self.sent:
-            if self.source is not None:
-                self.source.ref()
             for copy in self.copies:
                 copy.start()
             self.sent = True
@@ -124,6 +146,9 @@
 def call(body, takes, gives, scratch=(), flops=0, limit=40, later=()):
     takes = [t if isinstance(t, whole) else whole(t) for t in takes]
     arrays = [a for t in takes for a in t.arrays]
+    pinned = [True] * len(later)
+    for t in takes:
+        pinned += [True] * (len(t.arrays) - t.loose) + [False] * t.loose
     outs = [o for g in gives for o in g.outs]
     n_later, n_in, n_out = len(later), len(arrays), len(outs)
     n_copies = sum(t.copies() for t in takes) + sum(g.copies() for g in gives)
@@ -147,12 +172,11 @@
         for g in gives:
             mine, res = res[: len(g.outs)], res[len(g.outs) :]
             copies = []
-            source = taken[g.source] if g.dims is None else None
-            place = source.local if source else local.pop(0)
+            place = taken[g.source].local if g.dims is None else local.pop(0)
             for a, b in g.plan(place, mine):
                 copies.append(pltpu.make_async_copy(a, b, sems.at[used]))
                 used += 1
-            given.append(Given(place, copies, source))
+            given.append(Given(place, copies))
         body(*taken, *given, *local)
         for t in taken:
             t.ref()
@@ -164,10 +188,15 @@
 
     moved = sum(a.size * a.dtype.itemsize for a in arrays + outs)
     spec = pl.BlockSpec(memory_space=pltpu.HBM)
+    loose = pl.BlockSpec(memory_space=pl.ANY)
+    operands = [
+        pltpu.with_memory_space_constraint(a, pltpu.HBM) if pin else a
+        for a, pin in zip([*later, *arrays], pinned)
+    ]
     values = pl.pallas_call(
         kernel,
         out_shape=[pltpu.HBM(o.shape, o.dtype) for o in outs],
-        in_specs=[spec] * (n_later + n_in),
+        in_specs=[spec if pin else loose for pin in pinned],
         out_specs=[spec] * n_out,
         scratch_shapes=[pltpu.VMEM(t.dims, t.dtype) for t in takes]
         + [pltpu.VMEM(g.dims, g.dtype) for g in gives if g.dims is not None]
@@ -176,7 +205,7 @@
         compiler_params=pltpu.CompilerParams(vmem_limit_bytes=limit * 2**20),
         cost_estimate=pl.CostEstimate(flops=flops, bytes_accessed=moved, transcendentals=0),
         name=body.__name__,
-    )(*(pltpu.with_memory_space_constraint(a, pltpu.HBM) for a in [*later, *arrays]))
+    )(*operands)
     return list(values)
 
 
@@ -300,20 +329,16 @@
     return col_sum(x * x)
 
 
-def pack_weights(w, p, mask, w_next, out, out_next, rows):
+def pack_weights(w, p, mask, w_next, out, rows):
     depth, wide = p.shape
-    w_ref = w.ref()
+    w_ref, next_ref = w.ref(), w_next.ref()
     inside = widen(mask[...].astype(F32), wide)
     blank = jnp.zeros((TAIL - inside.shape[0], wide), F32)
-    pieces = [w_ref[pl.ds(tap, depth, stride=9), :] for tap in range(9)]
-    rows_all = jnp.concatenate(pieces + [p[...], inside, blank], axis=0).astype(BF)
-    out[...] = rows_all
+    pieces = [w_ref[pl.ds(tap, depth, stride=9), :] for tap in range(9)] + [p[...], inside, blank]
+    depth = w_next.shape[0] // 9
+    pieces += [next_ref[pl.ds(tap, depth, stride=9), :] for tap in range(9)]
+    out[...] = jnp.concatenate(pieces, axis=0).astype(BF)
     out.send()
-    depth = out_next.shape[1]
-    w_ref = w_next.ref()
-    for tap in range(9):
-        out_next[tap] = w_ref[pl.ds(tap, depth, stride=9), :].astype(BF)
-    out_next.send()
     rows[...] = rows_of(lane_row(w[...]), lane_row(p[...]), lane_row(w_next[...]))
 
 
@@ -328,7 +353,7 @@
             taken = scratch[k, pl.ds(col, half, stride=2), :].reshape(count, 2, SIDE, wide)
             odd = taken[:, 1].reshape(half // 2, wide).astype(BF)
             odd_out[col, :, cut] = odd
-            part_out[col, :, cut] = odd
+            part_out[col * (lanes // wide) + k] = odd
             even_out[col, :, cut] = taken[:, 0].reshape(half // 2, wide).astype(BF)
     part_out.send()
     inside = widen(mask[...].astype(F32), wide)
@@ -342,34 +367,34 @@
     return w.reshape(-1, 9, w.shape[1]).transpose(1, 0, 2)
 
 
-def taps_of(w):
+def taps_of(w, depth, first=0):
     def taps(*which):
-        return jnp.concatenate([w[:, t].reshape(-1, w.shape[3]) for t in which], axis=1)
+        starts = [first + t * depth for t in which]
+        return jnp.concatenate(
+            [w[:, a : a + depth].reshape(-1, w.shape[2]) for a in starts], axis=1
+        )
 
     return taps
 
 
-def first_taps_of(w):
-    depth = (w.shape[1] - TAIL) // 10
-
-    def taps(*which):
-        return jnp.concatenate(
-            [w[:, t * depth : (t + 1) * depth].reshape(-1, w.shape[2]) for t in which], axis=1
-        )
-
-    return taps
+def halo_of(blocks):
+    half = blocks.shape[0] // 2
+    return [
+        jnp.concatenate([blocks[col * half + k] for k in range(half)], axis=1) for col in range(2)
+    ]
 
 
 def make_conv_first(mask_rides):
     def conv_first(*refs):
         w, x0, x1, xh, n = refs[:5]
-        zb_out, zp_out, pay, sums_out, valid_out, w_out = refs[-6:]
-        taps = first_taps_of(w)
+        zb_out, zp_out, pay, sums_out, valid_out = refs[-5:]
+        taps = taps_of(w, (w.shape[1] - TAIL) // 10)
         wide = w.shape[2]
         y00 = dot(x0[0], taps(4, 9))
         y01 = dot(x0[1], taps(5, 3))
         y10 = dot(x1[0], taps(7))
         y11 = dot(x1[1], taps(8, 6))
+        xh = halo_of(xh)
         yh0 = dot(xh[0], taps(1))
         yh1 = dot(xh[1], taps(2, 0))
         here = (y00[:, :wide] + y01[:, :wide]) + (y10 + y11[:, :wide]) + (yh0 + yh1[:, :wide])
@@ -389,13 +414,16 @@
         pay[:, :part] = zb.reshape(SIDE, part, wide)
         pay[:, part:] = jnp.broadcast_to(rows[None], (SIDE, TAIL, wide))
         pay.send()
-        w_out.send()
         zb_out[...] = zb
         zp_out[...] = zp
         sums_out[...] = rows_of(col_sum(vzp), col_sum(vzp * zp))
         valid_out[...] = valid
 
     return conv_first
+
+
+def hand_on(w, *outs):
+    w.ref()
 
 
 def first_norm(z, rows):
@@ -405,7 +433,7 @@
     return hat, hat * rows[3:4] + rows[4:5], inverse
 
 
-def conv_second(got, m, w, zp, sums, h_out, z2_out, pay, tot_out, w_out):
+def conv_second(got, m, w, zp, sums, h_out, z2_out, pay, tot_out):
     blocks, wide = got.shape[0], got.shape[3]
     part = pay.shape[1] - TAIL
     pay[:, :part] = zp[...].astype(BF).reshape(SIDE, part, wide)
@@ -421,7 +449,8 @@
         hidden.append((lin * jax.nn.sigmoid(lin) * valid).astype(BF))
         h_out[:, k * wide : (k + 1) * wide] = hidden[-1]
     hidden = jnp.concatenate(hidden, axis=1)
-    taps = taps_of(w)
+    depth = hidden.shape[1] // w.shape[0]
+    taps = taps_of(w, depth)
     moved = []
     for col in range(3):
         y = dot(hidden, taps(col, 3 + col, 6 + col))
@@ -433,7 +462,6 @@
     rows = jnp.concatenate([col_sum(vz), col_sum(vz * z2), sums[0:1], sums[1:2]], axis=0)
     pay[:, part:] = jnp.broadcast_to(three_rows(rows)[None], (SIDE, TAIL, wide))
     pay.send()
-    w_out.send()
     z2_out[...] = z2
 
 
@@ -477,13 +505,14 @@
 
 def grad_hidden(w, g2, got, tot1, m, pay):
     blocks, _, wide = g2.shape
-    depth = w.shape[1] * w.shape[3]
+    count, part = w.shape[1], w.shape[2] // 9
+    depth = count * part
     moved = []
     for col in range(3):
         y = 0.0
         for k in range(blocks):
-            block = w[k]
-            taps = [block[:, 3 * row + col].reshape(depth, wide) for row in range(3)]
+            starts = [(3 * row + col) * part for row in range(3)]
+            taps = [w[k, :, a : a + part].reshape(depth, wide) for a in starts]
             y = y + dot_nt(g2[k], jnp.concatenate(taps, axis=0))
         moved.append(
             shift_row(y[:, :depth], -1) + y[:, depth : 2 * depth] + shift_row(y[:, 2 * depth :], 1)
@@ -497,14 +526,28 @@
     pay[:, part:] = jnp.broadcast_to(rows[None], (SIDE, TAIL, depth))
 
 
-def grad_second(h, g2, x, gp, g_out):
+def make_grad_second(on_ring):
+    def grad_second(h, g2, x, gp, g_out):
+        places = list(range(g_out.shape[0]))
+        if on_ring:
+            last, turn = len(RING) - 1, turn_round()
+            places = [RING.index(k) for k in places]
+            places = [p + turn * (last - 2 * p) for p in places]
+        grad_second_in(places, h, g2, x, gp, g_out)
+
+    return grad_second
+
+
+def grad_second_in(places, h, g2, x, gp, g_out):
     groups, rows, wide = g_out.shape
     share = h.shape[1] // groups
     h, g2 = h[...], g2[...].astype(F32)
     moved = [shift_col(g2, step).astype(BF) if step else g2.astype(BF) for step in (-1, 0, 1)]
 
     def put(rows, g):
-        g_out[:, rows] = g.astype(BF).reshape(groups, -1, wide)
+        g = g.astype(BF).reshape(groups, -1, wide)
+        for k, place in enumerate(places):
+            g_out[place, rows] = g[k]
 
     for tap in range(9):
         step = tap // 3 - 1
@@ -533,7 +576,7 @@
         rows = grad.astype(BF).reshape(groups, share, wide)
         blocks_out[:, tap * share : (tap + 1) * share] = rows
 
-    for x, plain, (right, left) in ((x0, 4, (5, 3)), (x1, 7, (8, 6)), (xh, 1, (2, 0))):
+    for x, plain, (right, left) in ((x0, 4, (5, 3)), (x1, 7, (8, 6)), (halo_of(xh), 1, (2, 0))):
         put(plain, dot_tn(x[0], here))
         pair = dot_tn(x[1], both)
         put(right, pair[:, :wide])
@@ -576,25 +619,23 @@
     out[...] = scratch[...][:, :half].astype(BF).reshape(out.shape)
 
 
-def reduce_second(*refs):
-    *parts, g_out, gp_out, rows = refs
-    total = add_up([part[...] for part in parts])
-    depth = g_out.shape[0] // 9
+def put_rows(out, total):
+    depth = out.shape[0] // 9
     for tap in range(9):
-        g_out.local[pl.ds(tap, depth, stride=9), :] = total[tap * depth : (tap + 1) * depth]
-    conv, proj = total[: 9 * depth], total[9 * depth :]
-    gp_out[...] = proj
-    rows[...] = rows_of(lane_row(conv), lane_row(proj))
-
-
-def reduce_first(x, sw, sg, t3, t4, n, g_out, pay):
-    total = add_up([x[k] for k in range(x.shape[0])])
-    depth = g_out.shape[0] // 9
-    conv = [sw[0:1], lane_row(total), sw[2:3], sg[0:1], sw[1:2], sg[1:2]]
+        out.local[pl.ds(tap, depth, stride=9), :] = total[tap * depth : (tap + 1) * depth]
+
+
+def reduce_all(second, x, sw, t3, t4, n, g1_out, g2_out, gp_out, pay):
+    second = second[...].astype(F32)
+    cut = g2_out.shape[0]
+    conv, proj = second[:cut], second[cut:]
+    parts = [lane_row(conv), lane_row(proj)]
+    first = add_up([x[k] for k in range(x.shape[0])])
+    rows = [sw[0:1], lane_row(first), sw[2:3], parts[0], sw[1:2], parts[1]]
     nw, gn = n[...], norm_grad(t3, t4)
     blank = jnp.zeros((2, nw.shape[1]), F32)
     cols = [
-        jnp.sum(jnp.concatenate(conv + [blank], axis=0), axis=1, keepdims=True),
+        jnp.sum(jnp.concatenate(rows + [blank], axis=0), axis=1, keepdims=True),
         jnp.sum(jnp.concatenate([nw * nw, blank], axis=0), axis=1, keepdims=True),
         jnp.sum(jnp.concatenate([gn * gn, blank], axis=0), axis=1, keepdims=True),
     ]
@@ -604,8 +645,10 @@
         block = jnp.where(lane == place, col, block)
     spread_rows(pay, block)
     pay.send()
-    for tap in range(9):
-        g_out.local[pl.ds(tap, depth, stride=9), :] = total[tap * depth : (tap + 1) * depth]
+    gp_out[...] = proj
+    put_rows(g2_out, conv)
+    g2_out.send()
+    put_rows(g1_out, first)
 
 
 def norm_grad(t3, t4):
@@ -643,7 +686,17 @@
 
 
 def exchange(blocks, axes):
-    return lax.all_to_all(blocks, axes, 0, 0)
+    groups = [list(range(lax.axis_size(axes)))]
+    return lax.all_to_all(blocks, axes, 0, 0, axis_index_groups=groups)
+
+
+def rings():
+    count = lax.axis_size("chan")
+    return [[(d ^ (c % 2)) * count + c for d in RING] for c in range(count)]
+
+
+def turn_round():
+    return lax.axis_index("chan") % 2
 
 
 def swap(array, axis, bits):
@@ -720,64 +773,63 @@
     def slot_ch(k):
         return lax.axis_index("chan") ^ k
 
+    first_rows, second_rows = 10 * d_in // groups + TAIL, 9 * d_out // groups
     if eight:
-        own, own_second, squares = call(
-            pack_weights,
-            [w_first, w_proj, mask, w_second],
-            [
-                result((10 * first_here + TAIL, wide), BF),
-                result((9, second_here, wide), BF),
-                square_rows,
-            ],
-        )
-        taps_second = whole(lax.all_gather(own_second, "dp"))
-        near = [swap(own, "dp", k) for k in (4, 1, 2, 3)]
         even, odd, send, valid = call(
             pack_images,
             [images, mask],
             [
                 result(pixel_pair, BF),
                 result(pixel_pair, BF),
-                split([lambda: lax.axis_index("chan") % 2], pixel_pair, BF),
+                split([away("chan", 0)], (ch_count, pix, wide), BF),
                 result((pix, wide)),
             ],
             scratch=[((d_in // wide, images.shape[0] * pix_here, wide), F32)],
-            later=[own],
         )
         come = lax.ppermute(send, "dp", [(i, i + 1) for i in range(dp_count - 1)])
-        come, *near = lax.optimization_barrier((come, *near))
-        pieces = [own, *near[1:], near[0]] + [swap(near[0], "dp", k) for k in (1, 2, 3)]
-        taps_first, masks = stack(pieces, slot_dp), []
-        halo = stack([come, swap(come, "chan", 1)], lambda k: (lax.axis_index("chan") % 2) ^ k)
+        own, squares = call(
+            pack_weights,
+            [w_first, w_proj, mask, w_second],
+            [result((first_rows + second_rows, wide), BF), square_rows],
+        )
+        gathered = lax.all_gather(own, everyone, axis_index_groups=rings())
+        order, masks = [lambda d=d: d ^ turn_round() for d in RING], []
+        far = swap(come, "chan", 2)
+        halo = stack([come, swap(come, "chan", 1), far, swap(far, "chan", 1)], slot_ch)
     else:
         inside = mask.reshape(batch, SIDE, SIDE).transpose(1, 0, 2).reshape(pix, 1).astype(F32)
         valid = jnp.broadcast_to(inside, (pix, wide))
         masks = [valid]
         own = jnp.concatenate([tap_major(w_first), w_proj[None]], axis=0).astype(BF)
         own = in_groups(lax.all_gather(own, "dp", axis=1, tiled=True), groups)
-        own = own.reshape(groups, 10 * d_in // groups, wide)
-        taps_first = whole(jnp.pad(own, ((0, 0), (0, TAIL), (0, 0))))
+        own = jnp.pad(own.reshape(groups, -1, wide), ((0, 0), (0, TAIL), (0, 0)))
+        next = lax.all_gather(tap_major(w_second).astype(BF), "dp", axis=1, tiled=True)
+        next = in_groups(next, groups).reshape(groups, -1, wide)
+        gathered = jnp.concatenate([own, next], axis=1)
+        order = [lambda g=g: g for g in range(groups)]
         squares = jnp.zeros((SIDE, wide), F32).at[0].set(jnp.sum(w_first * w_first, axis=0))
         squares = squares.at[1].set(jnp.sum(w_proj * w_proj, axis=0))
+        squares = squares.at[2].set(jnp.sum(w_second * w_second, axis=0))
         own = images.reshape(dp_count, batch, pix_here, d_in)
         own = exchange(own, "dp").transpose(1, 0, 2, 3)
         own = own.reshape(batch, SIDE, 2, SIDE, 2, d_in).transpose(2, 4, 1, 0, 3, 5)
         even, odd = own.reshape(2, 2, pix, d_in)
         halo = jnp.pad(odd, ((0, 0), (part, 0), (0, 0)))[:, :pix]
+        halo = halo.reshape(2, pix, 2, wide).transpose(0, 2, 1, 3).reshape(ch_count, pix, wide)
 
     macs = pix * 9 * wide * d_in
     per_block = groups // ch_count
+
     block_slots = [lambda k=k: (lax.axis_index("chan") ^ k) * per_block for k in range(ch_count)]
-    z_rows, z_proj, pay, sums_proj, valid_rows, *turned_first = call(
+    z_rows, z_proj, pay, sums_proj, valid_rows = call(
         make_conv_first(eight),
-        [taps_first, even, odd, halo, norm_params] + masks,
+        [spread(gathered, order, 0, first_rows), even, odd, halo, norm_params] + masks,
         [
             result((pix, wide), BF),
             result((pix, wide)),
             message,
             square_rows,
             result((pix, wide)),
-            parts_of(0, block_slots, per_block, taps_first.dims, BF),
         ],
         flops=2 * macs,
     )
@@ -787,81 +839,92 @@
         got1 = stack([got1_mine, swap(got1_mine, "chan", 1), far, swap(far, "chan", 1)], slot_ch)
     else:
         got1 = plain_forward(pay)
-        own_second = lax.all_gather(tap_major(w_second).astype(BF), "dp", axis=1, tiled=True)
-        taps_second = whole(in_groups(own_second, groups))
-        squares = squares.at[2].set(jnp.sum(w_second * w_second, axis=0))
-
-    hidden, z_second, pay, total1, *turned = call(
+
+    hidden, z_second, pay, total1 = call(
         conv_second,
-        [got1, valid, taps_second, z_proj, sums_proj],
+        [got1, valid, spread(gathered, order, first_rows, second_rows), z_proj, sums_proj],
         [
             result((pix, d_out), BF),
             result((pix, wide)),
             message,
             result((ch_count, SIDE, wide)),
-            parts_of(2, block_slots, per_block, taps_second.dims, BF),
         ],
         flops=4 * macs,
     )
+    turned = call(
+        hand_on,
+        [spread(gathered, order, 0, first_rows + second_rows)],
+        [
+            parts_of(0, block_slots, per_block, 0, first_rows, gathered),
+            parts_of(0, block_slots, per_block, first_rows, second_rows, gathered),
+        ],
+        later=[z_second],
+    )
+    turned_first, turned = turned[:ch_count], turned[ch_count:]
     turned = turned[:1] + [swap(block, "chan", k) for k, block in enumerate(turned) if k]
-    turned_first = turned_first[:1] + [
-        swap(block, "chan", k) for k, block in enumerate(turned_first) if k
-    ]
     total1_own = pick(total1, away("chan", 0))
     got2 = exchange(pay, "dp") if eight else plain_sums(pay, 4)
     output, e, pay, total2 = call(
         block_output,
-        [z_second, got2, total1_own, valid, norm_params, cotangent],
+        [z_second, fresh(got2), total1_own, valid, norm_params, cotangent],
         [result((batch, SIDE * SIDE, wide), BF), result((pix, wide)), message, square_rows],
     )
     got3 = exchange(pay, "dp") if eight else plain_sums(pay, 3)
 
     g_second_out, g_proj_out, total3 = call(
         grad_outputs,
-        [z_second, e, got3, total2, total1_own, norm_params, valid, valid_rows, z_proj],
+        [z_second, e, fresh(got3), total2, total1_own, norm_params, valid, valid_rows, z_proj],
         [result((pix, wide), BF), result((pix, wide), BF), square_rows],
-        later=turned[1:] + turned_first[1:],
-    )
-    far = swap(g_second_out, "chan", 2)
-    g_all = [g_second_out, swap(g_second_out, "chan", 1), far, swap(far, "chan", 1)]
-
+        later=turned[1:],
+    )
     rows_second = 9 * (d_out // groups) + d_in // groups
     takes = [hidden, g_second_out, pick(even, lambda: 0), g_proj_out]
     (grads,) = call(
-        grad_second,
+        make_grad_second(eight),
         takes,
         [result((groups, rows_second, wide), BF)],
         flops=4 * macs,
     )
+    far = swap(g_second_out, "chan", 2)
+    far, grads = lax.optimization_barrier((far, grads))
+    g_all = [g_second_out, swap(g_second_out, "chan", 1), far, swap(far, "chan", 1)]
     if eight:
-        *g_all, grads = lax.optimization_barrier((*g_all, grads))
-        grads = grads.reshape(groups * rows_second, wide)
-        for axis_groups in ([[0, 2, 4, 6], [1, 3, 5, 7]], [[0, 1], [2, 3], [4, 5], [6, 7]]):
-            grads = lax.psum_scatter(
-                grads, "dp", scatter_dimension=0, axis_index_groups=axis_groups, tiled=True
-            )
-        takes = [grads]
+        grads = lax.psum_scatter(
+            grads.reshape(groups * rows_second, wide),
+            everyone,
+            scatter_dimension=0,
+            axis_index_groups=rings(),
+            tiled=True,
+        )
+        grads_second = grads
     else:
         cut = 9 * (d_out // groups)
         grads = [regroup(grads[:, :cut], 9, dp_count), regroup(grads[:, cut:], 1, dp_count)]
         grads = jnp.concatenate(grads, axis=1)
-        takes = [jnp.sum(exchange(grads, "dp").astype(F32), axis=0)]
-    reduced_second, reduced_proj, squares_second = call(
-        reduce_second, takes, [result(w_second.shape), result(w_proj.shape), square_rows]
-    )
+        grads_second = jnp.sum(exchange(grads, "dp").astype(F32), axis=0)
 
     got1_own = got1_mine if eight else pick(got1, away("chan", 0))
     (pay,) = call(
         grad_hidden,
-        [stack(turned, slot_ch), stack(g_all, slot_ch), got1_own, total1_own, valid],
+        [
+            stack(turned, slot_ch),
+            stack(g_all, slot_ch, 3),
+            got1_own,
+            total1_own,
+            valid,
+        ],
         [message],
         flops=4 * macs,
     )
+    pay, *turned_first = lax.optimization_barrier((pay, *turned_first))
+    turned_first = turned_first[:1] + [
+        swap(block, "chan", k) for k, block in enumerate(turned_first) if k
+    ]
     got4 = exchange(pay, "dp") if eight else plain_sums(pay, 2)
 
     g_first_out, grads, total4 = call(
         grad_first,
-        [got4, z_rows, total1_own, norm_params, valid_rows, even, odd, halo, g_proj_out],
+        [fresh(got4), z_rows, total1_own, norm_params, valid_rows, even, odd, halo, g_proj_out],
         [
             result((2, pix, wide), BF),
             result((groups, 9 * (d_in // groups), wide), BF),
@@ -875,11 +938,37 @@
 
     far = swap(g_first_out, "chan", 2)
     g_all = [g_first_out, swap(g_first_out, "chan", 1), far, swap(far, "chan", 1)]
+    got_first, *g_all = lax.optimization_barrier((got_first, *g_all))
+    reduced_first, reduced_second, reduced_proj, pay = call(
+        reduce_all,
+        [grads_second, fresh(got_first), squares, total3, total4, norm_params],
+        [
+            result(w_first.shape),
+            result(w_second.shape),
+            result(w_proj.shape),
+            result((n_all, SIDE, wide)),
+        ],
+    )
+    got6 = exchange(pay, everyone)
+
     own, above = call(
         grad_images,
-        [stack(g_all, slot_ch), stack(turned_first, slot_ch)],
+        [stack(g_all, slot_ch, 3), stack(turned_first, slot_ch)],
         [result((2, pix, wide)), result((pix, wide), BF)],
         flops=2 * macs,
+        later=[pay],
+    )
+    conv = (
+        (w_first, reduced_first, mom_first, avg_first),
+        (w_second, reduced_second, mom_second, avg_second),
+        (w_proj, reduced_proj, mom_proj, avg_proj),
+    )
+    results = call(
+        make_update(dp_count),
+        [fresh(got6), total3, total4, *(array for group in conv for array in group)]
+        + [norm_params, mom_norm, avg_norm],
+        [result(group[0].shape) for group in conv for _ in range(3)]
+        + [result(norm_params.shape)] * 3,
     )
     half = wide // 2
     if eight:
@@ -889,34 +978,16 @@
             [own, come],
             [result((images.shape[0], pix_here, half), BF)],
             scratch=[((images.shape[0] * pix_here, wide), F32)],
+            later=results[:1],
         )
     else:
         cols = pix_here // 2
-        above = jnp.pad(above, ((0, part), (0, 0)))[part:].astype(F32)
-        total = jnp.stack([own[0], own[1] + above]).astype(BF)
+        below = jnp.pad(above, ((0, part), (0, 0)))[part:].astype(F32)
+        total = jnp.stack([own[0], own[1] + below]).astype(BF)
         total = total.reshape(2, SIDE, batch, SIDE // cols, cols, wide)
         total = total.transpose(1, 0, 3, 2, 4, 5).reshape(dp_count, batch, cols, wide)
         grad_pixels = exchange(total, "dp").reshape(dp_count * batch, pix_here, half)
 
-    reduced_first, pay = call(
-        reduce_first,
-        [got_first, squares, squares_second, total3, total4, norm_params],
-        [result(w_first.shape), result((n_all, SIDE, wide))],
-    )
-    got6 = exchange(pay, everyone)
-
-    conv = (
-        (w_first, reduced_first, mom_first, avg_first),
-        (w_second, reduced_second, mom_second, avg_second),
-        (w_proj, reduced_proj, mom_proj, avg_proj),
-    )
-    results = call(
-        make_update(dp_count),
-        [got6, total3, total4, *(array for group in conv for array in group)]
-        + [norm_params, mom_norm, avg_norm],
-        [result(group[0].shape) for group in conv for _ in range(3)]
-        + [result(norm_params.shape)] * 3,
-    )
     return (output, grad_pixels, *results)
 
 

time: 199 us -> 177 us (0.89)
  starting transfers between devices: 44.4 us -> 30.5 us
  blocking collectives: 33.4 us -> 25.4 us
  local copies, waits for them, and re-layouts: 6.56 us -> 2.71 us
  waiting for transfers between devices: 58.2 us -> 60.9 us
    all_gather x1, waiting for transfers between devices: 0.01 us -> 18.3 us  [per_device(): gathered = lax.all_gather(own, everyone, axis_index_groups=rings())]
    reduce_scatter x2 -> x1, waiting for transfers between devices: 13.5 us -> 0.01 us  [per_device(): lax.psum_scatter(grads.reshape(groups * rows_second, wide), everyone, sca...]
    ppermute x23 -> x18, starting transfers between devices: 22.9 us -> 10.1 us  [swap(): lax.ppermute(array, axis, [(i, i ^ bits) for i in range(lax.axis_size(axi...]
    ppermute x23 -> x18, waiting for transfers between devices: 32.3 us -> 21.8 us  [swap(): lax.ppermute(array, axis, [(i, i ^ bits) for i in range(lax.axis_size(axi...]
    all_to_all x4, waiting for transfers between devices: 5.9 us -> 14.6 us  [exchange(): return lax.all_to_all(blocks, axes, 0, 0, axis_index_groups=groups)]
    all_to_all x2, blocking collectives: 33.4 us -> 25.4 us  [exchange(): return lax.all_to_all(blocks, axes, 0, 0, axis_index_groups=groups)]
    ppermute x1, waiting for transfers between devices: 6.46 us -> 1.16 us  [per_device(): come = lax.ppermute(above, 'dp', [(i + 1, i) for i in range(dp_count - 1)])]
    ppermute x1, waiting for transfers between devices: 0.01 us -> 5.09 us  [per_device(): come = lax.ppermute(send, 'dp', [(i, i + 1) for i in range(dp_count - 1)])]
  transfers between devices with their start and end apart: 32 -> 26, of which waited for: 15 -> 15; matrix products, arithmetic and copies ran while one was open for 0% -> 0% of each run, Pallas kernels for 15% -> 16%
where the time goes in v1:
time: 177 us; the launch traced here: 176 us
  waiting for transfers between devices  60.9 us (34%)
  Pallas kernels  41.8 us (24%)
  starting transfers between devices  30.5 us (17%)
  blocking collectives  25.4 us (14%)
  between operations  14.4 us (8%)
  local copies, waits for them, and re-layouts  2.71 us (2%)
    pallas_call x14, Pallas kernels, call(): pl.pallas_call(kernel, out_shape=[pltpu.HBM(o.shape, o.dtype) for o in ou...  41.8 us
    all_to_all x2, blocking collectives, exchange(): return lax.all_to_all(blocks, axes, 0, 0, axis_index_groups=groups)  25.4 us
    ppermute x18, waiting for transfers between devices, swap(): lax.ppermute(array, axis, [(i, i ^ bits) for i in range(lax.axis_size(axi...  21.8 us
    all_gather x1, waiting for transfers between devices, per_device(): gathered = lax.all_gather(own, everyone, axis_index_groups=rings())  18.3 us
    all_to_all x4, waiting for transfers between devices, exchange(): return lax.all_to_all(blocks, axes, 0, 0, axis_index_groups=groups)  14.6 us
    all_to_all x4, starting transfers between devices, exchange(): return lax.all_to_all(blocks, axes, 0, 0, axis_index_groups=groups)  14.2 us
    ppermute x18, starting transfers between devices, swap(): lax.ppermute(array, axis, [(i, i ^ bits) for i in range(lax.axis_size(axi...  10.1 us
    ppermute x1, waiting for transfers between devices, per_device(): come = lax.ppermute(send, 'dp', [(i, i + 1) for i in range(dp_count - 1)])  5.09 us
  transfers between devices with their start and end apart: 26, of which 15 were waited for; matrix products, arithmetic and copies ran while one was open for 0% of the time, Pallas kernels for 16%

profile of v1, /device:TPU:0, one launch (start us, length us, event | category | flops | bytes accessed | tf_op | source)
XLA Modules:
  0.0 175.8 jit_solution(16515478185391085567)
XLA Ops:
  7.2 1.9 %pack_weights.1 = (bf16[912,128]{1,0:T(8,128)(2,1)}, f32[8,128]{1,0:T(8,128)}) custom-call(f32[288,128]{1,0:T(8,128)} %refs_3_.5, f32[32,128]{1,0:T(8,128)} %refs_11_.1, s32[8,64]{1,0:T(8,128)} %refs_1_.3, f32[576,128]{1,0:T(8,128)} %refs_7_.3), custom_call_target="tpu_custom_call" | custom-call | bytes 698368 | tf_op jit(solution)/shard_map/pack_weights/pallas_call | solution.py:196
  9.1 2.7 %pack_images.1 = (bf16[2,512,256]{2,1,0:T(8,128)(2,1)}, bf16[2,512,256]{2,1,0:T(8,128)(2,1)}, bf16[512,128]{1,0:T(8,128)(2,1)}, f32[512,128]{1,0:T(8,128)}) custom-call(bf16[64,32,256]{2,1,0:T(8,128)(2,1)} %refs_0_.3, s32[8,64]{1,0:T(8,128)} %refs_1_.3), custom_call_target="tpu_custom_call" | custom-call | bytes 2492416 | tf_op jit(solution)/shard_map/pack_images/pallas_call | solution.py:196
  11.8 4.9 %collective-permute-start = (bf16[512,128]{1,0:T(8,128)(2,1)}, bf16[512,128]{1,0:T(8,128)(2,1)S(1)}, u32[]{:S(2)}, u32[]{:S(2)}) collective-permute-start(bf16[512,128]{1,0:T(8,128)(2,1)} %get-tuple-element.80), channel_id=1, source_target_pairs={{0,4},{4,8},{8,12},{12,16},{16,20},{20,24},{24,28},{1,5},{5,9},{9,... | collective-permute-start | bytes 393224 | tf_op jit(solution)/shard_map/ppermute | solution.py:789
  16.7 5.1 %collective-permute-done.refs_3_.refs_7_ = bf16[512,128]{1,0:T(8,128)(2,1)S(1)} collective-permute-done((bf16[512,128]{1,0:T(8,128)(2,1)}, bf16[512,128]{1,0:T(8,128)(2,1)S(1)}, u32[]{:S(2)}, u32[]{:S(2)}) %collective-permute-start) | collective-permute-done | bytes 131104 | tf_op jit(solution)/shard_map/ppermute | solution.py:789
  21.8 1.0 collective-permute-start.2
  22.8 4.0 %collective-permute-done.2.refs_5_.refs_9_ = bf16[512,128]{1,0:T(8,128)(2,1)S(1)} collective-permute-done((bf16[512,128]{1,0:T(8,128)(2,1)S(1)}, bf16[512,128]{1,0:T(8,128)(2,1)S(1)}, u32[]{:S(2)}, u32[]{:S(2)}) %collective-permute-start.2) | collective-permute-done | bytes 131104 | tf_op jit(solution)/shard_map/ppermute | solution.py:703
  26.8 1.3 collective-permute-done.3.refs_6_.refs_10_
  28.1 18.3 %all-gather.3.cloned.1.call-done = bf16[7296,128]{1,0:T(8,128)(2,1)} async-done(((bf16[912,128]{1,0:T(8,128)(2,1)}), bf16[7296,128]{1,0:T(8,128)(2,1)}) %all-gather.3.cloned.1.call-update) | async-done | bytes 1867792 | tf_op jit(solution)/shard_map/all_gather | solution.py:795
  46.4 3.6 %conv_first.1 = (bf16[512,128]{1,0:T(8,128)(2,1)}, f32[512,128]{1,0:T(8,128)}, bf16[8,80,128]{2,1,0:T(8,128)(2,1)}, f32[8,128]{1,0:T(8,128)}, f32[512,128]{1,0:T(8,128)}) custom-call(bf16[8,912,128]{2,1,0:T(8,128)(2,1)} %bitcast.2, bf16[2,512,256]{2,1,0:T(8,128)(2,1)} %get-tuple-element.78.refs_1_.refs_2_.refs_5_, ...), custom_call_target="tpu_custom_call" | custom-call | flops 301989888 | bytes 4267008 | tf_op jit(solution)/shard_map/conv_first/pallas_call | solution.py:196
  50.0 11.2 %all_to_all.30.refs_0_.refs_8_ = bf16[8,80,128]{2,1,0:T(8,128)(2,1)S(1)} all-to-all(bf16[8,80,128]{2,1,0:T(8,128)(2,1)} %get-tuple-element.81), channel_id=1, replica_groups={{0,4,8,12,16,20,24,28},{1,5,9,13,17,21,25,29},{2,6,10,14,18,22,26,30},{..., dimensions={0} | all-to-all | bytes 327680 | tf_op jit(solution)/shard_map/all_to_all | solution.py:690
  61.2 1.5 collective-permute-start.5
  62.7 3.9 %collective-permute-done.5.refs_2_ = bf16[8,80,128]{2,1,0:T(8,128)(2,1)S(1)} collective-permute-done((bf16[8,80,128]{2,1,0:T(8,128)(2,1)S(1)}, bf16[8,80,128]{2,1,0:T(8,128)(2,1)S(1)}, u32[]{:S(2)}, u32[]{:S(2)}) %collective-permute-start.5) | collective-permute-done | bytes 163872 | tf_op jit(solution)/shard_map/ppermute | solution.py:703
  66.5 1.4 collective-permute-done.6.refs_3_
  67.9 0.7 copy-done.14
  68.6 4.4 %conv_second.1 = (bf16[512,512]{1,0:T(8,128)(2,1)}, f32[512,128]{1,0:T(8,128)}, bf16[8,80,128]{2,1,0:T(8,128)(2,1)}, f32[4,8,128]{2,1,0:T(8,128)}) custom-call(bf16[8,80,128]{2,1,0:T(8,128)(2,1)} %copy-done, bf16[8,80,128]{2,1,0:T(8,128)(2,1)} %copy-done.13, bf16[8,80,128]{2,1,0:T(8,128)(2,1)} %copy-done.12, bf16[8,80,128]{2,1,0:T(8,128)(2,1)} %copy-done.14, ...), custom_call_target="tpu_custom_call" | custom-call | flops 603979776 | bytes 4018176 | tf_op jit(solution)/shard_map/conv_second/pallas_call | solution.py:196
  73.0 3.4 %all-to-all-start.1 = ((bf16[8,80,128]{2,1,0:T(8,128)(2,1)}), bf16[8,80,128]{2,1,0:T(8,128)(2,1)S(1)}, u32[]{:S(2)}, u32[]{:S(2)}) async-start(bf16[8,80,128]{2,1,0:T(8,128)(2,1)} %get-tuple-element.86), calls=%async_computation.1 | async-start | bytes 327680 | tf_op jit(solution)/shard_map/all_to_all | solution.py:690
  76.4 2.9 %hand_on.1 = (bf16[2,336,128]{2,1,0:T(8,128)(2,1)}, bf16[2,336,128]{2,1,0:T(8,128)(2,1)}, bf16[2,336,128]{2,1,0:T(8,128)(2,1)}, bf16[2,336,128]{2,1,0:T(8,128)(2...) custom-call(f32[512,128]{1,0:T(8,128)} %get-tuple-element.85.refs_0_, ...), custom_call_target="tpu_custom_call" | custom-call | bytes 3735552 | tf_op jit(solution)/shard_map/hand_on/pallas_call | solution.py:196
  79.5 1.5 collective-permute-start.8
  81.2 3.1 %all-to-all-done.1.refs_1_ = bf16[8,80,128]{2,1,0:T(8,128)(2,1)S(1)} async-done(((bf16[8,80,128]{2,1,0:T(8,128)(2,1)}), bf16[8,80,128]{2,1,0:T(8,128)(2,1)S(1)}, u32[]{:S(2)}, u32[]{:S(2)}) %all-to-all-start.1) | async-done | bytes 163872 | tf_op jit(solution)/shard_map/all_to_all | solution.py:690
  84.3 2.2 %block_output.1 = (bf16[8,64,128]{2,1,0:T(8,128)(2,1)}, f32[512,128]{1,0:T(8,128)}, bf16[8,80,128]{2,1,0:T(8,128)(2,1)}, f32[8,128]{1,0:T(8,128)}) custom-call(f32[512,128]{1,0:T(8,128)} %get-tuple-element.85.refs_0_.refs_3_, bf16[8,80,128]{2,1,0:T(8,128)(2,1)S(1)} %all-to-all-done.1.refs_1_, f32[4,8,128]{2,1,0:T(8,128)} %get-tuple-element.87.refs_2_.refs_7_.refs_9_, ...), custom_call_target="tpu_custom_call" | custom-call | bytes 1399808 | tf_op jit(solution)/shard_map/block_output/pallas_call | solution.py:196
  86.6 3.4 %all-to-all-start.2 = ((bf16[8,80,128]{2,1,0:T(8,128)(2,1)}), bf16[8,80,128]{2,1,0:T(8,128)(2,1)S(1)}, u32[]{:S(2)}, u32[]{:S(2)}) async-start(bf16[8,80,128]{2,1,0:T(8,128)(2,1)} %get-tuple-element.93), calls=%async_computation.2 | async-start | bytes 327680 | tf_op jit(solution)/shard_map/all_to_all | solution.py:690
  90.1 4.7 %collective-permute-done.9.refs_2_.refs_3_ = bf16[2,576,128]{2,1,0:T(8,128)(2,1)S(1)} collective-permute-done((bf16[2,576,128]{2,1,0:T(8,128)(2,1)}, bf16[2,576,128]{2,1,0:T(8,128)(2,1)S(1)}, u32[]{:S(2)}, u32[]{:S(2)}) %collective-permute-start.9) | collective-permute-done | bytes 294944 | tf_op jit(solution)/shard_map/ppermute | solution.py:703
  94.8 2.7 %all-to-all-done.2.refs_5_ = bf16[8,80,128]{2,1,0:T(8,128)(2,1)S(1)} async-done(((bf16[8,80,128]{2,1,0:T(8,128)(2,1)}), bf16[8,80,128]{2,1,0:T(8,128)(2,1)S(1)}, u32[]{:S(2)}, u32[]{:S(2)}) %all-to-all-start.2) | async-done | bytes 163872 | tf_op jit(solution)/shard_map/all_to_all | solution.py:690
  97.5 2.3 %grad_outputs.1 = (bf16[512,128]{1,0:T(8,128)(2,1)}, bf16[512,128]{1,0:T(8,128)(2,1)}, f32[8,128]{1,0:T(8,128)}) custom-call(bf16[2,576,128]{2,1,0:T(8,128)(2,1)} %copy-done.1, bf16[2,576,128]{2,1,0:T(8,128)(2,1)} %copy-done.2, bf16[2,576,128]{2,1,0:T(8,128)(2,1)} %copy-done.3, f32[512,128]{1,0:T(8,128)} %get-tuple-element.85.refs_0_.refs_3_, ...), custom_call_target="tpu_custom_call" | custom-call | bytes 1764352 | tf_op jit(solution)/shard_map/grad_outputs/pallas_call | solution.py:196
  99.8 1.5 collective-permute-start.10
  101.3 4.0 %grad_second.1 = bf16[8,608,128]{2,1,0:T(8,128)(2,1)} custom-call(bf16[512,512]{1,0:T(8,128)(2,1)} %get-tuple-element.97.refs_0_, bf16[512,128]{1,0:T(8,128)(2,1)} %get-tuple-element.96.refs_1_.refs_4_, bf16[2,512,256]{2,1,0:T(8,128)(2,1)} %get-tuple-element.78.refs_1_.refs_2_.refs_5_, bf16[512,128]{1,0:T(8,128)(2,1)} %get-tuple-element.98.refs_3_.refs_11_), custom_call_target="tpu_custom_call" | custom-call | flops 603979776 | bytes 2555904 | tf_op jit(solution)/shard_map/grad_second/pallas_call | solution.py:196
  105.5 0.5 collective-permute-start.12
  106.0 0.8 collective-permute-done.11.refs_5_
  107.0 3.7 %grad_hidden.1 = bf16[8,80,128]{2,1,0:T(8,128)(2,1)} custom-call(bf16[2,576,128]{2,1,0:T(8,128)(2,1)} %get-tuple-element.100.refs_0_, bf16[2,576,128]{2,1,0:T(8,128)(2,1)} %copy-done.1, bf16[2,576,128]{2,1,0:T(8,128)(2,1)} %copy-done.2, bf16[2,576,128]{2,1,0:T(8,128)(2,1)} %copy-done.3, bf16[512,128]{1,0:T(8,128)(2,1)} %get-tuple-element.96.refs_1_.refs_4_, ...), custom_call_target="tpu_custom_call" | custom-call | flops 603979776 | bytes 2310144 | tf_op jit(solution)/shard_map/grad_hidden/pallas_call | solution.py:196
  110.7 14.2 %all_to_all.31.refs_0_ = bf16[8,80,128]{2,1,0:T(8,128)(2,1)S(1)} all-to-all(bf16[8,80,128]{2,1,0:T(8,128)(2,1)} %grad_hidden.1), channel_id=1, replica_groups={{0,4,8,12,16,20,24,28},{1,5,9,13,17,21,25,29},{2,6,10,14,18,22,26,30},{..., dimensions={0} | all-to-all | bytes 327680 | tf_op jit(solution)/shard_map/all_to_all | solution.py:690
  124.9 3.6 %grad_first.1 = (bf16[2,512,128]{2,1,0:T(8,128)(2,1)}, bf16[8,288,128]{2,1,0:T(8,128)(2,1)}, f32[8,128]{1,0:T(8,128)}) custom-call(bf16[8,80,128]{2,1,0:T(8,128)(2,1)S(1)} %all_to_all.31.refs_0_, bf16[512,128]{1,0:T(8,128)(2,1)} %get-tuple-element.107.refs_1_, f32[4,8,128]{2,1,0:T(8,128)} %get-tuple-element.87.refs_2_.refs_7_.refs_9_, f32[6,128]{1,0:T(8,128)} %refs_15_.1, ...), custom_call_target="tpu_custom_call" | custom-call | flops 301989888 | bytes 3136512 | tf_op jit(solution)/shard_map/grad_first/pallas_call | solution.py:196
  128.5 3.5 %all-to-all-start.4 = ((bf16[8,288,128]{2,1,0:T(8,128)(2,1)}), bf16[8,288,128]{2,1,0:T(8,128)(2,1)S(1)}, u32[]{:S(2)}, u32[]{:S(2)}) async-start(bf16[8,288,128]{2,1,0:T(8,128)(2,1)} %get-tuple-element.108), calls=%async_computation.5 | async-start | bytes 1179648 | tf_op jit(solution)/shard_map/all_to_all | solution.py:690
  132.1 1.3 collective-permute-start.14
  133.4 5.5 %collective-permute-done.14.refs_3_ = bf16[2,512,128]{2,1,0:T(8,128)(2,1)S(1)} collective-permute-done((bf16[2,512,128]{2,1,0:T(8,128)(2,1)}, bf16[2,512,128]{2,1,0:T(8,128)(2,1)S(1)}, u32[]{:S(2)}, u32[]{:S(2)}) %collective-permute-start.14) | collective-permute-done | bytes 262176 | tf_op jit(solution)/shard_map/ppermute | solution.py:703
  138.9 0.5 collective-permute-start.16
  139.4 1.7 collective-permute-start.17
  141.2 6.4 %all-to-all-done.4.refs_1_ = bf16[8,288,128]{2,1,0:T(8,128)(2,1)S(1)} async-done(((bf16[8,288,128]{2,1,0:T(8,128)(2,1)}), bf16[8,288,128]{2,1,0:T(8,128)(2,1)S(1)}, u32[]{:S(2)}, u32[]{:S(2)}) %all-to-all-start.4) | async-done | bytes 589856 | tf_op jit(solution)/shard_map/all_to_all | solution.py:690
  147.6 2.2 %reduce_all.1 = (f32[288,128]{1,0:T(8,128)}, f32[576,128]{1,0:T(8,128)}, f32[32,128]{1,0:T(8,128)}, f32[32,8,128]{2,1,0:T(8,128)}) custom-call(bf16[608,128]{1,0:T(8,128)(2,1)} %reduce-scatter.2.cloned.1.call-done.refs_0_, bf16[8,288,128]{2,1,0:T(8,128)(2,1)S(1)} %all-to-all-done.4.refs_1_, f32[8,128]{1,0:T(8,128)} %get-tuple-element.111.refs_2_, ...), custom_call_target="tpu_custom_call" | custom-call | bytes 1350656 | tf_op jit(solution)/shard_map/reduce_all/pallas_call | solution.py:196
  149.8 3.9 %all-to-all-start.5 = ((f32[32,8,128]{2,1,0:T(8,128)}), f32[32,8,128]{2,1,0:T(8,128)S(1)}, u32[]{:S(2)}, u32[]{:S(2)}) async-start(f32[32,8,128]{2,1,0:T(8,128)} %get-tuple-element.114.refs_0_), calls=%async_computation.6 | async-start | bytes 262144 | tf_op jit(solution)/shard_map/all_to_all | solution.py:690
  153.8 0.6 copy-done.9
  154.4 0.7 copy-done.11
  155.1 3.2 %grad_images.1 = (f32[2,512,128]{2,1,0:T(8,128)}, bf16[512,128]{1,0:T(8,128)(2,1)}) custom-call(f32[32,8,128]{2,1,0:T(8,128)} %get-tuple-element.114.refs_0_, bf16[2,512,128]{2,1,0:T(8,128)(2,1)} %get-tuple-element.119.refs_1_, bf16[2,512,128]{2,1,0:T(8,128)(2,1)S(1)} %collective-permute-done.13.refs_2_, ...), custom_call_target="tpu_custom_call" | custom-call | flops 301989888 | bytes 2392064 | tf_op jit(solution)/shard_map/grad_images/pallas_call | solution.py:196
  158.3 1.3 collective-permute-start.19
  159.6 2.3 %all-to-all-done.5.refs_0_ = f32[32,8,128]{2,1,0:T(8,128)S(1)} async-done(((f32[32,8,128]{2,1,0:T(8,128)}), f32[32,8,128]{2,1,0:T(8,128)S(1)}, u32[]{:S(2)}, u32[]{:S(2)}) %all-to-all-start.5) | async-done | bytes 131104 | tf_op jit(solution)/shard_map/all_to_all | solution.py:690
  161.9 3.0 %update.1 = (f32[288,128]{1,0:T(8,128)}, f32[288,128]{1,0:T(8,128)}, f32[288,128]{1,0:T(8,128)}, f32[576,128]{1,0:T(8,128)}, f32[576,128]{1,0:T(8,128)}, /*index...) custom-call(f32[32,8,128]{2,1,0:T(8,128)S(1)} %all-to-all-done.5.ref, ...), custom_call_target="tpu_custom_call" | custom-call | bytes 3368960 | tf_op jit(solution)/shard_map/update/pallas_call | solution.py:196
  164.9 1.2 collective-permute-done.19.refs_2_
  166.1 0.6 copy-done.15
  166.7 2.2 %finish_images.1 = bf16[64,32,64]{2,1,0:T(8,128)(2,1)} custom-call(f32[288,128]{1,0:T(8,128)} %get-tuple-element.65.refs_0_, f32[2,512,128]{2,1,0:T(8,128)} %get-tuple-element.127.refs_1_, bf16[512,128]{1,0:T(8,128)(2,1)} %copy-done.15), custom_call_target="tpu_custom_call" | custom-call | bytes 917504 | tf_op jit(solution)/shard_map/finish_images/pallas_call | solution.py:196
  (60 shorter events, 1.0 us)
Async XLA Ops:
  7.2 39.2 %all-gather.3.cloned.1.call-start = ((), (), s32[]{:S(2)}) async-start(), calls=%async_computation.8 | async-start | bytes 2101248 | tf_op jit(solution)/shard_map/all_gather | solution.py:795
  11.8 10.0 %collective-permute-start = (bf16[512,128]{1,0:T(8,128)(2,1)}, bf16[512,128]{1,0:T(8,128)(2,1)S(1)}, u32[]{:S(2)}, u32[]{:S(2)}) collective-permute-start(bf16[512,128]{1,0:T(8,128)(2,1)} %get-tuple-element.80), channel_id=1, source_target_pairs={{0,4},{4,8},{8,12},{12,16},{16,20},{20,24},{24,28},{1,5},{5,9},{9,... | collective-permute-start | bytes 393224 | tf_op jit(solution)/shard_map/ppermute | solution.py:789
  21.8 24.6 %copy-start.5 = (bf16[512,128]{1,0:T(8,128)(2,1)}, bf16[512,128]{1,0:T(8,128)(2,1)S(1)}, u32[]{:S(2)}) copy-start(bf16[512,128]{1,0:T(8,128)(2,1)S(1)} %collective-permute-done.refs_3_.refs_7_) | copy-start | bytes 393220
  21.8 5.0 %collective-permute-start.2 = (bf16[512,128]{1,0:T(8,128)(2,1)S(1)}, bf16[512,128]{1,0:T(8,128)(2,1)S(1)}, u32[]{:S(2)}, u32[]{:S(2)}) collective-permute-start(bf16[512,128]{1,0:T(8,128)(2,1)S(1)} %collective-permute-done.refs_3_.refs_7_), channel_id=1, source_target_pairs={{0,2},{1,3},{2,0},{3,1},{4,6},{5,7},{6,4},{7,5},{8,10},{9,11},{10,... | collective-permute-start | bytes 393224 | tf_op jit(solution)/shard_map/ppermute | solution.py:703
  22.8 4.0 %collective-permute-start.1 = (bf16[512,128]{1,0:T(8,128)(2,1)S(1)}, bf16[512,128]{1,0:T(8,128)(2,1)S(1)}, u32[]{:S(2)}, u32[]{:S(2)}) collective-permute-start(bf16[512,128]{1,0:T(8,128)(2,1)S(1)} %collective-permute-done.refs_3_.refs_7_), channel_id=1, source_target_pairs={{0,1},{1,0},{2,3},{3,2},{4,5},{5,4},{6,7},{7,6},{8,9},{9,8},{10,11... | collective-permute-start | bytes 393224 | tf_op jit(solution)/shard_map/ppermute | solution.py:703
  26.7 19.7 %copy-start.6 = (bf16[512,128]{1,0:T(8,128)(2,1)}, bf16[512,128]{1,0:T(8,128)(2,1)S(1)}, u32[]{:S(2)}) copy-start(bf16[512,128]{1,0:T(8,128)(2,1)S(1)} %collective-permute-done.2.refs_5_.refs_9_) | copy-start | bytes 393220
  26.7 1.3 collective-permute-start.3
  26.8 19.6 %copy-start.7 = (bf16[512,128]{1,0:T(8,128)(2,1)}, bf16[512,128]{1,0:T(8,128)(2,1)S(1)}, u32[]{:S(2)}) copy-start(bf16[512,128]{1,0:T(8,128)(2,1)S(1)} %collective-permute-done.1.refs_4_.refs_8_) | copy-start | bytes 393220
  28.1 18.3 %copy-start.8 = (bf16[512,128]{1,0:T(8,128)(2,1)}, bf16[512,128]{1,0:T(8,128)(2,1)S(1)}, u32[]{:S(2)}) copy-start(bf16[512,128]{1,0:T(8,128)(2,1)S(1)} %collective-permute-done.3.refs_6_.refs_10_) | copy-start | bytes 393220
  61.2 6.7 %copy-start = (bf16[8,80,128]{2,1,0:T(8,128)(2,1)}, bf16[8,80,128]{2,1,0:T(8,128)(2,1)S(1)}, u32[]{:S(2)}) copy-start(bf16[8,80,128]{2,1,0:T(8,128)(2,1)S(1)} %all_to_all.30.refs_0_.refs_8_) | copy-start | bytes 491524
  61.2 5.3 %collective-permute-start.5 = (bf16[8,80,128]{2,1,0:T(8,128)(2,1)S(1)}, bf16[8,80,128]{2,1,0:T(8,128)(2,1)S(1)}, u32[]{:S(2)}, u32[]{:S(2)}) collective-permute-start(bf16[8,80,128]{2,1,0:T(8,128)(2,1)S(1)} %all_to_all.30.refs_0_.refs_8_), channel_id=1, source_target_pairs={{0,2},{1,3},{2,0},{3,1},{4,6},{5,7},{6,4},{7,5},{8,10},{9,11},{10,... | collective-permute-start | bytes 491528 | tf_op jit(solution)/shard_map/ppermute | solution.py:703
  62.6 3.9 %collective-permute-start.4 = (bf16[8,80,128]{2,1,0:T(8,128)(2,1)S(1)}, bf16[8,80,128]{2,1,0:T(8,128)(2,1)S(1)}, u32[]{:S(2)}, u32[]{:S(2)}) collective-permute-start(bf16[8,80,128]{2,1,0:T(8,128)(2,1)S(1)} %all_to_all.30.refs_0_.refs_8_), channel_id=1, source_target_pairs={{0,1},{1,0},{2,3},{3,2},{4,5},{5,4},{6,7},{7,6},{8,9},{9,8},{10,11... | collective-permute-start | bytes 491528 | tf_op jit(solution)/shard_map/ppermute | solution.py:703
  66.5 1.4 copy-start.12
  66.5 1.4 collective-permute-start.6
  66.5 1.4 copy-start.13
  67.9 0.7 copy-start.14
  73.0 11.4 %all-to-all-start.1 = ((bf16[8,80,128]{2,1,0:T(8,128)(2,1)}), bf16[8,80,128]{2,1,0:T(8,128)(2,1)S(1)}, u32[]{:S(2)}, u32[]{:S(2)}) async-start(bf16[8,80,128]{2,1,0:T(8,128)(2,1)} %get-tuple-element.86), calls=%async_computation.1 | async-start | bytes 327680 | tf_op jit(solution)/shard_map/all_to_all | solution.py:690
  79.3 10.7 %collective-permute-start.7 = (bf16[2,576,128]{2,1,0:T(8,128)(2,1)}, bf16[2,576,128]{2,1,0:T(8,128)(2,1)S(1)}, u32[]{:S(2)}, u32[]{:S(2)}) collective-permute-start(bf16[2,576,128]{2,1,0:T(8,128)(2,1)} %get-tuple-element.89), channel_id=1, source_target_pairs={{0,1},{1,0},{2,3},{3,2},{4,5},{5,4},{6,7},{7,6},{8,9},{9,8},{10,11... | collective-permute-start | bytes 884744 | tf_op jit(solution)/shard_map/ppermute | solution.py:703
  79.5 10.6 %collective-permute-start.8 = (bf16[2,576,128]{2,1,0:T(8,128)(2,1)}, bf16[2,576,128]{2,1,0:T(8,128)(2,1)S(1)}, u32[]{:S(2)}, u32[]{:S(2)}) collective-permute-start(bf16[2,576,128]{2,1,0:T(8,128)(2,1)} %get-tuple-element.90), channel_id=1, source_target_pairs={{0,2},{1,3},{2,0},{3,1},{4,6},{5,7},{6,4},{7,5},{8,10},{9,11},{10,... | collective-permute-start | bytes 884744 | tf_op jit(solution)/shard_map/ppermute | solution.py:703
  81.0 13.8 %collective-permute-start.9 = (bf16[2,576,128]{2,1,0:T(8,128)(2,1)}, bf16[2,576,128]{2,1,0:T(8,128)(2,1)S(1)}, u32[]{:S(2)}, u32[]{:S(2)}) collective-permute-start(bf16[2,576,128]{2,1,0:T(8,128)(2,1)} %get-tuple-element.91), channel_id=1, source_target_pairs={{0,3},{1,2},{2,1},{3,0},{4,7},{5,6},{6,5},{7,4},{8,11},{9,10},{10,... | collective-permute-start | bytes 884744 | tf_op jit(solution)/shard_map/ppermute | solution.py:703
  86.6 10.9 %all-to-all-start.2 = ((bf16[8,80,128]{2,1,0:T(8,128)(2,1)}), bf16[8,80,128]{2,1,0:T(8,128)(2,1)S(1)}, u32[]{:S(2)}, u32[]{:S(2)}) async-start(bf16[8,80,128]{2,1,0:T(8,128)(2,1)} %get-tuple-element.93), calls=%async_computation.2 | async-start | bytes 327680 | tf_op jit(solution)/shard_map/all_to_all | solution.py:690
  90.0 57.6 %reduce-scatter.2.cloned.1.call-start = ((), (), s32[]{:S(2)}) async-start(), calls=%async_computation.7 | async-start | bytes 1400832 | tf_op jit(solution)/shard_map/reduce_scatter | solution.py:892
  90.1 7.4 %copy-start.1 = (bf16[2,576,128]{2,1,0:T(8,128)(2,1)}, bf16[2,576,128]{2,1,0:T(8,128)(2,1)S(1)}, u32[]{:S(2)}) copy-start(bf16[2,576,128]{2,1,0:T(8,128)(2,1)S(1)} %collective-permute-done.7.refs_0_.refs_1_) | copy-start | bytes 884740
  90.1 7.4 %copy-start.2 = (bf16[2,576,128]{2,1,0:T(8,128)(2,1)}, bf16[2,576,128]{2,1,0:T(8,128)(2,1)S(1)}, u32[]{:S(2)}) copy-start(bf16[2,576,128]{2,1,0:T(8,128)(2,1)S(1)} %collective-permute-done.8.refs_1_.refs_2_) | copy-start | bytes 884740
  94.8 2.7 %copy-start.3 = (bf16[2,576,128]{2,1,0:T(8,128)(2,1)}, bf16[2,576,128]{2,1,0:T(8,128)(2,1)S(1)}, u32[]{:S(2)}) copy-start(bf16[2,576,128]{2,1,0:T(8,128)(2,1)S(1)} %collective-permute-done.9.refs_2_.refs_3_) | copy-start | bytes 884740
  99.8 5.6 %collective-permute-start.10 = (bf16[512,128]{1,0:T(8,128)(2,1)}, bf16[512,128]{1,0:T(8,128)(2,1)S(1)}, u32[]{:S(2)}, u32[]{:S(2)}) collective-permute-start(bf16[512,128]{1,0:T(8,128)(2,1)} %get-tuple-element.96.refs_1_.refs_4_), channel_id=1, source_target_pairs={{0,2},{1,3},{2,0},{3,1},{4,6},{5,7},{6,4},{7,5},{8,10},{9,11},{10,... | collective-permute-start | bytes 393224 | tf_op jit(solution)/shard_map/ppermute | solution.py:703
  101.3 4.1 %copy-start.4 = (bf16[512,128]{1,0:T(8,128)(2,1)S(1)}, bf16[512,128]{1,0:T(8,128)(2,1)}, u32[]{:S(2)}) copy-start(bf16[512,128]{1,0:T(8,128)(2,1)} %get-tuple-element.96.refs_1_.refs_4_) | copy-start | bytes 393220
  105.4 1.4 collective-permute-start.11
  105.5 1.5 collective-permute-start.12
  110.7 28.3 %copy-start.18 = (bf16[2,336,128]{2,1,0:T(8,128)(2,1)S(1)}, bf16[2,336,128]{2,1,0:T(8,128)(2,1)}, u32[]{:S(2)}) copy-start(bf16[2,336,128]{2,1,0:T(8,128)(2,1)} %get-tuple-element.124) | copy-start | bytes 516100
  110.7 28.8 %copy-start.17 = (bf16[2,336,128]{2,1,0:T(8,128)(2,1)S(1)}, bf16[2,336,128]{2,1,0:T(8,128)(2,1)}, u32[]{:S(2)}) copy-start(bf16[2,336,128]{2,1,0:T(8,128)(2,1)} %get-tuple-element.125) | copy-start | bytes 516100
  110.7 30.5 %copy-start.16 = (bf16[2,336,128]{2,1,0:T(8,128)(2,1)S(1)}, bf16[2,336,128]{2,1,0:T(8,128)(2,1)}, u32[]{:S(2)}) copy-start(bf16[2,336,128]{2,1,0:T(8,128)(2,1)} %get-tuple-element.126) | copy-start | bytes 516100
  128.5 19.1 %all-to-all-start.4 = ((bf16[8,288,128]{2,1,0:T(8,128)(2,1)}), bf16[8,288,128]{2,1,0:T(8,128)(2,1)S(1)}, u32[]{:S(2)}, u32[]{:S(2)}) async-start(bf16[8,288,128]{2,1,0:T(8,128)(2,1)} %get-tuple-element.108), calls=%async_computation.5 | async-start | bytes 1179648 | tf_op jit(solution)/shard_map/all_to_all | solution.py:690
  132.1 6.8 %collective-permute-start.14 = (bf16[2,512,128]{2,1,0:T(8,128)(2,1)}, bf16[2,512,128]{2,1,0:T(8,128)(2,1)S(1)}, u32[]{:S(2)}, u32[]{:S(2)}) collective-permute-start(bf16[2,512,128]{2,1,0:T(8,128)(2,1)} %get-tuple-element.119.refs_1_), channel_id=1, source_target_pairs={{0,2},{1,3},{2,0},{3,1},{4,6},{5,7},{6,4},{7,5},{8,10},{9,11},{10,... | collective-permute-start | bytes 786440 | tf_op jit(solution)/shard_map/ppermute | solution.py:703
  133.4 7.8 %collective-permute-start.13 = (bf16[2,512,128]{2,1,0:T(8,128)(2,1)}, bf16[2,512,128]{2,1,0:T(8,128)(2,1)S(1)}, u32[]{:S(2)}, u32[]{:S(2)}) collective-permute-start(bf16[2,512,128]{2,1,0:T(8,128)(2,1)} %get-tuple-element.119.refs_1_), channel_id=1, source_target_pairs={{0,1},{1,0},{2,3},{3,2},{4,5},{5,4},{6,7},{7,6},{8,9},{9,8},{10,11... | collective-permute-start | bytes 786440 | tf_op jit(solution)/shard_map/ppermute | solution.py:703
  138.9 2.3 %collective-permute-start.15 = (bf16[2,512,128]{2,1,0:T(8,128)(2,1)S(1)}, bf16[2,512,128]{2,1,0:T(8,128)(2,1)S(1)}, u32[]{:S(2)}, u32[]{:S(2)}) collective-permute-start(bf16[2,512,128]{2,1,0:T(8,128)(2,1)S(1)} %collective-permute-done.14.refs_3_), channel_id=1, source_target_pairs={{0,1},{1,0},{2,3},{3,2},{4,5},{5,4},{6,7},{7,6},{8,9},{9,8},{10,11... | collective-permute-start | bytes 786440 | tf_op jit(solution)/shard_map/ppermute | solution.py:703
  138.9 14.8 %collective-permute-start.16 = (bf16[2,336,128]{2,1,0:T(8,128)(2,1)S(1)}, bf16[2,336,128]{2,1,0:T(8,128)(2,1)S(1)}, u32[]{:S(2)}, u32[]{:S(2)}) collective-permute-start(bf16[2,336,128]{2,1,0:T(8,128)(2,1)S(1)} %copy-done.18), channel_id=1, source_target_pairs={{0,1},{1,0},{2,3},{3,2},{4,5},{5,4},{6,7},{7,6},{8,9},{9,8},{10,11... | collective-permute-start | bytes 516104 | tf_op jit(solution)/shard_map/ppermute | solution.py:703
  139.4 14.3 %collective-permute-start.17 = (bf16[2,336,128]{2,1,0:T(8,128)(2,1)S(1)}, bf16[2,336,128]{2,1,0:T(8,128)(2,1)S(1)}, u32[]{:S(2)}, u32[]{:S(2)}) collective-permute-start(bf16[2,336,128]{2,1,0:T(8,128)(2,1)S(1)} %copy-done.17), channel_id=1, source_target_pairs={{0,2},{1,3},{2,0},{3,1},{4,6},{5,7},{6,4},{7,5},{8,10},{9,11},{10,... | collective-permute-start | bytes 516104 | tf_op jit(solution)/shard_map/ppermute | solution.py:703
  141.2 12.6 %collective-permute-start.18 = (bf16[2,336,128]{2,1,0:T(8,128)(2,1)S(1)}, bf16[2,336,128]{2,1,0:T(8,128)(2,1)S(1)}, u32[]{:S(2)}, u32[]{:S(2)}) collective-permute-start(bf16[2,336,128]{2,1,0:T(8,128)(2,1)S(1)} %copy-done.16), channel_id=1, source_target_pairs={{0,3},{1,2},{2,1},{3,0},{4,7},{5,6},{6,5},{7,4},{8,11},{9,10},{10,... | collective-permute-start | bytes 516104 | tf_op jit(solution)/shard_map/ppermute | solution.py:703
  149.8 12.1 %all-to-all-start.5 = ((f32[32,8,128]{2,1,0:T(8,128)}), f32[32,8,128]{2,1,0:T(8,128)S(1)}, u32[]{:S(2)}, u32[]{:S(2)}) async-start(f32[32,8,128]{2,1,0:T(8,128)} %get-tuple-element.114.refs_0_), calls=%async_computation.6 | async-start | bytes 262144 | tf_op jit(solution)/shard_map/all_to_all | solution.py:690
  153.7 0.7 copy-start.9
  153.7 0.7 copy-start.10
  154.4 0.7 copy-start.11
  158.3 7.8 %collective-permute-start.19 = (bf16[512,128]{1,0:T(8,128)(2,1)}, bf16[512,128]{1,0:T(8,128)(2,1)S(1)}, u32[]{:S(2)}, u32[]{:S(2)}) collective-permute-start(bf16[512,128]{1,0:T(8,128)(2,1)} %get-tuple-element.128), channel_id=1, source_target_pairs={{4,0},{8,4},{12,8},{16,12},{20,16},{24,20},{28,24},{5,1},{9,5},{13... | collective-permute-start | bytes 393224 | tf_op jit(solution)/shard_map/ppermute | solution.py:975
  166.1 0.6 copy-start.15
Sparse Core Ops, SparseCore 0:
  10.1 36.2 all-gather.2
  105.5 33.2 reduce-scatter.1

commit v2 on v1

--- a/solution.py
+++ b/solution.py
@@ -433,7 +433,7 @@
     return hat, hat * rows[3:4] + rows[4:5], inverse
 
 
-def conv_second(got, m, w, zp, sums, h_out, z2_out, pay, tot_out):
+def conv_second(got, m, w, zp, sums, h_out, z2_out, pay, tot_out, own_out):
     blocks, wide = got.shape[0], got.shape[3]
     part = pay.shape[1] - TAIL
     pay[:, :part] = zp[...].astype(BF).reshape(SIDE, part, wide)
@@ -463,6 +463,7 @@
     pay[:, part:] = jnp.broadcast_to(three_rows(rows)[None], (SIDE, TAIL, wide))
     pay.send()
     z2_out[...] = z2
+    own_out[...] = got[pl.ds(lax.axis_index("chan"), 1), :, :part].reshape(own_out.shape)
 
 
 def block_output(z2, got, tot1, m, n, cot, out, e_out, pay, tot_out):
@@ -503,7 +504,7 @@
     gp_out[...] = (n[4:5] * inverse_p * (pixels_of(got[...]) - loss)).astype(BF)
 
 
-def grad_hidden(w, g2, got, tot1, m, pay):
+def grad_hidden(w, g2, z, tot1, m, pay):
     blocks, _, wide = g2.shape
     count, part = w.shape[1], w.shape[2] // 9
     depth = count * part
@@ -520,7 +521,7 @@
     gh = moved[1] + shift_col(moved[0], -1) + shift_col(moved[2], 1)
     part = pay.shape[1] - TAIL
     pay[:, :part] = gh.astype(BF).reshape(SIDE, part, depth)
-    hat, lin, _ = first_norm(pixels_of(got[...]), tot1[...])
+    hat, lin, _ = first_norm(z[...].astype(F32), tot1[...])
     b = gh * (slope(lin) * m[...])
     rows = three_rows(jnp.concatenate([col_sum(b), col_sum(b * hat)], axis=0))
     pay[:, part:] = jnp.broadcast_to(rows[None], (SIDE, TAIL, depth))
@@ -836,11 +837,12 @@
     if eight:
         got1_mine = exchange(pay, "dp")
         far = swap(got1_mine, "chan", 2)
-        got1 = stack([got1_mine, swap(got1_mine, "chan", 1), far, swap(far, "chan", 1)], slot_ch)
+        got1 = [got1_mine, swap(got1_mine, "chan", 1), far, swap(far, "chan", 1)]
+        got1 = stack(got1, slot_ch, ch_count)
     else:
         got1 = plain_forward(pay)
 
-    hidden, z_second, pay, total1 = call(
+    hidden, z_second, pay, total1, z_own = call(
         conv_second,
         [got1, valid, spread(gathered, order, first_rows, second_rows), z_proj, sums_proj],
         [
@@ -848,6 +850,7 @@
             result((pix, wide)),
             message,
             result((ch_count, SIDE, wide)),
+            result((pix, wide), BF),
         ],
         flops=4 * macs,
     )
@@ -903,13 +906,12 @@
         grads = jnp.concatenate(grads, axis=1)
         grads_second = jnp.sum(exchange(grads, "dp").astype(F32), axis=0)
 
-    got1_own = got1_mine if eight else pick(got1, away("chan", 0))
     (pay,) = call(
         grad_hidden,
         [
             stack(turned, slot_ch),
             stack(g_all, slot_ch, 3),
-            got1_own,
+            z_own,
             total1_own,
             valid,
         ],
@@ -953,7 +955,7 @@
 
     own, above = call(
         grad_images,
-        [stack(g_all, slot_ch, 3), stack(turned_first, slot_ch)],
+        [stack(g_all, slot_ch, 3), stack(turned_first, slot_ch, 3)],
         [result((2, pix, wide)), result((pix, wide), BF)],
         flops=2 * macs,
         later=[pay],
@@ -975,7 +977,7 @@
         come = lax.ppermute(above, "dp", [(i + 1, i) for i in range(dp_count - 1)])
         (grad_pixels,) = call(
             finish_images,
-            [own, come],
+            [own, fresh(come)],
             [result((images.shape[0], pix_here, half), BF)],
             scratch=[((images.shape[0] * pix_here, wide), F32)],
             later=results[:1],

time: 177 us -> 175 us (0.989)
  local copies, waits for them, and re-layouts: 2.71 us -> 0.05 us
    unnamed x38 -> x22, local copies, waits for them, and re-layouts: 2.71 us -> 0.05 us
    all_to_all x4, waiting for transfers between devices: 14.6 us -> 16.4 us  [exchange(): return lax.all_to_all(blocks, axes, 0, 0, axis_index_groups=groups)]
  transfers between devices with their start and end apart: 26 -> 26, of which waited for: 15 -> 14; matrix products, arithmetic and copies ran while one was open for 0% -> 0% of each run, Pallas kernels for 16% -> 16%
where the time goes in v2:
time: 175 us; the launch traced here: 174 us
  waiting for transfers between devices  62 us (35%)
  Pallas kernels  42.1 us (24%)
  starting transfers between devices  30.2 us (17%)
  blocking collectives  25.3 us (14%)
  between operations  14.4 us (8%)
    pallas_call x14, Pallas kernels, call(): pl.pallas_call(kernel, out_shape=[pltpu.HBM(o.shape, o.dtype) for o in ou...  42.1 us
    all_to_all x2, blocking collectives, exchange(): return lax.all_to_all(blocks, axes, 0, 0, axis_index_groups=groups)  25.3 us
    ppermute x18, waiting for transfers between devices, swap(): lax.ppermute(array, axis, [(i, i ^ bits) for i in range(lax.axis_size(axi...  22.1 us
    all_gather x1, waiting for transfers between devices, per_device(): gathered = lax.all_gather(own, everyone, axis_index_groups=rings())  18.3 us
    all_to_all x4, waiting for transfers between devices, exchange(): return lax.all_to_all(blocks, axes, 0, 0, axis_index_groups=groups)  16.4 us
    all_to_all x4, starting transfers between devices, exchange(): return lax.all_to_all(blocks, axes, 0, 0, axis_index_groups=groups)  14 us
    ppermute x18, starting transfers between devices, swap(): lax.ppermute(array, axis, [(i, i ^ bits) for i in range(lax.axis_size(axi...  9.91 us
    ppermute x1, waiting for transfers between devices, per_device(): come = lax.ppermute(send, 'dp', [(i, i + 1) for i in range(dp_count - 1)])  5.08 us
  transfers between devices with their start and end apart: 26, of which 14 were waited for; matrix products, arithmetic and copies ran while one was open for 0% of the time, Pallas kernels for 16%

profile of v2, /device:TPU:0, one launch (start us, length us, event | category | flops | bytes accessed | tf_op | source)
XLA Modules:
  0.0 174.0 jit_solution(6538847395747243809)
XLA Ops:
  7.2 1.9 %pack_weights.1 = (bf16[912,128]{1,0:T(8,128)(2,1)}, f32[8,128]{1,0:T(8,128)}) custom-call(f32[288,128]{1,0:T(8,128)} %refs_3_.5, f32[32,128]{1,0:T(8,128)} %refs_11_.1, s32[8,64]{1,0:T(8,128)} %refs_1_.3, f32[576,128]{1,0:T(8,128)} %refs_7_.3), custom_call_target="tpu_custom_call" | custom-call | bytes 698368 | tf_op jit(solution)/shard_map/pack_weights/pallas_call | solution.py:196
  9.1 2.7 %pack_images.1 = (bf16[2,512,256]{2,1,0:T(8,128)(2,1)}, bf16[2,512,256]{2,1,0:T(8,128)(2,1)}, bf16[512,128]{1,0:T(8,128)(2,1)}, f32[512,128]{1,0:T(8,128)}) custom-call(bf16[64,32,256]{2,1,0:T(8,128)(2,1)} %refs_0_.3, s32[8,64]{1,0:T(8,128)} %refs_1_.3), custom_call_target="tpu_custom_call" | custom-call | bytes 2492416 | tf_op jit(solution)/shard_map/pack_images/pallas_call | solution.py:196
  11.8 4.9 %collective-permute-start = (bf16[512,128]{1,0:T(8,128)(2,1)}, bf16[512,128]{1,0:T(8,128)(2,1)S(1)}, u32[]{:S(2)}, u32[]{:S(2)}) collective-permute-start(bf16[512,128]{1,0:T(8,128)(2,1)} %get-tuple-element.81), channel_id=1, source_target_pairs={{0,4},{4,8},{8,12},{12,16},{16,20},{20,24},{24,28},{1,5},{5,9},{9,... | collective-permute-start | bytes 393224 | tf_op jit(solution)/shard_map/ppermute | solution.py:790
  16.7 5.1 %collective-permute-done.refs_3_.refs_7_ = bf16[512,128]{1,0:T(8,128)(2,1)S(1)} collective-permute-done((bf16[512,128]{1,0:T(8,128)(2,1)}, bf16[512,128]{1,0:T(8,128)(2,1)S(1)}, u32[]{:S(2)}, u32[]{:S(2)}) %collective-permute-start) | collective-permute-done | bytes 131104 | tf_op jit(solution)/shard_map/ppermute | solution.py:790
  21.8 1.0 collective-permute-start.2
  22.7 4.0 %collective-permute-done.2.refs_5_.refs_9_ = bf16[512,128]{1,0:T(8,128)(2,1)S(1)} collective-permute-done((bf16[512,128]{1,0:T(8,128)(2,1)S(1)}, bf16[512,128]{1,0:T(8,128)(2,1)S(1)}, u32[]{:S(2)}, u32[]{:S(2)}) %collective-permute-start.2) | collective-permute-done | bytes 131104 | tf_op jit(solution)/shard_map/ppermute | solution.py:704
  26.8 1.3 collective-permute-done.3.refs_6_.refs_10_
  28.1 18.3 %all-gather.3.cloned.1.call-done = bf16[7296,128]{1,0:T(8,128)(2,1)} async-done(((bf16[912,128]{1,0:T(8,128)(2,1)}), bf16[7296,128]{1,0:T(8,128)(2,1)}) %all-gather.3.cloned.1.call-update) | async-done | bytes 1867792 | tf_op jit(solution)/shard_map/all_gather | solution.py:796
  46.4 3.6 %conv_first.1 = (bf16[512,128]{1,0:T(8,128)(2,1)}, f32[512,128]{1,0:T(8,128)}, bf16[8,80,128]{2,1,0:T(8,128)(2,1)}, f32[8,128]{1,0:T(8,128)}, f32[512,128]{1,0:T(8,128)}) custom-call(bf16[8,912,128]{2,1,0:T(8,128)(2,1)} %bitcast.2, bf16[2,512,256]{2,1,0:T(8,128)(2,1)} %get-tuple-element.79.refs_1_.refs_2_.refs_5_, ...), custom_call_target="tpu_custom_call" | custom-call | flops 301989888 | bytes 4267008 | tf_op jit(solution)/shard_map/conv_first/pallas_call | solution.py:196
  50.0 11.2 %all_to_all.30.refs_0_ = bf16[8,80,128]{2,1,0:T(8,128)(2,1)S(1)} all-to-all(bf16[8,80,128]{2,1,0:T(8,128)(2,1)} %get-tuple-element.82), channel_id=1, replica_groups={{0,4,8,12,16,20,24,28},{1,5,9,13,17,21,25,29},{2,6,10,14,18,22,26,30},{..., dimensions={0} | all-to-all | bytes 327680 | tf_op jit(solution)/shard_map/all_to_all | solution.py:691
  61.2 1.4 collective-permute-start.5
  62.6 3.9 %collective-permute-done.5.refs_2_ = bf16[8,80,128]{2,1,0:T(8,128)(2,1)S(1)} collective-permute-done((bf16[8,80,128]{2,1,0:T(8,128)(2,1)S(1)}, bf16[8,80,128]{2,1,0:T(8,128)(2,1)S(1)}, u32[]{:S(2)}, u32[]{:S(2)}) %collective-permute-start.5) | collective-permute-done | bytes 163872 | tf_op jit(solution)/shard_map/ppermute | solution.py:704
  66.5 1.4 collective-permute-done.6.refs_3_
  67.9 4.9 %conv_second.1 = (bf16[512,512]{1,0:T(8,128)(2,1)}, f32[512,128]{1,0:T(8,128)}, bf16[8,80,128]{2,1,0:T(8,128)(2,1)}, f32[4,8,128]{2,1,0:T(8,128)}, bf16[512,128]{1,0:T(8,128)(2,1)}) custom-call(bf16[8,80,128]{2,1,0:T(8,128)(2,1)S(1)} %all_to_all.30.refs_0_, bf16[8,80,128]{2,1,0:T(8,128)(2,1)S(1)} %collective-permute-done.4.refs_1_, ...), custom_call_target="tpu_custom_call" | custom-call | flops 603979776 | bytes 4149248 | tf_op jit(solution)/shard_map/conv_second/pallas_call | solution.py:196
  72.8 3.4 %all-to-all-start.1 = ((bf16[8,80,128]{2,1,0:T(8,128)(2,1)}), bf16[8,80,128]{2,1,0:T(8,128)(2,1)S(1)}, u32[]{:S(2)}, u32[]{:S(2)}) async-start(bf16[8,80,128]{2,1,0:T(8,128)(2,1)} %get-tuple-element.87), calls=%async_computation.1 | async-start | bytes 327680 | tf_op jit(solution)/shard_map/all_to_all | solution.py:691
  76.2 2.9 %hand_on.1 = (bf16[2,336,128]{2,1,0:T(8,128)(2,1)}, bf16[2,336,128]{2,1,0:T(8,128)(2,1)}, bf16[2,336,128]{2,1,0:T(8,128)(2,1)}, bf16[2,336,128]{2,1,0:T(8,128)(2...) custom-call(f32[512,128]{1,0:T(8,128)} %get-tuple-element.86.refs_0_, ...), custom_call_target="tpu_custom_call" | custom-call | bytes 3735552 | tf_op jit(solution)/shard_map/hand_on/pallas_call | solution.py:196
  79.2 0.2 collective-permute-start.7
  79.4 1.5 collective-permute-start.8
  80.9 0.3 collective-permute-start.9
  81.1 3.1 %all-to-all-done.1.refs_1_ = bf16[8,80,128]{2,1,0:T(8,128)(2,1)S(1)} async-done(((bf16[8,80,128]{2,1,0:T(8,128)(2,1)}), bf16[8,80,128]{2,1,0:T(8,128)(2,1)S(1)}, u32[]{:S(2)}, u32[]{:S(2)}) %all-to-all-start.1) | async-done | bytes 163872 | tf_op jit(solution)/shard_map/all_to_all | solution.py:691
  84.2 2.3 %block_output.1 = (bf16[8,64,128]{2,1,0:T(8,128)(2,1)}, f32[512,128]{1,0:T(8,128)}, bf16[8,80,128]{2,1,0:T(8,128)(2,1)}, f32[8,128]{1,0:T(8,128)}) custom-call(f32[512,128]{1,0:T(8,128)} %get-tuple-element.86.refs_0_.refs_3_, bf16[8,80,128]{2,1,0:T(8,128)(2,1)S(1)} %all-to-all-done.1.refs_1_, f32[4,8,128]{2,1,0:T(8,128)} %get-tuple-element.88.refs_2_.refs_7_.refs_9_, ...), custom_call_target="tpu_custom_call" | custom-call | bytes 1399808 | tf_op jit(solution)/shard_map/block_output/pallas_call | solution.py:196
  86.5 3.4 %all-to-all-start.2 = ((bf16[8,80,128]{2,1,0:T(8,128)(2,1)}), bf16[8,80,128]{2,1,0:T(8,128)(2,1)S(1)}, u32[]{:S(2)}, u32[]{:S(2)}) async-start(bf16[8,80,128]{2,1,0:T(8,128)(2,1)} %get-tuple-element.94), calls=%async_computation.2 | async-start | bytes 327680 | tf_op jit(solution)/shard_map/all_to_all | solution.py:691
  89.9 0.0 reduce-scatter.2.cloned.1.call-start
  90.0 4.7 %collective-permute-done.9.refs_2_.refs_3_ = bf16[2,576,128]{2,1,0:T(8,128)(2,1)S(1)} collective-permute-done((bf16[2,576,128]{2,1,0:T(8,128)(2,1)}, bf16[2,576,128]{2,1,0:T(8,128)(2,1)S(1)}, u32[]{:S(2)}, u32[]{:S(2)}) %collective-permute-start.9) | collective-permute-done | bytes 294944 | tf_op jit(solution)/shard_map/ppermute | solution.py:704
  94.7 2.7 %all-to-all-done.2.refs_5_ = bf16[8,80,128]{2,1,0:T(8,128)(2,1)S(1)} async-done(((bf16[8,80,128]{2,1,0:T(8,128)(2,1)}), bf16[8,80,128]{2,1,0:T(8,128)(2,1)S(1)}, u32[]{:S(2)}, u32[]{:S(2)}) %all-to-all-start.2) | async-done | bytes 163872 | tf_op jit(solution)/shard_map/all_to_all | solution.py:691
  97.4 2.3 %grad_outputs.1 = (bf16[512,128]{1,0:T(8,128)(2,1)}, bf16[512,128]{1,0:T(8,128)(2,1)}, f32[8,128]{1,0:T(8,128)}) custom-call(bf16[2,576,128]{2,1,0:T(8,128)(2,1)} %copy-done, bf16[2,576,128]{2,1,0:T(8,128)(2,1)} %copy-done.1, bf16[2,576,128]{2,1,0:T(8,128)(2,1)} %copy-done.2, f32[512,128]{1,0:T(8,128)} %get-tuple-element.86.refs_0_.refs_3_, ...), custom_call_target="tpu_custom_call" | custom-call | bytes 1764352 | tf_op jit(solution)/shard_map/grad_outputs/pallas_call | solution.py:196
  99.7 1.5 collective-permute-start.10
  101.2 4.0 %grad_second.1 = bf16[8,608,128]{2,1,0:T(8,128)(2,1)} custom-call(bf16[512,512]{1,0:T(8,128)(2,1)} %get-tuple-element.98.refs_0_, bf16[512,128]{1,0:T(8,128)(2,1)} %get-tuple-element.97.refs_1_.refs_4_, bf16[2,512,256]{2,1,0:T(8,128)(2,1)} %get-tuple-element.79.refs_1_.refs_2_.refs_5_, bf16[512,128]{1,0:T(8,128)(2,1)} %get-tuple-element.99.refs_3_.refs_11_), custom_call_target="tpu_custom_call" | custom-call | flops 603979776 | bytes 2555904 | tf_op jit(solution)/shard_map/grad_second/pallas_call | solution.py:196
  105.3 0.1 collective-permute-start.11
  105.4 0.5 collective-permute-start.12
  105.8 0.8 collective-permute-done.11.refs_5_
  106.7 0.2 collective-permute-done.12.refs_7_
  106.9 3.7 %grad_hidden.1 = bf16[8,80,128]{2,1,0:T(8,128)(2,1)} custom-call(bf16[2,576,128]{2,1,0:T(8,128)(2,1)} %get-tuple-element.101.refs_0_, bf16[2,576,128]{2,1,0:T(8,128)(2,1)} %copy-done, bf16[2,576,128]{2,1,0:T(8,128)(2,1)} %copy-done.1, bf16[2,576,128]{2,1,0:T(8,128)(2,1)} %copy-done.2, bf16[512,128]{1,0:T(8,128)(2,1)} %get-tuple-element.97.refs_1_.refs_4_, ...), custom_call_target="tpu_custom_call" | custom-call | flops 603979776 | bytes 2277376 | tf_op jit(solution)/shard_map/grad_hidden/pallas_call | solution.py:196
  110.6 14.1 %all_to_all.31.refs_0_ = bf16[8,80,128]{2,1,0:T(8,128)(2,1)S(1)} all-to-all(bf16[8,80,128]{2,1,0:T(8,128)(2,1)} %grad_hidden.1), channel_id=1, replica_groups={{0,4,8,12,16,20,24,28},{1,5,9,13,17,21,25,29},{2,6,10,14,18,22,26,30},{..., dimensions={0} | all-to-all | bytes 327680 | tf_op jit(solution)/shard_map/all_to_all | solution.py:691
  124.7 3.6 %grad_first.1 = (bf16[2,512,128]{2,1,0:T(8,128)(2,1)}, bf16[8,288,128]{2,1,0:T(8,128)(2,1)}, f32[8,128]{1,0:T(8,128)}) custom-call(bf16[8,80,128]{2,1,0:T(8,128)(2,1)S(1)} %all_to_all.31.refs_0_, bf16[512,128]{1,0:T(8,128)(2,1)} %get-tuple-element.109.refs_1_, f32[4,8,128]{2,1,0:T(8,128)} %get-tuple-element.88.refs_2_.refs_7_.refs_9_, f32[6,128]{1,0:T(8,128)} %refs_15_.1, ...), custom_call_target="tpu_custom_call" | custom-call | flops 301989888 | bytes 3136512 | tf_op jit(solution)/shard_map/grad_first/pallas_call | solution.py:196
  128.2 3.5 %all-to-all-start.4 = ((bf16[8,288,128]{2,1,0:T(8,128)(2,1)}), bf16[8,288,128]{2,1,0:T(8,128)(2,1)S(1)}, u32[]{:S(2)}, u32[]{:S(2)}) async-start(bf16[8,288,128]{2,1,0:T(8,128)(2,1)} %get-tuple-element.110), calls=%async_computation.5 | async-start | bytes 1179648 | tf_op jit(solution)/shard_map/all_to_all | solution.py:691
  131.8 1.5 collective-permute-start.14
  133.3 5.8 %collective-permute-done.14.refs_3_ = bf16[2,512,128]{2,1,0:T(8,128)(2,1)S(1)} collective-permute-done((bf16[2,512,128]{2,1,0:T(8,128)(2,1)}, bf16[2,512,128]{2,1,0:T(8,128)(2,1)S(1)}, u32[]{:S(2)}, u32[]{:S(2)}) %collective-permute-start.14) | collective-permute-done | bytes 262176 | tf_op jit(solution)/shard_map/ppermute | solution.py:704
  139.1 0.5 collective-permute-start.16
  139.6 1.5 collective-permute-start.17
  141.1 6.6 %all-to-all-done.4.refs_1_ = bf16[8,288,128]{2,1,0:T(8,128)(2,1)S(1)} async-done(((bf16[8,288,128]{2,1,0:T(8,128)(2,1)}), bf16[8,288,128]{2,1,0:T(8,128)(2,1)S(1)}, u32[]{:S(2)}, u32[]{:S(2)}) %all-to-all-start.4) | async-done | bytes 589856 | tf_op jit(solution)/shard_map/all_to_all | solution.py:691
  147.7 2.2 %reduce_all.1 = (f32[288,128]{1,0:T(8,128)}, f32[576,128]{1,0:T(8,128)}, f32[32,128]{1,0:T(8,128)}, f32[32,8,128]{2,1,0:T(8,128)}) custom-call(bf16[608,128]{1,0:T(8,128)(2,1)} %reduce-scatter.2.cloned.1.call-done.refs_0_, bf16[8,288,128]{2,1,0:T(8,128)(2,1)S(1)} %all-to-all-done.4.refs_1_, f32[8,128]{1,0:T(8,128)} %get-tuple-element.113.refs_2_, ...), custom_call_target="tpu_custom_call" | custom-call | bytes 1350656 | tf_op jit(solution)/shard_map/reduce_all/pallas_call | solution.py:196
  149.9 3.7 %all-to-all-start.5 = ((f32[32,8,128]{2,1,0:T(8,128)}), f32[32,8,128]{2,1,0:T(8,128)S(1)}, u32[]{:S(2)}, u32[]{:S(2)}) async-start(f32[32,8,128]{2,1,0:T(8,128)} %get-tuple-element.116.refs_0_), calls=%async_computation.6 | async-start | bytes 262144 | tf_op jit(solution)/shard_map/all_to_all | solution.py:691
  153.6 3.0 %grad_images.1 = (f32[2,512,128]{2,1,0:T(8,128)}, bf16[512,128]{1,0:T(8,128)(2,1)}) custom-call(f32[32,8,128]{2,1,0:T(8,128)} %get-tuple-element.116.refs_0_, bf16[2,512,128]{2,1,0:T(8,128)(2,1)} %get-tuple-element.121.refs_1_, bf16[2,512,128]{2,1,0:T(8,128)(2,1)S(1)} %collective-permute-done.13.refs_2_, ...), custom_call_target="tpu_custom_call" | custom-call | flops 301989888 | bytes 2392064 | tf_op jit(solution)/shard_map/grad_images/pallas_call | solution.py:196
  156.7 1.3 collective-permute-start.19
  158.0 4.0 %all-to-all-done.5.refs_0_ = f32[32,8,128]{2,1,0:T(8,128)S(1)} async-done(((f32[32,8,128]{2,1,0:T(8,128)}), f32[32,8,128]{2,1,0:T(8,128)S(1)}, u32[]{:S(2)}, u32[]{:S(2)}) %all-to-all-start.5) | async-done | bytes 131104 | tf_op jit(solution)/shard_map/all_to_all | solution.py:691
  161.9 3.0 %update.1 = (f32[288,128]{1,0:T(8,128)}, f32[288,128]{1,0:T(8,128)}, f32[288,128]{1,0:T(8,128)}, f32[576,128]{1,0:T(8,128)}, f32[576,128]{1,0:T(8,128)}, /*index...) custom-call(f32[32,8,128]{2,1,0:T(8,128)S(1)} %all-to-all-done.5.ref, ...), custom_call_target="tpu_custom_call" | custom-call | bytes 3368960 | tf_op jit(solution)/shard_map/update/pallas_call | solution.py:196
  165.0 2.2 %finish_images.1 = bf16[64,32,64]{2,1,0:T(8,128)(2,1)} custom-call(f32[288,128]{1,0:T(8,128)} %get-tuple-element.66.refs_0_, f32[2,512,128]{2,1,0:T(8,128)} %get-tuple-element.129.refs_1_, bf16[512,128]{1,0:T(8,128)(2,1)S(1)} %collective-permute-done.19.refs_2_), custom_call_target="tpu_custom_call" | custom-call | bytes 917504 | tf_op jit(solution)/shard_map/finish_images/pallas_call | solution.py:196
  (44 shorter events, 0.2 us)
Async XLA Ops:
  7.2 39.2 %all-gather.3.cloned.1.call-start = ((), (), s32[]{:S(2)}) async-start(), calls=%async_computation.8 | async-start | bytes 2101248 | tf_op jit(solution)/shard_map/all_gather | solution.py:796
  11.8 10.0 %collective-permute-start = (bf16[512,128]{1,0:T(8,128)(2,1)}, bf16[512,128]{1,0:T(8,128)(2,1)S(1)}, u32[]{:S(2)}, u32[]{:S(2)}) collective-permute-start(bf16[512,128]{1,0:T(8,128)(2,1)} %get-tuple-element.81), channel_id=1, source_target_pairs={{0,4},{4,8},{8,12},{12,16},{16,20},{20,24},{24,28},{1,5},{5,9},{9,... | collective-permute-start | bytes 393224 | tf_op jit(solution)/shard_map/ppermute | solution.py:790
  21.8 24.6 %copy-start.4 = (bf16[512,128]{1,0:T(8,128)(2,1)}, bf16[512,128]{1,0:T(8,128)(2,1)S(1)}, u32[]{:S(2)}) copy-start(bf16[512,128]{1,0:T(8,128)(2,1)S(1)} %collective-permute-done.refs_3_.refs_7_) | copy-start | bytes 393220
  21.8 5.0 %collective-permute-start.2 = (bf16[512,128]{1,0:T(8,128)(2,1)S(1)}, bf16[512,128]{1,0:T(8,128)(2,1)S(1)}, u32[]{:S(2)}, u32[]{:S(2)}) collective-permute-start(bf16[512,128]{1,0:T(8,128)(2,1)S(1)} %collective-permute-done.refs_3_.refs_7_), channel_id=1, source_target_pairs={{0,2},{1,3},{2,0},{3,1},{4,6},{5,7},{6,4},{7,5},{8,10},{9,11},{10,... | collective-permute-start | bytes 393224 | tf_op jit(solution)/shard_map/ppermute | solution.py:704
  22.7 4.0 %collective-permute-start.1 = (bf16[512,128]{1,0:T(8,128)(2,1)S(1)}, bf16[512,128]{1,0:T(8,128)(2,1)S(1)}, u32[]{:S(2)}, u32[]{:S(2)}) collective-permute-start(bf16[512,128]{1,0:T(8,128)(2,1)S(1)} %collective-permute-done.refs_3_.refs_7_), channel_id=1, source_target_pairs={{0,1},{1,0},{2,3},{3,2},{4,5},{5,4},{6,7},{7,6},{8,9},{9,8},{10,11... | collective-permute-start | bytes 393224 | tf_op jit(solution)/shard_map/ppermute | solution.py:704
  26.7 19.7 %copy-start.5 = (bf16[512,128]{1,0:T(8,128)(2,1)}, bf16[512,128]{1,0:T(8,128)(2,1)S(1)}, u32[]{:S(2)}) copy-start(bf16[512,128]{1,0:T(8,128)(2,1)S(1)} %collective-permute-done.2.refs_5_.refs_9_) | copy-start | bytes 393220
  26.7 1.3 collective-permute-start.3
  26.7 19.7 %copy-start.6 = (bf16[512,128]{1,0:T(8,128)(2,1)}, bf16[512,128]{1,0:T(8,128)(2,1)S(1)}, u32[]{:S(2)}) copy-start(bf16[512,128]{1,0:T(8,128)(2,1)S(1)} %collective-permute-done.1.refs_4_.refs_8_) | copy-start | bytes 393220
  28.1 18.3 %copy-start.7 = (bf16[512,128]{1,0:T(8,128)(2,1)}, bf16[512,128]{1,0:T(8,128)(2,1)S(1)}, u32[]{:S(2)}) copy-start(bf16[512,128]{1,0:T(8,128)(2,1)S(1)} %collective-permute-done.3.refs_6_.refs_10_) | copy-start | bytes 393220
  61.2 5.3 %collective-permute-start.5 = (bf16[8,80,128]{2,1,0:T(8,128)(2,1)S(1)}, bf16[8,80,128]{2,1,0:T(8,128)(2,1)S(1)}, u32[]{:S(2)}, u32[]{:S(2)}) collective-permute-start(bf16[8,80,128]{2,1,0:T(8,128)(2,1)S(1)} %all_to_all.30.refs_0_), channel_id=1, source_target_pairs={{0,2},{1,3},{2,0},{3,1},{4,6},{5,7},{6,4},{7,5},{8,10},{9,11},{10,... | collective-permute-start | bytes 491528 | tf_op jit(solution)/shard_map/ppermute | solution.py:704
  62.6 3.9 %collective-permute-start.4 = (bf16[8,80,128]{2,1,0:T(8,128)(2,1)S(1)}, bf16[8,80,128]{2,1,0:T(8,128)(2,1)S(1)}, u32[]{:S(2)}, u32[]{:S(2)}) collective-permute-start(bf16[8,80,128]{2,1,0:T(8,128)(2,1)S(1)} %all_to_all.30.refs_0_), channel_id=1, source_target_pairs={{0,1},{1,0},{2,3},{3,2},{4,5},{5,4},{6,7},{7,6},{8,9},{9,8},{10,11... | collective-permute-start | bytes 491528 | tf_op jit(solution)/shard_map/ppermute | solution.py:704
  66.5 1.4 collective-permute-start.6
  72.8 11.4 %all-to-all-start.1 = ((bf16[8,80,128]{2,1,0:T(8,128)(2,1)}), bf16[8,80,128]{2,1,0:T(8,128)(2,1)S(1)}, u32[]{:S(2)}, u32[]{:S(2)}) async-start(bf16[8,80,128]{2,1,0:T(8,128)(2,1)} %get-tuple-element.87), calls=%async_computation.1 | async-start | bytes 327680 | tf_op jit(solution)/shard_map/all_to_all | solution.py:691
  79.2 10.7 %collective-permute-start.7 = (bf16[2,576,128]{2,1,0:T(8,128)(2,1)}, bf16[2,576,128]{2,1,0:T(8,128)(2,1)S(1)}, u32[]{:S(2)}, u32[]{:S(2)}) collective-permute-start(bf16[2,576,128]{2,1,0:T(8,128)(2,1)} %get-tuple-element.90), channel_id=1, source_target_pairs={{0,1},{1,0},{2,3},{3,2},{4,5},{5,4},{6,7},{7,6},{8,9},{9,8},{10,11... | collective-permute-start | bytes 884744 | tf_op jit(solution)/shard_map/ppermute | solution.py:704
  79.4 10.6 %collective-permute-start.8 = (bf16[2,576,128]{2,1,0:T(8,128)(2,1)}, bf16[2,576,128]{2,1,0:T(8,128)(2,1)S(1)}, u32[]{:S(2)}, u32[]{:S(2)}) collective-permute-start(bf16[2,576,128]{2,1,0:T(8,128)(2,1)} %get-tuple-element.91), channel_id=1, source_target_pairs={{0,2},{1,3},{2,0},{3,1},{4,6},{5,7},{6,4},{7,5},{8,10},{9,11},{10,... | collective-permute-start | bytes 884744 | tf_op jit(solution)/shard_map/ppermute | solution.py:704
  80.9 13.8 %collective-permute-start.9 = (bf16[2,576,128]{2,1,0:T(8,128)(2,1)}, bf16[2,576,128]{2,1,0:T(8,128)(2,1)S(1)}, u32[]{:S(2)}, u32[]{:S(2)}) collective-permute-start(bf16[2,576,128]{2,1,0:T(8,128)(2,1)} %get-tuple-element.92), channel_id=1, source_target_pairs={{0,3},{1,2},{2,1},{3,0},{4,7},{5,6},{6,5},{7,4},{8,11},{9,10},{10,... | collective-permute-start | bytes 884744 | tf_op jit(solution)/shard_map/ppermute | solution.py:704
  86.5 10.9 %all-to-all-start.2 = ((bf16[8,80,128]{2,1,0:T(8,128)(2,1)}), bf16[8,80,128]{2,1,0:T(8,128)(2,1)S(1)}, u32[]{:S(2)}, u32[]{:S(2)}) async-start(bf16[8,80,128]{2,1,0:T(8,128)(2,1)} %get-tuple-element.94), calls=%async_computation.2 | async-start | bytes 327680 | tf_op jit(solution)/shard_map/all_to_all | solution.py:691
  89.9 57.8 %reduce-scatter.2.cloned.1.call-start = ((), (), s32[]{:S(2)}) async-start(), calls=%async_computation.7 | async-start | bytes 1400832 | tf_op jit(solution)/shard_map/reduce_scatter | solution.py:895
  89.9 7.4 %copy-start = (bf16[2,576,128]{2,1,0:T(8,128)(2,1)}, bf16[2,576,128]{2,1,0:T(8,128)(2,1)S(1)}, u32[]{:S(2)}) copy-start(bf16[2,576,128]{2,1,0:T(8,128)(2,1)S(1)} %collective-permute-done.7.refs_0_.refs_1_) | copy-start | bytes 884740
  90.0 7.4 %copy-start.1 = (bf16[2,576,128]{2,1,0:T(8,128)(2,1)}, bf16[2,576,128]{2,1,0:T(8,128)(2,1)S(1)}, u32[]{:S(2)}) copy-start(bf16[2,576,128]{2,1,0:T(8,128)(2,1)S(1)} %collective-permute-done.8.refs_1_.refs_2_) | copy-start | bytes 884740
  94.7 2.7 %copy-start.2 = (bf16[2,576,128]{2,1,0:T(8,128)(2,1)}, bf16[2,576,128]{2,1,0:T(8,128)(2,1)S(1)}, u32[]{:S(2)}) copy-start(bf16[2,576,128]{2,1,0:T(8,128)(2,1)S(1)} %collective-permute-done.9.refs_2_.refs_3_) | copy-start | bytes 884740
  99.7 5.5 %collective-permute-start.10 = (bf16[512,128]{1,0:T(8,128)(2,1)}, bf16[512,128]{1,0:T(8,128)(2,1)S(1)}, u32[]{:S(2)}, u32[]{:S(2)}) collective-permute-start(bf16[512,128]{1,0:T(8,128)(2,1)} %get-tuple-element.97.refs_1_.refs_4_), channel_id=1, source_target_pairs={{0,2},{1,3},{2,0},{3,1},{4,6},{5,7},{6,4},{7,5},{8,10},{9,11},{10,... | collective-permute-start | bytes 393224 | tf_op jit(solution)/shard_map/ppermute | solution.py:704
  101.2 4.1 %copy-start.3 = (bf16[512,128]{1,0:T(8,128)(2,1)S(1)}, bf16[512,128]{1,0:T(8,128)(2,1)}, u32[]{:S(2)}) copy-start(bf16[512,128]{1,0:T(8,128)(2,1)} %get-tuple-element.97.refs_1_.refs_4_) | copy-start | bytes 393220
  105.3 1.4 collective-permute-start.11
  105.4 1.5 collective-permute-start.12
  110.6 28.5 %copy-start.10 = (bf16[2,336,128]{2,1,0:T(8,128)(2,1)S(1)}, bf16[2,336,128]{2,1,0:T(8,128)(2,1)}, u32[]{:S(2)}) copy-start(bf16[2,336,128]{2,1,0:T(8,128)(2,1)} %get-tuple-element.126) | copy-start | bytes 516100
  110.6 29.0 %copy-start.9 = (bf16[2,336,128]{2,1,0:T(8,128)(2,1)S(1)}, bf16[2,336,128]{2,1,0:T(8,128)(2,1)}, u32[]{:S(2)}) copy-start(bf16[2,336,128]{2,1,0:T(8,128)(2,1)} %get-tuple-element.127) | copy-start | bytes 516100
  110.6 30.5 %copy-start.8 = (bf16[2,336,128]{2,1,0:T(8,128)(2,1)S(1)}, bf16[2,336,128]{2,1,0:T(8,128)(2,1)}, u32[]{:S(2)}) copy-start(bf16[2,336,128]{2,1,0:T(8,128)(2,1)} %get-tuple-element.128) | copy-start | bytes 516100
  128.2 19.5 %all-to-all-start.4 = ((bf16[8,288,128]{2,1,0:T(8,128)(2,1)}), bf16[8,288,128]{2,1,0:T(8,128)(2,1)S(1)}, u32[]{:S(2)}, u32[]{:S(2)}) async-start(bf16[8,288,128]{2,1,0:T(8,128)(2,1)} %get-tuple-element.110), calls=%async_computation.5 | async-start | bytes 1179648 | tf_op jit(solution)/shard_map/all_to_all | solution.py:691
  131.8 7.3 %collective-permute-start.14 = (bf16[2,512,128]{2,1,0:T(8,128)(2,1)}, bf16[2,512,128]{2,1,0:T(8,128)(2,1)S(1)}, u32[]{:S(2)}, u32[]{:S(2)}) collective-permute-start(bf16[2,512,128]{2,1,0:T(8,128)(2,1)} %get-tuple-element.121.refs_1_), channel_id=1, source_target_pairs={{0,2},{1,3},{2,0},{3,1},{4,6},{5,7},{6,4},{7,5},{8,10},{9,11},{10,... | collective-permute-start | bytes 786440 | tf_op jit(solution)/shard_map/ppermute | solution.py:704
  133.3 7.8 %collective-permute-start.13 = (bf16[2,512,128]{2,1,0:T(8,128)(2,1)}, bf16[2,512,128]{2,1,0:T(8,128)(2,1)S(1)}, u32[]{:S(2)}, u32[]{:S(2)}) collective-permute-start(bf16[2,512,128]{2,1,0:T(8,128)(2,1)} %get-tuple-element.121.refs_1_), channel_id=1, source_target_pairs={{0,1},{1,0},{2,3},{3,2},{4,5},{5,4},{6,7},{7,6},{8,9},{9,8},{10,11... | collective-permute-start | bytes 786440 | tf_op jit(solution)/shard_map/ppermute | solution.py:704
  139.1 2.0 %collective-permute-start.15 = (bf16[2,512,128]{2,1,0:T(8,128)(2,1)S(1)}, bf16[2,512,128]{2,1,0:T(8,128)(2,1)S(1)}, u32[]{:S(2)}, u32[]{:S(2)}) collective-permute-start(bf16[2,512,128]{2,1,0:T(8,128)(2,1)S(1)} %collective-permute-done.14.refs_3_), channel_id=1, source_target_pairs={{0,1},{1,0},{2,3},{3,2},{4,5},{5,4},{6,7},{7,6},{8,9},{9,8},{10,11... | collective-permute-start | bytes 786440 | tf_op jit(solution)/shard_map/ppermute | solution.py:704
  139.1 14.5 %collective-permute-start.16 = (bf16[2,336,128]{2,1,0:T(8,128)(2,1)S(1)}, bf16[2,336,128]{2,1,0:T(8,128)(2,1)S(1)}, u32[]{:S(2)}, u32[]{:S(2)}) collective-permute-start(bf16[2,336,128]{2,1,0:T(8,128)(2,1)S(1)} %copy-done.10), channel_id=1, source_target_pairs={{0,1},{1,0},{2,3},{3,2},{4,5},{5,4},{6,7},{7,6},{8,9},{9,8},{10,11... | collective-permute-start | bytes 516104 | tf_op jit(solution)/shard_map/ppermute | solution.py:704
  139.6 14.0 %collective-permute-start.17 = (bf16[2,336,128]{2,1,0:T(8,128)(2,1)S(1)}, bf16[2,336,128]{2,1,0:T(8,128)(2,1)S(1)}, u32[]{:S(2)}, u32[]{:S(2)}) collective-permute-start(bf16[2,336,128]{2,1,0:T(8,128)(2,1)S(1)} %copy-done.9), channel_id=1, source_target_pairs={{0,2},{1,3},{2,0},{3,1},{4,6},{5,7},{6,4},{7,5},{8,10},{9,11},{10,... | collective-permute-start | bytes 516104 | tf_op jit(solution)/shard_map/ppermute | solution.py:704
  141.1 12.5 %collective-permute-start.18 = (bf16[2,336,128]{2,1,0:T(8,128)(2,1)S(1)}, bf16[2,336,128]{2,1,0:T(8,128)(2,1)S(1)}, u32[]{:S(2)}, u32[]{:S(2)}) collective-permute-start(bf16[2,336,128]{2,1,0:T(8,128)(2,1)S(1)} %copy-done.8), channel_id=1, source_target_pairs={{0,3},{1,2},{2,1},{3,0},{4,7},{5,6},{6,5},{7,4},{8,11},{9,10},{10,... | collective-permute-start | bytes 516104 | tf_op jit(solution)/shard_map/ppermute | solution.py:704
  149.9 12.1 %all-to-all-start.5 = ((f32[32,8,128]{2,1,0:T(8,128)}), f32[32,8,128]{2,1,0:T(8,128)S(1)}, u32[]{:S(2)}, u32[]{:S(2)}) async-start(f32[32,8,128]{2,1,0:T(8,128)} %get-tuple-element.116.refs_0_), calls=%async_computation.6 | async-start | bytes 262144 | tf_op jit(solution)/shard_map/all_to_all | solution.py:691
  156.7 8.3 %collective-permute-start.19 = (bf16[512,128]{1,0:T(8,128)(2,1)}, bf16[512,128]{1,0:T(8,128)(2,1)S(1)}, u32[]{:S(2)}, u32[]{:S(2)}) collective-permute-start(bf16[512,128]{1,0:T(8,128)(2,1)} %get-tuple-element.130), channel_id=1, source_target_pairs={{4,0},{8,4},{12,8},{16,12},{20,16},{24,20},{28,24},{5,1},{9,5},{13... | collective-permute-start | bytes 393224 | tf_op jit(solution)/shard_map/ppermute | solution.py:977
Sparse Core Ops, SparseCore 0:
  10.1 36.2 all-gather.2
  105.4 33.4 reduce-scatter.1

commit v3 on v2

v3 whole, which is shorter than its diff:
```python
import jax
import jax.numpy as jnp
from jax import lax
from jax.experimental import pallas as pl
from jax.experimental.pallas import tpu as pltpu
from jax.sharding import PartitionSpec as P

BF = jnp.bfloat16
F32 = jnp.float32

epsilon = 1e-05
learn_rate = 0.4
trust_coef = 0.5
momentum = 0.5
avg_decay = 0.6
weight_decay = 5e-05
tiny_term = 1e-06

SIDE = 8
TAIL = 16
RING = [0, 2, 4, 6, 7, 5, 3, 1]


class whole:
    loose = 0
    direct = False

    def __init__(self, array):
        self.arrays, self.dims, self.dtype = [array], array.shape, array.dtype

    def copies(self):
        return len(self.arrays)

    def plan(self, refs, local):
        return [(refs[0], local)]


class fresh(whole):
    loose = 1
    direct = True

    def copies(self):
        return 0

    def plan(self, refs, local):
        return []


class stack(whole):
    def __init__(self, arrays, slot, loose=0):
        self.arrays, self.dtype, self.loose = list(arrays), arrays[0].dtype, loose
        self.dims, self.slot = (len(arrays),) + arrays[0].shape, slot

    def plan(self, refs, local):
        return [(ref, local.at[self.slot(k)]) for k, ref in enumerate(refs)]


class pick(whole):
    def __init__(self, array, index):
        self.arrays, self.dtype, self.index = [array], array.dtype, index
        self.dims = array.shape[1:]

    def plan(self, refs, local):
        return [(refs[0].at[self.index()], local)]


class spread(whole):
    def __init__(self, array, order, first, rows):
        self.arrays, self.dtype, self.order = [array], array.dtype, order
        self.first, self.rows = first, rows
        self.dims = (array.shape[0], rows) + array.shape[2:]

    def copies(self):
        return self.dims[0]

    def plan(self, refs, local):
        cut = pl.ds(self.first, self.rows)
        return [(refs[0].at[k, cut], local.at[place()]) for k, place in enumerate(self.order)]


class stack_rows(stack):
    def __init__(self, arrays, slot, first, rows, loose=0):
        super().__init__(arrays, slot, loose)
        self.cut = pl.ds(first, rows)
        self.dims = self.dims[:2] + (rows,) + self.dims[3:]

    def plan(self, refs, local):
        return [(ref.at[:, self.cut], local.at[self.slot(k)]) for k, ref in enumerate(refs)]


class quarter(whole):
    def __init__(self, images, groups, count):
        self.arrays, self.dtype = [images], images.dtype
        self.per, self.count = images.shape[0] // groups, count
        self.dims = (groups, count) + images.shape[1:]

    def copies(self):
        return self.dims[0]

    def plan(self, refs, local):
        mine = lax.axis_index("chan") * self.count
        return [
            (refs[0].at[pl.ds(g * self.per + mine, self.count)], local.at[g])
            for g in range(self.dims[0])
        ]


class even_phase(stack):
    def __init__(self, arrays, slot):
        super().__init__(arrays, slot)
        self.lanes = arrays[0].shape[3] // 2
        self.dims = (len(arrays), arrays[0].shape[0], arrays[0].shape[2], self.lanes)

    def plan(self, refs, local):
        lanes = pl.ds(0, self.lanes)
        return [(ref.at[:, 0, :, lanes], local.at[self.slot(k)]) for k, ref in enumerate(refs)]


class result:
    pinned = True

    def __init__(self, dims, dtype=F32, pinned=True):
        self.dims, self.dtype, self.pinned = tuple(dims), dtype, pinned
        self.outs = [jax.ShapeDtypeStruct(self.dims, dtype)]

    def copies(self):
        return len(self.outs)

    def plan(self, local, refs):
        return [(local, refs[0])]


class split(result):
    def __init__(self, slots, dims, dtype=F32, part=None):
        self.dims, self.dtype, self.slots = tuple(dims), dtype, slots
        self.outs = [jax.ShapeDtypeStruct(self.dims[1:], dtype) for _ in slots]

    def plan(self, local, refs):
        return [(local.at[slot()], ref) for slot, ref in zip(self.slots, refs)]


class parts_of(result):
    dims = None

    def __init__(self, source, slots, count, first, rows, array):
        self.source, self.slots, self.count, self.cut = source, slots, count, pl.ds(first, rows)
        dims = (count, rows) + array.shape[2:]
        self.outs = [jax.ShapeDtypeStruct(dims, array.dtype) for _ in slots]

    def plan(self, local, refs):
        return [
            (local.at[pl.ds(slot(), self.count), self.cut], ref)
            for slot, ref in zip(self.slots, refs)
        ]


class Taken:
    def __init__(self, local, copies):
        self.local, self.copies, self.waited = local, copies, False

    def ref(self):
        if not self.waited:
            for copy in self.copies:
                copy.wait()
            self.waited = True
        return self.local

    def __getitem__(self, index):
        return self.ref()[index]

    @property
    def shape(self):
        return self.local.shape


class Given:
    def __init__(self, local, copies):
        self.local, self.copies, self.sent = local, copies, False

    def send(self):
        if not self.sent:
            for copy in self.copies:
                copy.start()
            self.sent = True

    def __setitem__(self, index, value):
        self.local[index] = value

    @property
    def shape(self):
        return self.local.shape


def call(body, takes, gives, scratch=(), flops=0, limit=40, later=()):
    takes = [t if isinstance(t, whole) else whole(t) for t in takes]
    arrays = [a for t in takes for a in t.arrays]
    spec = pl.BlockSpec(memory_space=pltpu.HBM)
    loose, vmem = pl.BlockSpec(memory_space=pl.ANY), pl.BlockSpec(memory_space=pltpu.VMEM)
    pinned = [False] * len(later)
    in_specs = [loose] * len(later)
    for t in takes:
        pinned += [True] * (len(t.arrays) - t.loose) + [False] * t.loose
        in_specs += [spec] * (len(t.arrays) - t.loose) + [vmem if t.direct else loose] * t.loose
    outs = [o for g in gives for o in g.outs]
    n_later, n_in, n_out = len(later), len(arrays), len(outs)
    n_copies = sum(t.copies() for t in takes) + sum(g.copies() for g in gives if g.pinned)

    def kernel(*refs):
        refs = refs[n_later:]
        ins, res = list(refs[:n_in]), list(refs[n_in : n_in + n_out])
        local = list(refs[n_in + n_out : -1])
        sems = refs[-1]
        used = 0
        taken, given = [], []
        for t in takes:
            mine, ins = ins[: len(t.arrays)], ins[len(t.arrays) :]
            place = mine[0] if t.direct else local.pop(0)
            copies = []
            for a, b in t.plan(mine, place):
                copies.append(pltpu.make_async_copy(a, b, sems.at[used]))
                used += 1
            for copy in copies:
                copy.start()
            taken.append(Taken(place, copies))
        for g in gives:
            mine, res = res[: len(g.outs)], res[len(g.outs) :]
            if g.dims is None:
                place = taken[g.source].local
            else:
                place = local.pop(0) if g.pinned else mine[0]
            copies = []
            for a, b in g.plan(place, mine) if g.pinned else ():
                copies.append(pltpu.make_async_copy(a, b, sems.at[used]))
                used += 1
            given.append(Given(place, copies))
        body(*taken, *given, *local)
        for t in taken:
            t.ref()
        for g in given:
            g.send()
        for g in given:
            for copy in g.copies:
                copy.wait()

    moved = sum(a.size * a.dtype.itemsize for a in arrays + outs)
    operands = [
        pltpu.with_memory_space_constraint(a, pltpu.HBM) if pin else a
        for a, pin in zip([*later, *arrays], pinned)
    ]
    values = pl.pallas_call(
        kernel,
        out_shape=[pltpu.HBM(o.shape, o.dtype) if g.pinned else o for g in gives for o in g.outs],
        in_specs=in_specs,
        out_specs=[spec if g.pinned else vmem for g in gives for _ in g.outs],
        scratch_shapes=[pltpu.VMEM(t.dims, t.dtype) for t in takes if not t.direct]
        + [pltpu.VMEM(g.dims, g.dtype) for g in gives if g.dims is not None and g.pinned]
        + [pltpu.VMEM(dims, dtype) for dims, dtype in scratch]
        + [pltpu.SemaphoreType.DMA((n_copies,))],
        compiler_params=pltpu.CompilerParams(vmem_limit_bytes=limit * 2**20),
        cost_estimate=pl.CostEstimate(flops=flops, bytes_accessed=moved, transcendentals=0),
        name=body.__name__,
    )(*operands)
    return list(values)


def dot(a, b):
    return jnp.dot(a, b, preferred_element_type=F32)


def dot_nt(a, b):
    return lax.dot_general(a, b, (((1,), (1,)), ((), ())), preferred_element_type=F32)


def dot_tn(a, b):
    return lax.dot_general(a, b, (((0,), (0,)), ((), ())), preferred_element_type=F32)


def shift_col(x, step):
    rows, lanes = x.shape
    grouped = x.reshape(rows // SIDE, SIDE, lanes)
    rolled = pltpu.roll(grouped, step % SIDE, 1)
    col = lax.broadcasted_iota(jnp.int32, grouped.shape, 1)
    edge = 0 if step > 0 else SIDE - 1
    return jnp.where(col == edge, 0.0, rolled).reshape(rows, lanes)


def shift_row(x, step):
    part = x.shape[0] // SIDE
    blank = jnp.zeros((part, x.shape[1]), x.dtype)
    if step > 0:
        return jnp.concatenate([blank, x[:-part]], axis=0)
    return jnp.concatenate([x[part:], blank], axis=0)


def swap_orders(x, batch):
    pieces = [
        x[(b * SIDE + r) * SIDE : (b * SIDE + r + 1) * SIDE] for r in range(SIDE) for b in range(batch)
    ]
    return jnp.concatenate(pieces, axis=0)


def swap_back(x, batch):
    pieces = [
        x[(r * batch + b) * SIDE : (r * batch + b + 1) * SIDE] for b in range(batch) for r in range(SIDE)
    ]
    return jnp.concatenate(pieces, axis=0)


def col_sum(x):
    return jnp.sum(x, axis=0, keepdims=True)


def lane_sum(x):
    return jnp.sum(col_sum(x), axis=1, keepdims=True)


def rows_of(*rows):
    pad = SIDE - len(rows)
    tail = [jnp.zeros((pad, rows[0].shape[1]), F32)] if pad else []
    return jnp.concatenate(list(rows) + tail, axis=0)


def spread_rows(out, rows):
    out[...] = jnp.broadcast_to(rows[None], out.shape)


def mean_inverse(total, squares, count):
    center = total / count
    spread = squares / count - center * center
    return center, lax.rsqrt(spread + epsilon)


def slope(v):
    sigma = jax.nn.sigmoid(v)
    return sigma * (1.0 + v * (1.0 - sigma))


def three_rows(values):
    high = values.astype(BF).astype(F32)
    rest = values - high
    middle = rest.astype(BF).astype(F32)
    low = rest - middle
    blank = jnp.zeros((TAIL - 3 * values.shape[0], values.shape[1]), F32)
    return jnp.concatenate([high, middle, low, blank], axis=0).astype(BF)


def one_row(parts, count):
    parts = parts.astype(F32)
    return parts[:count] + parts[count : 2 * count] + parts[2 * count : 3 * count]


def add_up(pieces):
    total = pieces[0].astype(F32)
    for piece in pieces[1:]:
        total = total + piece.astype(F32)
    return total


def expand_mask(inside):
    images, wide = inside.shape
    dims = (images, SIDE, wide)
    lane = lax.broadcasted_iota(jnp.int32, dims, 2)
    col = lax.broadcasted_iota(jnp.int32, dims, 1)
    picked = jnp.where(lane == col, jnp.broadcast_to(inside[:, None, :], dims), 0.0)
    return jnp.broadcast_to(jnp.sum(picked, axis=2, keepdims=True), dims).reshape(-1, wide)


def widen(mask, wide):
    return jnp.concatenate(
        [mask, jnp.zeros((mask.shape[0], wide - mask.shape[1]), mask.dtype)], axis=1
    )


def lane_row(x):
    return col_sum(x * x)


def pack_weights(w, p, w_next, out, rows):
    depth = p.shape[0]
    w_ref, next_ref = w.ref(), w_next.ref()
    pieces = [w_ref[pl.ds(tap, depth, stride=9), :] for tap in range(9)] + [p[...]]
    depth = w_next.shape[0] // 9
    pieces += [next_ref[pl.ds(tap, depth, stride=9), :] for tap in range(9)]
    out[...] = jnp.concatenate(pieces, axis=0).astype(BF)
    out.send()
    rows[...] = rows_of(lane_row(w[...]), lane_row(p[...]), lane_row(w_next[...]))


def pack_images(images, mask, out, valid_out, scratch):
    groups, count, pix, lanes = images.shape
    wide = valid_out.shape[1]
    half = groups * count * pix // 2
    for k in range(lanes // wide):
        cut = slice(k * wide, (k + 1) * wide)
        scratch[k] = images[:, :, :, cut].astype(F32).reshape(2 * half, wide)
        for col in range(2):
            taken = scratch[k, pl.ds(col, half, stride=2), :].reshape(groups, count, 2, SIDE, wide)
            for row in range(2):
                rows = jnp.concatenate([taken[:, i, row] for i in range(count)], axis=1)
                start = col * lanes + k * wide
                out[:, row, :, start : start + wide] = rows.astype(BF)
    out.send()
    inside = widen(mask[...].astype(F32), wide)
    part = inside.shape[0] * SIDE
    for row in range(SIDE):
        turned = pltpu.roll(inside, (wide - SIDE * row) % wide, 1)
        valid_out[row * part : (row + 1) * part] = expand_mask(turned)


def tap_major(w):
    return w.reshape(-1, 9, w.shape[1]).transpose(1, 0, 2)


def taps_of(w, depth, first=0):
    def taps(*which):
        starts = [first + t * depth for t in which]
        return jnp.concatenate(
            [w[:, a : a + depth].reshape(-1, w.shape[2]) for a in starts], axis=1
        )

    return taps


def phase_of(x, row, col):
    lanes = x.shape[4] // 2
    cut = slice(col * lanes, (col + 1) * lanes)
    pieces = [x[k, r, row, :, cut] for r in range(x.shape[1]) for k in range(x.shape[0])]
    return jnp.concatenate(pieces, axis=0)


def conv_first(w, x, m, n, zb_out, zp_out, pay):
    taps = taps_of(w, w.shape[1] // 10)
    wide = w.shape[2]
    y00 = dot(phase_of(x, 0, 0), taps(4, 9))
    y01 = dot(phase_of(x, 0, 1), taps(5, 3))
    y10 = dot(phase_of(x, 1, 0), taps(7, 1))
    y11 = dot(phase_of(x, 1, 1), taps(8, 6, 2, 0))
    here = y00[:, :wide] + y01[:, :wide] + y10[:, :wide] + y11[:, :wide]
    left = y01[:, wide:] + y11[:, wide : 2 * wide]
    above = y10[:, wide:] + y11[:, 2 * wide : 3 * wide]
    corner = y11[:, 3 * wide :]
    z = here + shift_row(above, 1) + shift_col(left + shift_row(corner, 1), 1)
    zb_out[...] = z.astype(BF)
    zb_out.send()
    zp = y00[:, wide:]
    valid = m[...]
    vz, vzp = valid * z, valid * zp
    sums = [col_sum(vz), col_sum(vz * z), col_sum(valid), n[0:1], n[1:2]]
    spread_rows(pay, rows_of(*sums, col_sum(vzp), col_sum(vzp * zp)))
    pay.send()
    zp_out[...] = zp


def hand_on(w, *outs):
    w.ref()


def first_norm(z, rows):
    count = rows[2:3]
    center, inverse = mean_inverse(rows[0:1], rows[1:2], count)
    hat = (z - center) * inverse
    return hat, hat * rows[3:4] + rows[4:5], inverse


def conv_second(z, got, m, w, zp, cot, h_out, z2_out, pay, tot_out, m_out, zp_out, cot_out, own_out):
    blocks, wide = z.shape[0], z.shape[2]
    valid = m[...]
    hidden = []
    for k in range(blocks):
        total = jnp.sum(got[:, k], axis=0)
        rows = jnp.concatenate([total[0:3], got[0, k, 3:5], total[5:8]], axis=0)
        tot_out[k] = rows
        _, lin, _ = first_norm(z[k].astype(F32), rows)
        hidden.append((lin * jax.nn.sigmoid(lin) * valid).astype(BF))
        h_out[:, k * wide : (k + 1) * wide] = hidden[-1]
    h_out.send()
    hidden = jnp.concatenate(hidden, axis=1)
    taps = taps_of(w, hidden.shape[1] // w.shape[0])
    moved = []
    for col in range(3):
        y = dot(hidden, taps(col, 3 + col, 6 + col))
        moved.append(
            shift_row(y[:, :wide], 1) + y[:, wide : 2 * wide] + shift_row(y[:, 2 * wide :], -1)
        )
    z2 = moved[1] + shift_col(moved[0], 1) + shift_col(moved[2], -1)
    vz = valid * z2
    spread_rows(pay, rows_of(col_sum(vz), col_sum(vz * z2)))
    pay.send()
    z2_out[...] = z2
    batch, pix, wide = cot.shape
    m_out[...] = valid
    zp_out[...] = zp[...]
    cot_out[...] = swap_orders(cot[...].astype(F32).reshape(batch * pix, wide), batch)
    own_out[...] = tot_out.local[pl.ds(lax.axis_index("chan"), 1)][0]


def block_output(z2, zp, got, tot1, m, n, cot, out, e_out, hat2_out, hat_p_out, rows_out, pay):
    total, count = jnp.sum(got[...], axis=0), tot1[2:3]
    center2, inverse2 = mean_inverse(total[0:1], total[1:2], count)
    center_p, inverse_p = mean_inverse(tot1[5:6], tot1[6:7], count)
    hat2, hat_p = (z2[...] - center2) * inverse2, (zp[...] - center_p) * inverse_p
    hat2_out[...] = hat2
    hat_p_out[...] = hat_p
    rows_out[...] = rows_of(n[2:3] * inverse2, n[4:5] * inverse_p, count)
    summed = hat2 * n[2:3] + n[3:4] + (hat_p * n[4:5] + n[5:6])
    sigma = jax.nn.sigmoid(summed)
    valid = m[...]
    batch, pix, wide = out.shape
    e = cot[...] * valid * (sigma * (1.0 + summed * (1.0 - sigma)))
    spread_rows(pay, rows_of(col_sum(e), col_sum(e * hat2), col_sum(e * hat_p)))
    pay.send()
    e_out[...] = e
    out[...] = swap_back(summed * sigma * valid, batch).astype(BF).reshape(out.shape)


def grad_outputs(e, hat2, hat_p, rows, got, m, g2_out, gp_out, tot_out):
    back, count = jnp.sum(got[...], axis=0), rows[2:3]
    tot_out[...] = back
    valid, e = m[...], e[...]
    loss = valid * ((back[0:1] + hat2[...] * back[1:2]) / count)
    g2_out[...] = (rows[0:1] * (e - loss)).astype(BF)
    g2_out.send()
    loss = valid * ((back[0:1] + hat_p[...] * back[2:3]) / count)
    gp_out[...] = (rows[1:2] * (e - loss)).astype(BF)


def grad_hidden(w, g2, z, gp, tot1, m, b_out, msg, pay):
    blocks, _, wide = g2.shape
    count, part = w.shape[1], w.shape[2] // 9
    depth = count * part
    moved = []
    for col in range(3):
        y = 0.0
        for k in range(blocks):
            starts = [(3 * row + col) * part for row in range(3)]
            taps = [w[k, :, a : a + part].reshape(depth, wide) for a in starts]
            y = y + dot_nt(g2[k], jnp.concatenate(taps, axis=0))
        moved.append(
            shift_row(y[:, :depth], -1) + y[:, depth : 2 * depth] + shift_row(y[:, 2 * depth :], 1)
        )
    gh = moved[1] + shift_col(moved[0], -1) + shift_col(moved[2], 1)
    hat, lin, _ = first_norm(z[...].astype(F32), tot1[...])
    valid = m[...]
    b = gh * (slope(lin) * valid)
    shift, scaled = col_sum(b), col_sum(b * hat)
    spread_rows(pay, rows_of(shift, scaled))
    pay.send()
    here = col_sum(valid)
    shift, scaled = shift / here, scaled / here
    pix = b.shape[0]
    msg[:pix] = (b - valid * (shift + hat * scaled)).astype(BF)
    msg[pix : 2 * pix] = gp[...]
    msg[2 * pix :] = three_rows(jnp.concatenate([shift, scaled], axis=0))
    msg.send()
    b_out[...] = b


def make_grad_second(on_ring):
    def grad_second(h, g2, x, gp, g_out):
        groups, rows, wide = g_out.shape
        places = list(range(groups))
        if on_ring:
            last, turn = len(RING) - 1, turn_round()
            places = [RING.index(k) for k in places]
            places = [p + turn * (last - 2 * p) for p in places]
        share = h.shape[1] // groups
        h, g2 = h[...], g2[...].astype(F32)
        moved = [shift_col(g2, step).astype(BF) if step else g2.astype(BF) for step in (-1, 0, 1)]

        def put(rows, g):
            g = g.astype(BF).reshape(groups, -1, wide)
            for k, place in enumerate(places):
                g_out[place, rows] = g[k]

        for tap in range(9):
            step = tap // 3 - 1
            g = shift_row(moved[tap % 3], step) if step else moved[tap % 3]
            put(slice(tap * share, (tap + 1) * share), dot_tn(h, g))
        pieces = [x[k, r] for r in range(SIDE) for k in range(x.shape[0])]
        put(slice(9 * share, rows), dot_tn(jnp.concatenate(pieces, axis=0), gp[...]))

    return grad_second


def grad_first(b, z, got, tot1, n, m, x, blocks_out, tot_out):
    own = got[:, pl.ds(lax.axis_index("chan"), 1)]
    back, count = jnp.sum(own, axis=0)[0], tot1[2:3]
    tot_out[...] = back
    hat, _, inverse = first_norm(z[...].astype(F32), tot1[...])
    g = n[0:1] * inverse * (b[...] - m[...] * ((back[0:1] + hat * back[1:2]) / count))
    here, left = g.astype(BF), shift_col(g, -1).astype(BF)
    wide = here.shape[1]
    groups = blocks_out.shape[0]
    share = x.shape[4] // 2 // groups

    def put(tap, grad):
        rows = grad.astype(BF).reshape(groups, share, wide)
        blocks_out[:, tap * share : (tap + 1) * share] = rows

    above, corner = shift_row(here, -1), shift_row(left, -1)
    for row, col, pairs in (
        (0, 0, ((4, here),)),
        (0, 1, ((5, here), (3, left))),
        (1, 0, ((7, here), (1, above))),
        (1, 1, ((8, here), (6, left), (2, above), (0, corner))),
    ):
        both = jnp.concatenate([grad for _, grad in pairs], axis=1)
        both = dot_tn(phase_of(x, row, col), both)
        for place, (tap, _) in enumerate(pairs):
            put(tap, both[:, place * wide : (place + 1) * wide])


def grad_images(msg, z, got, tot1, m, w, out):
    blocks, count = w.shape[0], w.shape[1]
    depth = w.shape[2] // 10
    half, wide = count * depth, w.shape[3]

    def taps(k, *which):
        return jnp.concatenate(
            [w[k, :, t * depth : (t + 1) * depth].reshape(half, wide) for t in which], axis=0
        )

    plain, moved, proj = 0.0, 0.0, 0.0
    valid = m[...]
    pix = valid.shape[0]
    for k in range(blocks):
        rows, back = tot1[k], jnp.sum(got[:, k], axis=0)
        hat, _, inverse = first_norm(z[k].astype(F32), rows)
        fit = back[0:2] / rows[2:3] - one_row(msg[k, 2 * pix :], 2)
        loss = valid * (fit[0:1] + hat * fit[1:2])
        g = (rows[3:4] * inverse * (msg[k, :pix].astype(F32) - loss)).astype(BF)
        plain = plain + dot_nt(g, taps(k, 4, 5, 7, 8, 1, 2))
        moved = moved + dot_nt(g, taps(k, 3, 3, 6, 6, 0, 0))
        proj = proj + dot_nt(msg[k, pix : 2 * pix], taps(k, 9, 9))
    lane = lax.broadcasted_iota(jnp.int32, moved.shape, 1) % (2 * half)
    total = plain + jnp.where(lane >= half, shift_col(moved, -1), 0.0)
    lane = lax.broadcasted_iota(jnp.int32, proj.shape, 1)
    even = total[:, : 2 * half] + jnp.where(lane < half, proj, 0.0)
    odd = total[:, 2 * half : 4 * half] + shift_row(total[:, 4 * half :], -1)
    for row, value in enumerate((even, odd)):
        out[:, row] = value.astype(BF).reshape(out.shape[0], -1, 2 * half)


def finish_images(x, out, scratch):
    images, pix, half = out.shape
    groups, _, part, wide = x.shape
    count = part // SIDE
    value = x[...].astype(F32).reshape(groups, 2, count, 1, SIDE, wide)
    value = jnp.concatenate([value[:, 0], value[:, 1]], axis=2)
    rows = images * pix // 2
    value = value.reshape(rows, wide)
    scratch[pl.ds(0, rows, stride=2), :] = value
    scratch[pl.ds(1, rows, stride=2), :] = pltpu.roll(value, half, 1)
    out[...] = scratch[...][:, :half].astype(BF).reshape(out.shape)


def put_rows(out, total):
    depth = out.shape[0] // 9
    for tap in range(9):
        out.local[pl.ds(tap, depth, stride=9), :] = total[tap * depth : (tap + 1) * depth]


def reduce_all(second, x, sw, t3, t4, n, g1_out, g2_out, gp_out, pay):
    second = second[...].astype(F32)
    cut = g2_out.shape[0]
    conv, proj = second[:cut], second[cut:]
    parts = [lane_row(conv), lane_row(proj)]
    first = add_up([x[k] for k in range(x.shape[0])])
    rows = [sw[0:1], lane_row(first), sw[2:3], parts[0], sw[1:2], parts[1]]
    nw, gn = n[...], norm_grad(t3, t4)
    blank = jnp.zeros((2, nw.shape[1]), F32)
    cols = [
        jnp.sum(jnp.concatenate(rows + [blank], axis=0), axis=1, keepdims=True),
        jnp.sum(jnp.concatenate([nw * nw, blank], axis=0), axis=1, keepdims=True),
        jnp.sum(jnp.concatenate([gn * gn, blank], axis=0), axis=1, keepdims=True),
    ]
    lane = lax.broadcasted_iota(jnp.int32, pay.shape[1:], 1)
    block = jnp.zeros(pay.shape[1:], F32)
    for place, col in enumerate(cols):
        block = jnp.where(lane == place, col, block)
    spread_rows(pay, block)
    pay.send()
    gp_out[...] = proj
    put_rows(g2_out, conv)
    g2_out.send()
    put_rows(g1_out, first)


def norm_grad(t3, t4):
    return jnp.concatenate([t4[1:2], t4[0:1], t3[1:2], t3[0:1], t3[2:3], t3[0:1]], axis=0)


def step_of(w, g, m, a, weight_sq, grad_sq):
    weight_len = jnp.sqrt(weight_sq)
    trust = trust_coef * weight_len / (jnp.sqrt(grad_sq) + weight_decay * weight_len + tiny_term)
    step = trust * (g + weight_decay * w)
    m_new = momentum * m + step
    w_new = w - learn_rate * (step + momentum * m_new)
    return w_new, m_new, avg_decay * a + (1.0 - avg_decay) * w_new


def make_update(dp_count):
    def update(*refs):
        r6, t3, t4 = refs[:3]
        ins, outs = refs[3:18], refs[18:]
        total = jnp.sum(r6[...], axis=0)
        for place in range(3):
            w, g, m, a = (ref[...] for ref in ins[4 * place : 4 * place + 4])
            weight_sq = total[2 * place : 2 * place + 1, 0:1]
            grad_sq = total[2 * place + 1 : 2 * place + 2, 0:1]
            for ref, value in zip(outs[3 * place :], step_of(w, g, m, a, weight_sq, grad_sq)):
                ref[...] = value
                ref.send()
        w, m, a = (ref[...] for ref in ins[12:15])
        weight_sq, grad_sq = total[0:6, 1:2] / dp_count, total[0:6, 2:3] / dp_count
        g = norm_grad(t3, t4)
        for ref, value in zip(outs[9:], step_of(w, g, m, a, weight_sq, grad_sq)):
            ref[...] = value

    return update


def exchange(blocks, axes):
    return lax.all_to_all(blocks, axes, 0, 0)


def rings():
    count = lax.axis_size("chan")
    return [[(d ^ (c % 2)) * count + c for d in RING] for c in range(count)]


def turn_round():
    return lax.axis_index("chan") % 2


def swap(array, axis, bits):
    return lax.ppermute(array, axis, [(i, i ^ bits) for i in range(lax.axis_size(axis))])


def away(axis, k):
    return lambda: lax.axis_index(axis) ^ k


def in_groups(taps, groups):
    return taps.reshape(taps.shape[0], groups, -1, taps.shape[2]).transpose(1, 0, 2, 3)


def regroup(blocks, taps, groups):
    blocks = blocks.reshape(blocks.shape[0], taps, -1, blocks.shape[2]).transpose(1, 0, 2, 3)
    blocks = in_groups(blocks.reshape(taps, -1, blocks.shape[3]), groups)
    return blocks.reshape(groups, -1, blocks.shape[3])


def per_device(
    images, mask, cotangent, w_first, w_second, w_proj, norm_params, mom_first, mom_second,
    mom_proj, mom_norm, avg_first, avg_second, avg_proj, avg_norm,
):
    everyone = ("dp", "chan")
    dp_count, ch_count = lax.axis_size("dp"), lax.axis_size("chan")
    n_all = dp_count * ch_count
    batch = mask.shape[0]
    pix_here, d_in = images.shape[1], images.shape[2]
    wide = w_first.shape[1]
    d_out = wide * ch_count
    part = batch * SIDE
    pix = SIDE * part
    share = batch // ch_count
    eight = dp_count == SIDE and pix_here == 4 * SIDE
    groups = SIDE
    first_rows, second_rows = 10 * d_in // groups, 9 * d_out // groups
    square_rows = result((SIDE, wide))
    sums = result((dp_count, SIDE, wide), pinned=False)
    passing, few = (result((n, wide), pinned=False) for n in (pix, SIDE))

    def slot_dp(k):
        return lax.axis_index("dp") ^ k

    def slot_ch(k):
        return lax.axis_index("chan") ^ k

    def share_out(own):
        far = swap(own, "chan", 2)
        return [own, swap(own, "chan", 1), far, swap(far, "chan", 1)]

    if eight:
        own, squares = call(
            pack_weights,
            [w_first, w_proj, w_second],
            [result((first_rows + second_rows, wide), BF), square_rows],
        )
        gathered = lax.all_gather(own, everyone, axis_index_groups=rings())
        order = [lambda d=d: d ^ turn_round() for d in RING]
        mine, valid = call(
            pack_images,
            [quarter(images, dp_count, share), mask],
            [result((dp_count, 2, share * SIDE, 2 * d_in), BF), result((pix, wide))],
            scratch=[((d_in // wide, dp_count * share * pix_here, wide), F32)],
            later=[own],
        )
        pixels, slot = share_out(exchange(mine, "dp")), slot_ch
    else:
        valid = mask.reshape(batch, SIDE, SIDE).transpose(1, 0, 2).reshape(pix, 1).astype(F32)
        valid = jnp.broadcast_to(valid, (pix, wide))
        own = jnp.concatenate([tap_major(w_first), w_proj[None]], axis=0).astype(BF)
        own = lax.all_gather(own, "dp", axis=1, tiled=True)
        next = lax.all_gather(tap_major(w_second).astype(BF), "dp", axis=1, tiled=True)
        gathered = [in_groups(taps, groups).reshape(groups, -1, wide) for taps in (own, next)]
        gathered = jnp.concatenate(gathered, axis=1)
        order = [lambda g=g: g for g in range(groups)]
        squares = [jnp.sum(w * w, axis=0) for w in (w_first, w_proj, w_second)]
        squares = jnp.zeros((SIDE, wide), F32).at[:3].set(jnp.stack(squares))
        mine = images.reshape(dp_count, ch_count, share, pix_here, d_in)
        mine = lax.dynamic_index_in_dim(mine, lax.axis_index("chan"), 1, keepdims=False)
        pixels = lax.all_gather(exchange(mine, "dp"), "chan")
        cols = pix_here // 2
        pixels = pixels.reshape(ch_count, SIDE, 2, SIDE // cols, share, cols, 2 * d_in)
        pixels = pixels.transpose(0, 1, 2, 4, 3, 5, 6)
        pixels = pixels.reshape(ch_count, SIDE, 2, share * SIDE, 2 * d_in)
        pixels, slot = [pixels[k] for k in range(ch_count)], lambda k: k

    macs = pix * 9 * wide * d_in
    per_block = groups // ch_count
    block_slots = [lambda k=k: (lax.axis_index("chan") ^ k) * per_block for k in range(ch_count)]
    z_own, z_proj, pay = call(
        conv_first,
        [spread(gathered, order, 0, first_rows), stack(pixels, slot), valid, norm_params],
        [result((pix, wide), BF), result((pix, wide)), result((n_all, SIDE, wide))],
        flops=2 * macs,
    )
    turned = call(
        hand_on,
        [spread(gathered, order, 0, first_rows + second_rows)],
        [parts_of(0, block_slots, per_block, 0, first_rows + second_rows, gathered)],
        later=[z_own],
    )
    got1 = exchange(pay, everyone).reshape(dp_count, ch_count, SIDE, wide)
    far = swap(z_own, "chan", 2)
    far, got1, *turned = lax.optimization_barrier((far, got1, *turned))
    z_all = [z_own, swap(z_own, "chan", 1), far, swap(far, "chan", 1)]

    hidden, z_second, pay, total1, *near = call(
        conv_second,
        [
            stack(z_all, slot_ch, 3),
            fresh(got1),
            valid,
            spread(gathered, order, first_rows, second_rows),
            z_proj,
            cotangent,
        ],
        [
            result((pix, d_out), BF, pinned=False),
            passing,
            sums,
            result((ch_count, SIDE, wide)),
            passing,
            passing,
            passing,
            few,
        ],
        flops=4 * macs,
    )
    turned = turned[:1] + [swap(block, "chan", k) for k, block in enumerate(turned) if k]
    total1_own = pick(total1, away("chan", 0))
    got2 = exchange(pay, "dp")
    near_valid, near_proj, near_cot, near_total = (fresh(array) for array in near)
    output, e, hat_second, hat_proj, near_rows, pay = call(
        block_output,
        [fresh(z_second), near_proj, fresh(got2), near_total, near_valid, norm_params, near_cot],
        [result((batch, SIDE * SIDE, wide), BF), passing, passing, passing, few, sums],
    )
    got3 = exchange(pay, "dp")

    g_second_out, g_proj_out, total3 = call(
        grad_outputs,
        [fresh(e), fresh(hat_second), fresh(hat_proj), fresh(near_rows), fresh(got3), near_valid],
        [result((pix, wide), BF), result((pix, wide), BF), square_rows],
        later=turned[1:],
    )
    rows = second_rows + d_in // groups
    (grads,) = call(
        make_grad_second(eight),
        [fresh(hidden), g_second_out, even_phase(pixels, slot), g_proj_out],
        [result((groups, rows, wide), BF)],
        flops=4 * macs,
    )
    far = swap(g_second_out, "chan", 2)
    far, grads = lax.optimization_barrier((far, grads))
    g_all = [g_second_out, swap(g_second_out, "chan", 1), far, swap(far, "chan", 1)]
    if eight:
        grads_second = lax.psum_scatter(
            grads.reshape(groups * rows, wide),
            everyone,
            scatter_dimension=0,
            axis_index_groups=rings(),
            tiled=True,
        )
    else:
        grads = [
            regroup(grads[:, :second_rows], 9, dp_count),
            regroup(grads[:, second_rows:], 1, dp_count),
        ]
        grads = jnp.concatenate(grads, axis=1)
        grads_second = jnp.sum(exchange(grads, "dp").astype(F32), axis=0)

    back, msg, pay = call(
        grad_hidden,
        [stack_rows(turned, slot_ch, first_rows, second_rows, 3), stack(g_all, slot_ch, 3)]
        + [z_own, g_proj_out, total1_own, valid],
        [passing, result((2 * pix + TAIL, wide), BF), result((n_all, SIDE, wide), pinned=False)],
        flops=4 * macs,
    )
    got4 = exchange(pay, everyone).reshape(dp_count, ch_count, SIDE, wide)
    far = swap(msg, "chan", 2)
    far, got4 = lax.optimization_barrier((far, got4))
    messages = [msg, swap(msg, "chan", 1), far, swap(far, "chan", 1)]

    grads, total4 = call(
        grad_first,
        [fresh(back), z_own, fresh(got4), total1_own, norm_params, valid, stack(pixels, slot)],
        [result((groups, 9 * (d_in // groups), wide), BF), square_rows],
        flops=2 * macs,
    )
    if not eight:
        grads = regroup(grads, 9, dp_count)
    got_first = exchange(grads, "dp")

    half = wide // 2
    takes = [
        stack(messages, slot_ch, 3),
        stack(z_all, slot_ch, 3),
        fresh(got4),
        total1,
        valid,
        stack_rows(turned, slot_ch, 0, first_rows, 3),
    ]
    dims = (SIDE, 2, part, wide)
    if eight:
        rows = call(
            grad_images,
            takes,
            [split([away("dp", k) for k in range(SIDE)], dims, BF)],
            flops=2 * macs,
        )
        rows = rows[:1] + [swap(row, "dp", k) for k, row in enumerate(rows) if k]
    else:
        (rows,) = call(grad_images, takes, [result(dims, BF)], flops=2 * macs)
        cols = pix_here // 2
        rows = rows.reshape(SIDE, 2, batch, SIDE // cols, cols, wide)
        rows = rows.transpose(0, 1, 3, 2, 4, 5).reshape(dp_count, batch, cols, wide)
        rows = [exchange(rows, "dp")]
    reduced_first, reduced_second, reduced_proj, pay = call(
        reduce_all,
        [grads_second, fresh(got_first), squares, total3, total4, norm_params],
        [
            result(w_first.shape),
            result(w_second.shape),
            result(w_proj.shape),
            result((n_all, SIDE, wide)),
        ],
    )
    pay, *rows = lax.optimization_barrier((pay, *rows))
    got6 = exchange(pay, everyone)

    conv = (
        (w_first, reduced_first, mom_first, avg_first),
        (w_second, reduced_second, mom_second, avg_second),
        (w_proj, reduced_proj, mom_proj, avg_proj),
    )
    results = call(
        make_update(dp_count),
        [fresh(got6), total3, total4, *(array for group in conv for array in group)]
        + [norm_params, mom_norm, avg_norm],
        [result(group[0].shape) for group in conv for _ in range(3)]
        + [result(norm_params.shape)] * 3,
    )
    if eight:
        (grad_pixels,) = call(
            finish_images,
            [stack(rows, slot_dp, 7)],
            [result((images.shape[0], pix_here, half), BF)],
            scratch=[((images.shape[0] * pix_here, wide), F32)],
        )
    else:
        grad_pixels = rows[0].reshape(dp_count * batch, pix_here, half)
    return (output, grad_pixels, *results)


def solution(mesh):
    rows, cols, batch = P("dp", "chan"), P(None, "chan"), P("dp", None, "chan")
    weights = (rows, rows, rows, cols)
    in_specs = (P(None, "dp", None), P("dp", None), batch) + weights * 3
    out_specs = (batch, P(None, "dp", "chan")) + (rows,) * 9 + (cols,) * 3
    return jax.shard_map(
        per_device, mesh=mesh, in_specs=in_specs, out_specs=out_specs, check_vma=False
    )
```

time: 175 us -> 168 us (0.960)
  waiting for transfers between devices: 62 us -> 32.9 us
  blocking collectives: 25.3 us -> 51.5 us
  Pallas kernels: 42.1 us -> 36.9 us
  local copies, waits for them, and re-layouts: 0.05 us -> 1.9 us
    all_to_all x2 -> x4, blocking collectives: 25.3 us -> 51.5 us  [exchange(): return lax.all_to_all(blocks, axes, 0, 0)]
    ppermute x18 -> x22, starting transfers between devices: 9.91 us -> 20.1 us  [swap(): lax.ppermute(array, axis, [(i, i ^ bits) for i in range(lax.axis_size(axi...]
    all_gather x1, waiting for transfers between devices: 18.3 us -> 9.06 us  [per_device(): gathered = lax.all_gather(own, everyone, axis_index_groups=rings())]
    all_to_all x4 -> x3, waiting for transfers between devices: 16.4 us -> 8.69 us  [exchange(): return lax.all_to_all(blocks, axes, 0, 0)]
    ppermute x18 -> x22, waiting for transfers between devices: 22.1 us -> 15.1 us  [swap(): lax.ppermute(array, axis, [(i, i ^ bits) for i in range(lax.axis_size(axi...]
    ppermute x2 -> x0, starting transfers between devices: 6.17 us -> none  [the longest x1 4.88 us: per_device(): come = lax.ppermute(send, 'dp', [(i, i + 1) for i in range(dp_count - 1)])]
    pallas_call x14, Pallas kernels: 42.1 us -> 36.9 us  [call(): pl.pallas_call(kernel, out_shape=[pltpu.HBM(o.shape, o.dtype) if g.pinned...]
    ppermute x2 -> x0, waiting for transfers between devices: 5.08 us -> none  [the longest x1 5.08 us: per_device(): come = lax.ppermute(send, 'dp', [(i, i + 1) for i in range(dp_count - 1)])]
  transfers between devices with their start and end apart: 26 -> 27, of which waited for: 14 -> 16; matrix products, arithmetic and copies ran while one was open for 0% -> 0% of each run, Pallas kernels for 16% -> 17%
where the time goes in v3:
time: 168 us; the launch traced here: 167 us
  blocking collectives  51.5 us (31%)
  Pallas kernels  36.9 us (22%)
  waiting for transfers between devices  32.9 us (20%)
  starting transfers between devices  29.9 us (18%)
  between operations  14.3 us (9%)
  local copies, waits for them, and re-layouts  1.9 us (1%)
    all_to_all x4, blocking collectives, exchange(): return lax.all_to_all(blocks, axes, 0, 0)  51.5 us
    pallas_call x14, Pallas kernels, call(): pl.pallas_call(kernel, out_shape=[pltpu.HBM(o.shape, o.dtype) if g.pinned...  36.9 us
    ppermute x22, starting transfers between devices, swap(): lax.ppermute(array, axis, [(i, i ^ bits) for i in range(lax.axis_size(axi...  20.1 us
    ppermute x22, waiting for transfers between devices, swap(): lax.ppermute(array, axis, [(i, i ^ bits) for i in range(lax.axis_size(axi...  15.1 us
    all_to_all x3, starting transfers between devices, exchange(): return lax.all_to_all(blocks, axes, 0, 0)  9.68 us
    all_gather x1, waiting for transfers between devices, per_device(): gathered = lax.all_gather(own, everyone, axis_index_groups=rings())  9.06 us
    all_to_all x3, waiting for transfers between devices, exchange(): return lax.all_to_all(blocks, axes, 0, 0)  8.69 us
  transfers between devices with their start and end apart: 27, of which 16 were waited for; matrix products, arithmetic and copies ran while one was open for 0% of the time, Pallas kernels for 17%

profile of v3, /device:TPU:0, one launch (start us, length us, event | category | flops | bytes accessed | tf_op | source)
XLA Modules:
  0.0 167.4 jit_solution(4388819215446677750)
XLA Ops:
  7.2 1.8 %pack_weights.1 = (bf16[896,128]{1,0:T(8,128)(2,1)}, f32[8,128]{1,0:T(8,128)}) custom-call(f32[288,128]{1,0:T(8,128)} %refs_3_.1, f32[32,128]{1,0:T(8,128)} %refs_11_.1, f32[576,128]{1,0:T(8,128)} %refs_7_.1), custom_call_target="tpu_custom_call" | custom-call | bytes 692224 | tf_op jit(solution)/shard_map/pack_weights/pallas_call | solution.py:250
  9.1 0.9 copy-done.2
  10.0 2.0 %pack_images.1 = (bf16[8,2,16,512]{3,2,1,0:T(8,128)(2,1)}, f32[512,128]{1,0:T(8,128)}) custom-call(bf16[896,128]{1,0:T(8,128)(2,1)S(1)} %copy-done.2, bf16[64,32,256]{2,1,0:T(8,128)(2,1)} %refs_1_.3, s32[8,64]{1,0:T(8,128)} %refs_2_.3), custom_call_target="tpu_custom_call" | custom-call | bytes 1574912 | tf_op jit(solution)/shard_map/pack_images/pallas_call | solution.py:250
  12.1 20.5 %all_to_all.35.refs_1_.refs_2_.refs_6_ = bf16[8,2,16,512]{3,2,1,0:T(8,128)(2,1)S(1)} all-to-all(bf16[8,2,16,512]{3,2,1,0:T(8,128)(2,1)} %get-tuple-element.91), channel_id=1, replica_groups=mesh['dp'=8,'chan'=4] {'dp'}, dimensions={0} | all-to-all | bytes 524288 | tf_op jit(solution)/shard_map/all_to_all | solution.py:724
  32.6 1.5 collective-permute-start.1
  34.0 4.9 %collective-permute-done.1.refs_3_.refs_4_.refs_8_ = bf16[8,2,16,512]{3,2,1,0:T(8,128)(2,1)S(1)} collective-permute-done((bf16[8,2,16,512]{3,2,1,0:T(8,128)(2,1)S(1)}, bf16[8,2,16,512]{3,2,1,0:T(8,128)(2,1)S(1)}, u32[]{:S(2)}, u32[]{:S(2)}) %collective-permute-start.1) | collective-permute-done | bytes 262176 | tf_op jit(solution)/shard_map/ppermute | solution.py:737
  39.0 1.5 collective-permute-done.2.refs_4_.refs_5_.refs_9_
  40.5 9.1 %all-gather.3.cloned.1.call-done = bf16[7168,128]{1,0:T(8,128)(2,1)} async-done(((bf16[896,128]{1,0:T(8,128)(2,1)}), bf16[7168,128]{1,0:T(8,128)(2,1)}) %all-gather.3.cloned.1.call-update) | async-done | bytes 1835024 | tf_op jit(solution)/shard_map/all_gather | solution.py:791
  49.5 3.2 %conv_first.1 = (bf16[512,128]{1,0:T(8,128)(2,1)}, f32[512,128]{1,0:T(8,128)}, f32[32,8,128]{2,1,0:T(8,128)}) custom-call(bf16[8,896,128]{2,1,0:T(8,128)(2,1)} %bitcast.7, bf16[8,2,16,512]{3,2,1,0:T(8,128)(2,1)} %copy-done.3, bf16[8,2,16,512]{3,2,1,0:T(8,128)(2,1)} %copy-done.5, bf16[8,2,16,512]{3,2,1,0:T(8,128)(2,1)} %copy-done.4, ...), custom_call_target="tpu_custom_call" | custom-call | flops 301989888 | bytes 3673088 | tf_op jit(solution)/shard_map/conv_first/pallas_call | solution.py:250
  52.7 3.6 %all-to-all-start.1 = ((f32[32,8,128]{2,1,0:T(8,128)}), f32[32,8,128]{2,1,0:T(8,128)S(1)}, u32[]{:S(2)}, u32[]{:S(2)}) async-start(f32[32,8,128]{2,1,0:T(8,128)} %get-tuple-element.94), calls=%async_computation.1 | async-start | bytes 262144 | tf_op jit(solution)/shard_map/all_to_all | solution.py:724
  56.3 1.8 %collective-permute-start.4 = (bf16[512,128]{1,0:T(8,128)(2,1)}, bf16[512,128]{1,0:T(8,128)(2,1)S(1)}, u32[]{:S(2)}, u32[]{:S(2)}) collective-permute-start(bf16[512,128]{1,0:T(8,128)(2,1)} %get-tuple-element.93.refs_0_.refs_8_.refs_1_.refs_4_), channel_id=1, source_target_pairs={{0,2},{1,3},{2,0},{3,1},{4,6},{5,7},{6,4},{7,5},{8,10},{9,11},{10,... | collective-permute-start | bytes 393224 | tf_op jit(solution)/shard_map/ppermute | solution.py:737
  58.2 0.9 copy-done
  59.1 2.9 %hand_on.1 = (bf16[2,896,128]{2,1,0:T(8,128)(2,1)}, bf16[2,896,128]{2,1,0:T(8,128)(2,1)}, bf16[2,896,128]{2,1,0:T(8,128)(2,1)}, bf16[2,896,128]{2,1,0:T(8,128)(2,1)}) custom-call(bf16[512,128]{1,0:T(8,128)(2,1)S(1)} %copy-done, bf16[8,896,128]{2,1,0:T(8,128)(2,1)} %bitcast.8), custom_call_target="tpu_custom_call" | custom-call | bytes 3670016 | tf_op jit(solution)/shard_map/hand_on/pallas_call | solution.py:250
  62.0 1.4 collective-permute-done.4.refs_2_.refs_6_
  63.4 1.1 all-to-all-done.1
  65.1 1.3 collective-permute-start.8
  66.4 0.5 collective-permute-start.3
  66.9 1.0 collective-permute-done.3.refs_1_.refs_5_
  68.2 3.7 %conv_second.1 = (bf16[512,512]{1,0:T(8,128)(2,1)S(1)}, f32[512,128]{1,0:T(8,128)S(1)}, f32[8,8,128]{2,1,0:T(8,128)S(1)}, f32[4,8,128]{2,1,0:T(8,128)}, f32[512,...) custom-call(bf16[512,128]{1,0:T(8,128)(2,1)} %get-tuple-element.93.refs_0_.refs_8_.refs_, ...), custom_call_target="tpu_custom_call" | custom-call | flops 603979776 | bytes 4771840 | tf_op jit(solution)/shard_map/conv_second/pallas_call | solution.py:250
  71.9 10.7 %all_to_all.36.refs_2_ = f32[8,8,128]{2,1,0:T(8,128)S(1)} all-to-all(f32[8,8,128]{2,1,0:T(8,128)S(1)} %get-tuple-element.104), channel_id=1, replica_groups=mesh['dp'=8,'chan'=4] {'dp'}, dimensions={0} | all-to-all | bytes 65536 | tf_op jit(solution)/shard_map/all_to_all | solution.py:724
  82.6 1.5 block_output.1
  84.1 9.1 %all_to_all.37.refs_7_ = f32[8,8,128]{2,1,0:T(8,128)S(1)} all-to-all(f32[8,8,128]{2,1,0:T(8,128)S(1)} %get-tuple-element.116), channel_id=1, replica_groups=mesh['dp'=8,'chan'=4] {'dp'}, dimensions={0} | all-to-all | bytes 65536 | tf_op jit(solution)/shard_map/all_to_all | solution.py:724
  93.2 0.8 grad_outputs.1
  94.0 0.9 collective-permute-start.9
  94.9 3.9 %grad_second.1 = bf16[8,608,128]{2,1,0:T(8,128)(2,1)} custom-call(bf16[512,512]{1,0:T(8,128)(2,1)S(1)} %get-tuple-element.118.refs_0_, bf16[512,128]{1,0:T(8,128)(2,1)} %get-tuple-element.117.refs_1_.refs_4_, bf16[8,2,16,512]{3,2,1,0:T(8,128)(2,1)} %copy-done.3, bf16[8,2,16,512]{3,2,1,0:T(8,128)(2,1)} %copy-done.5, bf16[8,2,16,512]{3,2,1,0:T(8,128)(2,1)} %copy-done.4, ...), custom_call_target="tpu_custom_call" | custom-call | flops 603979776 | bytes 3080192 | tf_op jit(solution)/shard_map/grad_second/pallas_call | solution.py:250
  99.4 0.5 collective-permute-start.11
  99.9 0.8 collective-permute-done.10.refs_5_
  100.9 3.5 %grad_hidden.1 = (f32[512,128]{1,0:T(8,128)S(1)}, bf16[1040,128]{1,0:T(8,128)(2,1)}, f32[32,8,128]{2,1,0:T(8,128)S(1)}) custom-call(bf16[2,896,128]{2,1,0:T(8,128)(2,1)} %get-tuple-element.121.refs_0_.refs_11_, bf16[2,896,128]{2,1,0:T(8,128)(2,1)S(1)} %collective-permute-done.6.refs_0_.refs_1_.refs_12_, ...), custom_call_target="tpu_custom_call" | custom-call | flops 603979776 | bytes 3559424 | tf_op jit(solution)/shard_map/grad_hidden/pallas_call | solution.py:250
  104.5 0.9 collective-permute-start.12
  105.4 11.3 %all_to_all.38 = f32[32,8,128]{2,1,0:T(8,128)S(1)} all-to-all(f32[32,8,128]{2,1,0:T(8,128)S(1)} %get-tuple-element.126), channel_id=1, replica_groups=mesh['dp'=8,'chan'=4] {'dp','chan'}, dimensions={0} | all-to-all | bytes 262144 | tf_op jit(solution)/shard_map/all_to_all | solution.py:724
  116.6 2.8 %grad_first.1 = (bf16[8,288,128]{2,1,0:T(8,128)(2,1)}, f32[8,128]{1,0:T(8,128)}) custom-call(f32[512,128]{1,0:T(8,128)S(1)} %get-tuple-element.124.refs_0_, bf16[512,128]{1,0:T(8,128)(2,1)} %get-tuple-element.93.refs_0_.refs_8_.refs_1_.refs_4_, f32[8,4,8,128]{3,2,1,0:T(8,128)S(1)} %bitcast.4, f32[4,8,128]{2,1,0:T(8,128)} %get-tuple-element.123.refs_10_.refs_3_.refs_9_, ...), custom_call_target="tpu_custom_call" | custom-call | flops 301989888 | bytes 2448384 | tf_op jit(solution)/shard_map/grad_first/pallas_call | solution.py:250
  119.5 3.6 %all-to-all-start.5 = ((bf16[8,288,128]{2,1,0:T(8,128)(2,1)}), bf16[8,288,128]{2,1,0:T(8,128)(2,1)S(1)}, u32[]{:S(2)}, u32[]{:S(2)}) async-start(bf16[8,288,128]{2,1,0:T(8,128)(2,1)} %get-tuple-element.128), calls=%async_computation.6 | async-start | bytes 1179648 | tf_op jit(solution)/shard_map/all_to_all | solution.py:724
  123.1 0.8 collective-permute-start.13
  123.9 1.1 collective-permute-done.13.refs_1_
  125.4 3.9 %grad_images.1 = (bf16[2,64,128]{2,1,0:T(8,128)(2,1)}, bf16[2,64,128]{2,1,0:T(8,128)(2,1)}, bf16[2,64,128]{2,1,0:T(8,128)(2,1)}, bf16[2,64,128]{2,1,0:T(8,128)(2...) custom-call(bf16[1040,128]{1,0:T(8,128)(2,1)} %get-tuple-element.125, ...), custom_call_target="tpu_custom_call" | custom-call | flops 301989888 | bytes 4096000 | tf_op jit(solution)/shard_map/grad_images/pallas_call | solution.py:250
  129.2 1.6 collective-permute-start.15
  130.9 1.5 collective-permute-start.16
  132.8 2.5 %collective-permute-start.18 = (bf16[2,64,128]{2,1,0:T(8,128)(2,1)}, bf16[2,64,128]{2,1,0:T(8,128)(2,1)S(1)}, u32[]{:S(2)}, u32[]{:S(2)}) collective-permute-start(bf16[2,64,128]{2,1,0:T(8,128)(2,1)} %get-tuple-element.138), channel_id=1, source_target_pairs={{0,16},{4,20},{8,24},{12,28},{16,0},{20,4},{24,8},{28,12},{1,17},{... | collective-permute-start | bytes 98312 | tf_op jit(solution)/shard_map/ppermute | solution.py:737
  135.3 1.4 collective-permute-start.19
  136.8 3.3 %collective-permute-start.20 = (bf16[2,64,128]{2,1,0:T(8,128)(2,1)}, bf16[2,64,128]{2,1,0:T(8,128)(2,1)S(1)}, u32[]{:S(2)}, u32[]{:S(2)}) collective-permute-start(bf16[2,64,128]{2,1,0:T(8,128)(2,1)} %get-tuple-element.140), channel_id=1, source_target_pairs={{0,24},{4,28},{8,16},{12,20},{16,8},{20,12},{24,0},{28,4},{1,25},{... | collective-permute-start | bytes 98312 | tf_op jit(solution)/shard_map/ppermute | solution.py:737
  140.5 1.2 all-to-all-done.5.refs_1_
  141.7 2.1 %reduce_all.1 = (f32[288,128]{1,0:T(8,128)}, f32[576,128]{1,0:T(8,128)}, f32[32,128]{1,0:T(8,128)}, f32[32,8,128]{2,1,0:T(8,128)}) custom-call(bf16[608,128]{1,0:T(8,128)(2,1)} %reduce-scatter.2.cloned.1.call-done.refs_0_, bf16[8,288,128]{2,1,0:T(8,128)(2,1)S(1)} %all-to-all-done.5.refs_1_, f32[8,128]{1,0:T(8,128)} %get-tuple-element.129.refs_2_, ...), custom_call_target="tpu_custom_call" | custom-call | bytes 1350656 | tf_op jit(solution)/shard_map/reduce_all/pallas_call | solution.py:250
  143.8 1.2 collective-permute-done.19.refs_5_
  145.0 1.8 %collective-permute-done.21.refs_7_ = bf16[2,64,128]{2,1,0:T(8,128)(2,1)S(1)} collective-permute-done((bf16[2,64,128]{2,1,0:T(8,128)(2,1)}, bf16[2,64,128]{2,1,0:T(8,128)(2,1)S(1)}, u32[]{:S(2)}, u32[]{:S(2)}) %collective-permute-start.21) | collective-permute-done | bytes 32800 | tf_op jit(solution)/shard_map/ppermute | solution.py:737
  146.9 2.6 %all-to-all-start.6 = ((f32[32,8,128]{2,1,0:T(8,128)}), f32[32,8,128]{2,1,0:T(8,128)S(1)}, u32[]{:S(2)}, u32[]{:S(2)}) async-start(f32[32,8,128]{2,1,0:T(8,128)} %get-tuple-element.150), calls=%async_computation.7 | async-start | bytes 262144 | tf_op jit(solution)/shard_map/all_to_all | solution.py:724
  149.5 1.9 %finish_images.1 = bf16[64,32,64]{2,1,0:T(8,128)(2,1)} custom-call(bf16[2,64,128]{2,1,0:T(8,128)(2,1)} %get-tuple-element.142.refs_0_, bf16[2,64,128]{2,1,0:T(8,128)(2,1)S(1)} %collective-permute-done.15.refs_1_, bf16[2,64,128]{2,1,0:T(8,128)(2,1)S(1)} %collective-permute-done.16.refs_2_, bf16[2,64,128]{2,1,0:T(8,128)(2,1)S(1)} %collective-permute-done.17.refs_3_, ...), custom_call_target="tpu_custom_call" | custom-call | bytes 524288 | tf_op jit(solution)/shard_map/finish_images/pallas_call | solution.py:250
  151.3 6.4 %all-to-all-done.6.refs_0_ = f32[32,8,128]{2,1,0:T(8,128)S(1)} async-done(((f32[32,8,128]{2,1,0:T(8,128)}), f32[32,8,128]{2,1,0:T(8,128)S(1)}, u32[]{:S(2)}, u32[]{:S(2)}) %all-to-all-start.6) | async-done | bytes 131104 | tf_op jit(solution)/shard_map/all_to_all | solution.py:724
  157.7 2.9 %update.1 = (f32[288,128]{1,0:T(8,128)}, f32[288,128]{1,0:T(8,128)}, f32[288,128]{1,0:T(8,128)}, f32[576,128]{1,0:T(8,128)}, f32[576,128]{1,0:T(8,128)}, /*index...) custom-call(f32[32,8,128]{2,1,0:T(8,128)S(1)} %all-to-all-done.6.ref, ...), custom_call_target="tpu_custom_call" | custom-call | bytes 3368960 | tf_op jit(solution)/shard_map/update/pallas_call | solution.py:250
  (44 shorter events, 3.1 us)
Async XLA Ops:
  7.2 42.4 %all-gather.3.cloned.1.call-start = ((), (), s32[]{:S(2)}) async-start(), calls=%async_computation.9 | async-start | bytes 2064384 | tf_op jit(solution)/shard_map/all_gather | solution.py:791
  9.1 0.9 copy-start.2
  32.6 17.0 %copy-start.3 = (bf16[8,2,16,512]{3,2,1,0:T(8,128)(2,1)}, bf16[8,2,16,512]{3,2,1,0:T(8,128)(2,1)S(1)}, u32[]{:S(2)}) copy-start(bf16[8,2,16,512]{3,2,1,0:T(8,128)(2,1)S(1)} %all_to_all.35.refs_1_.refs_2_.refs_6_) | copy-start | bytes 786436
  32.6 6.4 %collective-permute-start.1 = (bf16[8,2,16,512]{3,2,1,0:T(8,128)(2,1)S(1)}, bf16[8,2,16,512]{3,2,1,0:T(8,128)(2,1)S(1)}, u32[]{:S(2)}, u32[]{:S(2)}) collective-permute-start(bf16[8,2,16,512]{3,2,1,0:T(8,128)(2,1)S(1)} %all_to_all.35.refs_1_.refs_2_.refs_6_), channel_id=1, source_target_pairs={{0,2},{1,3},{2,0},{3,1},{4,6},{5,7},{6,4},{7,5},{8,10},{9,11},{10,... | collective-permute-start | bytes 786440 | tf_op jit(solution)/shard_map/ppermute | solution.py:737
  34.0 4.9 %collective-permute-start = (bf16[8,2,16,512]{3,2,1,0:T(8,128)(2,1)S(1)}, bf16[8,2,16,512]{3,2,1,0:T(8,128)(2,1)S(1)}, u32[]{:S(2)}, u32[]{:S(2)}) collective-permute-start(bf16[8,2,16,512]{3,2,1,0:T(8,128)(2,1)S(1)} %all_to_all.35.refs_1_.refs_2_.refs_6_), channel_id=1, source_target_pairs={{0,1},{1,0},{2,3},{3,2},{4,5},{5,4},{6,7},{7,6},{8,9},{9,8},{10,11... | collective-permute-start | bytes 786440 | tf_op jit(solution)/shard_map/ppermute | solution.py:737
  38.9 10.6 %copy-start.4 = (bf16[8,2,16,512]{3,2,1,0:T(8,128)(2,1)}, bf16[8,2,16,512]{3,2,1,0:T(8,128)(2,1)S(1)}, u32[]{:S(2)}) copy-start(bf16[8,2,16,512]{3,2,1,0:T(8,128)(2,1)S(1)} %collective-permute-done.1.refs_3_.refs_4_.refs_8_) | copy-start | bytes 786436
  38.9 1.5 collective-permute-start.2
  38.9 10.6 %copy-start.5 = (bf16[8,2,16,512]{3,2,1,0:T(8,128)(2,1)}, bf16[8,2,16,512]{3,2,1,0:T(8,128)(2,1)S(1)}, u32[]{:S(2)}) copy-start(bf16[8,2,16,512]{3,2,1,0:T(8,128)(2,1)S(1)} %collective-permute-done.refs_2_.refs_3_.refs_7_) | copy-start | bytes 786436
  40.5 9.1 %copy-start.6 = (bf16[8,2,16,512]{3,2,1,0:T(8,128)(2,1)}, bf16[8,2,16,512]{3,2,1,0:T(8,128)(2,1)S(1)}, u32[]{:S(2)}) copy-start(bf16[8,2,16,512]{3,2,1,0:T(8,128)(2,1)S(1)} %collective-permute-done.2.refs_4_.refs_5_.refs_9_) | copy-start | bytes 786436
  52.7 13.7 %copy-start.1 = (bf16[512,128]{1,0:T(8,128)(2,1)S(1)}, bf16[512,128]{1,0:T(8,128)(2,1)}, u32[]{:S(2)}) copy-start(bf16[512,128]{1,0:T(8,128)(2,1)} %get-tuple-element.93.refs_0_.refs_8_.refs_1_.refs_4_) | copy-start | bytes 393220
  52.7 11.8 %all-to-all-start.1 = ((f32[32,8,128]{2,1,0:T(8,128)}), f32[32,8,128]{2,1,0:T(8,128)S(1)}, u32[]{:S(2)}, u32[]{:S(2)}) async-start(f32[32,8,128]{2,1,0:T(8,128)} %get-tuple-element.94), calls=%async_computation.1 | async-start | bytes 262144 | tf_op jit(solution)/shard_map/all_to_all | solution.py:724
  56.3 85.4 %reduce-scatter.2.cloned.1.call-start = ((), (), s32[]{:S(2)}) async-start(), calls=%async_computation.8 | async-start | bytes 1400832 | tf_op jit(solution)/shard_map/reduce_scatter | solution.py:891
  56.3 7.1 %collective-permute-start.4 = (bf16[512,128]{1,0:T(8,128)(2,1)}, bf16[512,128]{1,0:T(8,128)(2,1)S(1)}, u32[]{:S(2)}, u32[]{:S(2)}) collective-permute-start(bf16[512,128]{1,0:T(8,128)(2,1)} %get-tuple-element.93.refs_0_.refs_8_.refs_1_.refs_4_), channel_id=1, source_target_pairs={{0,2},{1,3},{2,0},{3,1},{4,6},{5,7},{6,4},{7,5},{8,10},{9,11},{10,... | collective-permute-start | bytes 393224 | tf_op jit(solution)/shard_map/ppermute | solution.py:737
  58.2 0.9 copy-start
  64.5 28.7 %collective-permute-start.6 = (bf16[2,896,128]{2,1,0:T(8,128)(2,1)}, bf16[2,896,128]{2,1,0:T(8,128)(2,1)S(1)}, u32[]{:S(2)}, u32[]{:S(2)}) collective-permute-start(bf16[2,896,128]{2,1,0:T(8,128)(2,1)} %get-tuple-element.109), channel_id=1, source_target_pairs={{0,1},{1,0},{2,3},{3,2},{4,5},{5,4},{6,7},{7,6},{8,9},{9,8},{10,11... | collective-permute-start | bytes 1376264 | tf_op jit(solution)/shard_map/ppermute | solution.py:737
  64.7 28.4 %collective-permute-start.7 = (bf16[2,896,128]{2,1,0:T(8,128)(2,1)}, bf16[2,896,128]{2,1,0:T(8,128)(2,1)S(1)}, u32[]{:S(2)}, u32[]{:S(2)}) collective-permute-start(bf16[2,896,128]{2,1,0:T(8,128)(2,1)} %get-tuple-element.110), channel_id=1, source_target_pairs={{0,2},{1,3},{2,0},{3,1},{4,6},{5,7},{6,4},{7,5},{8,10},{9,11},{10,... | collective-permute-start | bytes 1376264 | tf_op jit(solution)/shard_map/ppermute | solution.py:737
  65.1 28.1 %collective-permute-start.8 = (bf16[2,896,128]{2,1,0:T(8,128)(2,1)}, bf16[2,896,128]{2,1,0:T(8,128)(2,1)S(1)}, u32[]{:S(2)}, u32[]{:S(2)}) collective-permute-start(bf16[2,896,128]{2,1,0:T(8,128)(2,1)} %get-tuple-element.111), channel_id=1, source_target_pairs={{0,3},{1,2},{2,1},{3,0},{4,7},{5,6},{6,5},{7,4},{8,11},{9,10},{10,... | collective-permute-start | bytes 1376264 | tf_op jit(solution)/shard_map/ppermute | solution.py:737
  66.4 1.5 collective-permute-start.3
  66.9 1.3 collective-permute-start.5
  94.0 5.2 %collective-permute-start.9 = (bf16[512,128]{1,0:T(8,128)(2,1)}, bf16[512,128]{1,0:T(8,128)(2,1)S(1)}, u32[]{:S(2)}, u32[]{:S(2)}) collective-permute-start(bf16[512,128]{1,0:T(8,128)(2,1)} %get-tuple-element.117.refs_1_.refs_4_), channel_id=1, source_target_pairs={{0,2},{1,3},{2,0},{3,1},{4,6},{5,7},{6,4},{7,5},{8,10},{9,11},{10,... | collective-permute-start | bytes 393224 | tf_op jit(solution)/shard_map/ppermute | solution.py:737
  94.9 4.4 %copy-start.7 = (bf16[512,128]{1,0:T(8,128)(2,1)S(1)}, bf16[512,128]{1,0:T(8,128)(2,1)}, u32[]{:S(2)}) copy-start(bf16[512,128]{1,0:T(8,128)(2,1)} %get-tuple-element.117.refs_1_.refs_4_) | copy-start | bytes 393220
  99.3 1.4 collective-permute-start.10
  99.4 1.5 collective-permute-start.11
  104.5 18.6 %copy-start.8 = (bf16[1040,128]{1,0:T(8,128)(2,1)S(1)}, bf16[1040,128]{1,0:T(8,128)(2,1)}, u32[]{:S(2)}) copy-start(bf16[1040,128]{1,0:T(8,128)(2,1)} %get-tuple-element.125.refs_0_) | copy-start | bytes 798724
  104.5 12.2 %collective-permute-start.12 = (bf16[1040,128]{1,0:T(8,128)(2,1)}, bf16[1040,128]{1,0:T(8,128)(2,1)S(1)}, u32[]{:S(2)}, u32[]{:S(2)}) collective-permute-start(bf16[1040,128]{1,0:T(8,128)(2,1)} %get-tuple-element.125.refs_0_), channel_id=1, source_target_pairs={{0,2},{1,3},{2,0},{3,1},{4,6},{5,7},{6,4},{7,5},{8,10},{9,11},{10,... | collective-permute-start | bytes 798728 | tf_op jit(solution)/shard_map/ppermute | solution.py:737
  119.5 22.2 %all-to-all-start.5 = ((bf16[8,288,128]{2,1,0:T(8,128)(2,1)}), bf16[8,288,128]{2,1,0:T(8,128)(2,1)S(1)}, u32[]{:S(2)}, u32[]{:S(2)}) async-start(bf16[8,288,128]{2,1,0:T(8,128)(2,1)} %get-tuple-element.128), calls=%async_computation.6 | async-start | bytes 1179648 | tf_op jit(solution)/shard_map/all_to_all | solution.py:724
  123.1 1.9 %collective-permute-start.13 = (bf16[1040,128]{1,0:T(8,128)(2,1)S(1)}, bf16[1040,128]{1,0:T(8,128)(2,1)S(1)}, u32[]{:S(2)}, u32[]{:S(2)}) collective-permute-start(bf16[1040,128]{1,0:T(8,128)(2,1)S(1)} %copy-done.8), channel_id=1, source_target_pairs={{0,1},{1,0},{2,3},{3,2},{4,5},{5,4},{6,7},{7,6},{8,9},{9,8},{10,11... | collective-permute-start | bytes 798728 | tf_op jit(solution)/shard_map/ppermute | solution.py:737
  123.8 1.5 collective-permute-start.14
  129.2 7.5 %collective-permute-start.15 = (bf16[2,64,128]{2,1,0:T(8,128)(2,1)}, bf16[2,64,128]{2,1,0:T(8,128)(2,1)S(1)}, u32[]{:S(2)}, u32[]{:S(2)}) collective-permute-start(bf16[2,64,128]{2,1,0:T(8,128)(2,1)} %get-tuple-element.135), channel_id=1, source_target_pairs={{0,4},{4,0},{8,12},{12,8},{16,20},{20,16},{24,28},{28,24},{1,5},{5... | collective-permute-start | bytes 98312 | tf_op jit(solution)/shard_map/ppermute | solution.py:737
  130.9 9.2 %collective-permute-start.16 = (bf16[2,64,128]{2,1,0:T(8,128)(2,1)}, bf16[2,64,128]{2,1,0:T(8,128)(2,1)S(1)}, u32[]{:S(2)}, u32[]{:S(2)}) collective-permute-start(bf16[2,64,128]{2,1,0:T(8,128)(2,1)} %get-tuple-element.136), channel_id=1, source_target_pairs={{0,8},{4,12},{8,0},{12,4},{16,24},{20,28},{24,16},{28,20},{1,9},{5... | collective-permute-start | bytes 98312 | tf_op jit(solution)/shard_map/ppermute | solution.py:737
  132.4 11.4 %collective-permute-start.17 = (bf16[2,64,128]{2,1,0:T(8,128)(2,1)}, bf16[2,64,128]{2,1,0:T(8,128)(2,1)S(1)}, u32[]{:S(2)}, u32[]{:S(2)}) collective-permute-start(bf16[2,64,128]{2,1,0:T(8,128)(2,1)} %get-tuple-element.137), channel_id=1, source_target_pairs={{0,12},{4,8},{8,4},{12,0},{16,28},{20,24},{24,20},{28,16},{1,13},{... | collective-permute-start | bytes 98312 | tf_op jit(solution)/shard_map/ppermute | solution.py:737
  132.8 11.0 %collective-permute-start.18 = (bf16[2,64,128]{2,1,0:T(8,128)(2,1)}, bf16[2,64,128]{2,1,0:T(8,128)(2,1)S(1)}, u32[]{:S(2)}, u32[]{:S(2)}) collective-permute-start(bf16[2,64,128]{2,1,0:T(8,128)(2,1)} %get-tuple-element.138), channel_id=1, source_target_pairs={{0,16},{4,20},{8,24},{12,28},{16,0},{20,4},{24,8},{28,12},{1,17},{... | collective-permute-start | bytes 98312 | tf_op jit(solution)/shard_map/ppermute | solution.py:737
  135.3 9.7 %collective-permute-start.19 = (bf16[2,64,128]{2,1,0:T(8,128)(2,1)}, bf16[2,64,128]{2,1,0:T(8,128)(2,1)S(1)}, u32[]{:S(2)}, u32[]{:S(2)}) collective-permute-start(bf16[2,64,128]{2,1,0:T(8,128)(2,1)} %get-tuple-element.139), channel_id=1, source_target_pairs={{0,20},{4,16},{8,28},{12,24},{16,4},{20,0},{24,12},{28,8},{1,21},{... | collective-permute-start | bytes 98312 | tf_op jit(solution)/shard_map/ppermute | solution.py:737
  136.8 8.3 %collective-permute-start.20 = (bf16[2,64,128]{2,1,0:T(8,128)(2,1)}, bf16[2,64,128]{2,1,0:T(8,128)(2,1)S(1)}, u32[]{:S(2)}, u32[]{:S(2)}) collective-permute-start(bf16[2,64,128]{2,1,0:T(8,128)(2,1)} %get-tuple-element.140), channel_id=1, source_target_pairs={{0,24},{4,28},{8,16},{12,20},{16,8},{20,12},{24,0},{28,4},{1,25},{... | collective-permute-start | bytes 98312 | tf_op jit(solution)/shard_map/ppermute | solution.py:737
  140.1 6.8 %collective-permute-start.21 = (bf16[2,64,128]{2,1,0:T(8,128)(2,1)}, bf16[2,64,128]{2,1,0:T(8,128)(2,1)S(1)}, u32[]{:S(2)}, u32[]{:S(2)}) collective-permute-start(bf16[2,64,128]{2,1,0:T(8,128)(2,1)} %get-tuple-element.141), channel_id=1, source_target_pairs={{0,28},{4,24},{8,20},{12,16},{16,12},{20,8},{24,4},{28,0},{1,29},{... | collective-permute-start | bytes 98312 | tf_op jit(solution)/shard_map/ppermute | solution.py:737
  146.9 10.8 %all-to-all-start.6 = ((f32[32,8,128]{2,1,0:T(8,128)}), f32[32,8,128]{2,1,0:T(8,128)S(1)}, u32[]{:S(2)}, u32[]{:S(2)}) async-start(f32[32,8,128]{2,1,0:T(8,128)} %get-tuple-element.150), calls=%async_computation.7 | async-start | bytes 262144 | tf_op jit(solution)/shard_map/all_to_all | solution.py:724
Sparse Core Ops, SparseCore 0:
  10.1 39.3 all-gather.2
  99.4 29.0 reduce-scatter.1

commit v4 on v3

--- a/solution.py
+++ b/solution.py
@@ -315,13 +315,13 @@
 
 
 def rows_of(*rows):
-    pad = SIDE - len(rows)
+    pad = SIDE - sum(row.shape[0] for row in rows)
     tail = [jnp.zeros((pad, rows[0].shape[1]), F32)] if pad else []
     return jnp.concatenate(list(rows) + tail, axis=0)
 
 
 def spread_rows(out, rows):
-    out[...] = jnp.broadcast_to(rows[None], out.shape)
+    out[...] = jnp.broadcast_to(rows[None, : out.shape[1]], out.shape)
 
 
 def mean_inverse(total, squares, count):
@@ -428,7 +428,7 @@
     return jnp.concatenate(pieces, axis=0)
 
 
-def conv_first(w, x, m, n, zb_out, zp_out, pay):
+def conv_first(w, x, m, n, zb_out, zp_out, sums_out, pay):
     taps = taps_of(w, w.shape[1] // 10)
     wide = w.shape[2]
     y00 = dot(phase_of(x, 0, 0), taps(4, 9))
@@ -440,14 +440,16 @@
     above = y10[:, wide:] + y11[:, 2 * wide : 3 * wide]
     corner = y11[:, 3 * wide :]
     z = here + shift_row(above, 1) + shift_col(left + shift_row(corner, 1), 1)
-    zb_out[...] = z.astype(BF)
+    pix = z.shape[0]
+    zb_out[:pix] = z.astype(BF)
+    zb_out[pix:] = three_rows(n[0:2])
     zb_out.send()
     zp = y00[:, wide:]
     valid = m[...]
     vz, vzp = valid * z, valid * zp
-    sums = [col_sum(vz), col_sum(vz * z), col_sum(valid), n[0:1], n[1:2]]
-    spread_rows(pay, rows_of(*sums, col_sum(vzp), col_sum(vzp * zp)))
+    spread_rows(pay, rows_of(col_sum(vz), col_sum(vz * z), col_sum(valid)))
     pay.send()
+    sums_out[...] = rows_of(col_sum(vzp), col_sum(vzp * zp))
     zp_out[...] = zp
 
 
@@ -462,15 +464,15 @@
     return hat, hat * rows[3:4] + rows[4:5], inverse
 
 
-def conv_second(z, got, m, w, zp, cot, h_out, z2_out, pay, tot_out, m_out, zp_out, cot_out, own_out):
+def conv_second(z, got, m, w, zp, sums, cot, h_out, z2_out, pay, tot_out, m_out, zp_out, cot_out, own_out):
     blocks, wide = z.shape[0], z.shape[2]
     valid = m[...]
+    pix = valid.shape[0]
     hidden = []
     for k in range(blocks):
-        total = jnp.sum(got[:, k], axis=0)
-        rows = jnp.concatenate([total[0:3], got[0, k, 3:5], total[5:8]], axis=0)
+        rows = rows_of(jnp.sum(got[:, k], axis=0)[0:3], one_row(z[k, pix:], 2))
         tot_out[k] = rows
-        _, lin, _ = first_norm(z[k].astype(F32), rows)
+        _, lin, _ = first_norm(z[k, :pix].astype(F32), rows)
         hidden.append((lin * jax.nn.sigmoid(lin) * valid).astype(BF))
         h_out[:, k * wide : (k + 1) * wide] = hidden[-1]
     h_out.send()
@@ -484,7 +486,7 @@
         )
     z2 = moved[1] + shift_col(moved[0], 1) + shift_col(moved[2], -1)
     vz = valid * z2
-    spread_rows(pay, rows_of(col_sum(vz), col_sum(vz * z2)))
+    spread_rows(pay, rows_of(col_sum(vz), col_sum(vz * z2), sums[0:2]))
     pay.send()
     z2_out[...] = z2
     batch, pix, wide = cot.shape
@@ -497,7 +499,7 @@
 def block_output(z2, zp, got, tot1, m, n, cot, out, e_out, hat2_out, hat_p_out, rows_out, pay):
     total, count = jnp.sum(got[...], axis=0), tot1[2:3]
     center2, inverse2 = mean_inverse(total[0:1], total[1:2], count)
-    center_p, inverse_p = mean_inverse(tot1[5:6], tot1[6:7], count)
+    center_p, inverse_p = mean_inverse(total[2:3], total[3:4], count)
     hat2, hat_p = (z2[...] - center2) * inverse2, (zp[...] - center_p) * inverse_p
     hat2_out[...] = hat2
     hat_p_out[...] = hat_p
@@ -515,7 +517,7 @@
 
 def grad_outputs(e, hat2, hat_p, rows, got, m, g2_out, gp_out, tot_out):
     back, count = jnp.sum(got[...], axis=0), rows[2:3]
-    tot_out[...] = back
+    tot_out[...] = rows_of(back)
     valid, e = m[...], e[...]
     loss = valid * ((back[0:1] + hat2[...] * back[1:2]) / count)
     g2_out[...] = (rows[0:1] * (e - loss)).astype(BF)
@@ -529,18 +531,20 @@
     count, part = w.shape[1], w.shape[2] // 9
     depth = count * part
     moved = []
+    grads = jnp.concatenate([g2[k] for k in range(blocks)], axis=1)
     for col in range(3):
-        y = 0.0
-        for k in range(blocks):
-            starts = [(3 * row + col) * part for row in range(3)]
-            taps = [w[k, :, a : a + part].reshape(depth, wide) for a in starts]
-            y = y + dot_nt(g2[k], jnp.concatenate(taps, axis=0))
+        starts = [(3 * row + col) * part for row in range(3)]
+        taps = [
+            jnp.concatenate([w[k, :, a : a + part].reshape(depth, wide) for k in range(blocks)], axis=1)
+            for a in starts
+        ]
+        y = dot_nt(grads, jnp.concatenate(taps, axis=0))
         moved.append(
             shift_row(y[:, :depth], -1) + y[:, depth : 2 * depth] + shift_row(y[:, 2 * depth :], 1)
         )
     gh = moved[1] + shift_col(moved[0], -1) + shift_col(moved[2], 1)
-    hat, lin, _ = first_norm(z[...].astype(F32), tot1[...])
     valid = m[...]
+    hat, lin, _ = first_norm(z[: valid.shape[0]].astype(F32), tot1[...])
     b = gh * (slope(lin) * valid)
     shift, scaled = col_sum(b), col_sum(b * hat)
     spread_rows(pay, rows_of(shift, scaled))
@@ -572,10 +576,14 @@
             for k, place in enumerate(places):
                 g_out[place, rows] = g[k]
 
+        spread_out = []
         for tap in range(9):
             step = tap // 3 - 1
-            g = shift_row(moved[tap % 3], step) if step else moved[tap % 3]
-            put(slice(tap * share, (tap + 1) * share), dot_tn(h, g))
+            spread_out.append(shift_row(moved[tap % 3], step) if step else moved[tap % 3])
+        spread_out = dot_tn(h, jnp.concatenate(spread_out, axis=1))
+        for tap in range(9):
+            g = spread_out[:, tap * wide : (tap + 1) * wide]
+            put(slice(tap * share, (tap + 1) * share), g)
         pieces = [x[k, r] for r in range(SIDE) for k in range(x.shape[0])]
         put(slice(9 * share, rows), dot_tn(jnp.concatenate(pieces, axis=0), gp[...]))
 
@@ -585,8 +593,8 @@
 def grad_first(b, z, got, tot1, n, m, x, blocks_out, tot_out):
     own = got[:, pl.ds(lax.axis_index("chan"), 1)]
     back, count = jnp.sum(own, axis=0)[0], tot1[2:3]
-    tot_out[...] = back
-    hat, _, inverse = first_norm(z[...].astype(F32), tot1[...])
+    tot_out[...] = rows_of(back)
+    hat, _, inverse = first_norm(z[: m.shape[0]].astype(F32), tot1[...])
     g = n[0:1] * inverse * (b[...] - m[...] * ((back[0:1] + hat * back[1:2]) / count))
     here, left = g.astype(BF), shift_col(g, -1).astype(BF)
     wide = here.shape[1]
@@ -615,23 +623,26 @@
     depth = w.shape[2] // 10
     half, wide = count * depth, w.shape[3]
 
-    def taps(k, *which):
-        return jnp.concatenate(
-            [w[k, :, t * depth : (t + 1) * depth].reshape(half, wide) for t in which], axis=0
-        )
-
-    plain, moved, proj = 0.0, 0.0, 0.0
+    def taps(*which):
+        blocks_of = [
+            [w[k, :, t * depth : (t + 1) * depth].reshape(half, wide) for k in range(blocks)]
+            for t in which
+        ]
+        return jnp.concatenate([jnp.concatenate(row, axis=1) for row in blocks_of], axis=0)
+
+    grads = []
     valid = m[...]
     pix = valid.shape[0]
     for k in range(blocks):
         rows, back = tot1[k], jnp.sum(got[:, k], axis=0)
-        hat, _, inverse = first_norm(z[k].astype(F32), rows)
+        hat, _, inverse = first_norm(z[k, :pix].astype(F32), rows)
         fit = back[0:2] / rows[2:3] - one_row(msg[k, 2 * pix :], 2)
         loss = valid * (fit[0:1] + hat * fit[1:2])
-        g = (rows[3:4] * inverse * (msg[k, :pix].astype(F32) - loss)).astype(BF)
-        plain = plain + dot_nt(g, taps(k, 4, 5, 7, 8, 1, 2))
-        moved = moved + dot_nt(g, taps(k, 3, 3, 6, 6, 0, 0))
-        proj = proj + dot_nt(msg[k, pix : 2 * pix], taps(k, 9, 9))
+        grads.append((rows[3:4] * inverse * (msg[k, :pix].astype(F32) - loss)).astype(BF))
+    grads = jnp.concatenate(grads, axis=1)
+    plain, moved = dot_nt(grads, taps(4, 5, 7, 8, 1, 2)), dot_nt(grads, taps(3, 3, 6, 6, 0, 0))
+    proj = jnp.concatenate([msg[k, pix : 2 * pix] for k in range(blocks)], axis=1)
+    proj = dot_nt(proj, taps(9, 9))
     lane = lax.broadcasted_iota(jnp.int32, moved.shape, 1) % (2 * half)
     total = plain + jnp.where(lane >= half, shift_col(moved, -1), 0.0)
     lane = lax.broadcasted_iota(jnp.int32, proj.shape, 1)
@@ -674,11 +685,12 @@
         jnp.sum(jnp.concatenate([nw * nw, blank], axis=0), axis=1, keepdims=True),
         jnp.sum(jnp.concatenate([gn * gn, blank], axis=0), axis=1, keepdims=True),
     ]
-    lane = lax.broadcasted_iota(jnp.int32, pay.shape[1:], 1)
-    block = jnp.zeros(pay.shape[1:], F32)
+    dims = (SIDE, pay.shape[2])
+    lane, row = (lax.broadcasted_iota(jnp.int32, dims, axis) for axis in (1, 0))
+    block = jnp.zeros(dims, F32)
     for place, col in enumerate(cols):
-        block = jnp.where(lane == place, col, block)
-    spread_rows(pay, block)
+        block = jnp.where(lane == SIDE * place + row, col, block)
+    spread_rows(pay, col_sum(block))
     pay.send()
     gp_out[...] = proj
     put_rows(g2_out, conv)
@@ -703,16 +715,21 @@
     def update(*refs):
         r6, t3, t4 = refs[:3]
         ins, outs = refs[3:18], refs[18:]
-        total = jnp.sum(r6[...], axis=0)
+        total = jnp.broadcast_to(jnp.sum(r6[...], axis=0), (SIDE, r6.shape[2]))
+        lane, row = (lax.broadcasted_iota(jnp.int32, total.shape, axis) for axis in (1, 0))
+        total = [
+            jnp.sum(jnp.where(lane == SIDE * k + row, total, 0.0), axis=1, keepdims=True)
+            for k in range(3)
+        ]
         for place in range(3):
             w, g, m, a = (ref[...] for ref in ins[4 * place : 4 * place + 4])
-            weight_sq = total[2 * place : 2 * place + 1, 0:1]
-            grad_sq = total[2 * place + 1 : 2 * place + 2, 0:1]
+            weight_sq = total[0][2 * place : 2 * place + 1]
+            grad_sq = total[0][2 * place + 1 : 2 * place + 2]
             for ref, value in zip(outs[3 * place :], step_of(w, g, m, a, weight_sq, grad_sq)):
                 ref[...] = value
                 ref.send()
         w, m, a = (ref[...] for ref in ins[12:15])
-        weight_sq, grad_sq = total[0:6, 1:2] / dp_count, total[0:6, 2:3] / dp_count
+        weight_sq, grad_sq = total[1][0:6] / dp_count, total[2][0:6] / dp_count
         g = norm_grad(t3, t4)
         for ref, value in zip(outs[9:], step_of(w, g, m, a, weight_sq, grad_sq)):
             ref[...] = value
@@ -769,7 +786,7 @@
     groups = SIDE
     first_rows, second_rows = 10 * d_in // groups, 9 * d_out // groups
     square_rows = result((SIDE, wide))
-    sums = result((dp_count, SIDE, wide), pinned=False)
+    four = result((dp_count, 4, wide), pinned=False)
     passing, few = (result((n, wide), pinned=False) for n in (pix, SIDE))
 
     def slot_dp(k):
@@ -821,10 +838,15 @@
     macs = pix * 9 * wide * d_in
     per_block = groups // ch_count
     block_slots = [lambda k=k: (lax.axis_index("chan") ^ k) * per_block for k in range(ch_count)]
-    z_own, z_proj, pay = call(
+    z_own, z_proj, sums_proj, pay = call(
         conv_first,
         [spread(gathered, order, 0, first_rows), stack(pixels, slot), valid, norm_params],
-        [result((pix, wide), BF), result((pix, wide)), result((n_all, SIDE, wide))],
+        [
+            result((pix + TAIL, wide), BF),
+            result((pix, wide)),
+            square_rows,
+            result((n_all, 4, wide)),
+        ],
         flops=2 * macs,
     )
     turned = call(
@@ -833,7 +855,7 @@
         [parts_of(0, block_slots, per_block, 0, first_rows + second_rows, gathered)],
         later=[z_own],
     )
-    got1 = exchange(pay, everyone).reshape(dp_count, ch_count, SIDE, wide)
+    got1 = exchange(pay, everyone).reshape(dp_count, ch_count, 4, wide)
     far = swap(z_own, "chan", 2)
     far, got1, *turned = lax.optimization_barrier((far, got1, *turned))
     z_all = [z_own, swap(z_own, "chan", 1), far, swap(far, "chan", 1)]
@@ -846,12 +868,13 @@
             valid,
             spread(gathered, order, first_rows, second_rows),
             z_proj,
+            sums_proj,
             cotangent,
         ],
         [
             result((pix, d_out), BF, pinned=False),
             passing,
-            sums,
+            four,
             result((ch_count, SIDE, wide)),
             passing,
             passing,
@@ -867,7 +890,7 @@
     output, e, hat_second, hat_proj, near_rows, pay = call(
         block_output,
         [fresh(z_second), near_proj, fresh(got2), near_total, near_valid, norm_params, near_cot],
-        [result((batch, SIDE * SIDE, wide), BF), passing, passing, passing, few, sums],
+        [result((batch, SIDE * SIDE, wide), BF), passing, passing, passing, few, four],
     )
     got3 = exchange(pay, "dp")
 
@@ -907,10 +930,10 @@
         grad_hidden,
         [stack_rows(turned, slot_ch, first_rows, second_rows, 3), stack(g_all, slot_ch, 3)]
         + [z_own, g_proj_out, total1_own, valid],
-        [passing, result((2 * pix + TAIL, wide), BF), result((n_all, SIDE, wide), pinned=False)],
+        [passing, result((2 * pix + TAIL, wide), BF), result((n_all, 2, wide), pinned=False)],
         flops=4 * macs,
     )
-    got4 = exchange(pay, everyone).reshape(dp_count, ch_count, SIDE, wide)
+    got4 = exchange(pay, everyone).reshape(dp_count, ch_count, 2, wide)
     far = swap(msg, "chan", 2)
     far, got4 = lax.optimization_barrier((far, got4))
     messages = [msg, swap(msg, "chan", 1), far, swap(far, "chan", 1)]
@@ -956,7 +979,7 @@
             result(w_first.shape),
             result(w_second.shape),
             result(w_proj.shape),
-            result((n_all, SIDE, wide)),
+            result((n_all, 1, wide)),
         ],
     )
     pay, *rows = lax.optimization_barrier((pay, *rows))

time: 168 us -> 163 us (0.970)
  blocking collectives: 51.5 us -> 47.4 us
    all_to_all x4, blocking collectives: 51.5 us -> 47.4 us  [exchange(): return lax.all_to_all(blocks, axes, 0, 0)]
    all_to_all x3, waiting for transfers between devices: 8.69 us -> 11.3 us  [exchange(): return lax.all_to_all(blocks, axes, 0, 0)]
    ppermute x22, waiting for transfers between devices: 15.1 us -> 12.6 us  [swap(): lax.ppermute(array, axis, [(i, i ^ bits) for i in range(lax.axis_size(axi...]
  transfers between devices with their start and end apart: 27 -> 27, of which waited for: 16 -> 15; matrix products, arithmetic and copies ran while one was open for 0% -> 0% of each run, Pallas kernels for 17% -> 17%
where the time goes in v4:
time: 163 us; the launch traced here: 162 us
  blocking collectives  47.4 us (29%)
  Pallas kernels  36.2 us (22%)
  waiting for transfers between devices  33.1 us (20%)
  starting transfers between devices  29.3 us (18%)
  between operations  14.3 us (9%)
  local copies, waits for them, and re-layouts  1.86 us (1%)
    all_to_all x4, blocking collectives, exchange(): return lax.all_to_all(blocks, axes, 0, 0)  47.4 us
    pallas_call x14, Pallas kernels, call(): pl.pallas_call(kernel, out_shape=[pltpu.HBM(o.shape, o.dtype) if g.pinned...  36.2 us
    ppermute x22, starting transfers between devices, swap(): lax.ppermute(array, axis, [(i, i ^ bits) for i in range(lax.axis_size(axi...  20.5 us
    ppermute x22, waiting for transfers between devices, swap(): lax.ppermute(array, axis, [(i, i ^ bits) for i in range(lax.axis_size(axi...  12.6 us
    all_to_all x3, waiting for transfers between devices, exchange(): return lax.all_to_all(blocks, axes, 0, 0)  11.3 us
    all_gather x1, waiting for transfers between devices, per_device(): gathered = lax.all_gather(own, everyone, axis_index_groups=rings())  9.06 us
    all_to_all x3, starting transfers between devices, exchange(): return lax.all_to_all(blocks, axes, 0, 0)  8.76 us
  transfers between devices with their start and end apart: 27, of which 15 were waited for; matrix products, arithmetic and copies ran while one was open for 0% of the time, Pallas kernels for 17%

profile of v4, /device:TPU:0, one launch (start us, length us, event | category | flops | bytes accessed | tf_op | source)
XLA Modules:
  0.0 162.1 jit_solution(15471663046592433982)
XLA Ops:
  7.2 1.8 %pack_weights.1 = (bf16[896,128]{1,0:T(8,128)(2,1)}, f32[8,128]{1,0:T(8,128)}) custom-call(f32[288,128]{1,0:T(8,128)} %refs_3_.1, f32[32,128]{1,0:T(8,128)} %refs_11_.1, f32[576,128]{1,0:T(8,128)} %refs_7_.1), custom_call_target="tpu_custom_call" | custom-call | bytes 692224 | tf_op jit(solution)/shard_map/pack_weights/pallas_call | solution.py:250
  9.1 0.9 copy-done.2
  10.0 2.0 %pack_images.1 = (bf16[8,2,16,512]{3,2,1,0:T(8,128)(2,1)}, f32[512,128]{1,0:T(8,128)}) custom-call(bf16[896,128]{1,0:T(8,128)(2,1)S(1)} %copy-done.2, bf16[64,32,256]{2,1,0:T(8,128)(2,1)} %refs_1_.3, s32[8,64]{1,0:T(8,128)} %refs_2_.3), custom_call_target="tpu_custom_call" | custom-call | bytes 1574912 | tf_op jit(solution)/shard_map/pack_images/pallas_call | solution.py:250
  12.1 20.5 %all_to_all.35.refs_1_.refs_2_.refs_6_ = bf16[8,2,16,512]{3,2,1,0:T(8,128)(2,1)S(1)} all-to-all(bf16[8,2,16,512]{3,2,1,0:T(8,128)(2,1)} %get-tuple-element.92), channel_id=1, replica_groups=mesh['dp'=8,'chan'=4] {'dp'}, dimensions={0} | all-to-all | bytes 524288 | tf_op jit(solution)/shard_map/all_to_all | solution.py:741
  32.6 1.5 collective-permute-start.1
  34.0 4.9 %collective-permute-done.1.refs_3_.refs_4_.refs_8_ = bf16[8,2,16,512]{3,2,1,0:T(8,128)(2,1)S(1)} collective-permute-done((bf16[8,2,16,512]{3,2,1,0:T(8,128)(2,1)S(1)}, bf16[8,2,16,512]{3,2,1,0:T(8,128)(2,1)S(1)}, u32[]{:S(2)}, u32[]{:S(2)}) %collective-permute-start.1) | collective-permute-done | bytes 262176 | tf_op jit(solution)/shard_map/ppermute | solution.py:754
  39.0 1.5 collective-permute-done.2.refs_4_.refs_5_.refs_9_
  40.5 9.1 %all-gather.3.cloned.1.call-done = bf16[7168,128]{1,0:T(8,128)(2,1)} async-done(((bf16[896,128]{1,0:T(8,128)(2,1)}), bf16[7168,128]{1,0:T(8,128)(2,1)}) %all-gather.3.cloned.1.call-update) | async-done | bytes 1835024 | tf_op jit(solution)/shard_map/all_gather | solution.py:808
  49.5 3.1 %conv_first.1 = (bf16[528,128]{1,0:T(8,128)(2,1)}, f32[512,128]{1,0:T(8,128)}, f32[8,128]{1,0:T(8,128)}, f32[32,4,128]{2,1,0:T(4,128)}) custom-call(bf16[8,896,128]{2,1,0:T(8,128)(2,1)} %bitcast.7, bf16[8,2,16,512]{3,2,1,0:T(8,128)(2,1)} %copy-done.3, bf16[8,2,16,512]{3,2,1,0:T(8,128)(2,1)} %copy-done.5, bf16[8,2,16,512]{3,2,1,0:T(8,128)(2,1)} %copy-done.4, ...), custom_call_target="tpu_custom_call" | custom-call | flops 301989888 | bytes 3615744 | tf_op jit(solution)/shard_map/conv_first/pallas_call | solution.py:250
  52.6 1.5 collective-permute-start.4
  54.2 2.7 %all-to-all-start.1 = ((f32[32,4,128]{2,1,0:T(4,128)}), f32[32,4,128]{2,1,0:T(4,128)S(1)}, u32[]{:S(2)}, u32[]{:S(2)}) async-start(f32[32,4,128]{2,1,0:T(4,128)} %get-tuple-element.95), calls=%async_computation.1 | async-start | bytes 131072 | tf_op jit(solution)/shard_map/all_to_all | solution.py:741
  56.9 0.9 copy-done
  57.8 2.9 %hand_on.1 = (bf16[2,896,128]{2,1,0:T(8,128)(2,1)}, bf16[2,896,128]{2,1,0:T(8,128)(2,1)}, bf16[2,896,128]{2,1,0:T(8,128)(2,1)}, bf16[2,896,128]{2,1,0:T(8,128)(2,1)}) custom-call(bf16[528,128]{1,0:T(8,128)(2,1)S(1)} %copy-done, bf16[8,896,128]{2,1,0:T(8,128)(2,1)} %bitcast.8), custom_call_target="tpu_custom_call" | custom-call | bytes 3670016 | tf_op jit(solution)/shard_map/hand_on/pallas_call | solution.py:250
  60.7 3.5 %all-to-all-done.1 = f32[32,4,128]{2,1,0:T(4,128)S(1)} async-done(((f32[32,4,128]{2,1,0:T(4,128)}), f32[32,4,128]{2,1,0:T(4,128)S(1)}, u32[]{:S(2)}, u32[]{:S(2)}) %all-to-all-start.1) | async-done | bytes 65568 | tf_op jit(solution)/shard_map/all_to_all | solution.py:741
  64.4 0.5 collective-permute-start.7
  64.8 1.3 collective-permute-start.8
  66.1 0.4 collective-permute-start.3
  66.6 0.9 collective-permute-done.3.refs_1_.refs_5_
  67.9 3.8 %conv_second.1 = (bf16[512,512]{1,0:T(8,128)(2,1)S(1)}, f32[512,128]{1,0:T(8,128)S(1)}, f32[8,4,128]{2,1,0:T(4,128)S(1)}, f32[4,8,128]{2,1,0:T(8,128)}, f32[512,...) custom-call(bf16[528,128]{1,0:T(8,128)(2,1)} %get-tuple-element.94.refs_0_.refs_8_.refs_, ...), custom_call_target="tpu_custom_call" | custom-call | flops 603979776 | bytes 4710400 | tf_op jit(solution)/shard_map/conv_second/pallas_call | solution.py:250
  71.7 8.9 %all_to_all.36.refs_2_ = f32[8,4,128]{2,1,0:T(4,128)S(1)} all-to-all(f32[8,4,128]{2,1,0:T(4,128)S(1)} %get-tuple-element.106), channel_id=1, replica_groups=mesh['dp'=8,'chan'=4] {'dp'}, dimensions={0} | all-to-all | bytes 32768 | tf_op jit(solution)/shard_map/all_to_all | solution.py:741
  80.6 1.5 block_output.1
  82.2 8.9 %all_to_all.37.refs_7_ = f32[8,4,128]{2,1,0:T(4,128)S(1)} all-to-all(f32[8,4,128]{2,1,0:T(4,128)S(1)} %get-tuple-element.118), channel_id=1, replica_groups=mesh['dp'=8,'chan'=4] {'dp'}, dimensions={0} | all-to-all | bytes 32768 | tf_op jit(solution)/shard_map/all_to_all | solution.py:741
  91.1 0.8 grad_outputs.1
  91.9 1.4 collective-permute-start.9
  93.3 3.4 %grad_second.1 = bf16[8,608,128]{2,1,0:T(8,128)(2,1)} custom-call(bf16[512,512]{1,0:T(8,128)(2,1)S(1)} %get-tuple-element.120.refs_0_, bf16[512,128]{1,0:T(8,128)(2,1)} %get-tuple-element.119.refs_1_.refs_4_, bf16[8,2,16,512]{3,2,1,0:T(8,128)(2,1)} %copy-done.3, bf16[8,2,16,512]{3,2,1,0:T(8,128)(2,1)} %copy-done.5, bf16[8,2,16,512]{3,2,1,0:T(8,128)(2,1)} %copy-done.4, ...), custom_call_target="tpu_custom_call" | custom-call | flops 603979776 | bytes 3080192 | tf_op jit(solution)/shard_map/grad_second/pallas_call | solution.py:250
  96.7 0.5 collective-permute-done.9.refs_6_
  97.3 0.5 collective-permute-start.11
  97.8 0.8 collective-permute-done.10.refs_5_
  98.8 3.2 %grad_hidden.1 = (f32[512,128]{1,0:T(8,128)S(1)}, bf16[1040,128]{1,0:T(8,128)(2,1)}, f32[32,2,128]{2,1,0:T(2,128)S(1)}) custom-call(bf16[2,896,128]{2,1,0:T(8,128)(2,1)} %get-tuple-element.123.refs_0_.refs_11_, bf16[2,896,128]{2,1,0:T(8,128)(2,1)S(1)} %collective-permute-done.6.refs_0_.refs_1_.refs_12_, ...), custom_call_target="tpu_custom_call" | custom-call | flops 603979776 | bytes 3465216 | tf_op jit(solution)/shard_map/grad_hidden/pallas_call | solution.py:250
  102.0 1.4 collective-permute-start.12
  103.4 9.0 %all_to_all.38 = f32[32,2,128]{2,1,0:T(2,128)S(1)} all-to-all(f32[32,2,128]{2,1,0:T(2,128)S(1)} %get-tuple-element.128), channel_id=1, replica_groups=mesh['dp'=8,'chan'=4] {'dp','chan'}, dimensions={0} | all-to-all | bytes 65536 | tf_op jit(solution)/shard_map/all_to_all | solution.py:741
  112.4 2.8 %grad_first.1 = (bf16[8,288,128]{2,1,0:T(8,128)(2,1)}, f32[8,128]{1,0:T(8,128)}) custom-call(f32[512,128]{1,0:T(8,128)S(1)} %get-tuple-element.126.refs_0_, bf16[528,128]{1,0:T(8,128)(2,1)} %get-tuple-element.94.refs_0_.refs_8_.refs_1_.refs_4_, f32[8,4,2,128]{3,2,1,0:T(2,128)S(1)} %bitcast.4, f32[4,8,128]{2,1,0:T(8,128)} %get-tuple-element.125.refs_10_.refs_3_.refs_9_, ...), custom_call_target="tpu_custom_call" | custom-call | flops 301989888 | bytes 2354176 | tf_op jit(solution)/shard_map/grad_first/pallas_call | solution.py:250
  115.2 3.6 %all-to-all-start.5 = ((bf16[8,288,128]{2,1,0:T(8,128)(2,1)}), bf16[8,288,128]{2,1,0:T(8,128)(2,1)S(1)}, u32[]{:S(2)}, u32[]{:S(2)}) async-start(bf16[8,288,128]{2,1,0:T(8,128)(2,1)} %get-tuple-element.130), calls=%async_computation.6 | async-start | bytes 1179648 | tf_op jit(solution)/shard_map/all_to_all | solution.py:741
  119.0 0.4 collective-permute-start.14
  119.4 1.0 collective-permute-done.13.refs_1_
  120.8 4.0 %grad_images.1 = (bf16[2,64,128]{2,1,0:T(8,128)(2,1)}, bf16[2,64,128]{2,1,0:T(8,128)(2,1)}, bf16[2,64,128]{2,1,0:T(8,128)(2,1)}, bf16[2,64,128]{2,1,0:T(8,128)(2...) custom-call(bf16[1040,128]{1,0:T(8,128)(2,1)} %get-tuple-element.127, ...), custom_call_target="tpu_custom_call" | custom-call | flops 301989888 | bytes 4014080 | tf_op jit(solution)/shard_map/grad_images/pallas_call | solution.py:250
  124.8 1.9 %collective-permute-start.15 = (bf16[2,64,128]{2,1,0:T(8,128)(2,1)}, bf16[2,64,128]{2,1,0:T(8,128)(2,1)S(1)}, u32[]{:S(2)}, u32[]{:S(2)}) collective-permute-start(bf16[2,64,128]{2,1,0:T(8,128)(2,1)} %get-tuple-element.137), channel_id=1, source_target_pairs={{0,4},{4,0},{8,12},{12,8},{16,20},{20,16},{24,28},{28,24},{1,5},{5... | collective-permute-start | bytes 98312 | tf_op jit(solution)/shard_map/ppermute | solution.py:754
  126.7 1.5 collective-permute-start.16
  128.4 2.8 %collective-permute-start.18 = (bf16[2,64,128]{2,1,0:T(8,128)(2,1)}, bf16[2,64,128]{2,1,0:T(8,128)(2,1)S(1)}, u32[]{:S(2)}, u32[]{:S(2)}) collective-permute-start(bf16[2,64,128]{2,1,0:T(8,128)(2,1)} %get-tuple-element.140), channel_id=1, source_target_pairs={{0,16},{4,20},{8,24},{12,28},{16,0},{20,4},{24,8},{28,12},{1,17},{... | collective-permute-start | bytes 98312 | tf_op jit(solution)/shard_map/ppermute | solution.py:754
  131.1 1.4 collective-permute-start.19
  132.6 3.3 %collective-permute-start.20 = (bf16[2,64,128]{2,1,0:T(8,128)(2,1)}, bf16[2,64,128]{2,1,0:T(8,128)(2,1)S(1)}, u32[]{:S(2)}, u32[]{:S(2)}) collective-permute-start(bf16[2,64,128]{2,1,0:T(8,128)(2,1)} %get-tuple-element.142), channel_id=1, source_target_pairs={{0,24},{4,28},{8,16},{12,20},{16,8},{20,12},{24,0},{28,4},{1,25},{... | collective-permute-start | bytes 98312 | tf_op jit(solution)/shard_map/ppermute | solution.py:754
  136.0 2.6 %all-to-all-done.5.refs_1_ = bf16[8,288,128]{2,1,0:T(8,128)(2,1)S(1)} async-done(((bf16[8,288,128]{2,1,0:T(8,128)(2,1)}), bf16[8,288,128]{2,1,0:T(8,128)(2,1)S(1)}, u32[]{:S(2)}, u32[]{:S(2)}) %all-to-all-start.5) | async-done | bytes 589856 | tf_op jit(solution)/shard_map/all_to_all | solution.py:741
  138.6 2.1 %reduce_all.1 = (f32[288,128]{1,0:T(8,128)}, f32[576,128]{1,0:T(8,128)}, f32[32,128]{1,0:T(8,128)}, f32[32,1,128]{2,1,0:T(1,128)}) custom-call(bf16[608,128]{1,0:T(8,128)(2,1)} %reduce-scatter.2.cloned.1.call-done.refs_0_, bf16[8,288,128]{2,1,0:T(8,128)(2,1)S(1)} %all-to-all-done.5.refs_1_, f32[8,128]{1,0:T(8,128)} %get-tuple-element.131.refs_2_, ...), custom_call_target="tpu_custom_call" | custom-call | bytes 1235968 | tf_op jit(solution)/shard_map/reduce_all/pallas_call | solution.py:250
  140.9 1.8 %collective-permute-done.21.refs_7_ = bf16[2,64,128]{2,1,0:T(8,128)(2,1)S(1)} collective-permute-done((bf16[2,64,128]{2,1,0:T(8,128)(2,1)}, bf16[2,64,128]{2,1,0:T(8,128)(2,1)S(1)}, u32[]{:S(2)}, u32[]{:S(2)}) %collective-permute-start.21) | collective-permute-done | bytes 32800 | tf_op jit(solution)/shard_map/ppermute | solution.py:754
  142.7 2.5 %all-to-all-start.6 = ((f32[32,1,128]{2,1,0:T(1,128)}), f32[32,1,128]{2,1,0:T(1,128)S(1)}, u32[]{:S(2)}, u32[]{:S(2)}) async-start(f32[32,1,128]{2,1,0:T(1,128)} %get-tuple-element.152), calls=%async_computation.7 | async-start | bytes 32768 | tf_op jit(solution)/shard_map/all_to_all | solution.py:741
  145.3 1.9 %finish_images.1 = bf16[64,32,64]{2,1,0:T(8,128)(2,1)} custom-call(bf16[2,64,128]{2,1,0:T(8,128)(2,1)} %get-tuple-element.144.refs_0_, bf16[2,64,128]{2,1,0:T(8,128)(2,1)S(1)} %collective-permute-done.15.refs_1_, bf16[2,64,128]{2,1,0:T(8,128)(2,1)S(1)} %collective-permute-done.16.refs_2_, bf16[2,64,128]{2,1,0:T(8,128)(2,1)S(1)} %collective-permute-done.17.refs_3_, ...), custom_call_target="tpu_custom_call" | custom-call | bytes 524288 | tf_op jit(solution)/shard_map/finish_images/pallas_call | solution.py:250
  147.1 5.2 %all-to-all-done.6.refs_0_ = f32[32,1,128]{2,1,0:T(1,128)S(1)} async-done(((f32[32,1,128]{2,1,0:T(1,128)}), f32[32,1,128]{2,1,0:T(1,128)S(1)}, u32[]{:S(2)}, u32[]{:S(2)}) %all-to-all-start.6) | async-done | bytes 16416 | tf_op jit(solution)/shard_map/all_to_all | solution.py:741
  152.3 2.9 %update.1 = (f32[288,128]{1,0:T(8,128)}, f32[288,128]{1,0:T(8,128)}, f32[288,128]{1,0:T(8,128)}, f32[576,128]{1,0:T(8,128)}, f32[576,128]{1,0:T(8,128)}, /*index...) custom-call(f32[32,1,128]{2,1,0:T(1,128)S(1)} %all-to-all-done.6.ref, ...), custom_call_target="tpu_custom_call" | custom-call | bytes 3254272 | tf_op jit(solution)/shard_map/update/pallas_call | solution.py:250
  (44 shorter events, 2.0 us)
Async XLA Ops:
  7.2 42.4 %all-gather.3.cloned.1.call-start = ((), (), s32[]{:S(2)}) async-start(), calls=%async_computation.9 | async-start | bytes 2064384 | tf_op jit(solution)/shard_map/all_gather | solution.py:808
  9.1 0.9 copy-start.2
  32.6 17.0 %copy-start.3 = (bf16[8,2,16,512]{3,2,1,0:T(8,128)(2,1)}, bf16[8,2,16,512]{3,2,1,0:T(8,128)(2,1)S(1)}, u32[]{:S(2)}) copy-start(bf16[8,2,16,512]{3,2,1,0:T(8,128)(2,1)S(1)} %all_to_all.35.refs_1_.refs_2_.refs_6_) | copy-start | bytes 786436
  32.6 6.4 %collective-permute-start.1 = (bf16[8,2,16,512]{3,2,1,0:T(8,128)(2,1)S(1)}, bf16[8,2,16,512]{3,2,1,0:T(8,128)(2,1)S(1)}, u32[]{:S(2)}, u32[]{:S(2)}) collective-permute-start(bf16[8,2,16,512]{3,2,1,0:T(8,128)(2,1)S(1)} %all_to_all.35.refs_1_.refs_2_.refs_6_), channel_id=1, source_target_pairs={{0,2},{1,3},{2,0},{3,1},{4,6},{5,7},{6,4},{7,5},{8,10},{9,11},{10,... | collective-permute-start | bytes 786440 | tf_op jit(solution)/shard_map/ppermute | solution.py:754
  34.0 4.9 %collective-permute-start = (bf16[8,2,16,512]{3,2,1,0:T(8,128)(2,1)S(1)}, bf16[8,2,16,512]{3,2,1,0:T(8,128)(2,1)S(1)}, u32[]{:S(2)}, u32[]{:S(2)}) collective-permute-start(bf16[8,2,16,512]{3,2,1,0:T(8,128)(2,1)S(1)} %all_to_all.35.refs_1_.refs_2_.refs_6_), channel_id=1, source_target_pairs={{0,1},{1,0},{2,3},{3,2},{4,5},{5,4},{6,7},{7,6},{8,9},{9,8},{10,11... | collective-permute-start | bytes 786440 | tf_op jit(solution)/shard_map/ppermute | solution.py:754
  38.9 10.6 %copy-start.4 = (bf16[8,2,16,512]{3,2,1,0:T(8,128)(2,1)}, bf16[8,2,16,512]{3,2,1,0:T(8,128)(2,1)S(1)}, u32[]{:S(2)}) copy-start(bf16[8,2,16,512]{3,2,1,0:T(8,128)(2,1)S(1)} %collective-permute-done.1.refs_3_.refs_4_.refs_8_) | copy-start | bytes 786436
  38.9 1.5 collective-permute-start.2
  38.9 10.6 %copy-start.5 = (bf16[8,2,16,512]{3,2,1,0:T(8,128)(2,1)}, bf16[8,2,16,512]{3,2,1,0:T(8,128)(2,1)S(1)}, u32[]{:S(2)}) copy-start(bf16[8,2,16,512]{3,2,1,0:T(8,128)(2,1)S(1)} %collective-permute-done.refs_2_.refs_3_.refs_7_) | copy-start | bytes 786436
  40.5 9.1 %copy-start.6 = (bf16[8,2,16,512]{3,2,1,0:T(8,128)(2,1)}, bf16[8,2,16,512]{3,2,1,0:T(8,128)(2,1)S(1)}, u32[]{:S(2)}) copy-start(bf16[8,2,16,512]{3,2,1,0:T(8,128)(2,1)S(1)} %collective-permute-done.2.refs_4_.refs_5_.refs_9_) | copy-start | bytes 786436
  52.6 11.6 %collective-permute-start.4 = (bf16[528,128]{1,0:T(8,128)(2,1)}, bf16[528,128]{1,0:T(8,128)(2,1)S(1)}, u32[]{:S(2)}, u32[]{:S(2)}) collective-permute-start(bf16[528,128]{1,0:T(8,128)(2,1)} %get-tuple-element.94.refs_0_.refs_8_.refs_1_.refs_4_), channel_id=1, source_target_pairs={{0,2},{1,3},{2,0},{3,1},{4,6},{5,7},{6,4},{7,5},{8,10},{9,11},{10,... | collective-permute-start | bytes 405512 | tf_op jit(solution)/shard_map/ppermute | solution.py:754
  54.2 10.1 %all-to-all-start.1 = ((f32[32,4,128]{2,1,0:T(4,128)}), f32[32,4,128]{2,1,0:T(4,128)S(1)}, u32[]{:S(2)}, u32[]{:S(2)}) async-start(f32[32,4,128]{2,1,0:T(4,128)} %get-tuple-element.95), calls=%async_computation.1 | async-start | bytes 131072 | tf_op jit(solution)/shard_map/all_to_all | solution.py:741
  56.8 81.8 %reduce-scatter.2.cloned.1.call-start = ((), (), s32[]{:S(2)}) async-start(), calls=%async_computation.8 | async-start | bytes 1400832 | tf_op jit(solution)/shard_map/reduce_scatter | solution.py:914
  56.9 0.9 copy-start
  57.8 8.3 %copy-start.1 = (bf16[528,128]{1,0:T(8,128)(2,1)S(1)}, bf16[528,128]{1,0:T(8,128)(2,1)}, u32[]{:S(2)}) copy-start(bf16[528,128]{1,0:T(8,128)(2,1)} %get-tuple-element.94.refs_0_.refs_8_.refs_1_.refs_4_) | copy-start | bytes 405508
  64.2 26.9 %collective-permute-start.6 = (bf16[2,896,128]{2,1,0:T(8,128)(2,1)}, bf16[2,896,128]{2,1,0:T(8,128)(2,1)S(1)}, u32[]{:S(2)}, u32[]{:S(2)}) collective-permute-start(bf16[2,896,128]{2,1,0:T(8,128)(2,1)} %get-tuple-element.111), channel_id=1, source_target_pairs={{0,1},{1,0},{2,3},{3,2},{4,5},{5,4},{6,7},{7,6},{8,9},{9,8},{10,11... | collective-permute-start | bytes 1376264 | tf_op jit(solution)/shard_map/ppermute | solution.py:754
  64.4 26.8 %collective-permute-start.7 = (bf16[2,896,128]{2,1,0:T(8,128)(2,1)}, bf16[2,896,128]{2,1,0:T(8,128)(2,1)S(1)}, u32[]{:S(2)}, u32[]{:S(2)}) collective-permute-start(bf16[2,896,128]{2,1,0:T(8,128)(2,1)} %get-tuple-element.112), channel_id=1, source_target_pairs={{0,2},{1,3},{2,0},{3,1},{4,6},{5,7},{6,4},{7,5},{8,10},{9,11},{10,... | collective-permute-start | bytes 1376264 | tf_op jit(solution)/shard_map/ppermute | solution.py:754
  64.8 26.3 %collective-permute-start.8 = (bf16[2,896,128]{2,1,0:T(8,128)(2,1)}, bf16[2,896,128]{2,1,0:T(8,128)(2,1)S(1)}, u32[]{:S(2)}, u32[]{:S(2)}) collective-permute-start(bf16[2,896,128]{2,1,0:T(8,128)(2,1)} %get-tuple-element.113), channel_id=1, source_target_pairs={{0,3},{1,2},{2,1},{3,0},{4,7},{5,6},{6,5},{7,4},{8,11},{9,10},{10,... | collective-permute-start | bytes 1376264 | tf_op jit(solution)/shard_map/ppermute | solution.py:754
  66.1 1.4 collective-permute-start.3
  66.5 1.4 collective-permute-start.5
  91.9 5.2 %collective-permute-start.9 = (bf16[512,128]{1,0:T(8,128)(2,1)}, bf16[512,128]{1,0:T(8,128)(2,1)S(1)}, u32[]{:S(2)}, u32[]{:S(2)}) collective-permute-start(bf16[512,128]{1,0:T(8,128)(2,1)} %get-tuple-element.119.refs_1_.refs_4_), channel_id=1, source_target_pairs={{0,2},{1,3},{2,0},{3,1},{4,6},{5,7},{6,4},{7,5},{8,10},{9,11},{10,... | collective-permute-start | bytes 393224 | tf_op jit(solution)/shard_map/ppermute | solution.py:754
  93.3 3.9 %copy-start.7 = (bf16[512,128]{1,0:T(8,128)(2,1)S(1)}, bf16[512,128]{1,0:T(8,128)(2,1)}, u32[]{:S(2)}) copy-start(bf16[512,128]{1,0:T(8,128)(2,1)} %get-tuple-element.119.refs_1_.refs_4_) | copy-start | bytes 393220
  97.2 1.4 collective-permute-start.10
  97.3 1.5 collective-permute-start.11
  102.0 16.8 %copy-start.8 = (bf16[1040,128]{1,0:T(8,128)(2,1)S(1)}, bf16[1040,128]{1,0:T(8,128)(2,1)}, u32[]{:S(2)}) copy-start(bf16[1040,128]{1,0:T(8,128)(2,1)} %get-tuple-element.127.refs_0_) | copy-start | bytes 798724
  102.0 10.4 %collective-permute-start.12 = (bf16[1040,128]{1,0:T(8,128)(2,1)}, bf16[1040,128]{1,0:T(8,128)(2,1)S(1)}, u32[]{:S(2)}, u32[]{:S(2)}) collective-permute-start(bf16[1040,128]{1,0:T(8,128)(2,1)} %get-tuple-element.127.refs_0_), channel_id=1, source_target_pairs={{0,2},{1,3},{2,0},{3,1},{4,6},{5,7},{6,4},{7,5},{8,10},{9,11},{10,... | collective-permute-start | bytes 798728 | tf_op jit(solution)/shard_map/ppermute | solution.py:754
  115.2 23.4 %all-to-all-start.5 = ((bf16[8,288,128]{2,1,0:T(8,128)(2,1)}), bf16[8,288,128]{2,1,0:T(8,128)(2,1)S(1)}, u32[]{:S(2)}, u32[]{:S(2)}) async-start(bf16[8,288,128]{2,1,0:T(8,128)(2,1)} %get-tuple-element.130), calls=%async_computation.6 | async-start | bytes 1179648 | tf_op jit(solution)/shard_map/all_to_all | solution.py:741
  118.8 1.6 collective-permute-start.13
  119.0 1.8 %collective-permute-start.14 = (bf16[1040,128]{1,0:T(8,128)(2,1)S(1)}, bf16[1040,128]{1,0:T(8,128)(2,1)S(1)}, u32[]{:S(2)}, u32[]{:S(2)}) collective-permute-start(bf16[1040,128]{1,0:T(8,128)(2,1)S(1)} %collective-permute-done.12.refs_2_), channel_id=1, source_target_pairs={{0,1},{1,0},{2,3},{3,2},{4,5},{5,4},{6,7},{7,6},{8,9},{9,8},{10,11... | collective-permute-start | bytes 798728 | tf_op jit(solution)/shard_map/ppermute | solution.py:754
  124.8 7.8 %collective-permute-start.15 = (bf16[2,64,128]{2,1,0:T(8,128)(2,1)}, bf16[2,64,128]{2,1,0:T(8,128)(2,1)S(1)}, u32[]{:S(2)}, u32[]{:S(2)}) collective-permute-start(bf16[2,64,128]{2,1,0:T(8,128)(2,1)} %get-tuple-element.137), channel_id=1, source_target_pairs={{0,4},{4,0},{8,12},{12,8},{16,20},{20,16},{24,28},{28,24},{1,5},{5... | collective-permute-start | bytes 98312 | tf_op jit(solution)/shard_map/ppermute | solution.py:754
  126.7 9.2 %collective-permute-start.16 = (bf16[2,64,128]{2,1,0:T(8,128)(2,1)}, bf16[2,64,128]{2,1,0:T(8,128)(2,1)S(1)}, u32[]{:S(2)}, u32[]{:S(2)}) collective-permute-start(bf16[2,64,128]{2,1,0:T(8,128)(2,1)} %get-tuple-element.138), channel_id=1, source_target_pairs={{0,8},{4,12},{8,0},{12,4},{16,24},{20,28},{24,16},{28,20},{1,9},{5... | collective-permute-start | bytes 98312 | tf_op jit(solution)/shard_map/ppermute | solution.py:754
  128.2 12.5 %collective-permute-start.17 = (bf16[2,64,128]{2,1,0:T(8,128)(2,1)}, bf16[2,64,128]{2,1,0:T(8,128)(2,1)S(1)}, u32[]{:S(2)}, u32[]{:S(2)}) collective-permute-start(bf16[2,64,128]{2,1,0:T(8,128)(2,1)} %get-tuple-element.139), channel_id=1, source_target_pairs={{0,12},{4,8},{8,4},{12,0},{16,28},{20,24},{24,20},{28,16},{1,13},{... | collective-permute-start | bytes 98312 | tf_op jit(solution)/shard_map/ppermute | solution.py:754
  128.4 12.4 %collective-permute-start.18 = (bf16[2,64,128]{2,1,0:T(8,128)(2,1)}, bf16[2,64,128]{2,1,0:T(8,128)(2,1)S(1)}, u32[]{:S(2)}, u32[]{:S(2)}) collective-permute-start(bf16[2,64,128]{2,1,0:T(8,128)(2,1)} %get-tuple-element.140), channel_id=1, source_target_pairs={{0,16},{4,20},{8,24},{12,28},{16,0},{20,4},{24,8},{28,12},{1,17},{... | collective-permute-start | bytes 98312 | tf_op jit(solution)/shard_map/ppermute | solution.py:754
  131.1 9.8 %collective-permute-start.19 = (bf16[2,64,128]{2,1,0:T(8,128)(2,1)}, bf16[2,64,128]{2,1,0:T(8,128)(2,1)S(1)}, u32[]{:S(2)}, u32[]{:S(2)}) collective-permute-start(bf16[2,64,128]{2,1,0:T(8,128)(2,1)} %get-tuple-element.141), channel_id=1, source_target_pairs={{0,20},{4,16},{8,28},{12,24},{16,4},{20,0},{24,12},{28,8},{1,21},{... | collective-permute-start | bytes 98312 | tf_op jit(solution)/shard_map/ppermute | solution.py:754
  132.6 8.3 %collective-permute-start.20 = (bf16[2,64,128]{2,1,0:T(8,128)(2,1)}, bf16[2,64,128]{2,1,0:T(8,128)(2,1)S(1)}, u32[]{:S(2)}, u32[]{:S(2)}) collective-permute-start(bf16[2,64,128]{2,1,0:T(8,128)(2,1)} %get-tuple-element.142), channel_id=1, source_target_pairs={{0,24},{4,28},{8,16},{12,20},{16,8},{20,12},{24,0},{28,4},{1,25},{... | collective-permute-start | bytes 98312 | tf_op jit(solution)/shard_map/ppermute | solution.py:754
  135.9 6.8 %collective-permute-start.21 = (bf16[2,64,128]{2,1,0:T(8,128)(2,1)}, bf16[2,64,128]{2,1,0:T(8,128)(2,1)S(1)}, u32[]{:S(2)}, u32[]{:S(2)}) collective-permute-start(bf16[2,64,128]{2,1,0:T(8,128)(2,1)} %get-tuple-element.143), channel_id=1, source_target_pairs={{0,28},{4,24},{8,20},{12,16},{16,12},{20,8},{24,4},{28,0},{1,29},{... | collective-permute-start | bytes 98312 | tf_op jit(solution)/shard_map/ppermute | solution.py:754
  142.7 9.6 %all-to-all-start.6 = ((f32[32,1,128]{2,1,0:T(1,128)}), f32[32,1,128]{2,1,0:T(1,128)S(1)}, u32[]{:S(2)}, u32[]{:S(2)}) async-start(f32[32,1,128]{2,1,0:T(1,128)} %get-tuple-element.152), calls=%async_computation.7 | async-start | bytes 32768 | tf_op jit(solution)/shard_map/all_to_all | solution.py:741
Sparse Core Ops, SparseCore 0:
  10.1 39.3 all-gather.2
  97.3 27.9 reduce-scatter.1

commit v5 on v4

--- a/solution.py
+++ b/solution.py
@@ -856,9 +856,9 @@
         later=[z_own],
     )
     got1 = exchange(pay, everyone).reshape(dp_count, ch_count, 4, wide)
-    far = swap(z_own, "chan", 2)
-    far, got1, *turned = lax.optimization_barrier((far, got1, *turned))
-    z_all = [z_own, swap(z_own, "chan", 1), far, swap(far, "chan", 1)]
+    z_all = [swap(z_own, "chan", k) for k in range(1, ch_count)]
+    got1, *both = lax.optimization_barrier((got1, *z_all, *turned))
+    z_all, turned = [z_own, *both[: ch_count - 1]], both[ch_count - 1 :]
 
     hidden, z_second, pay, total1, *near = call(
         conv_second,

time: 163 us -> 162 us (level)
  transfers between devices with their start and end apart: 27 -> 27, of which waited for: 15 -> 13; matrix products, arithmetic and copies ran while one was open for 0% -> 0% of each run, Pallas kernels for 17% -> 17%
where the time goes in v5:
time: 162 us
  blocking collectives  47.4 us (29%)
  Pallas kernels  36.1 us (22%)
  waiting for transfers between devices  31.9 us (20%)
  starting transfers between devices  29.9 us (18%)
  between operations  14.3 us (9%)
  local copies, waits for them, and re-layouts  1.86 us (1%)
    all_to_all x4, blocking collectives, exchange(): return lax.all_to_all(blocks, axes, 0, 0)  47.4 us
    pallas_call x14, Pallas kernels, call(): pl.pallas_call(kernel, out_shape=[pltpu.HBM(o.shape, o.dtype) if g.pinned...  36.1 us
    ppermute x22, starting transfers between devices, swap(): lax.ppermute(array, axis, [(i, i ^ bits) for i in range(lax.axis_size(axi...  20.2 us
    all_to_all x3, waiting for transfers between devices, exchange(): return lax.all_to_all(blocks, axes, 0, 0)  11.5 us
    ppermute x22, waiting for transfers between devices, swap(): lax.ppermute(array, axis, [(i, i ^ bits) for i in range(lax.axis_size(axi...  11.4 us
    all_to_all x3, starting transfers between devices, exchange(): return lax.all_to_all(blocks, axes, 0, 0)  9.65 us
    all_gather x1, waiting for transfers between devices, per_device(): gathered = lax.all_gather(own, everyone, axis_index_groups=rings())  9.06 us
  transfers between devices with their start and end apart: 27, of which 13 were waited for; matrix products, arithmetic and copies ran while one was open for 0% of the time, Pallas kernels for 17%

profile of v5, /device:TPU:0, one launch (start us, length us, event | category | flops | bytes accessed | tf_op | source)
XLA Modules:
  0.0 161.5 jit_solution(4458613389904267696)
XLA Ops:
  7.2 1.8 %pack_weights.1 = (bf16[896,128]{1,0:T(8,128)(2,1)}, f32[8,128]{1,0:T(8,128)}) custom-call(f32[288,128]{1,0:T(8,128)} %refs_3_.1, f32[32,128]{1,0:T(8,128)} %refs_11_.1, f32[576,128]{1,0:T(8,128)} %refs_7_.1), custom_call_target="tpu_custom_call" | custom-call | bytes 692224 | tf_op jit(solution)/shard_map/pack_weights/pallas_call | solution.py:250
  9.1 0.9 copy-done.1
  10.0 2.0 %pack_images.1 = (bf16[8,2,16,512]{3,2,1,0:T(8,128)(2,1)}, f32[512,128]{1,0:T(8,128)}) custom-call(bf16[896,128]{1,0:T(8,128)(2,1)S(1)} %copy-done.1, bf16[64,32,256]{2,1,0:T(8,128)(2,1)} %refs_1_.3, s32[8,64]{1,0:T(8,128)} %refs_2_.3), custom_call_target="tpu_custom_call" | custom-call | bytes 1574912 | tf_op jit(solution)/shard_map/pack_images/pallas_call | solution.py:250
  12.1 20.5 %all_to_all.35.refs_1_.refs_2_.refs_6_ = bf16[8,2,16,512]{3,2,1,0:T(8,128)(2,1)S(1)} all-to-all(bf16[8,2,16,512]{3,2,1,0:T(8,128)(2,1)} %get-tuple-element.94), channel_id=1, replica_groups=mesh['dp'=8,'chan'=4] {'dp'}, dimensions={0} | all-to-all | bytes 524288 | tf_op jit(solution)/shard_map/all_to_all | solution.py:741
  32.6 1.5 collective-permute-start.1
  34.0 4.9 %collective-permute-done.1.refs_3_.refs_4_.refs_8_ = bf16[8,2,16,512]{3,2,1,0:T(8,128)(2,1)S(1)} collective-permute-done((bf16[8,2,16,512]{3,2,1,0:T(8,128)(2,1)S(1)}, bf16[8,2,16,512]{3,2,1,0:T(8,128)(2,1)S(1)}, u32[]{:S(2)}, u32[]{:S(2)}) %collective-permute-start.1) | collective-permute-done | bytes 262176 | tf_op jit(solution)/shard_map/ppermute | solution.py:754
  39.0 1.5 collective-permute-done.2.refs_4_.refs_5_.refs_9_
  40.5 9.1 %all-gather.3.cloned.1.call-done = bf16[7168,128]{1,0:T(8,128)(2,1)} async-done(((bf16[896,128]{1,0:T(8,128)(2,1)}), bf16[7168,128]{1,0:T(8,128)(2,1)}) %all-gather.3.cloned.1.call-update) | async-done | bytes 1835024 | tf_op jit(solution)/shard_map/all_gather | solution.py:808
  49.5 3.1 %conv_first.1 = (bf16[528,128]{1,0:T(8,128)(2,1)}, f32[512,128]{1,0:T(8,128)}, f32[8,128]{1,0:T(8,128)}, f32[32,4,128]{2,1,0:T(4,128)}) custom-call(bf16[8,896,128]{2,1,0:T(8,128)(2,1)} %bitcast.7, bf16[8,2,16,512]{3,2,1,0:T(8,128)(2,1)} %copy-done.2, bf16[8,2,16,512]{3,2,1,0:T(8,128)(2,1)} %copy-done.4, bf16[8,2,16,512]{3,2,1,0:T(8,128)(2,1)} %copy-done.3, ...), custom_call_target="tpu_custom_call" | custom-call | flops 301989888 | bytes 3615744 | tf_op jit(solution)/shard_map/conv_first/pallas_call | solution.py:250
  52.7 1.5 collective-permute-start.4
  54.2 0.3 collective-permute-start.3
  54.6 3.6 %all-to-all-start.1 = ((f32[32,4,128]{2,1,0:T(4,128)}), f32[32,4,128]{2,1,0:T(4,128)S(1)}, u32[]{:S(2)}, u32[]{:S(2)}) async-start(f32[32,4,128]{2,1,0:T(4,128)} %get-tuple-element.97), calls=%async_computation.1 | async-start | bytes 131072 | tf_op jit(solution)/shard_map/all_to_all | solution.py:741
  58.2 0.9 copy-done
  59.1 2.9 %hand_on.1 = (bf16[2,896,128]{2,1,0:T(8,128)(2,1)}, bf16[2,896,128]{2,1,0:T(8,128)(2,1)}, bf16[2,896,128]{2,1,0:T(8,128)(2,1)}, bf16[2,896,128]{2,1,0:T(8,128)(2,1)}) custom-call(bf16[528,128]{1,0:T(8,128)(2,1)S(1)} %copy-done, bf16[8,896,128]{2,1,0:T(8,128)(2,1)} %bitcast.8), custom_call_target="tpu_custom_call" | custom-call | bytes 3670016 | tf_op jit(solution)/shard_map/hand_on/pallas_call | solution.py:250
  61.9 3.6 %all-to-all-done.1 = f32[32,4,128]{2,1,0:T(4,128)S(1)} async-done(((f32[32,4,128]{2,1,0:T(4,128)}), f32[32,4,128]{2,1,0:T(4,128)S(1)}, u32[]{:S(2)}, u32[]{:S(2)}) %all-to-all-start.1) | async-done | bytes 65568 | tf_op jit(solution)/shard_map/all_to_all | solution.py:741
  65.7 0.5 collective-permute-start.7
  66.2 1.3 collective-permute-start.8
  67.5 3.8 %conv_second.1 = (bf16[512,512]{1,0:T(8,128)(2,1)S(1)}, f32[512,128]{1,0:T(8,128)S(1)}, f32[8,4,128]{2,1,0:T(4,128)S(1)}, f32[4,8,128]{2,1,0:T(8,128)}, f32[512,...) custom-call(bf16[528,128]{1,0:T(8,128)(2,1)} %get-tuple-element.96.refs_0_.refs_8_.refs_, ...), custom_call_target="tpu_custom_call" | custom-call | flops 603979776 | bytes 4710400 | tf_op jit(solution)/shard_map/conv_second/pallas_call | solution.py:250
  71.3 8.9 %all_to_all.36.refs_2_ = f32[8,4,128]{2,1,0:T(4,128)S(1)} all-to-all(f32[8,4,128]{2,1,0:T(4,128)S(1)} %get-tuple-element.110), channel_id=1, replica_groups=mesh['dp'=8,'chan'=4] {'dp'}, dimensions={0} | all-to-all | bytes 32768 | tf_op jit(solution)/shard_map/all_to_all | solution.py:741
  80.2 1.5 block_output.1
  81.7 8.9 %all_to_all.37.refs_7_ = f32[8,4,128]{2,1,0:T(4,128)S(1)} all-to-all(f32[8,4,128]{2,1,0:T(4,128)S(1)} %get-tuple-element.122), channel_id=1, replica_groups=mesh['dp'=8,'chan'=4] {'dp'}, dimensions={0} | all-to-all | bytes 32768 | tf_op jit(solution)/shard_map/all_to_all | solution.py:741
  90.7 0.8 grad_outputs.1
  91.5 1.3 collective-permute-start.9
  92.8 3.4 %grad_second.1 = bf16[8,608,128]{2,1,0:T(8,128)(2,1)} custom-call(bf16[512,512]{1,0:T(8,128)(2,1)S(1)} %get-tuple-element.124.refs_0_, bf16[512,128]{1,0:T(8,128)(2,1)} %get-tuple-element.123.refs_1_.refs_4_, bf16[8,2,16,512]{3,2,1,0:T(8,128)(2,1)} %copy-done.2, bf16[8,2,16,512]{3,2,1,0:T(8,128)(2,1)} %copy-done.4, bf16[8,2,16,512]{3,2,1,0:T(8,128)(2,1)} %copy-done.3, ...), custom_call_target="tpu_custom_call" | custom-call | flops 603979776 | bytes 3080192 | tf_op jit(solution)/shard_map/grad_second/pallas_call | solution.py:250
  96.1 0.6 collective-permute-done.9.refs_6_
  96.9 0.5 collective-permute-start.11
  97.4 0.8 collective-permute-done.10.refs_5_
  98.4 3.2 %grad_hidden.1 = (f32[512,128]{1,0:T(8,128)S(1)}, bf16[1040,128]{1,0:T(8,128)(2,1)}, f32[32,2,128]{2,1,0:T(2,128)S(1)}) custom-call(bf16[2,896,128]{2,1,0:T(8,128)(2,1)} %get-tuple-element.127.refs_0_.refs_11_, bf16[2,896,128]{2,1,0:T(8,128)(2,1)S(1)} %collective-permute-done.6.refs_0_.refs_1_.refs_12_, ...), custom_call_target="tpu_custom_call" | custom-call | flops 603979776 | bytes 3465216 | tf_op jit(solution)/shard_map/grad_hidden/pallas_call | solution.py:250
  101.6 1.3 collective-permute-start.12
  102.8 9.0 %all_to_all.38 = f32[32,2,128]{2,1,0:T(2,128)S(1)} all-to-all(f32[32,2,128]{2,1,0:T(2,128)S(1)} %get-tuple-element.132), channel_id=1, replica_groups=mesh['dp'=8,'chan'=4] {'dp','chan'}, dimensions={0} | all-to-all | bytes 65536 | tf_op jit(solution)/shard_map/all_to_all | solution.py:741
  111.8 2.8 %grad_first.1 = (bf16[8,288,128]{2,1,0:T(8,128)(2,1)}, f32[8,128]{1,0:T(8,128)}) custom-call(f32[512,128]{1,0:T(8,128)S(1)} %get-tuple-element.130.refs_0_, bf16[528,128]{1,0:T(8,128)(2,1)} %get-tuple-element.96.refs_0_.refs_8_.refs_1_.refs_4_, f32[8,4,2,128]{3,2,1,0:T(2,128)S(1)} %bitcast.4, f32[4,8,128]{2,1,0:T(8,128)} %get-tuple-element.129.refs_10_.refs_3_.refs_9_, ...), custom_call_target="tpu_custom_call" | custom-call | flops 301989888 | bytes 2354176 | tf_op jit(solution)/shard_map/grad_first/pallas_call | solution.py:250
  114.7 3.6 %all-to-all-start.5 = ((bf16[8,288,128]{2,1,0:T(8,128)(2,1)}), bf16[8,288,128]{2,1,0:T(8,128)(2,1)S(1)}, u32[]{:S(2)}, u32[]{:S(2)}) async-start(bf16[8,288,128]{2,1,0:T(8,128)(2,1)} %get-tuple-element.134), calls=%async_computation.6 | async-start | bytes 1179648 | tf_op jit(solution)/shard_map/all_to_all | solution.py:741
  118.4 0.4 collective-permute-start.14
  118.8 1.0 collective-permute-done.13.refs_1_
  119.9 0.4 collective-permute-done.14.refs_3_
  120.2 4.0 %grad_images.1 = (bf16[2,64,128]{2,1,0:T(8,128)(2,1)}, bf16[2,64,128]{2,1,0:T(8,128)(2,1)}, bf16[2,64,128]{2,1,0:T(8,128)(2,1)}, bf16[2,64,128]{2,1,0:T(8,128)(2...) custom-call(bf16[1040,128]{1,0:T(8,128)(2,1)} %get-tuple-element.131, ...), custom_call_target="tpu_custom_call" | custom-call | flops 301989888 | bytes 4014080 | tf_op jit(solution)/shard_map/grad_images/pallas_call | solution.py:250
  124.3 1.9 %collective-permute-start.15 = (bf16[2,64,128]{2,1,0:T(8,128)(2,1)}, bf16[2,64,128]{2,1,0:T(8,128)(2,1)S(1)}, u32[]{:S(2)}, u32[]{:S(2)}) collective-permute-start(bf16[2,64,128]{2,1,0:T(8,128)(2,1)} %get-tuple-element.141), channel_id=1, source_target_pairs={{0,4},{4,0},{8,12},{12,8},{16,20},{20,16},{24,28},{28,24},{1,5},{5... | collective-permute-start | bytes 98312 | tf_op jit(solution)/shard_map/ppermute | solution.py:754
  126.2 1.5 collective-permute-start.16
  127.8 2.8 %collective-permute-start.18 = (bf16[2,64,128]{2,1,0:T(8,128)(2,1)}, bf16[2,64,128]{2,1,0:T(8,128)(2,1)S(1)}, u32[]{:S(2)}, u32[]{:S(2)}) collective-permute-start(bf16[2,64,128]{2,1,0:T(8,128)(2,1)} %get-tuple-element.144), channel_id=1, source_target_pairs={{0,16},{4,20},{8,24},{12,28},{16,0},{20,4},{24,8},{28,12},{1,17},{... | collective-permute-start | bytes 98312 | tf_op jit(solution)/shard_map/ppermute | solution.py:754
  130.6 1.4 collective-permute-start.19
  132.0 3.3 %collective-permute-start.20 = (bf16[2,64,128]{2,1,0:T(8,128)(2,1)}, bf16[2,64,128]{2,1,0:T(8,128)(2,1)S(1)}, u32[]{:S(2)}, u32[]{:S(2)}) collective-permute-start(bf16[2,64,128]{2,1,0:T(8,128)(2,1)} %get-tuple-element.146), channel_id=1, source_target_pairs={{0,24},{4,28},{8,16},{12,20},{16,8},{20,12},{24,0},{28,4},{1,25},{... | collective-permute-start | bytes 98312 | tf_op jit(solution)/shard_map/ppermute | solution.py:754
  135.5 2.7 %all-to-all-done.5.refs_1_ = bf16[8,288,128]{2,1,0:T(8,128)(2,1)S(1)} async-done(((bf16[8,288,128]{2,1,0:T(8,128)(2,1)}), bf16[8,288,128]{2,1,0:T(8,128)(2,1)S(1)}, u32[]{:S(2)}, u32[]{:S(2)}) %all-to-all-start.5) | async-done | bytes 589856 | tf_op jit(solution)/shard_map/all_to_all | solution.py:741
  138.2 2.1 %reduce_all.1 = (f32[288,128]{1,0:T(8,128)}, f32[576,128]{1,0:T(8,128)}, f32[32,128]{1,0:T(8,128)}, f32[32,1,128]{2,1,0:T(1,128)}) custom-call(bf16[608,128]{1,0:T(8,128)(2,1)} %reduce-scatter.2.cloned.1.call-done.refs_0_, bf16[8,288,128]{2,1,0:T(8,128)(2,1)S(1)} %all-to-all-done.5.refs_1_, f32[8,128]{1,0:T(8,128)} %get-tuple-element.135.refs_2_, ...), custom_call_target="tpu_custom_call" | custom-call | bytes 1235968 | tf_op jit(solution)/shard_map/reduce_all/pallas_call | solution.py:250
  140.4 1.8 %collective-permute-done.21.refs_7_ = bf16[2,64,128]{2,1,0:T(8,128)(2,1)S(1)} collective-permute-done((bf16[2,64,128]{2,1,0:T(8,128)(2,1)}, bf16[2,64,128]{2,1,0:T(8,128)(2,1)S(1)}, u32[]{:S(2)}, u32[]{:S(2)}) %collective-permute-start.21) | collective-permute-done | bytes 32800 | tf_op jit(solution)/shard_map/ppermute | solution.py:754
  142.2 2.5 %all-to-all-start.6 = ((f32[32,1,128]{2,1,0:T(1,128)}), f32[32,1,128]{2,1,0:T(1,128)S(1)}, u32[]{:S(2)}, u32[]{:S(2)}) async-start(f32[32,1,128]{2,1,0:T(1,128)} %get-tuple-element.156), calls=%async_computation.7 | async-start | bytes 32768 | tf_op jit(solution)/shard_map/all_to_all | solution.py:741
  144.7 1.9 %finish_images.1 = bf16[64,32,64]{2,1,0:T(8,128)(2,1)} custom-call(bf16[2,64,128]{2,1,0:T(8,128)(2,1)} %get-tuple-element.148.refs_0_, bf16[2,64,128]{2,1,0:T(8,128)(2,1)S(1)} %collective-permute-done.15.refs_1_, bf16[2,64,128]{2,1,0:T(8,128)(2,1)S(1)} %collective-permute-done.16.refs_2_, bf16[2,64,128]{2,1,0:T(8,128)(2,1)S(1)} %collective-permute-done.17.refs_3_, ...), custom_call_target="tpu_custom_call" | custom-call | bytes 524288 | tf_op jit(solution)/shard_map/finish_images/pallas_call | solution.py:250
  146.6 5.2 %all-to-all-done.6.refs_0_ = f32[32,1,128]{2,1,0:T(1,128)S(1)} async-done(((f32[32,1,128]{2,1,0:T(1,128)}), f32[32,1,128]{2,1,0:T(1,128)S(1)}, u32[]{:S(2)}, u32[]{:S(2)}) %all-to-all-start.6) | async-done | bytes 16416 | tf_op jit(solution)/shard_map/all_to_all | solution.py:741
  151.8 2.9 %update.1 = (f32[288,128]{1,0:T(8,128)}, f32[288,128]{1,0:T(8,128)}, f32[288,128]{1,0:T(8,128)}, f32[576,128]{1,0:T(8,128)}, f32[576,128]{1,0:T(8,128)}, /*index...) custom-call(f32[32,1,128]{2,1,0:T(1,128)S(1)} %all-to-all-done.6.ref, ...), custom_call_target="tpu_custom_call" | custom-call | bytes 3254272 | tf_op jit(solution)/shard_map/update/pallas_call | solution.py:250
  (42 shorter events, 1.3 us)
Async XLA Ops:
  7.2 42.4 %all-gather.3.cloned.1.call-start = ((), (), s32[]{:S(2)}) async-start(), calls=%async_computation.9 | async-start | bytes 2064384 | tf_op jit(solution)/shard_map/all_gather | solution.py:808
  9.1 0.9 copy-start.1
  32.6 17.0 %copy-start.2 = (bf16[8,2,16,512]{3,2,1,0:T(8,128)(2,1)}, bf16[8,2,16,512]{3,2,1,0:T(8,128)(2,1)S(1)}, u32[]{:S(2)}) copy-start(bf16[8,2,16,512]{3,2,1,0:T(8,128)(2,1)S(1)} %all_to_all.35.refs_1_.refs_2_.refs_6_) | copy-start | bytes 786436
  32.6 6.4 %collective-permute-start.1 = (bf16[8,2,16,512]{3,2,1,0:T(8,128)(2,1)S(1)}, bf16[8,2,16,512]{3,2,1,0:T(8,128)(2,1)S(1)}, u32[]{:S(2)}, u32[]{:S(2)}) collective-permute-start(bf16[8,2,16,512]{3,2,1,0:T(8,128)(2,1)S(1)} %all_to_all.35.refs_1_.refs_2_.refs_6_), channel_id=1, source_target_pairs={{0,2},{1,3},{2,0},{3,1},{4,6},{5,7},{6,4},{7,5},{8,10},{9,11},{10,... | collective-permute-start | bytes 786440 | tf_op jit(solution)/shard_map/ppermute | solution.py:754
  34.0 4.9 %collective-permute-start = (bf16[8,2,16,512]{3,2,1,0:T(8,128)(2,1)S(1)}, bf16[8,2,16,512]{3,2,1,0:T(8,128)(2,1)S(1)}, u32[]{:S(2)}, u32[]{:S(2)}) collective-permute-start(bf16[8,2,16,512]{3,2,1,0:T(8,128)(2,1)S(1)} %all_to_all.35.refs_1_.refs_2_.refs_6_), channel_id=1, source_target_pairs={{0,1},{1,0},{2,3},{3,2},{4,5},{5,4},{6,7},{7,6},{8,9},{9,8},{10,11... | collective-permute-start | bytes 786440 | tf_op jit(solution)/shard_map/ppermute | solution.py:754
  38.9 10.6 %copy-start.3 = (bf16[8,2,16,512]{3,2,1,0:T(8,128)(2,1)}, bf16[8,2,16,512]{3,2,1,0:T(8,128)(2,1)S(1)}, u32[]{:S(2)}) copy-start(bf16[8,2,16,512]{3,2,1,0:T(8,128)(2,1)S(1)} %collective-permute-done.1.refs_3_.refs_4_.refs_8_) | copy-start | bytes 786436
  38.9 1.5 collective-permute-start.2
  38.9 10.6 %copy-start.4 = (bf16[8,2,16,512]{3,2,1,0:T(8,128)(2,1)}, bf16[8,2,16,512]{3,2,1,0:T(8,128)(2,1)S(1)}, u32[]{:S(2)}) copy-start(bf16[8,2,16,512]{3,2,1,0:T(8,128)(2,1)S(1)} %collective-permute-done.refs_2_.refs_3_.refs_7_) | copy-start | bytes 786436
  40.5 9.1 %copy-start.5 = (bf16[8,2,16,512]{3,2,1,0:T(8,128)(2,1)}, bf16[8,2,16,512]{3,2,1,0:T(8,128)(2,1)S(1)}, u32[]{:S(2)}) copy-start(bf16[8,2,16,512]{3,2,1,0:T(8,128)(2,1)S(1)} %collective-permute-done.2.refs_4_.refs_5_.refs_9_) | copy-start | bytes 786436
  52.6 12.9 %collective-permute-start.5 = (bf16[528,128]{1,0:T(8,128)(2,1)}, bf16[528,128]{1,0:T(8,128)(2,1)S(1)}, u32[]{:S(2)}, u32[]{:S(2)}) collective-permute-start(bf16[528,128]{1,0:T(8,128)(2,1)} %get-tuple-element.96.refs_0_.refs_8_.refs_1_.refs_4_), channel_id=1, source_target_pairs={{0,3},{1,2},{2,1},{3,0},{4,7},{5,6},{6,5},{7,4},{8,11},{9,10},{10,... | collective-permute-start | bytes 405512 | tf_op jit(solution)/shard_map/ppermute | solution.py:754
  52.7 12.8 %collective-permute-start.4 = (bf16[528,128]{1,0:T(8,128)(2,1)}, bf16[528,128]{1,0:T(8,128)(2,1)S(1)}, u32[]{:S(2)}, u32[]{:S(2)}) collective-permute-start(bf16[528,128]{1,0:T(8,128)(2,1)} %get-tuple-element.96.refs_0_.refs_8_.refs_1_.refs_4_), channel_id=1, source_target_pairs={{0,2},{1,3},{2,0},{3,1},{4,6},{5,7},{6,4},{7,5},{8,10},{9,11},{10,... | collective-permute-start | bytes 405512 | tf_op jit(solution)/shard_map/ppermute | solution.py:754
  54.2 11.3 %collective-permute-start.3 = (bf16[528,128]{1,0:T(8,128)(2,1)}, bf16[528,128]{1,0:T(8,128)(2,1)S(1)}, u32[]{:S(2)}, u32[]{:S(2)}) collective-permute-start(bf16[528,128]{1,0:T(8,128)(2,1)} %get-tuple-element.96.refs_0_.refs_8_.refs_1_.refs_4_), channel_id=1, source_target_pairs={{0,1},{1,0},{2,3},{3,2},{4,5},{5,4},{6,7},{7,6},{8,9},{9,8},{10,11... | collective-permute-start | bytes 405512 | tf_op jit(solution)/shard_map/ppermute | solution.py:754
  54.6 11.0 %all-to-all-start.1 = ((f32[32,4,128]{2,1,0:T(4,128)}), f32[32,4,128]{2,1,0:T(4,128)S(1)}, u32[]{:S(2)}, u32[]{:S(2)}) async-start(f32[32,4,128]{2,1,0:T(4,128)} %get-tuple-element.97), calls=%async_computation.1 | async-start | bytes 131072 | tf_op jit(solution)/shard_map/all_to_all | solution.py:741
  58.1 80.1 %reduce-scatter.2.cloned.1.call-start = ((), (), s32[]{:S(2)}) async-start(), calls=%async_computation.8 | async-start | bytes 1400832 | tf_op jit(solution)/shard_map/reduce_scatter | solution.py:914
  58.2 0.9 copy-start
  65.5 25.1 %collective-permute-start.6 = (bf16[2,896,128]{2,1,0:T(8,128)(2,1)}, bf16[2,896,128]{2,1,0:T(8,128)(2,1)S(1)}, u32[]{:S(2)}, u32[]{:S(2)}) collective-permute-start(bf16[2,896,128]{2,1,0:T(8,128)(2,1)} %get-tuple-element.115), channel_id=1, source_target_pairs={{0,1},{1,0},{2,3},{3,2},{4,5},{5,4},{6,7},{7,6},{8,9},{9,8},{10,11... | collective-permute-start | bytes 1376264 | tf_op jit(solution)/shard_map/ppermute | solution.py:754
  65.7 25.0 %collective-permute-start.7 = (bf16[2,896,128]{2,1,0:T(8,128)(2,1)}, bf16[2,896,128]{2,1,0:T(8,128)(2,1)S(1)}, u32[]{:S(2)}, u32[]{:S(2)}) collective-permute-start(bf16[2,896,128]{2,1,0:T(8,128)(2,1)} %get-tuple-element.116), channel_id=1, source_target_pairs={{0,2},{1,3},{2,0},{3,1},{4,6},{5,7},{6,4},{7,5},{8,10},{9,11},{10,... | collective-permute-start | bytes 1376264 | tf_op jit(solution)/shard_map/ppermute | solution.py:754
  66.2 24.5 %collective-permute-start.8 = (bf16[2,896,128]{2,1,0:T(8,128)(2,1)}, bf16[2,896,128]{2,1,0:T(8,128)(2,1)S(1)}, u32[]{:S(2)}, u32[]{:S(2)}) collective-permute-start(bf16[2,896,128]{2,1,0:T(8,128)(2,1)} %get-tuple-element.117), channel_id=1, source_target_pairs={{0,3},{1,2},{2,1},{3,0},{4,7},{5,6},{6,5},{7,4},{8,11},{9,10},{10,... | collective-permute-start | bytes 1376264 | tf_op jit(solution)/shard_map/ppermute | solution.py:754
  91.5 5.2 %collective-permute-start.9 = (bf16[512,128]{1,0:T(8,128)(2,1)}, bf16[512,128]{1,0:T(8,128)(2,1)S(1)}, u32[]{:S(2)}, u32[]{:S(2)}) collective-permute-start(bf16[512,128]{1,0:T(8,128)(2,1)} %get-tuple-element.123.refs_1_.refs_4_), channel_id=1, source_target_pairs={{0,2},{1,3},{2,0},{3,1},{4,6},{5,7},{6,4},{7,5},{8,10},{9,11},{10,... | collective-permute-start | bytes 393224 | tf_op jit(solution)/shard_map/ppermute | solution.py:754
  92.8 4.0 %copy-start.6 = (bf16[512,128]{1,0:T(8,128)(2,1)S(1)}, bf16[512,128]{1,0:T(8,128)(2,1)}, u32[]{:S(2)}) copy-start(bf16[512,128]{1,0:T(8,128)(2,1)} %get-tuple-element.123.refs_1_.refs_4_) | copy-start | bytes 393220
  96.8 1.4 collective-permute-start.10
  96.9 1.5 collective-permute-start.11
  101.6 16.7 %copy-start.7 = (bf16[1040,128]{1,0:T(8,128)(2,1)S(1)}, bf16[1040,128]{1,0:T(8,128)(2,1)}, u32[]{:S(2)}) copy-start(bf16[1040,128]{1,0:T(8,128)(2,1)} %get-tuple-element.131.refs_0_) | copy-start | bytes 798724
  101.6 10.3 %collective-permute-start.12 = (bf16[1040,128]{1,0:T(8,128)(2,1)}, bf16[1040,128]{1,0:T(8,128)(2,1)S(1)}, u32[]{:S(2)}, u32[]{:S(2)}) collective-permute-start(bf16[1040,128]{1,0:T(8,128)(2,1)} %get-tuple-element.131.refs_0_), channel_id=1, source_target_pairs={{0,2},{1,3},{2,0},{3,1},{4,6},{5,7},{6,4},{7,5},{8,10},{9,11},{10,... | collective-permute-start | bytes 798728 | tf_op jit(solution)/shard_map/ppermute | solution.py:754
  114.7 23.5 %all-to-all-start.5 = ((bf16[8,288,128]{2,1,0:T(8,128)(2,1)}), bf16[8,288,128]{2,1,0:T(8,128)(2,1)S(1)}, u32[]{:S(2)}, u32[]{:S(2)}) async-start(bf16[8,288,128]{2,1,0:T(8,128)(2,1)} %get-tuple-element.134), calls=%async_computation.6 | async-start | bytes 1179648 | tf_op jit(solution)/shard_map/all_to_all | solution.py:741
  118.3 1.6 collective-permute-start.13
  118.4 1.8 %collective-permute-start.14 = (bf16[1040,128]{1,0:T(8,128)(2,1)S(1)}, bf16[1040,128]{1,0:T(8,128)(2,1)S(1)}, u32[]{:S(2)}, u32[]{:S(2)}) collective-permute-start(bf16[1040,128]{1,0:T(8,128)(2,1)S(1)} %collective-permute-done.12.refs_2_), channel_id=1, source_target_pairs={{0,1},{1,0},{2,3},{3,2},{4,5},{5,4},{6,7},{7,6},{8,9},{9,8},{10,11... | collective-permute-start | bytes 798728 | tf_op jit(solution)/shard_map/ppermute | solution.py:754
  124.3 7.8 %collective-permute-start.15 = (bf16[2,64,128]{2,1,0:T(8,128)(2,1)}, bf16[2,64,128]{2,1,0:T(8,128)(2,1)S(1)}, u32[]{:S(2)}, u32[]{:S(2)}) collective-permute-start(bf16[2,64,128]{2,1,0:T(8,128)(2,1)} %get-tuple-element.141), channel_id=1, source_target_pairs={{0,4},{4,0},{8,12},{12,8},{16,20},{20,16},{24,28},{28,24},{1,5},{5... | collective-permute-start | bytes 98312 | tf_op jit(solution)/shard_map/ppermute | solution.py:754
  126.2 9.2 %collective-permute-start.16 = (bf16[2,64,128]{2,1,0:T(8,128)(2,1)}, bf16[2,64,128]{2,1,0:T(8,128)(2,1)S(1)}, u32[]{:S(2)}, u32[]{:S(2)}) collective-permute-start(bf16[2,64,128]{2,1,0:T(8,128)(2,1)} %get-tuple-element.142), channel_id=1, source_target_pairs={{0,8},{4,12},{8,0},{12,4},{16,24},{20,28},{24,16},{28,20},{1,9},{5... | collective-permute-start | bytes 98312 | tf_op jit(solution)/shard_map/ppermute | solution.py:754
  127.7 12.6 %collective-permute-start.17 = (bf16[2,64,128]{2,1,0:T(8,128)(2,1)}, bf16[2,64,128]{2,1,0:T(8,128)(2,1)S(1)}, u32[]{:S(2)}, u32[]{:S(2)}) collective-permute-start(bf16[2,64,128]{2,1,0:T(8,128)(2,1)} %get-tuple-element.143), channel_id=1, source_target_pairs={{0,12},{4,8},{8,4},{12,0},{16,28},{20,24},{24,20},{28,16},{1,13},{... | collective-permute-start | bytes 98312 | tf_op jit(solution)/shard_map/ppermute | solution.py:754
  127.8 12.5 %collective-permute-start.18 = (bf16[2,64,128]{2,1,0:T(8,128)(2,1)}, bf16[2,64,128]{2,1,0:T(8,128)(2,1)S(1)}, u32[]{:S(2)}, u32[]{:S(2)}) collective-permute-start(bf16[2,64,128]{2,1,0:T(8,128)(2,1)} %get-tuple-element.144), channel_id=1, source_target_pairs={{0,16},{4,20},{8,24},{12,28},{16,0},{20,4},{24,8},{28,12},{1,17},{... | collective-permute-start | bytes 98312 | tf_op jit(solution)/shard_map/ppermute | solution.py:754
  130.6 9.8 %collective-permute-start.19 = (bf16[2,64,128]{2,1,0:T(8,128)(2,1)}, bf16[2,64,128]{2,1,0:T(8,128)(2,1)S(1)}, u32[]{:S(2)}, u32[]{:S(2)}) collective-permute-start(bf16[2,64,128]{2,1,0:T(8,128)(2,1)} %get-tuple-element.145), channel_id=1, source_target_pairs={{0,20},{4,16},{8,28},{12,24},{16,4},{20,0},{24,12},{28,8},{1,21},{... | collective-permute-start | bytes 98312 | tf_op jit(solution)/shard_map/ppermute | solution.py:754
  132.0 8.3 %collective-permute-start.20 = (bf16[2,64,128]{2,1,0:T(8,128)(2,1)}, bf16[2,64,128]{2,1,0:T(8,128)(2,1)S(1)}, u32[]{:S(2)}, u32[]{:S(2)}) collective-permute-start(bf16[2,64,128]{2,1,0:T(8,128)(2,1)} %get-tuple-element.146), channel_id=1, source_target_pairs={{0,24},{4,28},{8,16},{12,20},{16,8},{20,12},{24,0},{28,4},{1,25},{... | collective-permute-start | bytes 98312 | tf_op jit(solution)/shard_map/ppermute | solution.py:754
  135.3 6.8 %collective-permute-start.21 = (bf16[2,64,128]{2,1,0:T(8,128)(2,1)}, bf16[2,64,128]{2,1,0:T(8,128)(2,1)S(1)}, u32[]{:S(2)}, u32[]{:S(2)}) collective-permute-start(bf16[2,64,128]{2,1,0:T(8,128)(2,1)} %get-tuple-element.147), channel_id=1, source_target_pairs={{0,28},{4,24},{8,20},{12,16},{16,12},{20,8},{24,4},{28,0},{1,29},{... | collective-permute-start | bytes 98312 | tf_op jit(solution)/shard_map/ppermute | solution.py:754
  142.2 9.6 %all-to-all-start.6 = ((f32[32,1,128]{2,1,0:T(1,128)}), f32[32,1,128]{2,1,0:T(1,128)S(1)}, u32[]{:S(2)}, u32[]{:S(2)}) async-start(f32[32,1,128]{2,1,0:T(1,128)} %get-tuple-element.156), calls=%async_computation.7 | async-start | bytes 32768 | tf_op jit(solution)/shard_map/all_to_all | solution.py:741
Sparse Core Ops, SparseCore 0:
  10.1 39.3 all-gather.2
  96.9 27.8 reduce-scatter.1

commit v6 on v5

--- a/solution.py
+++ b/solution.py
@@ -982,7 +982,12 @@
             result((n_all, 1, wide)),
         ],
     )
-    pay, *rows = lax.optimization_barrier((pay, *rows))
+    if eight:
+        order = (0, 1, 2, 4, 5, 7, 3, 6)
+        *sent, pay = lax.optimization_barrier((*(rows[k] for k in order), pay))
+        rows = [sent[order.index(k)] for k in range(SIDE)]
+    else:
+        pay, *rows = lax.optimization_barrier((pay, *rows))
     got6 = exchange(pay, everyone)
 
     conv = (

time: 162 us -> 161 us (level)
    ppermute x22, waiting for transfers between devices: 11.4 us -> 9.49 us  [swap(): lax.ppermute(array, axis, [(i, i ^ bits) for i in range(lax.axis_size(axi...]
  transfers between devices with their start and end apart: 27 -> 27, of which waited for: 13 -> 11; matrix products, arithmetic and copies ran while one was open for 0% -> 0% of each run, Pallas kernels for 17% -> 17%
where the time goes in v6:
time: 161 us; the launch traced here: 160 us
  blocking collectives  47.4 us (29%)
  Pallas kernels  36.1 us (22%)
  waiting for transfers between devices  30.6 us (19%)
  starting transfers between devices  29.8 us (19%)
  between operations  14.3 us (9%)
  local copies, waits for them, and re-layouts  1.86 us (1%)
    all_to_all x4, blocking collectives, exchange(): return lax.all_to_all(blocks, axes, 0, 0)  47.4 us
    pallas_call x14, Pallas kernels, call(): pl.pallas_call(kernel, out_shape=[pltpu.HBM(o.shape, o.dtype) if g.pinned...  36.1 us
    ppermute x22, starting transfers between devices, swap(): lax.ppermute(array, axis, [(i, i ^ bits) for i in range(lax.axis_size(axi...  20.1 us
    all_to_all x3, waiting for transfers between devices, exchange(): return lax.all_to_all(blocks, axes, 0, 0)  12 us
    all_to_all x3, starting transfers between devices, exchange(): return lax.all_to_all(blocks, axes, 0, 0)  9.66 us
    ppermute x22, waiting for transfers between devices, swap(): lax.ppermute(array, axis, [(i, i ^ bits) for i in range(lax.axis_size(axi...  9.49 us
    all_gather x1, waiting for transfers between devices, per_device(): gathered = lax.all_gather(own, everyone, axis_index_groups=rings())  9.06 us
  transfers between devices with their start and end apart: 27, of which 11 were waited for; matrix products, arithmetic and copies ran while one was open for 0% of the time, Pallas kernels for 17%

profile of v6, /device:TPU:0, one launch (start us, length us, event | category | flops | bytes accessed | tf_op | source)
XLA Modules:
  0.0 160.1 jit_solution(10212883247666835179)
XLA Ops:
  7.2 1.8 %pack_weights.1 = (bf16[896,128]{1,0:T(8,128)(2,1)}, f32[8,128]{1,0:T(8,128)}) custom-call(f32[288,128]{1,0:T(8,128)} %refs_3_.1, f32[32,128]{1,0:T(8,128)} %refs_11_.1, f32[576,128]{1,0:T(8,128)} %refs_7_.1), custom_call_target="tpu_custom_call" | custom-call | bytes 692224 | tf_op jit(solution)/shard_map/pack_weights/pallas_call | solution.py:250
  9.1 0.9 copy-done.1
  10.0 2.0 %pack_images.1 = (bf16[8,2,16,512]{3,2,1,0:T(8,128)(2,1)}, f32[512,128]{1,0:T(8,128)}) custom-call(bf16[896,128]{1,0:T(8,128)(2,1)S(1)} %copy-done.1, bf16[64,32,256]{2,1,0:T(8,128)(2,1)} %refs_1_.3, s32[8,64]{1,0:T(8,128)} %refs_2_.3), custom_call_target="tpu_custom_call" | custom-call | bytes 1574912 | tf_op jit(solution)/shard_map/pack_images/pallas_call | solution.py:250
  12.1 20.5 %all_to_all.35.refs_1_.refs_2_.refs_6_ = bf16[8,2,16,512]{3,2,1,0:T(8,128)(2,1)S(1)} all-to-all(bf16[8,2,16,512]{3,2,1,0:T(8,128)(2,1)} %get-tuple-element.94), channel_id=1, replica_groups=mesh['dp'=8,'chan'=4] {'dp'}, dimensions={0} | all-to-all | bytes 524288 | tf_op jit(solution)/shard_map/all_to_all | solution.py:741
  32.6 1.5 collective-permute-start.1
  34.0 4.9 %collective-permute-done.1.refs_3_.refs_4_.refs_8_ = bf16[8,2,16,512]{3,2,1,0:T(8,128)(2,1)S(1)} collective-permute-done((bf16[8,2,16,512]{3,2,1,0:T(8,128)(2,1)S(1)}, bf16[8,2,16,512]{3,2,1,0:T(8,128)(2,1)S(1)}, u32[]{:S(2)}, u32[]{:S(2)}) %collective-permute-start.1) | collective-permute-done | bytes 262176 | tf_op jit(solution)/shard_map/ppermute | solution.py:754
  39.0 1.5 collective-permute-done.2.refs_4_.refs_5_.refs_9_
  40.5 9.1 %all-gather.3.cloned.1.call-done = bf16[7168,128]{1,0:T(8,128)(2,1)} async-done(((bf16[896,128]{1,0:T(8,128)(2,1)}), bf16[7168,128]{1,0:T(8,128)(2,1)}) %all-gather.3.cloned.1.call-update) | async-done | bytes 1835024 | tf_op jit(solution)/shard_map/all_gather | solution.py:808
  49.5 3.1 %conv_first.1 = (bf16[528,128]{1,0:T(8,128)(2,1)}, f32[512,128]{1,0:T(8,128)}, f32[8,128]{1,0:T(8,128)}, f32[32,4,128]{2,1,0:T(4,128)}) custom-call(bf16[8,896,128]{2,1,0:T(8,128)(2,1)} %bitcast.7, bf16[8,2,16,512]{3,2,1,0:T(8,128)(2,1)} %copy-done.2, bf16[8,2,16,512]{3,2,1,0:T(8,128)(2,1)} %copy-done.4, bf16[8,2,16,512]{3,2,1,0:T(8,128)(2,1)} %copy-done.3, ...), custom_call_target="tpu_custom_call" | custom-call | flops 301989888 | bytes 3615744 | tf_op jit(solution)/shard_map/conv_first/pallas_call | solution.py:250
  52.7 1.5 collective-permute-start.4
  54.6 3.6 %all-to-all-start.1 = ((f32[32,4,128]{2,1,0:T(4,128)}), f32[32,4,128]{2,1,0:T(4,128)S(1)}, u32[]{:S(2)}, u32[]{:S(2)}) async-start(f32[32,4,128]{2,1,0:T(4,128)} %get-tuple-element.97), calls=%async_computation.1 | async-start | bytes 131072 | tf_op jit(solution)/shard_map/all_to_all | solution.py:741
  58.2 0.9 copy-done
  59.1 2.9 %hand_on.1 = (bf16[2,896,128]{2,1,0:T(8,128)(2,1)}, bf16[2,896,128]{2,1,0:T(8,128)(2,1)}, bf16[2,896,128]{2,1,0:T(8,128)(2,1)}, bf16[2,896,128]{2,1,0:T(8,128)(2,1)}) custom-call(bf16[528,128]{1,0:T(8,128)(2,1)S(1)} %copy-done, bf16[8,896,128]{2,1,0:T(8,128)(2,1)} %bitcast.8), custom_call_target="tpu_custom_call" | custom-call | bytes 3670016 | tf_op jit(solution)/shard_map/hand_on/pallas_call | solution.py:250
  61.9 3.6 %all-to-all-done.1 = f32[32,4,128]{2,1,0:T(4,128)S(1)} async-done(((f32[32,4,128]{2,1,0:T(4,128)}), f32[32,4,128]{2,1,0:T(4,128)S(1)}, u32[]{:S(2)}, u32[]{:S(2)}) %all-to-all-start.1) | async-done | bytes 65568 | tf_op jit(solution)/shard_map/all_to_all | solution.py:741
  65.7 0.5 collective-permute-start.7
  66.2 1.3 collective-permute-start.8
  67.5 3.8 %conv_second.1 = (bf16[512,512]{1,0:T(8,128)(2,1)S(1)}, f32[512,128]{1,0:T(8,128)S(1)}, f32[8,4,128]{2,1,0:T(4,128)S(1)}, f32[4,8,128]{2,1,0:T(8,128)}, f32[512,...) custom-call(bf16[528,128]{1,0:T(8,128)(2,1)} %get-tuple-element.96.refs_0_.refs_8_.refs_, ...), custom_call_target="tpu_custom_call" | custom-call | flops 603979776 | bytes 4710400 | tf_op jit(solution)/shard_map/conv_second/pallas_call | solution.py:250
  71.3 8.9 %all_to_all.36.refs_2_ = f32[8,4,128]{2,1,0:T(4,128)S(1)} all-to-all(f32[8,4,128]{2,1,0:T(4,128)S(1)} %get-tuple-element.110), channel_id=1, replica_groups=mesh['dp'=8,'chan'=4] {'dp'}, dimensions={0} | all-to-all | bytes 32768 | tf_op jit(solution)/shard_map/all_to_all | solution.py:741
  80.2 1.5 block_output.1
  81.7 8.9 %all_to_all.37.refs_7_ = f32[8,4,128]{2,1,0:T(4,128)S(1)} all-to-all(f32[8,4,128]{2,1,0:T(4,128)S(1)} %get-tuple-element.123), channel_id=1, replica_groups=mesh['dp'=8,'chan'=4] {'dp'}, dimensions={0} | all-to-all | bytes 32768 | tf_op jit(solution)/shard_map/all_to_all | solution.py:741
  90.7 0.8 grad_outputs.1
  91.5 1.3 collective-permute-start.10
  92.8 3.4 %grad_second.1 = bf16[8,608,128]{2,1,0:T(8,128)(2,1)} custom-call(bf16[512,512]{1,0:T(8,128)(2,1)S(1)} %get-tuple-element.125.refs_0_, bf16[512,128]{1,0:T(8,128)(2,1)} %get-tuple-element.124.refs_1_.refs_4_, bf16[8,2,16,512]{3,2,1,0:T(8,128)(2,1)} %copy-done.2, bf16[8,2,16,512]{3,2,1,0:T(8,128)(2,1)} %copy-done.4, bf16[8,2,16,512]{3,2,1,0:T(8,128)(2,1)} %copy-done.3, ...), custom_call_target="tpu_custom_call" | custom-call | flops 603979776 | bytes 3080192 | tf_op jit(solution)/shard_map/grad_second/pallas_call | solution.py:250
  96.1 0.6 collective-permute-done.10.refs_6_
  96.9 0.5 collective-permute-start.11
  97.4 0.8 collective-permute-done.9.refs_5_
  98.4 3.2 %grad_hidden.1 = (f32[512,128]{1,0:T(8,128)S(1)}, bf16[1040,128]{1,0:T(8,128)(2,1)}, f32[32,2,128]{2,1,0:T(2,128)S(1)}) custom-call(bf16[2,896,128]{2,1,0:T(8,128)(2,1)} %get-tuple-element.115.refs_0_.refs_11_, bf16[2,896,128]{2,1,0:T(8,128)(2,1)S(1)} %collective-permute-done.6.refs_0_.refs_1_.refs_12_, ...), custom_call_target="tpu_custom_call" | custom-call | flops 603979776 | bytes 3465216 | tf_op jit(solution)/shard_map/grad_hidden/pallas_call | solution.py:250
  101.6 1.3 collective-permute-start.13
  102.8 9.0 %all_to_all.38 = f32[32,2,128]{2,1,0:T(2,128)S(1)} all-to-all(f32[32,2,128]{2,1,0:T(2,128)S(1)} %get-tuple-element.130), channel_id=1, replica_groups=mesh['dp'=8,'chan'=4] {'dp','chan'}, dimensions={0} | all-to-all | bytes 65536 | tf_op jit(solution)/shard_map/all_to_all | solution.py:741
  111.8 2.8 %grad_first.1 = (bf16[8,288,128]{2,1,0:T(8,128)(2,1)}, f32[8,128]{1,0:T(8,128)}) custom-call(f32[512,128]{1,0:T(8,128)S(1)} %get-tuple-element.142.refs_0_, bf16[528,128]{1,0:T(8,128)(2,1)} %get-tuple-element.96.refs_0_.refs_8_.refs_4_.refs_1_, f32[8,4,2,128]{3,2,1,0:T(2,128)S(1)} %bitcast.4, f32[4,8,128]{2,1,0:T(8,128)} %get-tuple-element.128.refs_10_.refs_9_.refs_3_, ...), custom_call_target="tpu_custom_call" | custom-call | flops 301989888 | bytes 2354176 | tf_op jit(solution)/shard_map/grad_first/pallas_call | solution.py:250
  114.7 3.6 %all-to-all-start.5 = ((bf16[8,288,128]{2,1,0:T(8,128)(2,1)}), bf16[8,288,128]{2,1,0:T(8,128)(2,1)S(1)}, u32[]{:S(2)}, u32[]{:S(2)}) async-start(bf16[8,288,128]{2,1,0:T(8,128)(2,1)} %get-tuple-element.143), calls=%async_computation.6 | async-start | bytes 1179648 | tf_op jit(solution)/shard_map/all_to_all | solution.py:741
  118.4 0.4 collective-permute-start.14
  118.8 1.0 collective-permute-done.12.refs_1_
  119.9 0.4 collective-permute-done.14.refs_3_
  120.2 4.0 %grad_images.1 = (bf16[2,64,128]{2,1,0:T(8,128)(2,1)}, bf16[2,64,128]{2,1,0:T(8,128)(2,1)}, bf16[2,64,128]{2,1,0:T(8,128)(2,1)}, bf16[2,64,128]{2,1,0:T(8,128)(2...) custom-call(bf16[1040,128]{1,0:T(8,128)(2,1)} %get-tuple-element.129, ...), custom_call_target="tpu_custom_call" | custom-call | flops 301989888 | bytes 4014080 | tf_op jit(solution)/shard_map/grad_images/pallas_call | solution.py:250
  124.3 1.9 %collective-permute-start.15 = (bf16[2,64,128]{2,1,0:T(8,128)(2,1)}, bf16[2,64,128]{2,1,0:T(8,128)(2,1)S(1)}, u32[]{:S(2)}, u32[]{:S(2)}) collective-permute-start(bf16[2,64,128]{2,1,0:T(8,128)(2,1)} %get-tuple-element.134), channel_id=1, source_target_pairs={{0,4},{4,0},{8,12},{12,8},{16,20},{20,16},{24,28},{28,24},{1,5},{5... | collective-permute-start | bytes 98312 | tf_op jit(solution)/shard_map/ppermute | solution.py:754
  126.2 1.5 collective-permute-start.16
  127.7 2.4 %collective-permute-start.17 = (bf16[2,64,128]{2,1,0:T(8,128)(2,1)}, bf16[2,64,128]{2,1,0:T(8,128)(2,1)S(1)}, u32[]{:S(2)}, u32[]{:S(2)}) collective-permute-start(bf16[2,64,128]{2,1,0:T(8,128)(2,1)} %get-tuple-element.136), channel_id=1, source_target_pairs={{0,16},{4,20},{8,24},{12,28},{16,0},{20,4},{24,8},{28,12},{1,17},{... | collective-permute-start | bytes 98312 | tf_op jit(solution)/shard_map/ppermute | solution.py:754
  130.0 0.5 collective-permute-start.18
  130.6 3.3 %collective-permute-start.19 = (bf16[2,64,128]{2,1,0:T(8,128)(2,1)}, bf16[2,64,128]{2,1,0:T(8,128)(2,1)S(1)}, u32[]{:S(2)}, u32[]{:S(2)}) collective-permute-start(bf16[2,64,128]{2,1,0:T(8,128)(2,1)} %get-tuple-element.138), channel_id=1, source_target_pairs={{0,28},{4,24},{8,20},{12,16},{16,12},{20,8},{24,4},{28,0},{1,29},{... | collective-permute-start | bytes 98312 | tf_op jit(solution)/shard_map/ppermute | solution.py:754
  133.9 0.6 collective-permute-start.20
  134.4 0.9 collective-permute-start.21
  135.4 3.2 %all-to-all-done.5.refs_1_ = bf16[8,288,128]{2,1,0:T(8,128)(2,1)S(1)} async-done(((bf16[8,288,128]{2,1,0:T(8,128)(2,1)}), bf16[8,288,128]{2,1,0:T(8,128)(2,1)S(1)}, u32[]{:S(2)}, u32[]{:S(2)}) %all-to-all-start.5) | async-done | bytes 589856 | tf_op jit(solution)/shard_map/all_to_all | solution.py:741
  138.6 2.1 %reduce_all.1 = (f32[288,128]{1,0:T(8,128)}, f32[576,128]{1,0:T(8,128)}, f32[32,128]{1,0:T(8,128)}, f32[32,1,128]{2,1,0:T(1,128)}) custom-call(bf16[608,128]{1,0:T(8,128)(2,1)} %reduce-scatter.2.cloned.1.call-done.refs_0_, bf16[8,288,128]{2,1,0:T(8,128)(2,1)S(1)} %all-to-all-done.5.refs_1_, f32[8,128]{1,0:T(8,128)} %get-tuple-element.144.refs_2_, ...), custom_call_target="tpu_custom_call" | custom-call | bytes 1235968 | tf_op jit(solution)/shard_map/reduce_all/pallas_call | solution.py:250
  140.8 2.6 %all-to-all-start.6 = ((f32[32,1,128]{2,1,0:T(1,128)}), f32[32,1,128]{2,1,0:T(1,128)S(1)}, u32[]{:S(2)}, u32[]{:S(2)}) async-start(f32[32,1,128]{2,1,0:T(1,128)} %get-tuple-element.156), calls=%async_computation.7 | async-start | bytes 32768 | tf_op jit(solution)/shard_map/all_to_all | solution.py:741
  143.3 1.9 %finish_images.1 = bf16[64,32,64]{2,1,0:T(8,128)(2,1)} custom-call(bf16[2,64,128]{2,1,0:T(8,128)(2,1)} %get-tuple-element.148.refs_0_, bf16[2,64,128]{2,1,0:T(8,128)(2,1)S(1)} %collective-permute-done.15.refs_1_, bf16[2,64,128]{2,1,0:T(8,128)(2,1)S(1)} %collective-permute-done.16.refs_2_, bf16[2,64,128]{2,1,0:T(8,128)(2,1)S(1)} %collective-permute-done.20.refs_3_, ...), custom_call_target="tpu_custom_call" | custom-call | bytes 524288 | tf_op jit(solution)/shard_map/finish_images/pallas_call | solution.py:250
  145.2 5.2 %all-to-all-done.6.refs_0_ = f32[32,1,128]{2,1,0:T(1,128)S(1)} async-done(((f32[32,1,128]{2,1,0:T(1,128)}), f32[32,1,128]{2,1,0:T(1,128)S(1)}, u32[]{:S(2)}, u32[]{:S(2)}) %all-to-all-start.6) | async-done | bytes 16416 | tf_op jit(solution)/shard_map/all_to_all | solution.py:741
  150.4 2.9 %update.1 = (f32[288,128]{1,0:T(8,128)}, f32[288,128]{1,0:T(8,128)}, f32[288,128]{1,0:T(8,128)}, f32[576,128]{1,0:T(8,128)}, f32[576,128]{1,0:T(8,128)}, /*index...) custom-call(f32[32,1,128]{2,1,0:T(1,128)S(1)} %all-to-all-done.6.ref, ...), custom_call_target="tpu_custom_call" | custom-call | bytes 3254272 | tf_op jit(solution)/shard_map/update/pallas_call | solution.py:250
  (42 shorter events, 1.2 us)
Async XLA Ops:
  7.2 42.4 %all-gather.3.cloned.1.call-start = ((), (), s32[]{:S(2)}) async-start(), calls=%async_computation.9 | async-start | bytes 2064384 | tf_op jit(solution)/shard_map/all_gather | solution.py:808
  9.1 0.9 copy-start.1
  32.6 17.0 %copy-start.2 = (bf16[8,2,16,512]{3,2,1,0:T(8,128)(2,1)}, bf16[8,2,16,512]{3,2,1,0:T(8,128)(2,1)S(1)}, u32[]{:S(2)}) copy-start(bf16[8,2,16,512]{3,2,1,0:T(8,128)(2,1)S(1)} %all_to_all.35.refs_1_.refs_2_.refs_6_) | copy-start | bytes 786436
  32.6 6.4 %collective-permute-start.1 = (bf16[8,2,16,512]{3,2,1,0:T(8,128)(2,1)S(1)}, bf16[8,2,16,512]{3,2,1,0:T(8,128)(2,1)S(1)}, u32[]{:S(2)}, u32[]{:S(2)}) collective-permute-start(bf16[8,2,16,512]{3,2,1,0:T(8,128)(2,1)S(1)} %all_to_all.35.refs_1_.refs_2_.refs_6_), channel_id=1, source_target_pairs={{0,2},{1,3},{2,0},{3,1},{4,6},{5,7},{6,4},{7,5},{8,10},{9,11},{10,... | collective-permute-start | bytes 786440 | tf_op jit(solution)/shard_map/ppermute | solution.py:754
  34.0 4.9 %collective-permute-start = (bf16[8,2,16,512]{3,2,1,0:T(8,128)(2,1)S(1)}, bf16[8,2,16,512]{3,2,1,0:T(8,128)(2,1)S(1)}, u32[]{:S(2)}, u32[]{:S(2)}) collective-permute-start(bf16[8,2,16,512]{3,2,1,0:T(8,128)(2,1)S(1)} %all_to_all.35.refs_1_.refs_2_.refs_6_), channel_id=1, source_target_pairs={{0,1},{1,0},{2,3},{3,2},{4,5},{5,4},{6,7},{7,6},{8,9},{9,8},{10,11... | collective-permute-start | bytes 786440 | tf_op jit(solution)/shard_map/ppermute | solution.py:754
  38.9 10.6 %copy-start.3 = (bf16[8,2,16,512]{3,2,1,0:T(8,128)(2,1)}, bf16[8,2,16,512]{3,2,1,0:T(8,128)(2,1)S(1)}, u32[]{:S(2)}) copy-start(bf16[8,2,16,512]{3,2,1,0:T(8,128)(2,1)S(1)} %collective-permute-done.1.refs_3_.refs_4_.refs_8_) | copy-start | bytes 786436
  38.9 1.5 collective-permute-start.2
  38.9 10.6 %copy-start.4 = (bf16[8,2,16,512]{3,2,1,0:T(8,128)(2,1)}, bf16[8,2,16,512]{3,2,1,0:T(8,128)(2,1)S(1)}, u32[]{:S(2)}) copy-start(bf16[8,2,16,512]{3,2,1,0:T(8,128)(2,1)S(1)} %collective-permute-done.refs_2_.refs_3_.refs_7_) | copy-start | bytes 786436
  40.5 9.1 %copy-start.5 = (bf16[8,2,16,512]{3,2,1,0:T(8,128)(2,1)}, bf16[8,2,16,512]{3,2,1,0:T(8,128)(2,1)S(1)}, u32[]{:S(2)}) copy-start(bf16[8,2,16,512]{3,2,1,0:T(8,128)(2,1)S(1)} %collective-permute-done.2.refs_4_.refs_5_.refs_9_) | copy-start | bytes 786436
  52.6 12.9 %collective-permute-start.5 = (bf16[528,128]{1,0:T(8,128)(2,1)}, bf16[528,128]{1,0:T(8,128)(2,1)S(1)}, u32[]{:S(2)}, u32[]{:S(2)}) collective-permute-start(bf16[528,128]{1,0:T(8,128)(2,1)} %get-tuple-element.96.refs_0_.refs_8_.refs_4_.refs_1_), channel_id=1, source_target_pairs={{0,3},{1,2},{2,1},{3,0},{4,7},{5,6},{6,5},{7,4},{8,11},{9,10},{10,... | collective-permute-start | bytes 405512 | tf_op jit(solution)/shard_map/ppermute | solution.py:754
  52.7 12.8 %collective-permute-start.4 = (bf16[528,128]{1,0:T(8,128)(2,1)}, bf16[528,128]{1,0:T(8,128)(2,1)S(1)}, u32[]{:S(2)}, u32[]{:S(2)}) collective-permute-start(bf16[528,128]{1,0:T(8,128)(2,1)} %get-tuple-element.96.refs_0_.refs_8_.refs_4_.refs_1_), channel_id=1, source_target_pairs={{0,2},{1,3},{2,0},{3,1},{4,6},{5,7},{6,4},{7,5},{8,10},{9,11},{10,... | collective-permute-start | bytes 405512 | tf_op jit(solution)/shard_map/ppermute | solution.py:754
  54.2 11.3 %collective-permute-start.3 = (bf16[528,128]{1,0:T(8,128)(2,1)}, bf16[528,128]{1,0:T(8,128)(2,1)S(1)}, u32[]{:S(2)}, u32[]{:S(2)}) collective-permute-start(bf16[528,128]{1,0:T(8,128)(2,1)} %get-tuple-element.96.refs_0_.refs_8_.refs_4_.refs_1_), channel_id=1, source_target_pairs={{0,1},{1,0},{2,3},{3,2},{4,5},{5,4},{6,7},{7,6},{8,9},{9,8},{10,11... | collective-permute-start | bytes 405512 | tf_op jit(solution)/shard_map/ppermute | solution.py:754
  54.6 11.0 %all-to-all-start.1 = ((f32[32,4,128]{2,1,0:T(4,128)}), f32[32,4,128]{2,1,0:T(4,128)S(1)}, u32[]{:S(2)}, u32[]{:S(2)}) async-start(f32[32,4,128]{2,1,0:T(4,128)} %get-tuple-element.97), calls=%async_computation.1 | async-start | bytes 131072 | tf_op jit(solution)/shard_map/all_to_all | solution.py:741
  58.1 80.5 %reduce-scatter.2.cloned.1.call-start = ((), (), s32[]{:S(2)}) async-start(), calls=%async_computation.8 | async-start | bytes 1400832 | tf_op jit(solution)/shard_map/reduce_scatter | solution.py:914
  58.2 0.9 copy-start
  65.5 25.1 %collective-permute-start.6 = (bf16[2,896,128]{2,1,0:T(8,128)(2,1)}, bf16[2,896,128]{2,1,0:T(8,128)(2,1)S(1)}, u32[]{:S(2)}, u32[]{:S(2)}) collective-permute-start(bf16[2,896,128]{2,1,0:T(8,128)(2,1)} %get-tuple-element.116), channel_id=1, source_target_pairs={{0,1},{1,0},{2,3},{3,2},{4,5},{5,4},{6,7},{7,6},{8,9},{9,8},{10,11... | collective-permute-start | bytes 1376264 | tf_op jit(solution)/shard_map/ppermute | solution.py:754
  65.7 25.0 %collective-permute-start.7 = (bf16[2,896,128]{2,1,0:T(8,128)(2,1)}, bf16[2,896,128]{2,1,0:T(8,128)(2,1)S(1)}, u32[]{:S(2)}, u32[]{:S(2)}) collective-permute-start(bf16[2,896,128]{2,1,0:T(8,128)(2,1)} %get-tuple-element.117), channel_id=1, source_target_pairs={{0,2},{1,3},{2,0},{3,1},{4,6},{5,7},{6,4},{7,5},{8,10},{9,11},{10,... | collective-permute-start | bytes 1376264 | tf_op jit(solution)/shard_map/ppermute | solution.py:754
  66.2 24.5 %collective-permute-start.8 = (bf16[2,896,128]{2,1,0:T(8,128)(2,1)}, bf16[2,896,128]{2,1,0:T(8,128)(2,1)S(1)}, u32[]{:S(2)}, u32[]{:S(2)}) collective-permute-start(bf16[2,896,128]{2,1,0:T(8,128)(2,1)} %get-tuple-element.118), channel_id=1, source_target_pairs={{0,3},{1,2},{2,1},{3,0},{4,7},{5,6},{6,5},{7,4},{8,11},{9,10},{10,... | collective-permute-start | bytes 1376264 | tf_op jit(solution)/shard_map/ppermute | solution.py:754
  91.5 5.2 %collective-permute-start.10 = (bf16[512,128]{1,0:T(8,128)(2,1)}, bf16[512,128]{1,0:T(8,128)(2,1)S(1)}, u32[]{:S(2)}, u32[]{:S(2)}) collective-permute-start(bf16[512,128]{1,0:T(8,128)(2,1)} %get-tuple-element.124.refs_1_.refs_4_), channel_id=1, source_target_pairs={{0,2},{1,3},{2,0},{3,1},{4,6},{5,7},{6,4},{7,5},{8,10},{9,11},{10,... | collective-permute-start | bytes 393224 | tf_op jit(solution)/shard_map/ppermute | solution.py:754
  92.8 4.0 %copy-start.6 = (bf16[512,128]{1,0:T(8,128)(2,1)S(1)}, bf16[512,128]{1,0:T(8,128)(2,1)}, u32[]{:S(2)}) copy-start(bf16[512,128]{1,0:T(8,128)(2,1)} %get-tuple-element.124.refs_1_.refs_4_) | copy-start | bytes 393220
  96.8 1.4 collective-permute-start.9
  96.9 1.5 collective-permute-start.11
  101.6 16.7 %copy-start.7 = (bf16[1040,128]{1,0:T(8,128)(2,1)S(1)}, bf16[1040,128]{1,0:T(8,128)(2,1)}, u32[]{:S(2)}) copy-start(bf16[1040,128]{1,0:T(8,128)(2,1)} %get-tuple-element.129.refs_0_) | copy-start | bytes 798724
  101.6 10.3 %collective-permute-start.13 = (bf16[1040,128]{1,0:T(8,128)(2,1)}, bf16[1040,128]{1,0:T(8,128)(2,1)S(1)}, u32[]{:S(2)}, u32[]{:S(2)}) collective-permute-start(bf16[1040,128]{1,0:T(8,128)(2,1)} %get-tuple-element.129.refs_0_), channel_id=1, source_target_pairs={{0,2},{1,3},{2,0},{3,1},{4,6},{5,7},{6,4},{7,5},{8,10},{9,11},{10,... | collective-permute-start | bytes 798728 | tf_op jit(solution)/shard_map/ppermute | solution.py:754
  114.7 23.9 %all-to-all-start.5 = ((bf16[8,288,128]{2,1,0:T(8,128)(2,1)}), bf16[8,288,128]{2,1,0:T(8,128)(2,1)S(1)}, u32[]{:S(2)}, u32[]{:S(2)}) async-start(bf16[8,288,128]{2,1,0:T(8,128)(2,1)} %get-tuple-element.143), calls=%async_computation.6 | async-start | bytes 1179648 | tf_op jit(solution)/shard_map/all_to_all | solution.py:741
  118.3 1.6 %collective-permute-start.12 = (bf16[1040,128]{1,0:T(8,128)(2,1)S(1)}, bf16[1040,128]{1,0:T(8,128)(2,1)S(1)}, u32[]{:S(2)}, u32[]{:S(2)}) collective-permute-start(bf16[1040,128]{1,0:T(8,128)(2,1)S(1)} %copy-done.7), channel_id=1, source_target_pairs={{0,1},{1,0},{2,3},{3,2},{4,5},{5,4},{6,7},{7,6},{8,9},{9,8},{10,11... | collective-permute-start | bytes 798728 | tf_op jit(solution)/shard_map/ppermute | solution.py:754
  118.4 1.8 %collective-permute-start.14 = (bf16[1040,128]{1,0:T(8,128)(2,1)S(1)}, bf16[1040,128]{1,0:T(8,128)(2,1)S(1)}, u32[]{:S(2)}, u32[]{:S(2)}) collective-permute-start(bf16[1040,128]{1,0:T(8,128)(2,1)S(1)} %collective-permute-done.13.refs_2_), channel_id=1, source_target_pairs={{0,1},{1,0},{2,3},{3,2},{4,5},{5,4},{6,7},{7,6},{8,9},{9,8},{10,11... | collective-permute-start | bytes 798728 | tf_op jit(solution)/shard_map/ppermute | solution.py:754
  124.3 9.6 %collective-permute-start.15 = (bf16[2,64,128]{2,1,0:T(8,128)(2,1)}, bf16[2,64,128]{2,1,0:T(8,128)(2,1)S(1)}, u32[]{:S(2)}, u32[]{:S(2)}) collective-permute-start(bf16[2,64,128]{2,1,0:T(8,128)(2,1)} %get-tuple-element.134), channel_id=1, source_target_pairs={{0,4},{4,0},{8,12},{12,8},{16,20},{20,16},{24,28},{28,24},{1,5},{5... | collective-permute-start | bytes 98312 | tf_op jit(solution)/shard_map/ppermute | solution.py:754
  126.2 8.3 %collective-permute-start.16 = (bf16[2,64,128]{2,1,0:T(8,128)(2,1)}, bf16[2,64,128]{2,1,0:T(8,128)(2,1)S(1)}, u32[]{:S(2)}, u32[]{:S(2)}) collective-permute-start(bf16[2,64,128]{2,1,0:T(8,128)(2,1)} %get-tuple-element.135), channel_id=1, source_target_pairs={{0,8},{4,12},{8,0},{12,4},{16,24},{20,28},{24,16},{28,20},{1,9},{5... | collective-permute-start | bytes 98312 | tf_op jit(solution)/shard_map/ppermute | solution.py:754
  127.7 13.1 %collective-permute-start.17 = (bf16[2,64,128]{2,1,0:T(8,128)(2,1)}, bf16[2,64,128]{2,1,0:T(8,128)(2,1)S(1)}, u32[]{:S(2)}, u32[]{:S(2)}) collective-permute-start(bf16[2,64,128]{2,1,0:T(8,128)(2,1)} %get-tuple-element.136), channel_id=1, source_target_pairs={{0,16},{4,20},{8,24},{12,28},{16,0},{20,4},{24,8},{28,12},{1,17},{... | collective-permute-start | bytes 98312 | tf_op jit(solution)/shard_map/ppermute | solution.py:754
  130.0 10.7 %collective-permute-start.18 = (bf16[2,64,128]{2,1,0:T(8,128)(2,1)}, bf16[2,64,128]{2,1,0:T(8,128)(2,1)S(1)}, u32[]{:S(2)}, u32[]{:S(2)}) collective-permute-start(bf16[2,64,128]{2,1,0:T(8,128)(2,1)} %get-tuple-element.137), channel_id=1, source_target_pairs={{0,20},{4,16},{8,28},{12,24},{16,4},{20,0},{24,12},{28,8},{1,21},{... | collective-permute-start | bytes 98312 | tf_op jit(solution)/shard_map/ppermute | solution.py:754
  130.6 10.2 %collective-permute-start.19 = (bf16[2,64,128]{2,1,0:T(8,128)(2,1)}, bf16[2,64,128]{2,1,0:T(8,128)(2,1)S(1)}, u32[]{:S(2)}, u32[]{:S(2)}) collective-permute-start(bf16[2,64,128]{2,1,0:T(8,128)(2,1)} %get-tuple-element.138), channel_id=1, source_target_pairs={{0,28},{4,24},{8,20},{12,16},{16,12},{20,8},{24,4},{28,0},{1,29},{... | collective-permute-start | bytes 98312 | tf_op jit(solution)/shard_map/ppermute | solution.py:754
  133.9 6.9 %collective-permute-start.20 = (bf16[2,64,128]{2,1,0:T(8,128)(2,1)}, bf16[2,64,128]{2,1,0:T(8,128)(2,1)S(1)}, u32[]{:S(2)}, u32[]{:S(2)}) collective-permute-start(bf16[2,64,128]{2,1,0:T(8,128)(2,1)} %get-tuple-element.139), channel_id=1, source_target_pairs={{0,12},{4,8},{8,4},{12,0},{16,28},{20,24},{24,20},{28,16},{1,13},{... | collective-permute-start | bytes 98312 | tf_op jit(solution)/shard_map/ppermute | solution.py:754
  134.4 6.3 %collective-permute-start.21 = (bf16[2,64,128]{2,1,0:T(8,128)(2,1)}, bf16[2,64,128]{2,1,0:T(8,128)(2,1)S(1)}, u32[]{:S(2)}, u32[]{:S(2)}) collective-permute-start(bf16[2,64,128]{2,1,0:T(8,128)(2,1)} %get-tuple-element.140), channel_id=1, source_target_pairs={{0,24},{4,28},{8,16},{12,20},{16,8},{20,12},{24,0},{28,4},{1,25},{... | collective-permute-start | bytes 98312 | tf_op jit(solution)/shard_map/ppermute | solution.py:754
  140.8 9.6 %all-to-all-start.6 = ((f32[32,1,128]{2,1,0:T(1,128)}), f32[32,1,128]{2,1,0:T(1,128)S(1)}, u32[]{:S(2)}, u32[]{:S(2)}) async-start(f32[32,1,128]{2,1,0:T(1,128)} %get-tuple-element.156), calls=%async_computation.7 | async-start | bytes 32768 | tf_op jit(solution)/shard_map/all_to_all | solution.py:741
Sparse Core Ops, SparseCore 0:
  10.1 39.3 all-gather.2
  96.9 27.8 reduce-scatter.1

commit v7 on v6

--- a/solution.py
+++ b/solution.py
@@ -983,7 +983,7 @@
         ],
     )
     if eight:
-        order = (0, 1, 2, 4, 5, 7, 3, 6)
+        order = (0, 1, 2, 5, 4, 7, 3, 6)
         *sent, pay = lax.optimization_barrier((*(rows[k] for k in order), pay))
         rows = [sent[order.index(k)] for k in range(SIDE)]
     else:

time: 161 us -> 161 us (level)
  no operation moved by 1% of the time
where the time goes in v7:
time: 161 us; the launch traced here: 160 us
  blocking collectives  47.4 us (29%)
  Pallas kernels  36.1 us (22%)
  waiting for transfers between devices  30.6 us (19%)
  starting transfers between devices  29.8 us (19%)
  between operations  14.3 us (9%)
  local copies, waits for them, and re-layouts  1.86 us (1%)
    all_to_all x4, blocking collectives, exchange(): return lax.all_to_all(blocks, axes, 0, 0)  47.4 us
    pallas_call x14, Pallas kernels, call(): pl.pallas_call(kernel, out_shape=[pltpu.HBM(o.shape, o.dtype) if g.pinned...  36.1 us
    ppermute x22, starting transfers between devices, swap(): lax.ppermute(array, axis, [(i, i ^ bits) for i in range(lax.axis_size(axi...  20.1 us
    all_to_all x3, waiting for transfers between devices, exchange(): return lax.all_to_all(blocks, axes, 0, 0)  12 us
    all_to_all x3, starting transfers between devices, exchange(): return lax.all_to_all(blocks, axes, 0, 0)  9.66 us
    ppermute x22, waiting for transfers between devices, swap(): lax.ppermute(array, axis, [(i, i ^ bits) for i in range(lax.axis_size(axi...  9.49 us
    all_gather x1, waiting for transfers between devices, per_device(): gathered = lax.all_gather(own, everyone, axis_index_groups=rings())  9.06 us
  transfers between devices with their start and end apart: 27, of which 11 were waited for; matrix products, arithmetic and copies ran while one was open for 0% of the time, Pallas kernels for 17%

profile of v7, /device:TPU:0, one launch (start us, length us, event | category | flops | bytes accessed | tf_op | source)
XLA Modules:
  0.0 160.1 jit_solution(12638738343906673889)
XLA Ops:
  7.2 1.8 %pack_weights.1 = (bf16[896,128]{1,0:T(8,128)(2,1)}, f32[8,128]{1,0:T(8,128)}) custom-call(f32[288,128]{1,0:T(8,128)} %refs_3_.1, f32[32,128]{1,0:T(8,128)} %refs_11_.1, f32[576,128]{1,0:T(8,128)} %refs_7_.1), custom_call_target="tpu_custom_call" | custom-call | bytes 692224 | tf_op jit(solution)/shard_map/pack_weights/pallas_call | solution.py:250
  9.1 0.9 copy-done.1
  10.0 2.0 %pack_images.1 = (bf16[8,2,16,512]{3,2,1,0:T(8,128)(2,1)}, f32[512,128]{1,0:T(8,128)}) custom-call(bf16[896,128]{1,0:T(8,128)(2,1)S(1)} %copy-done.1, bf16[64,32,256]{2,1,0:T(8,128)(2,1)} %refs_1_.3, s32[8,64]{1,0:T(8,128)} %refs_2_.3), custom_call_target="tpu_custom_call" | custom-call | bytes 1574912 | tf_op jit(solution)/shard_map/pack_images/pallas_call | solution.py:250
  12.1 20.5 %all_to_all.35.refs_1_.refs_2_.refs_6_ = bf16[8,2,16,512]{3,2,1,0:T(8,128)(2,1)S(1)} all-to-all(bf16[8,2,16,512]{3,2,1,0:T(8,128)(2,1)} %get-tuple-element.94), channel_id=1, replica_groups=mesh['dp'=8,'chan'=4] {'dp'}, dimensions={0} | all-to-all | bytes 524288 | tf_op jit(solution)/shard_map/all_to_all | solution.py:741
  32.6 1.5 collective-permute-start.1
  34.0 4.9 %collective-permute-done.1.refs_3_.refs_4_.refs_8_ = bf16[8,2,16,512]{3,2,1,0:T(8,128)(2,1)S(1)} collective-permute-done((bf16[8,2,16,512]{3,2,1,0:T(8,128)(2,1)S(1)}, bf16[8,2,16,512]{3,2,1,0:T(8,128)(2,1)S(1)}, u32[]{:S(2)}, u32[]{:S(2)}) %collective-permute-start.1) | collective-permute-done | bytes 262176 | tf_op jit(solution)/shard_map/ppermute | solution.py:754
  39.0 1.5 collective-permute-done.2.refs_4_.refs_5_.refs_9_
  40.5 9.1 %all-gather.3.cloned.1.call-done = bf16[7168,128]{1,0:T(8,128)(2,1)} async-done(((bf16[896,128]{1,0:T(8,128)(2,1)}), bf16[7168,128]{1,0:T(8,128)(2,1)}) %all-gather.3.cloned.1.call-update) | async-done | bytes 1835024 | tf_op jit(solution)/shard_map/all_gather | solution.py:808
  49.5 3.1 %conv_first.1 = (bf16[528,128]{1,0:T(8,128)(2,1)}, f32[512,128]{1,0:T(8,128)}, f32[8,128]{1,0:T(8,128)}, f32[32,4,128]{2,1,0:T(4,128)}) custom-call(bf16[8,896,128]{2,1,0:T(8,128)(2,1)} %bitcast.7, bf16[8,2,16,512]{3,2,1,0:T(8,128)(2,1)} %copy-done.2, bf16[8,2,16,512]{3,2,1,0:T(8,128)(2,1)} %copy-done.4, bf16[8,2,16,512]{3,2,1,0:T(8,128)(2,1)} %copy-done.3, ...), custom_call_target="tpu_custom_call" | custom-call | flops 301989888 | bytes 3615744 | tf_op jit(solution)/shard_map/conv_first/pallas_call | solution.py:250
  52.7 1.5 collective-permute-start.4
  54.6 3.6 %all-to-all-start.1 = ((f32[32,4,128]{2,1,0:T(4,128)}), f32[32,4,128]{2,1,0:T(4,128)S(1)}, u32[]{:S(2)}, u32[]{:S(2)}) async-start(f32[32,4,128]{2,1,0:T(4,128)} %get-tuple-element.97), calls=%async_computation.1 | async-start | bytes 131072 | tf_op jit(solution)/shard_map/all_to_all | solution.py:741
  58.2 0.9 copy-done
  59.1 2.9 %hand_on.1 = (bf16[2,896,128]{2,1,0:T(8,128)(2,1)}, bf16[2,896,128]{2,1,0:T(8,128)(2,1)}, bf16[2,896,128]{2,1,0:T(8,128)(2,1)}, bf16[2,896,128]{2,1,0:T(8,128)(2,1)}) custom-call(bf16[528,128]{1,0:T(8,128)(2,1)S(1)} %copy-done, bf16[8,896,128]{2,1,0:T(8,128)(2,1)} %bitcast.8), custom_call_target="tpu_custom_call" | custom-call | bytes 3670016 | tf_op jit(solution)/shard_map/hand_on/pallas_call | solution.py:250
  61.9 3.6 %all-to-all-done.1 = f32[32,4,128]{2,1,0:T(4,128)S(1)} async-done(((f32[32,4,128]{2,1,0:T(4,128)}), f32[32,4,128]{2,1,0:T(4,128)S(1)}, u32[]{:S(2)}, u32[]{:S(2)}) %all-to-all-start.1) | async-done | bytes 65568 | tf_op jit(solution)/shard_map/all_to_all | solution.py:741
  65.7 0.5 collective-permute-start.7
  66.2 1.3 collective-permute-start.8
  67.5 3.8 %conv_second.1 = (bf16[512,512]{1,0:T(8,128)(2,1)S(1)}, f32[512,128]{1,0:T(8,128)S(1)}, f32[8,4,128]{2,1,0:T(4,128)S(1)}, f32[4,8,128]{2,1,0:T(8,128)}, f32[512,...) custom-call(bf16[528,128]{1,0:T(8,128)(2,1)} %get-tuple-element.96.refs_0_.refs_8_.refs_, ...), custom_call_target="tpu_custom_call" | custom-call | flops 603979776 | bytes 4710400 | tf_op jit(solution)/shard_map/conv_second/pallas_call | solution.py:250
  71.3 8.9 %all_to_all.36.refs_2_ = f32[8,4,128]{2,1,0:T(4,128)S(1)} all-to-all(f32[8,4,128]{2,1,0:T(4,128)S(1)} %get-tuple-element.110), channel_id=1, replica_groups=mesh['dp'=8,'chan'=4] {'dp'}, dimensions={0} | all-to-all | bytes 32768 | tf_op jit(solution)/shard_map/all_to_all | solution.py:741
  80.2 1.5 block_output.1
  81.7 8.9 %all_to_all.37.refs_7_ = f32[8,4,128]{2,1,0:T(4,128)S(1)} all-to-all(f32[8,4,128]{2,1,0:T(4,128)S(1)} %get-tuple-element.123), channel_id=1, replica_groups=mesh['dp'=8,'chan'=4] {'dp'}, dimensions={0} | all-to-all | bytes 32768 | tf_op jit(solution)/shard_map/all_to_all | solution.py:741
  90.7 0.8 grad_outputs.1
  91.5 1.3 collective-permute-start.10
  92.8 3.4 %grad_second.1 = bf16[8,608,128]{2,1,0:T(8,128)(2,1)} custom-call(bf16[512,512]{1,0:T(8,128)(2,1)S(1)} %get-tuple-element.125.refs_0_, bf16[512,128]{1,0:T(8,128)(2,1)} %get-tuple-element.124.refs_1_.refs_4_, bf16[8,2,16,512]{3,2,1,0:T(8,128)(2,1)} %copy-done.2, bf16[8,2,16,512]{3,2,1,0:T(8,128)(2,1)} %copy-done.4, bf16[8,2,16,512]{3,2,1,0:T(8,128)(2,1)} %copy-done.3, ...), custom_call_target="tpu_custom_call" | custom-call | flops 603979776 | bytes 3080192 | tf_op jit(solution)/shard_map/grad_second/pallas_call | solution.py:250
  96.1 0.6 collective-permute-done.10.refs_6_
  96.9 0.5 collective-permute-start.11
  97.4 0.8 collective-permute-done.9.refs_5_
  98.4 3.2 %grad_hidden.1 = (f32[512,128]{1,0:T(8,128)S(1)}, bf16[1040,128]{1,0:T(8,128)(2,1)}, f32[32,2,128]{2,1,0:T(2,128)S(1)}) custom-call(bf16[2,896,128]{2,1,0:T(8,128)(2,1)} %get-tuple-element.115.refs_0_.refs_11_, bf16[2,896,128]{2,1,0:T(8,128)(2,1)S(1)} %collective-permute-done.6.refs_0_.refs_1_.refs_12_, ...), custom_call_target="tpu_custom_call" | custom-call | flops 603979776 | bytes 3465216 | tf_op jit(solution)/shard_map/grad_hidden/pallas_call | solution.py:250
  101.6 1.3 collective-permute-start.13
  102.8 9.0 %all_to_all.38 = f32[32,2,128]{2,1,0:T(2,128)S(1)} all-to-all(f32[32,2,128]{2,1,0:T(2,128)S(1)} %get-tuple-element.130), channel_id=1, replica_groups=mesh['dp'=8,'chan'=4] {'dp','chan'}, dimensions={0} | all-to-all | bytes 65536 | tf_op jit(solution)/shard_map/all_to_all | solution.py:741
  111.8 2.8 %grad_first.1 = (bf16[8,288,128]{2,1,0:T(8,128)(2,1)}, f32[8,128]{1,0:T(8,128)}) custom-call(f32[512,128]{1,0:T(8,128)S(1)} %get-tuple-element.142.refs_0_, bf16[528,128]{1,0:T(8,128)(2,1)} %get-tuple-element.96.refs_0_.refs_8_.refs_4_.refs_1_, f32[8,4,2,128]{3,2,1,0:T(2,128)S(1)} %bitcast.4, f32[4,8,128]{2,1,0:T(8,128)} %get-tuple-element.128.refs_10_.refs_9_.refs_3_, ...), custom_call_target="tpu_custom_call" | custom-call | flops 301989888 | bytes 2354176 | tf_op jit(solution)/shard_map/grad_first/pallas_call | solution.py:250
  114.7 3.6 %all-to-all-start.5 = ((bf16[8,288,128]{2,1,0:T(8,128)(2,1)}), bf16[8,288,128]{2,1,0:T(8,128)(2,1)S(1)}, u32[]{:S(2)}, u32[]{:S(2)}) async-start(bf16[8,288,128]{2,1,0:T(8,128)(2,1)} %get-tuple-element.143), calls=%async_computation.6 | async-start | bytes 1179648 | tf_op jit(solution)/shard_map/all_to_all | solution.py:741
  118.4 0.4 collective-permute-start.14
  118.8 1.0 collective-permute-done.12.refs_1_
  119.9 0.4 collective-permute-done.14.refs_3_
  120.2 4.0 %grad_images.1 = (bf16[2,64,128]{2,1,0:T(8,128)(2,1)}, bf16[2,64,128]{2,1,0:T(8,128)(2,1)}, bf16[2,64,128]{2,1,0:T(8,128)(2,1)}, bf16[2,64,128]{2,1,0:T(8,128)(2...) custom-call(bf16[1040,128]{1,0:T(8,128)(2,1)} %get-tuple-element.129, ...), custom_call_target="tpu_custom_call" | custom-call | flops 301989888 | bytes 4014080 | tf_op jit(solution)/shard_map/grad_images/pallas_call | solution.py:250
  124.3 1.9 %collective-permute-start.15 = (bf16[2,64,128]{2,1,0:T(8,128)(2,1)}, bf16[2,64,128]{2,1,0:T(8,128)(2,1)S(1)}, u32[]{:S(2)}, u32[]{:S(2)}) collective-permute-start(bf16[2,64,128]{2,1,0:T(8,128)(2,1)} %get-tuple-element.134), channel_id=1, source_target_pairs={{0,4},{4,0},{8,12},{12,8},{16,20},{20,16},{24,28},{28,24},{1,5},{5... | collective-permute-start | bytes 98312 | tf_op jit(solution)/shard_map/ppermute | solution.py:754
  126.2 1.5 collective-permute-start.16
  127.7 2.4 %collective-permute-start.17 = (bf16[2,64,128]{2,1,0:T(8,128)(2,1)}, bf16[2,64,128]{2,1,0:T(8,128)(2,1)S(1)}, u32[]{:S(2)}, u32[]{:S(2)}) collective-permute-start(bf16[2,64,128]{2,1,0:T(8,128)(2,1)} %get-tuple-element.136), channel_id=1, source_target_pairs={{0,20},{4,16},{8,28},{12,24},{16,4},{20,0},{24,12},{28,8},{1,21},{... | collective-permute-start | bytes 98312 | tf_op jit(solution)/shard_map/ppermute | solution.py:754
  130.0 0.5 collective-permute-start.18
  130.6 3.3 %collective-permute-start.19 = (bf16[2,64,128]{2,1,0:T(8,128)(2,1)}, bf16[2,64,128]{2,1,0:T(8,128)(2,1)S(1)}, u32[]{:S(2)}, u32[]{:S(2)}) collective-permute-start(bf16[2,64,128]{2,1,0:T(8,128)(2,1)} %get-tuple-element.138), channel_id=1, source_target_pairs={{0,28},{4,24},{8,20},{12,16},{16,12},{20,8},{24,4},{28,0},{1,29},{... | collective-permute-start | bytes 98312 | tf_op jit(solution)/shard_map/ppermute | solution.py:754
  133.9 0.6 collective-permute-start.20
  134.4 0.9 collective-permute-start.21
  135.4 3.2 %all-to-all-done.5.refs_1_ = bf16[8,288,128]{2,1,0:T(8,128)(2,1)S(1)} async-done(((bf16[8,288,128]{2,1,0:T(8,128)(2,1)}), bf16[8,288,128]{2,1,0:T(8,128)(2,1)S(1)}, u32[]{:S(2)}, u32[]{:S(2)}) %all-to-all-start.5) | async-done | bytes 589856 | tf_op jit(solution)/shard_map/all_to_all | solution.py:741
  138.6 2.1 %reduce_all.1 = (f32[288,128]{1,0:T(8,128)}, f32[576,128]{1,0:T(8,128)}, f32[32,128]{1,0:T(8,128)}, f32[32,1,128]{2,1,0:T(1,128)}) custom-call(bf16[608,128]{1,0:T(8,128)(2,1)} %reduce-scatter.2.cloned.1.call-done.refs_0_, bf16[8,288,128]{2,1,0:T(8,128)(2,1)S(1)} %all-to-all-done.5.refs_1_, f32[8,128]{1,0:T(8,128)} %get-tuple-element.144.refs_2_, ...), custom_call_target="tpu_custom_call" | custom-call | bytes 1235968 | tf_op jit(solution)/shard_map/reduce_all/pallas_call | solution.py:250
  140.8 2.6 %all-to-all-start.6 = ((f32[32,1,128]{2,1,0:T(1,128)}), f32[32,1,128]{2,1,0:T(1,128)S(1)}, u32[]{:S(2)}, u32[]{:S(2)}) async-start(f32[32,1,128]{2,1,0:T(1,128)} %get-tuple-element.156), calls=%async_computation.7 | async-start | bytes 32768 | tf_op jit(solution)/shard_map/all_to_all | solution.py:741
  143.3 1.9 %finish_images.1 = bf16[64,32,64]{2,1,0:T(8,128)(2,1)} custom-call(bf16[2,64,128]{2,1,0:T(8,128)(2,1)} %get-tuple-element.148.refs_0_, bf16[2,64,128]{2,1,0:T(8,128)(2,1)S(1)} %collective-permute-done.15.refs_1_, bf16[2,64,128]{2,1,0:T(8,128)(2,1)S(1)} %collective-permute-done.16.refs_2_, bf16[2,64,128]{2,1,0:T(8,128)(2,1)S(1)} %collective-permute-done.20.refs_3_, ...), custom_call_target="tpu_custom_call" | custom-call | bytes 524288 | tf_op jit(solution)/shard_map/finish_images/pallas_call | solution.py:250
  145.2 5.2 %all-to-all-done.6.refs_0_ = f32[32,1,128]{2,1,0:T(1,128)S(1)} async-done(((f32[32,1,128]{2,1,0:T(1,128)}), f32[32,1,128]{2,1,0:T(1,128)S(1)}, u32[]{:S(2)}, u32[]{:S(2)}) %all-to-all-start.6) | async-done | bytes 16416 | tf_op jit(solution)/shard_map/all_to_all | solution.py:741
  150.4 2.9 %update.1 = (f32[288,128]{1,0:T(8,128)}, f32[288,128]{1,0:T(8,128)}, f32[288,128]{1,0:T(8,128)}, f32[576,128]{1,0:T(8,128)}, f32[576,128]{1,0:T(8,128)}, /*index...) custom-call(f32[32,1,128]{2,1,0:T(1,128)S(1)} %all-to-all-done.6.ref, ...), custom_call_target="tpu_custom_call" | custom-call | bytes 3254272 | tf_op jit(solution)/shard_map/update/pallas_call | solution.py:250
  (42 shorter events, 1.2 us)
Async XLA Ops:
  7.2 42.4 %all-gather.3.cloned.1.call-start = ((), (), s32[]{:S(2)}) async-start(), calls=%async_computation.9 | async-start | bytes 2064384 | tf_op jit(solution)/shard_map/all_gather | solution.py:808
  9.1 0.9 copy-start.1
  32.6 17.0 %copy-start.2 = (bf16[8,2,16,512]{3,2,1,0:T(8,128)(2,1)}, bf16[8,2,16,512]{3,2,1,0:T(8,128)(2,1)S(1)}, u32[]{:S(2)}) copy-start(bf16[8,2,16,512]{3,2,1,0:T(8,128)(2,1)S(1)} %all_to_all.35.refs_1_.refs_2_.refs_6_) | copy-start | bytes 786436
  32.6 6.4 %collective-permute-start.1 = (bf16[8,2,16,512]{3,2,1,0:T(8,128)(2,1)S(1)}, bf16[8,2,16,512]{3,2,1,0:T(8,128)(2,1)S(1)}, u32[]{:S(2)}, u32[]{:S(2)}) collective-permute-start(bf16[8,2,16,512]{3,2,1,0:T(8,128)(2,1)S(1)} %all_to_all.35.refs_1_.refs_2_.refs_6_), channel_id=1, source_target_pairs={{0,2},{1,3},{2,0},{3,1},{4,6},{5,7},{6,4},{7,5},{8,10},{9,11},{10,... | collective-permute-start | bytes 786440 | tf_op jit(solution)/shard_map/ppermute | solution.py:754
  34.0 4.9 %collective-permute-start = (bf16[8,2,16,512]{3,2,1,0:T(8,128)(2,1)S(1)}, bf16[8,2,16,512]{3,2,1,0:T(8,128)(2,1)S(1)}, u32[]{:S(2)}, u32[]{:S(2)}) collective-permute-start(bf16[8,2,16,512]{3,2,1,0:T(8,128)(2,1)S(1)} %all_to_all.35.refs_1_.refs_2_.refs_6_), channel_id=1, source_target_pairs={{0,1},{1,0},{2,3},{3,2},{4,5},{5,4},{6,7},{7,6},{8,9},{9,8},{10,11... | collective-permute-start | bytes 786440 | tf_op jit(solution)/shard_map/ppermute | solution.py:754
  38.9 10.6 %copy-start.3 = (bf16[8,2,16,512]{3,2,1,0:T(8,128)(2,1)}, bf16[8,2,16,512]{3,2,1,0:T(8,128)(2,1)S(1)}, u32[]{:S(2)}) copy-start(bf16[8,2,16,512]{3,2,1,0:T(8,128)(2,1)S(1)} %collective-permute-done.1.refs_3_.refs_4_.refs_8_) | copy-start | bytes 786436
  38.9 1.5 collective-permute-start.2
  38.9 10.6 %copy-start.4 = (bf16[8,2,16,512]{3,2,1,0:T(8,128)(2,1)}, bf16[8,2,16,512]{3,2,1,0:T(8,128)(2,1)S(1)}, u32[]{:S(2)}) copy-start(bf16[8,2,16,512]{3,2,1,0:T(8,128)(2,1)S(1)} %collective-permute-done.refs_2_.refs_3_.refs_7_) | copy-start | bytes 786436
  40.5 9.1 %copy-start.5 = (bf16[8,2,16,512]{3,2,1,0:T(8,128)(2,1)}, bf16[8,2,16,512]{3,2,1,0:T(8,128)(2,1)S(1)}, u32[]{:S(2)}) copy-start(bf16[8,2,16,512]{3,2,1,0:T(8,128)(2,1)S(1)} %collective-permute-done.2.refs_4_.refs_5_.refs_9_) | copy-start | bytes 786436
  52.6 12.9 %collective-permute-start.5 = (bf16[528,128]{1,0:T(8,128)(2,1)}, bf16[528,128]{1,0:T(8,128)(2,1)S(1)}, u32[]{:S(2)}, u32[]{:S(2)}) collective-permute-start(bf16[528,128]{1,0:T(8,128)(2,1)} %get-tuple-element.96.refs_0_.refs_8_.refs_4_.refs_1_), channel_id=1, source_target_pairs={{0,3},{1,2},{2,1},{3,0},{4,7},{5,6},{6,5},{7,4},{8,11},{9,10},{10,... | collective-permute-start | bytes 405512 | tf_op jit(solution)/shard_map/ppermute | solution.py:754
  52.7 12.8 %collective-permute-start.4 = (bf16[528,128]{1,0:T(8,128)(2,1)}, bf16[528,128]{1,0:T(8,128)(2,1)S(1)}, u32[]{:S(2)}, u32[]{:S(2)}) collective-permute-start(bf16[528,128]{1,0:T(8,128)(2,1)} %get-tuple-element.96.refs_0_.refs_8_.refs_4_.refs_1_), channel_id=1, source_target_pairs={{0,2},{1,3},{2,0},{3,1},{4,6},{5,7},{6,4},{7,5},{8,10},{9,11},{10,... | collective-permute-start | bytes 405512 | tf_op jit(solution)/shard_map/ppermute | solution.py:754
  54.2 11.3 %collective-permute-start.3 = (bf16[528,128]{1,0:T(8,128)(2,1)}, bf16[528,128]{1,0:T(8,128)(2,1)S(1)}, u32[]{:S(2)}, u32[]{:S(2)}) collective-permute-start(bf16[528,128]{1,0:T(8,128)(2,1)} %get-tuple-element.96.refs_0_.refs_8_.refs_4_.refs_1_), channel_id=1, source_target_pairs={{0,1},{1,0},{2,3},{3,2},{4,5},{5,4},{6,7},{7,6},{8,9},{9,8},{10,11... | collective-permute-start | bytes 405512 | tf_op jit(solution)/shard_map/ppermute | solution.py:754
  54.6 11.0 %all-to-all-start.1 = ((f32[32,4,128]{2,1,0:T(4,128)}), f32[32,4,128]{2,1,0:T(4,128)S(1)}, u32[]{:S(2)}, u32[]{:S(2)}) async-start(f32[32,4,128]{2,1,0:T(4,128)} %get-tuple-element.97), calls=%async_computation.1 | async-start | bytes 131072 | tf_op jit(solution)/shard_map/all_to_all | solution.py:741
  58.1 80.5 %reduce-scatter.2.cloned.1.call-start = ((), (), s32[]{:S(2)}) async-start(), calls=%async_computation.8 | async-start | bytes 1400832 | tf_op jit(solution)/shard_map/reduce_scatter | solution.py:914
  58.2 0.9 copy-start
  65.5 25.1 %collective-permute-start.6 = (bf16[2,896,128]{2,1,0:T(8,128)(2,1)}, bf16[2,896,128]{2,1,0:T(8,128)(2,1)S(1)}, u32[]{:S(2)}, u32[]{:S(2)}) collective-permute-start(bf16[2,896,128]{2,1,0:T(8,128)(2,1)} %get-tuple-element.116), channel_id=1, source_target_pairs={{0,1},{1,0},{2,3},{3,2},{4,5},{5,4},{6,7},{7,6},{8,9},{9,8},{10,11... | collective-permute-start | bytes 1376264 | tf_op jit(solution)/shard_map/ppermute | solution.py:754
  65.7 25.0 %collective-permute-start.7 = (bf16[2,896,128]{2,1,0:T(8,128)(2,1)}, bf16[2,896,128]{2,1,0:T(8,128)(2,1)S(1)}, u32[]{:S(2)}, u32[]{:S(2)}) collective-permute-start(bf16[2,896,128]{2,1,0:T(8,128)(2,1)} %get-tuple-element.117), channel_id=1, source_target_pairs={{0,2},{1,3},{2,0},{3,1},{4,6},{5,7},{6,4},{7,5},{8,10},{9,11},{10,... | collective-permute-start | bytes 1376264 | tf_op jit(solution)/shard_map/ppermute | solution.py:754
  66.2 24.5 %collective-permute-start.8 = (bf16[2,896,128]{2,1,0:T(8,128)(2,1)}, bf16[2,896,128]{2,1,0:T(8,128)(2,1)S(1)}, u32[]{:S(2)}, u32[]{:S(2)}) collective-permute-start(bf16[2,896,128]{2,1,0:T(8,128)(2,1)} %get-tuple-element.118), channel_id=1, source_target_pairs={{0,3},{1,2},{2,1},{3,0},{4,7},{5,6},{6,5},{7,4},{8,11},{9,10},{10,... | collective-permute-start | bytes 1376264 | tf_op jit(solution)/shard_map/ppermute | solution.py:754
  91.5 5.2 %collective-permute-start.10 = (bf16[512,128]{1,0:T(8,128)(2,1)}, bf16[512,128]{1,0:T(8,128)(2,1)S(1)}, u32[]{:S(2)}, u32[]{:S(2)}) collective-permute-start(bf16[512,128]{1,0:T(8,128)(2,1)} %get-tuple-element.124.refs_1_.refs_4_), channel_id=1, source_target_pairs={{0,2},{1,3},{2,0},{3,1},{4,6},{5,7},{6,4},{7,5},{8,10},{9,11},{10,... | collective-permute-start | bytes 393224 | tf_op jit(solution)/shard_map/ppermute | solution.py:754
  92.8 4.0 %copy-start.6 = (bf16[512,128]{1,0:T(8,128)(2,1)S(1)}, bf16[512,128]{1,0:T(8,128)(2,1)}, u32[]{:S(2)}) copy-start(bf16[512,128]{1,0:T(8,128)(2,1)} %get-tuple-element.124.refs_1_.refs_4_) | copy-start | bytes 393220
  96.8 1.4 collective-permute-start.9
  96.9 1.5 collective-permute-start.11
  101.6 16.7 %copy-start.7 = (bf16[1040,128]{1,0:T(8,128)(2,1)S(1)}, bf16[1040,128]{1,0:T(8,128)(2,1)}, u32[]{:S(2)}) copy-start(bf16[1040,128]{1,0:T(8,128)(2,1)} %get-tuple-element.129.refs_0_) | copy-start | bytes 798724
  101.6 10.3 %collective-permute-start.13 = (bf16[1040,128]{1,0:T(8,128)(2,1)}, bf16[1040,128]{1,0:T(8,128)(2,1)S(1)}, u32[]{:S(2)}, u32[]{:S(2)}) collective-permute-start(bf16[1040,128]{1,0:T(8,128)(2,1)} %get-tuple-element.129.refs_0_), channel_id=1, source_target_pairs={{0,2},{1,3},{2,0},{3,1},{4,6},{5,7},{6,4},{7,5},{8,10},{9,11},{10,... | collective-permute-start | bytes 798728 | tf_op jit(solution)/shard_map/ppermute | solution.py:754
  114.7 23.9 %all-to-all-start.5 = ((bf16[8,288,128]{2,1,0:T(8,128)(2,1)}), bf16[8,288,128]{2,1,0:T(8,128)(2,1)S(1)}, u32[]{:S(2)}, u32[]{:S(2)}) async-start(bf16[8,288,128]{2,1,0:T(8,128)(2,1)} %get-tuple-element.143), calls=%async_computation.6 | async-start | bytes 1179648 | tf_op jit(solution)/shard_map/all_to_all | solution.py:741
  118.3 1.6 %collective-permute-start.12 = (bf16[1040,128]{1,0:T(8,128)(2,1)S(1)}, bf16[1040,128]{1,0:T(8,128)(2,1)S(1)}, u32[]{:S(2)}, u32[]{:S(2)}) collective-permute-start(bf16[1040,128]{1,0:T(8,128)(2,1)S(1)} %copy-done.7), channel_id=1, source_target_pairs={{0,1},{1,0},{2,3},{3,2},{4,5},{5,4},{6,7},{7,6},{8,9},{9,8},{10,11... | collective-permute-start | bytes 798728 | tf_op jit(solution)/shard_map/ppermute | solution.py:754
  118.4 1.8 %collective-permute-start.14 = (bf16[1040,128]{1,0:T(8,128)(2,1)S(1)}, bf16[1040,128]{1,0:T(8,128)(2,1)S(1)}, u32[]{:S(2)}, u32[]{:S(2)}) collective-permute-start(bf16[1040,128]{1,0:T(8,128)(2,1)S(1)} %collective-permute-done.13.refs_2_), channel_id=1, source_target_pairs={{0,1},{1,0},{2,3},{3,2},{4,5},{5,4},{6,7},{7,6},{8,9},{9,8},{10,11... | collective-permute-start | bytes 798728 | tf_op jit(solution)/shard_map/ppermute | solution.py:754
  124.3 9.6 %collective-permute-start.15 = (bf16[2,64,128]{2,1,0:T(8,128)(2,1)}, bf16[2,64,128]{2,1,0:T(8,128)(2,1)S(1)}, u32[]{:S(2)}, u32[]{:S(2)}) collective-permute-start(bf16[2,64,128]{2,1,0:T(8,128)(2,1)} %get-tuple-element.134), channel_id=1, source_target_pairs={{0,4},{4,0},{8,12},{12,8},{16,20},{20,16},{24,28},{28,24},{1,5},{5... | collective-permute-start | bytes 98312 | tf_op jit(solution)/shard_map/ppermute | solution.py:754
  126.2 8.3 %collective-permute-start.16 = (bf16[2,64,128]{2,1,0:T(8,128)(2,1)}, bf16[2,64,128]{2,1,0:T(8,128)(2,1)S(1)}, u32[]{:S(2)}, u32[]{:S(2)}) collective-permute-start(bf16[2,64,128]{2,1,0:T(8,128)(2,1)} %get-tuple-element.135), channel_id=1, source_target_pairs={{0,8},{4,12},{8,0},{12,4},{16,24},{20,28},{24,16},{28,20},{1,9},{5... | collective-permute-start | bytes 98312 | tf_op jit(solution)/shard_map/ppermute | solution.py:754
  127.7 13.1 %collective-permute-start.17 = (bf16[2,64,128]{2,1,0:T(8,128)(2,1)}, bf16[2,64,128]{2,1,0:T(8,128)(2,1)S(1)}, u32[]{:S(2)}, u32[]{:S(2)}) collective-permute-start(bf16[2,64,128]{2,1,0:T(8,128)(2,1)} %get-tuple-element.136), channel_id=1, source_target_pairs={{0,20},{4,16},{8,28},{12,24},{16,4},{20,0},{24,12},{28,8},{1,21},{... | collective-permute-start | bytes 98312 | tf_op jit(solution)/shard_map/ppermute | solution.py:754
  130.0 10.7 %collective-permute-start.18 = (bf16[2,64,128]{2,1,0:T(8,128)(2,1)}, bf16[2,64,128]{2,1,0:T(8,128)(2,1)S(1)}, u32[]{:S(2)}, u32[]{:S(2)}) collective-permute-start(bf16[2,64,128]{2,1,0:T(8,128)(2,1)} %get-tuple-element.137), channel_id=1, source_target_pairs={{0,16},{4,20},{8,24},{12,28},{16,0},{20,4},{24,8},{28,12},{1,17},{... | collective-permute-start | bytes 98312 | tf_op jit(solution)/shard_map/ppermute | solution.py:754
  130.6 10.2 %collective-permute-start.19 = (bf16[2,64,128]{2,1,0:T(8,128)(2,1)}, bf16[2,64,128]{2,1,0:T(8,128)(2,1)S(1)}, u32[]{:S(2)}, u32[]{:S(2)}) collective-permute-start(bf16[2,64,128]{2,1,0:T(8,128)(2,1)} %get-tuple-element.138), channel_id=1, source_target_pairs={{0,28},{4,24},{8,20},{12,16},{16,12},{20,8},{24,4},{28,0},{1,29},{... | collective-permute-start | bytes 98312 | tf_op jit(solution)/shard_map/ppermute | solution.py:754
  133.9 6.9 %collective-permute-start.20 = (bf16[2,64,128]{2,1,0:T(8,128)(2,1)}, bf16[2,64,128]{2,1,0:T(8,128)(2,1)S(1)}, u32[]{:S(2)}, u32[]{:S(2)}) collective-permute-start(bf16[2,64,128]{2,1,0:T(8,128)(2,1)} %get-tuple-element.139), channel_id=1, source_target_pairs={{0,12},{4,8},{8,4},{12,0},{16,28},{20,24},{24,20},{28,16},{1,13},{... | collective-permute-start | bytes 98312 | tf_op jit(solution)/shard_map/ppermute | solution.py:754
  134.4 6.3 %collective-permute-start.21 = (bf16[2,64,128]{2,1,0:T(8,128)(2,1)}, bf16[2,64,128]{2,1,0:T(8,128)(2,1)S(1)}, u32[]{:S(2)}, u32[]{:S(2)}) collective-permute-start(bf16[2,64,128]{2,1,0:T(8,128)(2,1)} %get-tuple-element.140), channel_id=1, source_target_pairs={{0,24},{4,28},{8,16},{12,20},{16,8},{20,12},{24,0},{28,4},{1,25},{... | collective-permute-start | bytes 98312 | tf_op jit(solution)/shard_map/ppermute | solution.py:754
  140.8 9.6 %all-to-all-start.6 = ((f32[32,1,128]{2,1,0:T(1,128)}), f32[32,1,128]{2,1,0:T(1,128)S(1)}, u32[]{:S(2)}, u32[]{:S(2)}) async-start(f32[32,1,128]{2,1,0:T(1,128)} %get-tuple-element.156), calls=%async_computation.7 | async-start | bytes 32768 | tf_op jit(solution)/shard_map/all_to_all | solution.py:741
Sparse Core Ops, SparseCore 0:
  10.1 39.3 all-gather.2
  96.9 27.8 reduce-scatter.1
